TPU v7x, 32 devices: a whole 2x2x4 slice. The times are simulated.
32 devices in a mesh: groups: 2 (over x), tensor: 4 (over y, core), dp: 4 (over z).
Axes of the slice: x: 2, y: 2, z: 4, core: 2. Of those that a mesh axis runs over, the one named last changes fastest.
Arguments:
- layer_input: bfloat16 [1024, 8192], P(('groups', 'dp'), 'tensor'), parts along dimension 0, may hold values from -6 to 6
- out_grad: bfloat16 [1024, 8192], P(('groups', 'dp'), 'tensor'), parts along dimension 0, may hold values from -6 to 6
- gate_pre: bfloat16 [1024, 14336], P(('groups', 'tensor'), 'dp'), parts along dimension 0, may hold values from -6 to 6
- up_pre: bfloat16 [1024, 14336], P(('groups', 'tensor'), 'dp'), parts along dimension 0, may hold values from -6 to 6
- adapter_acts: bfloat16 [1024, 48], P('groups'), parts along dimension 0, may hold values from -6 to 6
- gate_weight: bfloat16 [8192, 14336], P('tensor', 'dp'), may hold values from -0.0625 to 0.0625
- up_weight: bfloat16 [8192, 14336], P('tensor', 'dp'), may hold values from -0.0625 to 0.0625
- down_weight: bfloat16 [14336, 8192], P('dp', 'tensor'), may hold values from -0.046875 to 0.046875
- adapter_a_gu: bfloat16 [4, 8192, 32], P(None, 'tensor'), may hold values from -0.5 to 0.5
- adapter_b_gu: bfloat16 [4, 32, 14336], P(None, None, 'dp'), may hold values from -0.046875 to 0.046875
- adapter_a_down: bfloat16 [4, 14336, 16], P(None, 'dp'), may hold values from -0.75 to 0.75
- adapter_b_down: bfloat16 [4, 16, 8192], P(None, None, 'tensor'), may hold values from -0.0625 to 0.0625
- block_tenant: int32 [8], P('groups'), parts along dimension 0, may hold values from 0 to 3, as said below
Outputs:
- block_input_grad: bfloat16 [1024, 8192], P(('groups', 'dp'), 'tensor'), parts along dimension 0
- grad_a_gu: float32 [8, 8192, 32], P('groups', 'tensor'), parts along dimension 0
- grad_b_gu: float32 [8, 32, 14336], P('groups', None, 'dp'), parts along dimension 0
- grad_a_down: float32 [8, 14336, 16], P('groups', 'dp'), parts along dimension 0
- grad_b_down: float32 [8, 16, 8192], P('groups', None, 'tensor'), parts along dimension 0
There are 2 independent parts, one for each index of `groups`. A program takes and returns all parts, laid end to end along the dimension named above; an argument that names none is the same for every part. Nothing has to cross between parts.
Inputs may be any that keep to these rules, and one draw needn't show every extreme that they name: `block_tenant`: entry b names the tenant of tokens b * 128 to (b + 1) * 128 - 1. Every tenant owns at least one block, and the block counts of any two tenants differ by at most one.
All inputs are finite; a program needn't handle non-finite values.
Results may differ from a plain program's by a relative error of at most 0.017.
Values may be sent and summed in bfloat16 or wider, within the bound.
No kernel may reach another device: no remote copies, remote signals or barrier semaphores. Data moves between devices by JAX's collectives and lax.ppermute only.
A program may use at most 192 MiB of HBM per device.

v0:
```python
import functools

import jax
import jax.numpy as jnp
from jax import lax
from jax.experimental import pallas as pl
from jax.experimental.pallas import tpu as pltpu
from jax.sharding import PartitionSpec as P

R = 16
TENANTS = 4
BLOCK = 128
SHARES = (1, 1)
LANES = 128
VMEM_LIMIT = 60 * 1024 * 1024

ADAPTER_SCALE = 2.0

NT = (((1,), (1,)), ((), ()))
NN = (((1,), (0,)), ((), ()))
TN = (((0,), (0,)), ((), ()))
NO_COST = pl.CostEstimate(flops=1, bytes_accessed=1, transcendentals=0)


def fdot(lhs, rhs, dims):
    return lax.dot_general(lhs, rhs, dims, preferred_element_type=jnp.float32)


def tile_of(width, most):
    tile = most
    while width % tile:
        tile -= LANES
    return tile


def whole(shape):
    return pl.BlockSpec(shape, lambda *_: (0,) * len(shape))


def tenant_of(meta, owner, own_t):
    return meta[2 + (owner * own_t) // BLOCK]


def owner_of(p, y, c, ny):
    return lax.rem(y + ny - p // 2, ny) * 2 + (c if p % 2 == 0 else 1 - c)


def hidden_kernel(sizes, meta, *refs):
    n_dp, n_t, g, own_t, rc, tile = sizes
    ny = n_t // 2
    pieces, (w_ref, bd_ref, ad_ref, keep_ref, send_ref, x_scr, p_scr) = refs[:n_dp], refs[n_dp:]
    step = pl.program_id(0)
    z, t = meta[0], meta[1]
    y, c = t // 2, t % 2
    width = w_ref.shape[1]
    hidden_width = keep_ref.shape[2] - LANES

    @pl.when(step == 0)
    def _():
        for k in range(n_dp):
            for j in range(g):
                owner = lax.rem(z + (n_dp - k), n_dp) * g + j
                away = jnp.where(owner % 2 == c, 0, ny)
                x_scr[away + lax.rem(owner // 2 + ny - y, ny)] = pieces[k][j]
        proj = fdot(x_scr[...].reshape(n_t * rc, width), bd_ref[...], NT)
        lane = lax.broadcasted_iota(jnp.int32, (rc, TENANTS * R), 1) // R
        zeros = jnp.zeros((rc, LANES - TENANTS * R), jnp.bfloat16)
        for s in range(n_t):
            owner = lax.rem(y + s % ny, ny) * 2 + (c if s < ny else 1 - c)
            own = jnp.where(lane == tenant_of(meta, owner, own_t), proj[s * rc : (s + 1) * rc], 0.0)
            p_scr[s * rc : (s + 1) * rc, :] = (ADAPTER_SCALE * own).astype(jnp.bfloat16)
            out = keep_ref if s < ny else send_ref
            out[s % ny, :, hidden_width:] = jnp.concatenate([own.astype(jnp.bfloat16), zeros], axis=1)

    acc = fdot(x_scr[...].reshape(n_t * rc, width), w_ref[...], NT) + fdot(p_scr[...], ad_ref[...], NN)
    acc = acc.astype(jnp.bfloat16).reshape(n_t, rc, tile)
    at = pl.ds(pl.multiple_of(step * tile, LANES), tile)
    keep_ref[:, :, at] = acc[:ny]
    send_ref[:, :, at] = acc[ny:]


def hidden_partial(meta, pieces, down_weight, b_down, a_down, n_t, own_t):
    n_dp = len(pieces)
    g, rc, width = pieces[0].shape
    ny = n_t // 2
    hidden_width = down_weight.shape[0]
    tile = tile_of(hidden_width, 896)
    low = TENANTS * R
    out = jax.ShapeDtypeStruct((ny, rc, hidden_width + LANES), jnp.bfloat16)
    return pl.pallas_call(
        functools.partial(hidden_kernel, (n_dp, n_t, g, own_t, rc, tile)),
        out_shape=(out, out),
        grid_spec=pltpu.PrefetchScalarGridSpec(
            num_scalar_prefetch=1,
            grid=(hidden_width // tile,),
            in_specs=[whole((g, rc, width))] * n_dp
            + [
                pl.BlockSpec((tile, width), lambda f, *_: (f, 0)),
                whole((low, width)),
                pl.BlockSpec((low, tile), lambda f, *_: (0, f)),
            ],
            out_specs=[whole(out.shape)] * 2,
            scratch_shapes=[
                pltpu.VMEM((n_t, rc, width), jnp.bfloat16),
                pltpu.VMEM((n_t * rc, low), jnp.bfloat16),
            ],
        ),
        compiler_params=pltpu.CompilerParams(vmem_limit_bytes=VMEM_LIMIT),
        cost_estimate=NO_COST,
        name="hidden_partial",
    )(meta, *pieces, down_weight, b_down, a_down)


def grads_of(total, factors):
    total = total.astype(jnp.float32)
    return [(total * factor[...].astype(jnp.float32)).astype(jnp.bfloat16) for factor in factors]


def input_kernel(sizes, meta, *refs):
    n_dp, n_t, g, own_t, rc, tile = sizes
    ny = n_t // 2
    factors, refs = [refs[2 * p : 2 * p + 2] for p in range(n_t)], refs[2 * n_t :]
    sums, (gw_ref, uw_ref, b_ref, a_ref) = refs[:2], refs[2:6]
    outs, (g_scr, u_scr, acc, query) = refs[6 : 6 + n_dp], refs[6 + n_dp :]
    step = pl.program_id(0)
    z, t = meta[0], meta[1]
    y, c = t // 2, t % 2
    rows = n_t * rc
    width = gw_ref.shape[0]

    @pl.when(step == 0)
    def _():
        acc[...] = jnp.zeros_like(acc)
        query[...] = jnp.zeros_like(query)

    for p in range(n_t):
        owner = owner_of(p, y, c, ny)
        slot = lax.rem(owner // g + n_dp - z, n_dp) * g + owner % g
        g_scr[slot], u_scr[slot] = grads_of(sums[p % 2][(ny - p // 2) % ny], factors[p])
    gate = g_scr[...].reshape(rows, tile).T
    up = u_scr[...].reshape(rows, tile).T
    low = lax.broadcasted_iota(jnp.int32, (2 * R * TENANTS, rows), 0) % (2 * R)
    query[...] += jnp.where(low < R, fdot(b_ref[...], gate, NN), fdot(b_ref[...], up, NN))
    cols = tile_of(width, 512)
    for d in range(0, width, cols):
        at = slice(d, d + cols)
        acc[at, :] += fdot(gw_ref[at, :], gate, NN) + fdot(uw_ref[at, :], up, NN)

    @pl.when(step == pl.num_programs(0) - 1)
    def _():
        lane = lax.broadcasted_iota(jnp.int32, (rc, 2 * R * TENANTS), 1) // (2 * R)
        turned = query[...].T
        own, shares = [], []
        for r in range(n_dp):
            share = []
            for j in range(g):
                s = r * g + j
                tenant = tenant_of(meta, lax.rem(z + r, n_dp) * g + j, own_t)
                mine = jnp.where(lane == tenant, turned[s * rc : (s + 1) * rc], 0.0)
                own.append(mine)
                share.append(sum(mine[:, e * 2 * R : (e + 1) * 2 * R] for e in range(TENANTS)))
            shares.append(jnp.concatenate(share, axis=0))
        share = jnp.concatenate(shares, axis=1).astype(jnp.bfloat16)
        own = (ADAPTER_SCALE * jnp.concatenate(own, axis=0)).astype(jnp.bfloat16)
        for d in range(0, width, cols):
            part = acc[d : d + cols, :].T + fdot(own, a_ref[:, d : d + cols], NN)
            part = part.astype(jnp.bfloat16)
            for r in range(n_dp):
                outs[r][:, d : d + cols] = part[r * g * rc : (r + 1) * g * rc]
        for r in range(n_dp):
            outs[r][:, width:] = share


def input_partial(meta, factors, q, sums, gate_weight, up_weight, b_gu, a_gu, n_dp, own_t):
    n_t = len(factors)
    ny, rc, _ = sums[0].shape
    g = n_t // n_dp
    width, hidden_width = gate_weight.shape
    tile = tile_of(hidden_width, 512)
    low = 2 * R * TENANTS
    rows = n_t * rc
    outs = [jax.ShapeDtypeStruct((g * rc, width + n_dp * 2 * R), jnp.bfloat16)] * n_dp
    return pl.pallas_call(
        functools.partial(input_kernel, (n_dp, n_t, g, own_t, rc, tile)),
        out_shape=outs,
        grid_spec=pltpu.PrefetchScalarGridSpec(
            num_scalar_prefetch=1,
            grid=(hidden_width // tile,),
            in_specs=[pl.BlockSpec((rc, tile), lambda f, *_: (q, f))] * (2 * n_t)
            + [pl.BlockSpec((ny, rc, tile), lambda f, *_: (0, 0, f))] * 2
            + [pl.BlockSpec((width, tile), lambda f, *_: (0, f))] * 2
            + [pl.BlockSpec((low, tile), lambda f, *_: (0, f)), whole((low, width))],
            out_specs=[whole(o.shape) for o in outs],
            scratch_shapes=[
                pltpu.VMEM((n_t, rc, tile), jnp.bfloat16),
                pltpu.VMEM((n_t, rc, tile), jnp.bfloat16),
                pltpu.VMEM((width, rows), jnp.float32),
                pltpu.VMEM((low, rows), jnp.float32),
            ],
        ),
        compiler_params=pltpu.CompilerParams(vmem_limit_bytes=VMEM_LIMIT),
        cost_estimate=NO_COST,
        name="input_partial",
    )(meta, *[x for pair in factors for x in pair], *sums, gate_weight, up_weight, b_gu, a_gu)


def left_of(left_ref, layer, owners):
    return jnp.concatenate([left_ref[layer, owner] for owner in owners], axis=1)


def down_outer_kernel(n_dp, g, chunks, meta, *refs):
    pieces, (left_ref, out_ref) = refs[: n_dp * chunks], refs[n_dp * chunks :]
    owners = [lax.rem(meta[0] + (n_dp - k), n_dp) * g + j for k in range(n_dp) for j in range(g)]
    right = [pieces[q * n_dp + k][j] for k in range(n_dp) for j in range(g) for q in range(chunks)]
    out = ADAPTER_SCALE * fdot(left_of(left_ref, 0, owners), jnp.concatenate(right, axis=0), NN)
    out_ref[...] = out.reshape(out_ref.shape)


def down_outer(meta, grads, left):
    n_dp, chunks = len(grads[0]), len(grads)
    pieces = [piece for pieces in grads for piece in pieces]
    g, _, width = pieces[0].shape
    tile = tile_of(width, 512)
    return pl.pallas_call(
        functools.partial(down_outer_kernel, n_dp, g, chunks),
        out_shape=jax.ShapeDtypeStruct((TENANTS, R, width), jnp.float32),
        grid_spec=pltpu.PrefetchScalarGridSpec(
            num_scalar_prefetch=1,
            grid=(width // tile,),
            in_specs=[
                pl.BlockSpec(piece.shape[:2] + (tile,), lambda f, *_: (0, 0, f)) for piece in pieces
            ]
            + [whole(left.shape)],
            out_specs=pl.BlockSpec((TENANTS, R, tile), lambda f, *_: (0, 0, f)),
        ),
        compiler_params=pltpu.CompilerParams(vmem_limit_bytes=VMEM_LIMIT),
        cost_estimate=NO_COST,
        name="down_outer",
    )(meta, *pieces, left)


def gate_up_outer_kernel(n_t, meta, *refs):
    ny = n_t // 2
    factors, refs = [refs[2 * p : 2 * p + 2] for p in range(n_t)], refs[2 * n_t :]
    sums, (left_ref, so_far, out_ref) = refs[:2], refs[2:]
    y, c = meta[1] // 2, meta[1] % 2
    owners = [owner_of(p, y, c, ny) for p in range(n_t)]
    grads = [grads_of(sums[p % 2][(ny - p // 2) % ny], factors[p]) for p in range(n_t)]
    for layer in range(2):
        right = jnp.concatenate([grad[layer] for grad in grads], axis=0)
        out = ADAPTER_SCALE * fdot(left_of(left_ref, layer, owners), right, NN)
        at = slice(layer * R, (layer + 1) * R)
        out_ref[:, at, :] = so_far[:, at, :] + out.reshape(TENANTS, R, out.shape[1])


def gate_up_outer(meta, factors, q, sums, left, so_far):
    n_t = len(factors)
    rc, width = sums[0].shape[1], factors[0][0].shape[1]
    tile = tile_of(width, 896)
    block = pl.BlockSpec((TENANTS, 2 * R, tile), lambda f, *_: (0, 0, f))
    return pl.pallas_call(
        functools.partial(gate_up_outer_kernel, n_t),
        out_shape=jax.ShapeDtypeStruct((TENANTS, 2 * R, width), jnp.float32),
        grid_spec=pltpu.PrefetchScalarGridSpec(
            num_scalar_prefetch=1,
            grid=(width // tile,),
            in_specs=[pl.BlockSpec((rc, tile), lambda f, *_: (q, f))] * (2 * n_t)
            + [pl.BlockSpec((n_t // 2, rc, tile), lambda f, *_: (0, 0, f))] * 2
            + [whole(left.shape), block],
            out_specs=block,
        ),
        compiler_params=pltpu.CompilerParams(vmem_limit_bytes=VMEM_LIMIT),
        cost_estimate=NO_COST,
        name="gate_up_outer",
    )(meta, *[x for pair in factors for x in pair], *sums, left, so_far)


def spread_kernel(tenant_at, rows, meta, *refs):
    parts, out_ref = refs[:-1], refs[-1]
    out_ref[...] = jnp.zeros_like(out_ref)
    at = 0
    for part in parts:
        for k in range(part.shape[0] // rows):
            tenant = tenant_at(at, meta)
            term = part[k * rows : (k + 1) * rows].astype(jnp.float32)
            out_ref[tenant] = out_ref[tenant] + ADAPTER_SCALE * term
            at += 1


def spread(meta, parts, tenant_at, rows, name):
    width = parts[0].shape[1]
    out = jax.ShapeDtypeStruct((TENANTS, rows, width), jnp.float32)
    tile = tile_of(width, 1024)
    return pl.pallas_call(
        functools.partial(spread_kernel, tenant_at, rows),
        out_shape=out,
        grid_spec=pltpu.PrefetchScalarGridSpec(
            num_scalar_prefetch=1,
            grid=(width // tile,),
            in_specs=[pl.BlockSpec((part.shape[0], tile), lambda f, *_: (0, f)) for part in parts],
            out_specs=pl.BlockSpec((TENANTS, rows, tile), lambda f, *_: (0, 0, f)),
        ),
        compiler_params=pltpu.CompilerParams(vmem_limit_bytes=VMEM_LIMIT),
        cost_estimate=NO_COST,
        name=name,
    )(meta, *parts)


def in_outer_kernel(n_dp, chunks, g, meta, *refs):
    shares, inputs, out_ref = refs[: n_dp * chunks], refs[n_dp * chunks : -1], refs[-1]
    out_ref[...] = jnp.zeros_like(out_ref)
    own_t = inputs[0].shape[0] // g
    rc = own_t // chunks
    for k in range(n_dp):
        tenant = meta[2 + lax.rem(meta[0] + n_dp - k, n_dp)]
        total = 0.0
        for q in range(chunks):
            query = 0.0
            for s in range(n_dp):
                at = (s + n_dp - k) % n_dp * 2 * R
                query = query + shares[q * n_dp + s][:, at : at + 2 * R].astype(jnp.float32)
            query = query.astype(jnp.bfloat16)
            for j in range(g):
                rows = inputs[k][j * own_t + q * rc : j * own_t + (q + 1) * rc, :]
                total = total + fdot(query[j * rc : (j + 1) * rc], rows, TN)
        out_ref[tenant] = out_ref[tenant] + ADAPTER_SCALE * total


def in_outer(meta, shares, inputs, g):
    n_dp, chunks = len(inputs), len(shares)
    shares = [share for there in shares for share in there]
    rows, width = inputs[0].shape
    rc = shares[0].shape[0]
    low = n_dp * 2 * R
    tile = tile_of(width, 1024)
    return pl.pallas_call(
        functools.partial(in_outer_kernel, n_dp, chunks, g),
        out_shape=jax.ShapeDtypeStruct((TENANTS, 2 * R, width), jnp.float32),
        grid_spec=pltpu.PrefetchScalarGridSpec(
            num_scalar_prefetch=1,
            grid=(width // tile,),
            in_specs=[pl.BlockSpec((rc, low), lambda f, *_: (0, width // low))] * len(shares)
            + [pl.BlockSpec((rows, tile), lambda f, *_: (0, f))] * n_dp,
            out_specs=pl.BlockSpec((TENANTS, 2 * R, tile), lambda f, *_: (0, 0, f)),
        ),
        compiler_params=pltpu.CompilerParams(vmem_limit_bytes=VMEM_LIMIT),
        cost_estimate=NO_COST,
        name="in_outer",
    )(meta, *shares, *inputs)


def ring(n, by):
    return [(k, (k + by) % n) for k in range(n)]


def add32(*terms):
    return sum(term.astype(jnp.float32) for term in terms)


def after(value, *done):
    return lax.optimization_barrier((value,) + done)[0]


def per_device(
    layer_input,
    out_grad,
    gate_pre,
    up_pre,
    adapter_acts,
    gate_weight,
    up_weight,
    down_weight,
    adapter_a_gu,
    adapter_b_gu,
    adapter_a_down,
    adapter_b_down,
    block_tenant,
):
    n_dp, n_t = lax.axis_size("dp"), lax.axis_size("tensor")
    ny = n_t // 2
    z, t = lax.axis_index("dp"), lax.axis_index("tensor")
    own_rows, width = out_grad.shape
    own_t, hidden_width = gate_pre.shape
    tokens = adapter_acts.shape[0]
    g = own_rows // own_t
    assert own_rows == BLOCK and g * own_t == own_rows and n_t == 2 * ny and n_t == g * n_dp
    chunks, at = [], 0
    for share in SHARES:
        chunks.append((at, own_t * share // sum(SHARES)))
        at += chunks[-1][1]

    meta = jnp.concatenate([jnp.stack([z, t]).astype(jnp.int32), block_tenant])
    b_down = adapter_b_down.reshape(TENANTS * R, width)
    a_down = jnp.transpose(adapter_a_down, (0, 2, 1)).reshape(TENANTS * R, hidden_width)
    b_gu = adapter_b_gu.reshape(TENANTS * 2 * R, hidden_width)
    a_gu = jnp.transpose(adapter_a_gu, (0, 2, 1)).reshape(TENANTS * 2 * R, width)

    pair = [(k, k ^ 1) for k in range(n_t)]
    z_next = ring(n_dp, 1)

    grads = [[out_grad.reshape(g, own_t, width)[:, at : at + rc]] for at, rc in chunks]
    for _ in range(n_dp - 1):
        for pieces in grads:
            pieces.append(lax.ppermute(pieces[-1], "dp", z_next))
    stored = (gate_pre, up_pre)
    far_stored = [[lax.ppermute(x, "tensor", ring(n_t, 2 * s)) for x in stored] for s in range(1, ny)]
    pair_stored = [lax.ppermute(x, "tensor", pair) for x in stored]

    onehot = (
        jnp.arange(TENANTS, dtype=jnp.int32)[:, None] == jnp.repeat(block_tenant, BLOCK)[None, :]
    ).astype(jnp.bfloat16)
    acts = adapter_acts.T.reshape(3, 1, R, tokens) * onehot[None, :, None, :]
    acts = acts.reshape(3, TENANTS * R, n_t, own_t).transpose(0, 2, 1, 3)

    def factors_of(gate_pre, up_pre):
        gate_value = gate_pre.astype(jnp.float32)
        up_value = up_pre.astype(jnp.float32)
        sigmoid_value = jax.nn.sigmoid(gate_value)
        dgate = up_value * sigmoid_value * (1.0 + gate_value * (1.0 - sigmoid_value))
        dup = gate_value * sigmoid_value
        return [x.astype(jnp.bfloat16) for x in (dgate, dup, dup * up_value)]

    def first(q, done):
        pieces = [after(grads[q][0], *done)] + grads[q][1:]
        keep, send = hidden_partial(meta, pieces, down_weight, b_down, a_down, n_t, own_t)
        return keep, lax.ppermute(send, "tensor", pair)

    def exchange(keep, other):
        mine = add32(keep, other).astype(jnp.bfloat16)
        return mine, [lax.ppermute(mine, "tensor", ring(n_t, 2 * s)) for s in range(1, ny)]

    def total(mine, far):
        turned = [jnp.roll(there, -(s + 1), axis=0) for s, there in enumerate(far)]
        both = add32(mine, *turned).astype(jnp.bfloat16)
        return [both, lax.ppermute(both, "tensor", pair)]

    def second(q, sums, done):
        sums = [after(sums[0], *done), sums[1]]
        outs = input_partial(meta, factors, q, sums, gate_weight, up_weight, b_gu, a_gu, n_dp, own_t)
        return [outs[0]] + [lax.ppermute(outs[r], "dp", ring(n_dp, r)) for r in range(1, n_dp)]

    def finish(there, rc):
        return add32(*[x[:, :width] for x in there]).astype(jnp.bfloat16).reshape(g, rc, width)

    keep_a, other_a = first(0, (grads[1][n_dp - 2],))
    mine_a, far_a = exchange(keep_a, other_a)
    inputs = [after(layer_input, grads[-1][-1])]
    for _ in range(n_dp - 1):
        inputs.append(lax.ppermute(inputs[-1], "dp", z_next))
    *near, hidden = factors_of(*stored)
    factors = [near, factors_of(*pair_stored)[:2]]
    keep_b, other_b = first(1, (mine_a, near[0], factors[1][0]))
    mine_b, far_b = exchange(keep_b, other_b)
    for there in far_stored:
        there = [after(x, keep_a) for x in there]
        beside = [lax.ppermute(x, "tensor", pair) for x in there]
        there[0] = after(there[0], mine_b)
        factors += [factors_of(*there)[:2], factors_of(*beside)[:2]]
    grad_b_down = down_outer(meta, grads, after(acts[2:], *[pair[0] for pair in factors]))
    sums_a = total(after(mine_a, grad_b_down), far_a)
    there_a = second(0, sums_a, ())
    left = [acts[:2, :, :, at : at + rc] for at, rc in chunks]
    zeros = jnp.zeros((TENANTS, 2 * R, hidden_width), jnp.float32)
    grad_b_gu = gate_up_outer(meta, factors, 0, sums_a, after(left[0], there_a[0]), zeros)
    sums_b = total(after(mine_b, grad_b_gu, inputs[-1], there_a[1]), far_b)

    low = jnp.concatenate([sums_a[0][0], sums_b[0][0]], axis=0)
    low = low[:, hidden_width : hidden_width + TENANTS * R]
    a_part = fdot(low, hidden, TN).reshape(TENANTS, R, hidden_width).sum(0).astype(jnp.bfloat16)
    a_column = [a_part] + [lax.ppermute(a_part, "tensor", ring(n_t, 2 * s)) for s in range(1, ny)]
    there_b = second(1, sums_b, (a_part,))

    a_column = [after(a_column[0], there_b[0])] + a_column[1:]
    a_beside = lax.ppermute(jnp.concatenate(a_column, axis=0), "tensor", pair)
    half_a = finish([after(there_a[0], there_b[0])] + there_a[1:], chunks[0][1])
    grad_b_gu = gate_up_outer(meta, factors, 1, sums_b, after(left[1], half_a), grad_b_gu)

    def column_tenant(p, m):
        owner = lax.rem(m[1] // 2 + ny - p % ny, ny) * 2
        return tenant_of(m, owner + (m[1] % 2 if p < ny else 1 - m[1] % 2), own_t)

    a_column[0] = after(a_column[0], grad_b_gu)
    grad_a_down = spread(meta, a_column + [a_beside], column_tenant, R, "spread_a_down")
    there_b[0] = after(there_b[0], grad_a_down)
    grad_a_gu = in_outer(meta, [there_a, there_b], inputs, g)
    half_b = finish(there_b, chunks[1][1])
    block_input_grad = jnp.concatenate([half_a, half_b], axis=1).reshape(own_rows, width)
    return (
        block_input_grad,
        grad_a_gu.transpose(0, 2, 1),
        grad_b_gu,
        grad_a_down.transpose(0, 2, 1),
        grad_b_down,
    )


def solution(mesh):
    placed = (
        P(("groups", "dp"), "tensor"),
        P(("groups", "dp"), "tensor"),
        P(("groups", "tensor"), "dp"),
        P(("groups", "tensor"), "dp"),
        P("groups", None),
        P("tensor", "dp"),
        P("tensor", "dp"),
        P("dp", "tensor"),
        P(None, "tensor", None),
        P(None, None, "dp"),
        P(None, "dp", None),
        P(None, None, "tensor"),
        P("groups"),
    )
    return jax.shard_map(
        per_device,
        mesh=mesh,
        in_specs=placed,
        out_specs=(
            P(("groups", "dp"), "tensor"),
            P("groups", "tensor", None),
            P("groups", None, "dp"),
            P("groups", "dp", None),
            P("groups", None, "tensor"),
        ),
        check_vma=False,
    )
```

profile of v0, /device:TPU:0, one launch (start us, length us, event | category | flops | bytes accessed | tf_op | source)
XLA Modules:
  0.0 192.0 jit_solution(16486202630714486229)
XLA Ops:
  1.7 3.1 %collective-permute-start.3 = (bf16[1,64,2048]{2,1,0:T(8,128)(2,1)S(1)}, bf16[1,64,2048]{2,1,0:T(8,128)(2,1)S(1)}, u32[]{:S(2)}, u32[]{:S(2)}) collective-permute-start(bf16[1,64,2048]{2,1,0:T(8,128)(2,1)S(1)} %get-tuple-element.38.refs_0_.refs_4_), channel_id=1, source_target_pairs={{0,1},{1,2},{2,3},{3,0},{4,5},{5,6},{6,7},{7,4},{8,9},{9,10},{10,1... | collective-permute-start | bytes 786440 | tf_op jit(solution)/shard_map/ppermute | solution.py:404
  6.4 7.6 %collective-permute-done.3.refs_1_.refs_5_ = bf16[1,64,2048]{2,1,0:T(8,128)(2,1)S(1)} collective-permute-done((bf16[1,64,2048]{2,1,0:T(8,128)(2,1)S(1)}, bf16[1,64,2048]{2,1,0:T(8,128)(2,1)S(1)}, u32[]{:S(2)}, u32[]{:S(2)}) %collective-permute-start.3) | collective-permute-done | bytes 262176 | tf_op jit(solution)/shard_map/ppermute | solution.py:404
  14.0 1.8 collective-permute-start.8
  16.0 3.6 %collective-permute-done.5.refs_1_ = bf16[1,64,2048]{2,1,0:T(8,128)(2,1)S(1)} collective-permute-done((bf16[1,64,2048]{2,1,0:T(8,128)(2,1)S(1)}, bf16[1,64,2048]{2,1,0:T(8,128)(2,1)S(1)}, u32[]{:S(2)}, u32[]{:S(2)}) %collective-permute-start.5) | collective-permute-done | bytes 262176 | tf_op jit(solution)/shard_map/ppermute | solution.py:404
  21.3 3.0 %collective-permute-done.4.refs_2_.refs_6_ = bf16[1,64,2048]{2,1,0:T(8,128)(2,1)S(1)} collective-permute-done((bf16[1,64,2048]{2,1,0:T(8,128)(2,1)S(1)}, bf16[1,64,2048]{2,1,0:T(8,128)(2,1)S(1)}, u32[]{:S(2)}, u32[]{:S(2)}) %collective-permute-start.4) | collective-permute-done | bytes 262176 | tf_op jit(solution)/shard_map/ppermute | solution.py:404
  24.4 3.6 %fusion.30 = (bf16[128,3584]{1,0:T(8,128)(2,1)}, bf16[128,3584]{1,0:T(8,128)(2,1)}) fusion(bf16[128,3584]{1,0:T(8,128)(2,1)} %param.15, bf16[128,3584]{1,0:T(8,128)(2,1)} %param.16), kind=kLoop, calls=%fused_computation.47 | loop fusion | flops 5963776 | bytes 3670016 | tf_op jit(solution)/shard_map/convert_element_type | solution.py:421
  28.0 5.6 %collective-permute-done.6.refs_2_ = bf16[1,64,2048]{2,1,0:T(8,128)(2,1)S(1)} collective-permute-done((bf16[1,64,2048]{2,1,0:T(8,128)(2,1)S(1)}, bf16[1,64,2048]{2,1,0:T(8,128)(2,1)S(1)}, u32[]{:S(2)}, u32[]{:S(2)}) %collective-permute-start.6) | collective-permute-done | bytes 262176 | tf_op jit(solution)/shard_map/ppermute | solution.py:404
  33.9 8.1 %collective-permute-done.7.refs_3_ = bf16[1,64,2048]{2,1,0:T(8,128)(2,1)S(1)} collective-permute-done((bf16[1,64,2048]{2,1,0:T(8,128)(2,1)S(1)}, bf16[1,64,2048]{2,1,0:T(8,128)(2,1)S(1)}, u32[]{:S(2)}, u32[]{:S(2)}) %collective-permute-start.7) | collective-permute-done | bytes 262176 | tf_op jit(solution)/shard_map/ppermute | solution.py:404
  43.4 11.3 %hidden_partial.2 = (bf16[2,64,3712]{2,1,0:T(8,128)(2,1)}, bf16[2,64,3712]{2,1,0:T(8,128)(2,1)}) custom-call(s32[6]{0:T(128)} %pad_add_fusion.meta, bf16[1,64,2048]{2,1,0:T(8,128)(2,1)} %copy-done.5, bf16[1,64,2048]{2,1,0:T(8,128)(2,1)} %copy-done.15, bf16[1,64,2048]{2,1,0:T(8,128)(2,1)} %copy-done.17, bf16[1,64,2048]{2,1,0:T(8,128)(2,1)} %copy-done.18, ...), custom_call_target="tpu_custom_call" | custom-call | flops 1 | bytes 1 | tf_op jit(solution)/shard_map/hidden_partial/pallas_call | solution.py:90
  57.3 3.3 %fusion.13 = (bf16[128,3584]{1,0:T(8,128)(2,1)}, bf16[128,3584]{1,0:T(8,128)(2,1)}) fusion(bf16[128,3584]{1,0:T(8,128)(2,1)S(1)} %collective-permute-done.1, bf16[128,3584]{1,0:T(8,128)(2,1)} %collective-permute-done), kind=kLoop, calls=%fused_computation.31 | loop fusion | flops 5963776 | bytes 3670016 | tf_op jit(solution)/shard_map/convert_element_type | solution.py:421
  60.5 10.7 %collective-permute-done.16.refs_9_ = bf16[128,2048]{1,0:T(8,128)(2,1)S(1)} collective-permute-done((bf16[128,2048]{1,0:T(8,128)(2,1)S(1)}, bf16[128,2048]{1,0:T(8,128)(2,1)S(1)}, u32[]{:S(2)}, u32[]{:S(2)}) %collective-permute-start.16) | collective-permute-done | bytes 524320 | tf_op jit(solution)/shard_map/ppermute | solution.py:449
  72.6 11.2 %hidden_partial.3 = (bf16[2,64,3712]{2,1,0:T(8,128)(2,1)}, bf16[2,64,3712]{2,1,0:T(8,128)(2,1)}) custom-call(s32[6]{0:T(128)} %pad_add_fusion.meta, bf16[1,64,2048]{2,1,0:T(8,128)(2,1)} %copy-done.4, bf16[1,64,2048]{2,1,0:T(8,128)(2,1)} %copy-done.14, bf16[1,64,2048]{2,1,0:T(8,128)(2,1)} %copy-done.16, bf16[1,64,2048]{2,1,0:T(8,128)(2,1)} %copy-done.19, ...), custom_call_target="tpu_custom_call" | custom-call | flops 1 | bytes 1 | tf_op jit(solution)/shard_map/hidden_partial/pallas_call | solution.py:90
  83.9 3.6 %fusion.27 = (bf16[128,3584]{1,0:T(8,128)(2,1)}, bf16[128,3584]{1,0:T(8,128)(2,1)}) fusion(bf16[128,3584]{1,0:T(8,128)(2,1)} %collective-permute-done.13, bf16[128,3584]{1,0:T(8,128)(2,1)} %collective-permute-done.12), kind=kLoop, calls=%fused_computation.45 | loop fusion | flops 5963776 | bytes 3670016 | tf_op jit(solution)/shard_map/convert_element_type | solution.py:421
  88.7 3.6 %fusion.20 = (bf16[128,3584]{1,0:T(8,128)(2,1)}, bf16[128,3584]{1,0:T(8,128)(2,1)}) fusion(bf16[128,3584]{1,0:T(8,128)(2,1)} %collective-permute-done.8, bf16[128,3584]{1,0:T(8,128)(2,1)} %collective-permute-done.2), kind=kLoop, calls=%fused_computation.38 | loop fusion | flops 5963776 | bytes 3670016 | tf_op jit(solution)/shard_map/convert_element_type | solution.py:421
  92.3 4.6 %down_outer.1 = f32[4,16,2048]{2,1,0:T(8,128)} custom-call(s32[6]{0:T(128)} %pad_add_fusion.meta, bf16[1,64,2048]{2,1,0:T(8,128)(2,1)} %copy-done.5, bf16[1,64,2048]{2,1,0:T(8,128)(2,1)} %copy-done.15, bf16[1,64,2048]{2,1,0:T(8,128)(2,1)} %copy-done.17, bf16[1,64,2048]{2,1,0:T(8,128)(2,1)} %copy-done.18, bf16[1,64,2048]{2,1,0:T(8,128)(2,1)} %copy-done.4, ...), custom_call_target="tpu_custom_call" | custom-call | flops 1 | bytes 1 | tf_op jit(solution)/shard_map/down_outer/pallas_call | solution.py:224
  100.8 19.3 %input_partial.2 = (bf16[64,2176]{1,0:T(8,128)(2,1)}, bf16[64,2176]{1,0:T(8,128)(2,1)}, bf16[64,2176]{1,0:T(8,128)(2,1)}, bf16[64,2176]{1,0:T(8,128)(2,1)}) custom-call(s32[6]{0:T(128)} %pad_add_fusion.meta, bf16[128,3584]{1,0:T(8,128)(2,1)} %get-tuple-element.72.refs_0_, bf16[128,3584]{1,0:T(8,128)(2,1)} %get-tuple-element.71.refs_1_, ...), custom_call_target="tpu_custom_call" | custom-call | flops 1 | bytes 1 | tf_op jit(solution)/shard_map/input_partial/pallas_call | solution.py:183
  120.1 2.2 %collective-permute-start.19 = (bf16[64,2176]{1,0:T(8,128)(2,1)}, bf16[64,2176]{1,0:T(8,128)(2,1)S(1)}, u32[]{:S(2)}, u32[]{:S(2)}) collective-permute-start(bf16[64,2176]{1,0:T(8,128)(2,1)} %get-tuple-element.47), channel_id=1, source_target_pairs={{0,1},{1,2},{2,3},{3,0},{4,5},{5,6},{6,7},{7,4},{8,9},{9,10},{10,1... | collective-permute-start | bytes 835592 | tf_op jit(solution)/shard_map/ppermute | solution.py:440
  124.9 6.3 %gate_up_outer.2.refs_11_ = f32[4,32,3584]{2,1,0:T(8,128)} custom-call(s32[6]{0:T(128)} %pad_add_fusion.meta, bf16[128,3584]{1,0:T(8,128)(2,1)} %get-tuple-element.72.refs_0_, bf16[128,3584]{1,0:T(8,128)(2,1)} %get-tuple-element.71.refs_1_, bf16[128,3584]{1,0:T(8,128)(2,1)} %get-tuple-element.70.refs_2_, bf16[128,3584]{1,0:T(8,128)(2,1)} %get-tuple-element.69.refs_3_, ...), custom_call_target="tpu_custom_call" | custom-call | flops 1 | bytes 1 | tf_op jit(solution)/shard_map/gate_up_outer/pallas_call | solution.py:261
  139.0 1.8 collective-permute-start.22
  141.8 19.3 %input_partial.3 = (bf16[64,2176]{1,0:T(8,128)(2,1)}, bf16[64,2176]{1,0:T(8,128)(2,1)}, bf16[64,2176]{1,0:T(8,128)(2,1)}, bf16[64,2176]{1,0:T(8,128)(2,1)}) custom-call(s32[6]{0:T(128)} %pad_add_fusion.meta, bf16[128,3584]{1,0:T(8,128)(2,1)} %get-tuple-element.72.refs_0_, bf16[128,3584]{1,0:T(8,128)(2,1)} %get-tuple-element.71.refs_1_, ...), custom_call_target="tpu_custom_call" | custom-call | flops 1 | bytes 1 | tf_op jit(solution)/shard_map/input_partial/pallas_call | solution.py:183
  164.6 6.3 %gate_up_outer.3 = f32[4,32,3584]{2,1,0:T(8,128)} custom-call(s32[6]{0:T(128)} %pad_add_fusion.meta, bf16[128,3584]{1,0:T(8,128)(2,1)} %get-tuple-element.72.refs_0_, bf16[128,3584]{1,0:T(8,128)(2,1)} %get-tuple-element.71.refs_1_, bf16[128,3584]{1,0:T(8,128)(2,1)} %get-tuple-element.70.refs_2_, bf16[128,3584]{1,0:T(8,128)(2,1)} %get-tuple-element.69.refs_3_, ...), custom_call_target="tpu_custom_call" | custom-call | flops 1 | bytes 1 | tf_op jit(solution)/shard_map/gate_up_outer/pallas_call | solution.py:261
  171.7 3.9 %spread_a_down.1 = f32[4,16,3584]{2,1,0:T(8,128)} custom-call(s32[6]{0:T(128)} %pad_add_fusion.meta, bf16[16,3584]{1,0:T(8,128)(2,1)} %copy-done.20, bf16[16,3584]{1,0:T(8,128)(2,1)} %copy-done.28, bf16[32,3584]{1,0:T(8,128)(2,1)} %copy-done.29), custom_call_target="tpu_custom_call" | custom-call | flops 1 | bytes 1 | tf_op jit(solution)/shard_map/spread_a_down/pallas_call | solution.py:294
  175.6 11.5 %collective-permute-done.27.refs_6_ = bf16[64,2176]{1,0:T(8,128)(2,1)S(1)} collective-permute-done((bf16[64,2176]{1,0:T(8,128)(2,1)}, bf16[64,2176]{1,0:T(8,128)(2,1)S(1)}, u32[]{:S(2)}, u32[]{:S(2)}) %collective-permute-start.27) | collective-permute-done | bytes 278560 | tf_op jit(solution)/shard_map/ppermute | solution.py:440
  188.0 4.0 %in_outer.1 = f32[4,32,2048]{2,1,0:T(8,128)} custom-call(s32[6]{0:T(128)} %pad_add_fusion.meta, bf16[64,2176]{1,0:T(8,128)(2,1)} %get-tuple-element.51.refs_0_, bf16[64,2176]{1,0:T(8,128)(2,1)} %copy-done.7, bf16[64,2176]{1,0:T(8,128)(2,1)} %copy-done.9, bf16[64,2176]{1,0:T(8,128)(2,1)} %copy-done.8, bf16[64,2176]{1,0:T(8,128)(2,1)} %get-tuple-element.57.refs_4_, ...), custom_call_target="tpu_custom_call" | custom-call | flops 1 | bytes 1 | tf_op jit(solution)/shard_map/in_outer/pallas_call | solution.py:336
  (140 shorter events, 31.7 us)
Async XLA Ops:
  1.7 12.2 %collective-permute-start.3 = (bf16[1,64,2048]{2,1,0:T(8,128)(2,1)S(1)}, bf16[1,64,2048]{2,1,0:T(8,128)(2,1)S(1)}, u32[]{:S(2)}, u32[]{:S(2)}) collective-permute-start(bf16[1,64,2048]{2,1,0:T(8,128)(2,1)S(1)} %get-tuple-element.38.refs_0_.refs_4_), channel_id=1, source_target_pairs={{0,1},{1,2},{2,3},{3,0},{4,5},{5,6},{6,7},{7,4},{8,9},{9,10},{10,1... | collective-permute-start | bytes 786440 | tf_op jit(solution)/shard_map/ppermute | solution.py:404
  4.8 14.8 %collective-permute-start.5 = (bf16[1,64,2048]{2,1,0:T(8,128)(2,1)S(1)}, bf16[1,64,2048]{2,1,0:T(8,128)(2,1)S(1)}, u32[]{:S(2)}, u32[]{:S(2)}) collective-permute-start(bf16[1,64,2048]{2,1,0:T(8,128)(2,1)S(1)} %get-tuple-element.33.refs_0_), channel_id=1, source_target_pairs={{0,1},{1,2},{2,3},{3,0},{4,5},{5,6},{6,7},{7,4},{8,9},{9,10},{10,1... | collective-permute-start | bytes 786440 | tf_op jit(solution)/shard_map/ppermute | solution.py:404
  14.0 10.4 %collective-permute-start.4 = (bf16[1,64,2048]{2,1,0:T(8,128)(2,1)S(1)}, bf16[1,64,2048]{2,1,0:T(8,128)(2,1)S(1)}, u32[]{:S(2)}, u32[]{:S(2)}) collective-permute-start(bf16[1,64,2048]{2,1,0:T(8,128)(2,1)S(1)} %collective-permute-done.3.refs_1_.refs_5_), channel_id=1, source_target_pairs={{0,1},{1,2},{2,3},{3,0},{4,5},{5,6},{6,7},{7,4},{8,9},{9,10},{10,1... | collective-permute-start | bytes 786440 | tf_op jit(solution)/shard_map/ppermute | solution.py:404
  14.0 42.8 %collective-permute-start.1 = (bf16[128,3584]{1,0:T(8,128)(2,1)}, bf16[128,3584]{1,0:T(8,128)(2,1)S(1)}, u32[]{:S(2)}, u32[]{:S(2)}) collective-permute-start(bf16[128,3584]{1,0:T(8,128)(2,1)} %param.15), channel_id=1, source_target_pairs={{0,4},{4,0},{8,12},{12,8},{1,5},{5,1},{9,13},{13,9},{2,6},{6,2},{1... | collective-permute-start | bytes 2752520 | tf_op jit(solution)/shard_map/ppermute | solution.py:407
  14.0 40.9 %collective-permute-start.8 = (bf16[128,3584]{1,0:T(8,128)(2,1)}, bf16[128,3584]{1,0:T(8,128)(2,1)}, u32[]{:S(2)}, u32[]{:S(2)}) collective-permute-start(bf16[128,3584]{1,0:T(8,128)(2,1)} %param.15), channel_id=1, source_target_pairs={{0,8},{4,12},{8,0},{12,4},{1,9},{5,13},{9,1},{13,5},{2,10},{6,14},... | collective-permute-start | bytes 2752520 | tf_op jit(solution)/shard_map/ppermute | solution.py:406
  15.8 41.5 %collective-permute-start = (bf16[128,3584]{1,0:T(8,128)(2,1)}, bf16[128,3584]{1,0:T(8,128)(2,1)}, u32[]{:S(2)}, u32[]{:S(2)}) collective-permute-start(bf16[128,3584]{1,0:T(8,128)(2,1)} %param.16), channel_id=1, source_target_pairs={{0,4},{4,0},{8,12},{12,8},{1,5},{5,1},{9,13},{13,9},{2,6},{6,2},{1... | collective-permute-start | bytes 2752520 | tf_op jit(solution)/shard_map/ppermute | solution.py:407
  19.6 37.2 %collective-permute-start.2 = (bf16[128,3584]{1,0:T(8,128)(2,1)}, bf16[128,3584]{1,0:T(8,128)(2,1)}, u32[]{:S(2)}, u32[]{:S(2)}) collective-permute-start(bf16[128,3584]{1,0:T(8,128)(2,1)} %param.16), channel_id=1, source_target_pairs={{0,8},{4,12},{8,0},{12,4},{1,9},{5,13},{9,1},{13,5},{2,10},{6,14},... | collective-permute-start | bytes 2752520 | tf_op jit(solution)/shard_map/ppermute | solution.py:406
  42.0 12.7 %collective-permute-start.10 = (bf16[1,64,2048]{2,1,0:T(8,128)(2,1)S(1)}, bf16[1,64,2048]{2,1,0:T(8,128)(2,1)S(1)}, u32[]{:S(2)}, u32[]{:S(2)}) collective-permute-start(bf16[1,64,2048]{2,1,0:T(8,128)(2,1)S(1)} %collective-permute-done.4.refs_2_.refs_6_), channel_id=1, source_target_pairs={{0,1},{1,2},{2,3},{3,0},{4,5},{5,6},{6,7},{7,4},{8,9},{9,10},{10,1... | collective-permute-start | bytes 786440 | tf_op jit(solution)/shard_map/ppermute | solution.py:404
  54.8 16.4 %collective-permute-start.9 = (bf16[2,64,3712]{2,1,0:T(8,128)(2,1)}, bf16[2,64,3712]{2,1,0:T(8,128)(2,1)S(1)}, u32[]{:S(2)}, u32[]{:S(2)}) collective-permute-start(bf16[2,64,3712]{2,1,0:T(8,128)(2,1)} %get-tuple-element.37), channel_id=1, source_target_pairs={{0,4},{4,0},{8,12},{12,8},{1,5},{5,1},{9,13},{13,9},{2,6},{6,2},{1... | collective-permute-start | bytes 2850824 | tf_op jit(solution)/shard_map/ppermute | solution.py:426
  54.9 16.3 %collective-permute-start.16 = (bf16[128,2048]{1,0:T(8,128)(2,1)S(1)}, bf16[128,2048]{1,0:T(8,128)(2,1)S(1)}, u32[]{:S(2)}, u32[]{:S(2)}) collective-permute-start(bf16[128,2048]{1,0:T(8,128)(2,1)S(1)} %copy-done.25), channel_id=1, source_target_pairs={{0,1},{1,2},{2,3},{3,0},{4,5},{5,6},{6,7},{7,4},{8,9},{9,10},{10,1... | collective-permute-start | bytes 1572872 | tf_op jit(solution)/shard_map/ppermute | solution.py:449
  56.7 27.1 %collective-permute-start.13 = (bf16[128,3584]{1,0:T(8,128)(2,1)}, bf16[128,3584]{1,0:T(8,128)(2,1)}, u32[]{:S(2)}, u32[]{:S(2)}) collective-permute-start(bf16[128,3584]{1,0:T(8,128)(2,1)} %collective-permute-done.8), channel_id=1, source_target_pairs={{0,4},{4,0},{8,12},{12,8},{1,5},{5,1},{9,13},{13,9},{2,6},{6,2},{1... | collective-permute-start | bytes 2752520 | tf_op jit(solution)/shard_map/ppermute | solution.py:456
  56.7 27.1 %collective-permute-start.12 = (bf16[128,3584]{1,0:T(8,128)(2,1)}, bf16[128,3584]{1,0:T(8,128)(2,1)}, u32[]{:S(2)}, u32[]{:S(2)}) collective-permute-start(bf16[128,3584]{1,0:T(8,128)(2,1)} %collective-permute-done.2), channel_id=1, source_target_pairs={{0,4},{4,0},{8,12},{12,8},{1,5},{5,1},{9,13},{13,9},{2,6},{6,2},{1... | collective-permute-start | bytes 2752520 | tf_op jit(solution)/shard_map/ppermute | solution.py:456
  71.2 27.1 %collective-permute-start.17 = (bf16[128,2048]{1,0:T(8,128)(2,1)S(1)}, bf16[128,2048]{1,0:T(8,128)(2,1)}, u32[]{:S(2)}, u32[]{:S(2)}) collective-permute-start(bf16[128,2048]{1,0:T(8,128)(2,1)S(1)} %collective-permute-done.16.refs_9_), channel_id=1, source_target_pairs={{0,1},{1,2},{2,3},{3,0},{4,5},{5,6},{6,7},{7,4},{8,9},{9,10},{10,1... | collective-permute-start | bytes 1572872 | tf_op jit(solution)/shard_map/ppermute | solution.py:449
  71.4 25.5 %collective-permute-start.14 = (bf16[2,64,3712]{2,1,0:T(8,128)(2,1)S(1)}, bf16[2,64,3712]{2,1,0:T(8,128)(2,1)S(1)}, u32[]{:S(2)}, u32[]{:S(2)}) collective-permute-start(bf16[2,64,3712]{2,1,0:T(8,128)(2,1)S(1)} %add_convert_fusion.3), channel_id=1, source_target_pairs={{0,8},{4,12},{8,0},{12,4},{1,9},{5,13},{9,1},{13,5},{2,10},{6,14},... | collective-permute-start | bytes 2850824 | tf_op jit(solution)/shard_map/ppermute | solution.py:430
  87.7 34.5 %collective-permute-start.20 = (bf16[2,64,3712]{2,1,0:T(8,128)(2,1)S(1)}, bf16[2,64,3712]{2,1,0:T(8,128)(2,1)}, u32[]{:S(2)}, u32[]{:S(2)}) collective-permute-start(bf16[2,64,3712]{2,1,0:T(8,128)(2,1)S(1)} %add_convert_fusion.2), channel_id=1, source_target_pairs={{0,8},{4,12},{8,0},{12,4},{1,9},{5,13},{9,1},{13,5},{2,10},{6,14},... | collective-permute-start | bytes 2850824 | tf_op jit(solution)/shard_map/ppermute | solution.py:430
  98.3 32.9 %collective-permute-start.18 = (bf16[128,2048]{1,0:T(8,128)(2,1)}, bf16[128,2048]{1,0:T(8,128)(2,1)}, u32[]{:S(2)}, u32[]{:S(2)}) collective-permute-start(bf16[128,2048]{1,0:T(8,128)(2,1)} %collective-permute-done.17.refs_10_), channel_id=1, source_target_pairs={{0,1},{1,2},{2,3},{3,0},{4,5},{5,6},{6,7},{7,4},{8,9},{9,10},{10,1... | collective-permute-start | bytes 1572872 | tf_op jit(solution)/shard_map/ppermute | solution.py:449
  120.1 11.1 %collective-permute-start.19 = (bf16[64,2176]{1,0:T(8,128)(2,1)}, bf16[64,2176]{1,0:T(8,128)(2,1)S(1)}, u32[]{:S(2)}, u32[]{:S(2)}) collective-permute-start(bf16[64,2176]{1,0:T(8,128)(2,1)} %get-tuple-element.47), channel_id=1, source_target_pairs={{0,1},{1,2},{2,3},{3,0},{4,5},{5,6},{6,7},{7,4},{8,9},{9,10},{10,1... | collective-permute-start | bytes 835592 | tf_op jit(solution)/shard_map/ppermute | solution.py:440
  131.5 9.4 %collective-permute-start.21 = (bf16[2,64,3712]{2,1,0:T(8,128)(2,1)S(1)}, bf16[2,64,3712]{2,1,0:T(8,128)(2,1)S(1)}, u32[]{:S(2)}, u32[]{:S(2)}) collective-permute-start(bf16[2,64,3712]{2,1,0:T(8,128)(2,1)S(1)} %add_convert_fusion.refs_8_), channel_id=1, source_target_pairs={{0,4},{4,0},{8,12},{12,8},{1,5},{5,1},{9,13},{13,9},{2,6},{6,2},{1... | collective-permute-start | bytes 2850824 | tf_op jit(solution)/shard_map/ppermute | solution.py:435
  136.2 27.2 %collective-permute-start.24 = (bf16[16,3584]{1,0:T(8,128)(2,1)S(1)}, bf16[16,3584]{1,0:T(8,128)(2,1)S(1)}, u32[]{:S(2)}, u32[]{:S(2)}) collective-permute-start(bf16[16,3584]{1,0:T(8,128)(2,1)S(1)} %reduce_sum.9.refs_0_), channel_id=1, source_target_pairs={{0,8},{4,12},{8,0},{12,4},{1,9},{5,13},{9,1},{13,5},{2,10},{6,14},... | collective-permute-start | bytes 344072 | tf_op jit(solution)/shard_map/ppermute | solution.py:470
  137.3 27.0 %collective-permute-start.23 = (bf16[64,2176]{1,0:T(8,128)(2,1)}, bf16[64,2176]{1,0:T(8,128)(2,1)S(1)}, u32[]{:S(2)}, u32[]{:S(2)}) collective-permute-start(bf16[64,2176]{1,0:T(8,128)(2,1)} %get-tuple-element.53), channel_id=1, source_target_pairs={{0,3},{1,0},{2,1},{3,2},{4,7},{5,4},{6,5},{7,6},{8,11},{9,8},{10,9... | collective-permute-start | bytes 835592 | tf_op jit(solution)/shard_map/ppermute | solution.py:440
  139.0 25.4 %collective-permute-start.22 = (bf16[64,2176]{1,0:T(8,128)(2,1)S(1)}, bf16[64,2176]{1,0:T(8,128)(2,1)S(1)}, u32[]{:S(2)}, u32[]{:S(2)}) collective-permute-start(bf16[64,2176]{1,0:T(8,128)(2,1)S(1)} %copy-done.32), channel_id=1, source_target_pairs={{0,2},{1,3},{2,0},{3,1},{4,6},{5,7},{6,4},{7,5},{8,10},{9,11},{10,... | collective-permute-start | bytes 835592 | tf_op jit(solution)/shard_map/ppermute | solution.py:440
  161.1 14.5 %collective-permute-start.28 = (bf16[64,2176]{1,0:T(8,128)(2,1)}, bf16[64,2176]{1,0:T(8,128)(2,1)S(1)}, u32[]{:S(2)}, u32[]{:S(2)}) collective-permute-start(bf16[64,2176]{1,0:T(8,128)(2,1)} %get-tuple-element.60), channel_id=1, source_target_pairs={{0,3},{1,0},{2,1},{3,2},{4,7},{5,4},{6,5},{7,6},{8,11},{9,8},{10,9... | collective-permute-start | bytes 835592 | tf_op jit(solution)/shard_map/ppermute | solution.py:440
  162.1 24.9 %collective-permute-start.27 = (bf16[64,2176]{1,0:T(8,128)(2,1)}, bf16[64,2176]{1,0:T(8,128)(2,1)S(1)}, u32[]{:S(2)}, u32[]{:S(2)}) collective-permute-start(bf16[64,2176]{1,0:T(8,128)(2,1)} %get-tuple-element.59), channel_id=1, source_target_pairs={{0,2},{1,3},{2,0},{3,1},{4,6},{5,7},{6,4},{7,5},{8,10},{9,11},{10,... | collective-permute-start | bytes 835592 | tf_op jit(solution)/shard_map/ppermute | solution.py:440
  163.4 23.7 %collective-permute-start.26 = (bf16[64,2176]{1,0:T(8,128)(2,1)}, bf16[64,2176]{1,0:T(8,128)(2,1)S(1)}, u32[]{:S(2)}, u32[]{:S(2)}) collective-permute-start(bf16[64,2176]{1,0:T(8,128)(2,1)} %get-tuple-element.58), channel_id=1, source_target_pairs={{0,1},{1,2},{2,3},{3,0},{4,5},{5,6},{6,7},{7,4},{8,9},{9,10},{10,1... | collective-permute-start | bytes 835592 | tf_op jit(solution)/shard_map/ppermute | solution.py:440
  (38 other events, 406.3 us)
where the time goes:
time: 193 us; the launch traced here: 192 us
  Pallas kernels  86.2 us (45%)
  waiting for transfers between devices  52.3 us (27%)
  starting transfers between devices  22.1 us (11%)
  other arithmetic  18 us (9%)
  local copies, waits for them, and re-layouts  10.6 us (5%)
    pallas_call x2, Pallas kernels, input_partial(): pl.pallas_call(functools.partial(input_kernel, (n_dp, n_t, g, own_t, rc,...  38.6 us
    ppermute x6, waiting for transfers between devices, per_device(): pieces.append(lax.ppermute(pieces[-1], 'dp', z_next))  28 us
    pallas_call x2, Pallas kernels, hidden_partial(): pl.pallas_call(functools.partial(hidden_kernel, (n_dp, n_t, g, own_t, rc,...  22.5 us
    convert_element_type x4, other arithmetic, factors_of(): return [x.astype(jnp.bfloat16) for x in (dgate, dup, dup * up_value)]  14 us
    pallas_call x2, Pallas kernels, gate_up_outer(): pl.pallas_call(functools.partial(gate_up_outer_kernel, n_t), out_shape=ja...  12.6 us
    ppermute x6, waiting for transfers between devices, second(): lax.ppermute(outs[r], 'dp', ring(n_dp, r))  11.5 us
    ppermute x3, waiting for transfers between devices, per_device(): inputs.append(lax.ppermute(inputs[-1], 'dp', z_next))  10.7 us
    ppermute x6, starting transfers between devices, second(): lax.ppermute(outs[r], 'dp', ring(n_dp, r))  8.88 us
  transfers between devices with their start and end apart: 29, of which 9 were waited for; matrix products, arithmetic and copies ran while one was open for 12% of the time, Pallas kernels for 43%

commit v1 on v0

--- a/solution.py
+++ b/solution.py
@@ -12,13 +12,17 @@
 BLOCK = 128
 SHARES = (1, 1)
 LANES = 128
-VMEM_LIMIT = 60 * 1024 * 1024
+VMEM_LIMIT = 12 * 1024 * 1024
+STREAM_LIMIT = 50 * 1024 * 1024
 
 ADAPTER_SCALE = 2.0
 
 NT = (((1,), (1,)), ((), ()))
 NN = (((1,), (0,)), ((), ()))
 TN = (((0,), (0,)), ((), ()))
+ANY = pl.BlockSpec(memory_space=pl.ANY)
+SMEM = pl.BlockSpec(memory_space=pltpu.SMEM)
+VMEM = pl.BlockSpec(memory_space=pltpu.VMEM)
 NO_COST = pl.CostEstimate(flops=1, bytes_accessed=1, transcendentals=0)
 
 
@@ -48,35 +52,45 @@
 def hidden_kernel(sizes, meta, *refs):
     n_dp, n_t, g, own_t, rc, tile = sizes
     ny = n_t // 2
-    pieces, (w_ref, bd_ref, ad_ref, keep_ref, send_ref, x_scr, p_scr) = refs[:n_dp], refs[n_dp:]
-    step = pl.program_id(0)
+    pieces, (w_ref, bd_ref, ad_ref, keep_ref, send_ref), refs = refs[:n_dp], refs[n_dp : n_dp + 5], refs[n_dp + 5 :]
+    x_scr, p_scr, w_scr, w_sem = refs
     z, t = meta[0], meta[1]
     y, c = t // 2, t % 2
-    width = w_ref.shape[1]
-    hidden_width = keep_ref.shape[2] - LANES
-
-    @pl.when(step == 0)
-    def _():
-        for k in range(n_dp):
-            for j in range(g):
-                owner = lax.rem(z + (n_dp - k), n_dp) * g + j
-                away = jnp.where(owner % 2 == c, 0, ny)
-                x_scr[away + lax.rem(owner // 2 + ny - y, ny)] = pieces[k][j]
-        proj = fdot(x_scr[...].reshape(n_t * rc, width), bd_ref[...], NT)
-        lane = lax.broadcasted_iota(jnp.int32, (rc, TENANTS * R), 1) // R
-        zeros = jnp.zeros((rc, LANES - TENANTS * R), jnp.bfloat16)
-        for s in range(n_t):
-            owner = lax.rem(y + s % ny, ny) * 2 + (c if s < ny else 1 - c)
-            own = jnp.where(lane == tenant_of(meta, owner, own_t), proj[s * rc : (s + 1) * rc], 0.0)
-            p_scr[s * rc : (s + 1) * rc, :] = (ADAPTER_SCALE * own).astype(jnp.bfloat16)
-            out = keep_ref if s < ny else send_ref
-            out[s % ny, :, hidden_width:] = jnp.concatenate([own.astype(jnp.bfloat16), zeros], axis=1)
-
-    acc = fdot(x_scr[...].reshape(n_t * rc, width), w_ref[...], NT) + fdot(p_scr[...], ad_ref[...], NN)
-    acc = acc.astype(jnp.bfloat16).reshape(n_t, rc, tile)
-    at = pl.ds(pl.multiple_of(step * tile, LANES), tile)
-    keep_ref[:, :, at] = acc[:ny]
-    send_ref[:, :, at] = acc[ny:]
+    hidden_width, width = w_ref.shape
+    steps = hidden_width // tile
+
+    def fetch(f):
+        rows = pl.ds(pl.multiple_of(f * tile, LANES), tile)
+        return pltpu.make_async_copy(w_ref.at[rows], w_scr.at[f], w_sem.at[f])
+
+    for f in range(steps):
+        fetch(f).start()
+
+    for k in range(n_dp):
+        for j in range(g):
+            owner = lax.rem(z + (n_dp - k), n_dp) * g + j
+            away = jnp.where(owner % 2 == c, 0, ny)
+            x_scr[away + lax.rem(owner // 2 + ny - y, ny)] = pieces[k][j]
+    proj = fdot(x_scr[...].reshape(n_t * rc, width), bd_ref[...], NT)
+    lane = lax.broadcasted_iota(jnp.int32, (rc, TENANTS * R), 1) // R
+    zeros = jnp.zeros((rc, LANES - TENANTS * R), jnp.bfloat16)
+    for s in range(n_t):
+        owner = lax.rem(y + s % ny, ny) * 2 + (c if s < ny else 1 - c)
+        own = jnp.where(lane == tenant_of(meta, owner, own_t), proj[s * rc : (s + 1) * rc], 0.0)
+        p_scr[s * rc : (s + 1) * rc, :] = (ADAPTER_SCALE * own).astype(jnp.bfloat16)
+        out = keep_ref if s < ny else send_ref
+        out[s % ny, :, hidden_width:] = jnp.concatenate([own.astype(jnp.bfloat16), zeros], axis=1)
+
+    def body(step, carry):
+        at = pl.ds(pl.multiple_of(step * tile, LANES), tile)
+        fetch(step).wait()
+        acc = fdot(x_scr[...].reshape(n_t * rc, width), w_scr[step], NT)
+        acc = (acc + fdot(p_scr[...], ad_ref[:, at], NN)).astype(jnp.bfloat16).reshape(n_t, rc, tile)
+        keep_ref[:, :, at] = acc[:ny]
+        send_ref[:, :, at] = acc[ny:]
+        return carry
+
+    lax.fori_loop(0, steps, body, 0)
 
 
 def hidden_partial(meta, pieces, down_weight, b_down, a_down, n_t, own_t):
@@ -84,28 +98,21 @@
     g, rc, width = pieces[0].shape
     ny = n_t // 2
     hidden_width = down_weight.shape[0]
-    tile = tile_of(hidden_width, 896)
+    tile = tile_of(hidden_width, 512)
     low = TENANTS * R
     out = jax.ShapeDtypeStruct((ny, rc, hidden_width + LANES), jnp.bfloat16)
     return pl.pallas_call(
         functools.partial(hidden_kernel, (n_dp, n_t, g, own_t, rc, tile)),
         out_shape=(out, out),
-        grid_spec=pltpu.PrefetchScalarGridSpec(
-            num_scalar_prefetch=1,
-            grid=(hidden_width // tile,),
-            in_specs=[whole((g, rc, width))] * n_dp
-            + [
-                pl.BlockSpec((tile, width), lambda f, *_: (f, 0)),
-                whole((low, width)),
-                pl.BlockSpec((low, tile), lambda f, *_: (0, f)),
-            ],
-            out_specs=[whole(out.shape)] * 2,
-            scratch_shapes=[
-                pltpu.VMEM((n_t, rc, width), jnp.bfloat16),
-                pltpu.VMEM((n_t * rc, low), jnp.bfloat16),
-            ],
-        ),
-        compiler_params=pltpu.CompilerParams(vmem_limit_bytes=VMEM_LIMIT),
+        in_specs=[SMEM] + [VMEM] * n_dp + [ANY] + [VMEM] * 2,
+        out_specs=[VMEM] * 2,
+        scratch_shapes=[
+            pltpu.VMEM((n_t, rc, width), jnp.bfloat16),
+            pltpu.VMEM((n_t * rc, low), jnp.bfloat16),
+            pltpu.VMEM((hidden_width // tile, tile, width), jnp.bfloat16),
+            pltpu.SemaphoreType.DMA((hidden_width // tile,)),
+        ],
+        compiler_params=pltpu.CompilerParams(vmem_limit_bytes=STREAM_LIMIT),
         cost_estimate=NO_COST,
         name="hidden_partial",
     )(meta, *pieces, down_weight, b_down, a_down)
@@ -117,58 +124,62 @@
 
 
 def input_kernel(sizes, meta, *refs):
-    n_dp, n_t, g, own_t, rc, tile = sizes
+    n_dp, n_t, g, own_t, rc, q, tile = sizes
     ny = n_t // 2
     factors, refs = [refs[2 * p : 2 * p + 2] for p in range(n_t)], refs[2 * n_t :]
     sums, (gw_ref, uw_ref, b_ref, a_ref) = refs[:2], refs[2:6]
-    outs, (g_scr, u_scr, acc, query) = refs[6 : 6 + n_dp], refs[6 + n_dp :]
-    step = pl.program_id(0)
+    outs, (g_scr, u_scr, q_scr, w_scr, w_sem) = refs[6 : 6 + n_dp], refs[6 + n_dp :]
     z, t = meta[0], meta[1]
     y, c = t // 2, t % 2
     rows = n_t * rc
-    width = gw_ref.shape[0]
-
-    @pl.when(step == 0)
-    def _():
-        acc[...] = jnp.zeros_like(acc)
-        query[...] = jnp.zeros_like(query)
+    width, hidden_width = gw_ref.shape
+    steps = width // tile
+
+    def fetch(f):
+        at = pl.ds(pl.multiple_of(f * tile, LANES), tile)
+        return [
+            pltpu.make_async_copy(w.at[at], w_scr.at[f, k], w_sem.at[f, k]) for k, w in enumerate((gw_ref, uw_ref))
+        ]
+
+    for f in range(steps):
+        for copy in fetch(f):
+            copy.start()
 
     for p in range(n_t):
         owner = owner_of(p, y, c, ny)
         slot = lax.rem(owner // g + n_dp - z, n_dp) * g + owner % g
-        g_scr[slot], u_scr[slot] = grads_of(sums[p % 2][(ny - p // 2) % ny], factors[p])
-    gate = g_scr[...].reshape(rows, tile).T
-    up = u_scr[...].reshape(rows, tile).T
-    low = lax.broadcasted_iota(jnp.int32, (2 * R * TENANTS, rows), 0) % (2 * R)
-    query[...] += jnp.where(low < R, fdot(b_ref[...], gate, NN), fdot(b_ref[...], up, NN))
-    cols = tile_of(width, 512)
-    for d in range(0, width, cols):
-        at = slice(d, d + cols)
-        acc[at, :] += fdot(gw_ref[at, :], gate, NN) + fdot(uw_ref[at, :], up, NN)
-
-    @pl.when(step == pl.num_programs(0) - 1)
-    def _():
-        lane = lax.broadcasted_iota(jnp.int32, (rc, 2 * R * TENANTS), 1) // (2 * R)
-        turned = query[...].T
-        own, shares = [], []
+        mine = [factor[q * rc : (q + 1) * rc, :] for factor in factors[p]]
+        g_scr[slot], u_scr[slot] = grads_of(sums[p % 2][(ny - p // 2) % ny, :, :hidden_width], mine)
+    q_gate = fdot(g_scr[...].reshape(rows, hidden_width), b_ref[...], NT)
+    q_up = fdot(u_scr[...].reshape(rows, hidden_width), b_ref[...], NT)
+    lane = lax.broadcasted_iota(jnp.int32, (rc, 2 * R * TENANTS), 1)
+    shares = []
+    for r in range(n_dp):
+        share = []
+        for j in range(g):
+            at = slice((r * g + j) * rc, (r * g + j + 1) * rc)
+            tenant = tenant_of(meta, lax.rem(z + r, n_dp) * g + j, own_t)
+            mine = jnp.where(lane % (2 * R) < R, q_gate[at], q_up[at])
+            mine = jnp.where(lane // (2 * R) == tenant, mine, 0.0)
+            q_scr[at, :] = (ADAPTER_SCALE * mine).astype(jnp.bfloat16)
+            share.append(sum(mine[:, e * 2 * R : (e + 1) * 2 * R] for e in range(TENANTS)))
+        shares.append(jnp.concatenate(share, axis=0))
+    share = jnp.concatenate(shares, axis=1).astype(jnp.bfloat16)
+    for r in range(n_dp):
+        outs[r][:, width:] = share
+
+    def body(step, carry):
+        at = pl.ds(pl.multiple_of(step * tile, LANES), tile)
+        for copy in fetch(step):
+            copy.wait()
+        acc = fdot(g_scr[...].reshape(rows, hidden_width), w_scr[step, 0], NT)
+        acc = acc + fdot(u_scr[...].reshape(rows, hidden_width), w_scr[step, 1], NT)
+        acc = (acc + fdot(q_scr[...], a_ref[:, at], NN)).astype(jnp.bfloat16)
         for r in range(n_dp):
-            share = []
-            for j in range(g):
-                s = r * g + j
-                tenant = tenant_of(meta, lax.rem(z + r, n_dp) * g + j, own_t)
-                mine = jnp.where(lane == tenant, turned[s * rc : (s + 1) * rc], 0.0)
-                own.append(mine)
-                share.append(sum(mine[:, e * 2 * R : (e + 1) * 2 * R] for e in range(TENANTS)))
-            shares.append(jnp.concatenate(share, axis=0))
-        share = jnp.concatenate(shares, axis=1).astype(jnp.bfloat16)
-        own = (ADAPTER_SCALE * jnp.concatenate(own, axis=0)).astype(jnp.bfloat16)
-        for d in range(0, width, cols):
-            part = acc[d : d + cols, :].T + fdot(own, a_ref[:, d : d + cols], NN)
-            part = part.astype(jnp.bfloat16)
-            for r in range(n_dp):
-                outs[r][:, d : d + cols] = part[r * g * rc : (r + 1) * g * rc]
-        for r in range(n_dp):
-            outs[r][:, width:] = share
+            outs[r][:, at] = acc[r * g * rc : (r + 1) * g * rc]
+        return carry
+
+    lax.fori_loop(0, steps, body, 0)
 
 
 def input_partial(meta, factors, q, sums, gate_weight, up_weight, b_gu, a_gu, n_dp, own_t):
@@ -176,29 +187,23 @@
     ny, rc, _ = sums[0].shape
     g = n_t // n_dp
     width, hidden_width = gate_weight.shape
-    tile = tile_of(hidden_width, 512)
+    tile = tile_of(width, 256)
     low = 2 * R * TENANTS
     rows = n_t * rc
     outs = [jax.ShapeDtypeStruct((g * rc, width + n_dp * 2 * R), jnp.bfloat16)] * n_dp
     return pl.pallas_call(
-        functools.partial(input_kernel, (n_dp, n_t, g, own_t, rc, tile)),
+        functools.partial(input_kernel, (n_dp, n_t, g, own_t, rc, q, tile)),
         out_shape=outs,
-        grid_spec=pltpu.PrefetchScalarGridSpec(
-            num_scalar_prefetch=1,
-            grid=(hidden_width // tile,),
-            in_specs=[pl.BlockSpec((rc, tile), lambda f, *_: (q, f))] * (2 * n_t)
-            + [pl.BlockSpec((ny, rc, tile), lambda f, *_: (0, 0, f))] * 2
-            + [pl.BlockSpec((width, tile), lambda f, *_: (0, f))] * 2
-            + [pl.BlockSpec((low, tile), lambda f, *_: (0, f)), whole((low, width))],
-            out_specs=[whole(o.shape) for o in outs],
-            scratch_shapes=[
-                pltpu.VMEM((n_t, rc, tile), jnp.bfloat16),
-                pltpu.VMEM((n_t, rc, tile), jnp.bfloat16),
-                pltpu.VMEM((width, rows), jnp.float32),
-                pltpu.VMEM((low, rows), jnp.float32),
-            ],
-        ),
-        compiler_params=pltpu.CompilerParams(vmem_limit_bytes=VMEM_LIMIT),
+        in_specs=[SMEM] + [VMEM] * (2 * n_t + 2) + [ANY] * 2 + [VMEM] * 2,
+        out_specs=[VMEM] * n_dp,
+        scratch_shapes=[
+            pltpu.VMEM((n_t, rc, hidden_width), jnp.bfloat16),
+            pltpu.VMEM((n_t, rc, hidden_width), jnp.bfloat16),
+            pltpu.VMEM((rows, low), jnp.bfloat16),
+            pltpu.VMEM((width // tile, 2, tile, hidden_width), jnp.bfloat16),
+            pltpu.SemaphoreType.DMA((width // tile, 2)),
+        ],
+        compiler_params=pltpu.CompilerParams(vmem_limit_bytes=STREAM_LIMIT),
         cost_estimate=NO_COST,
         name="input_partial",
     )(meta, *[x for pair in factors for x in pair], *sums, gate_weight, up_weight, b_gu, a_gu)
@@ -404,7 +409,7 @@
             pieces.append(lax.ppermute(pieces[-1], "dp", z_next))
     stored = (gate_pre, up_pre)
     far_stored = [[lax.ppermute(x, "tensor", ring(n_t, 2 * s)) for x in stored] for s in range(1, ny)]
-    pair_stored = [lax.ppermute(x, "tensor", pair) for x in stored]
+    pair_stored = [lax.ppermute(after(x, grads[0][2]), "tensor", pair) for x in stored]
 
     onehot = (
         jnp.arange(TENANTS, dtype=jnp.int32)[:, None] == jnp.repeat(block_tenant, BLOCK)[None, :]

time: 193 us -> 188 us (0.974)
  Pallas kernels: 86.2 us -> 67.1 us
  local copies, waits for them, and re-layouts: 10.6 us -> 21.1 us
  waiting for transfers between devices: 52.3 us -> 57.3 us
  other arithmetic: 18 us -> 14.8 us
    ppermute x3, waiting for transfers between devices: 10.7 us -> 0.01 us  [per_device(): inputs.append(lax.ppermute(inputs[-1], 'dp', z_next))]
    unnamed x66 -> x100, local copies, waits for them, and re-layouts: 4.31 us -> 12.9 us
    pallas_call x2, Pallas kernels: 22.5 us -> 16.1 us  [hidden_partial(): pl.pallas_call(functools.partial(hidden_kernel, (n_dp, n_t, g, own_t, rc,...]
    ppermute x2, waiting for transfers between devices: 1.79 us -> 8.21 us  [per_device(): lax.ppermute(x, 'tensor', ring(n_t, 2 * s))]
    pallas_call x2, Pallas kernels: 38.6 us -> 33.1 us  [input_partial(): pl.pallas_call(functools.partial(input_kernel, (n_dp, n_t, g, own_t, rc,...]
    mul x5, local copies, waits for them, and re-layouts: 0.11 us -> 4.65 us  [per_device(): acts = adapter_acts.T.reshape(3, 1, R, tokens) * onehot[None, :, None, :]]
    pallas_call x2, Pallas kernels: 12.6 us -> 8.18 us  [gate_up_outer(): pl.pallas_call(functools.partial(gate_up_outer_kernel, n_t), out_shape=ja...]
    ppermute x2, waiting for transfers between devices: 0.01 us -> 3.4 us  [exchange(): lax.ppermute(mine, 'tensor', ring(n_t, 2 * s))]
  transfers between devices with their start and end apart: 29 -> 29, of which waited for: 9 -> 10; matrix products, arithmetic and copies ran while one was open for 12% -> 12% of each run, Pallas kernels for 43% -> 34%
where the time goes in v1:
time: 188 us; the launch traced here: 187 us
  Pallas kernels  67.1 us (36%)
  waiting for transfers between devices  57.3 us (30%)
  starting transfers between devices  23.6 us (13%)
  local copies, waits for them, and re-layouts  21.1 us (11%)
  other arithmetic  14.8 us (8%)
    pallas_call x2, Pallas kernels, input_partial(): pl.pallas_call(functools.partial(input_kernel, (n_dp, n_t, g, own_t, rc,...  33.1 us
    ppermute x6, waiting for transfers between devices, per_device(): pieces.append(lax.ppermute(pieces[-1], 'dp', z_next))  30.7 us
    pallas_call x2, Pallas kernels, hidden_partial(): pl.pallas_call(functools.partial(hidden_kernel, (n_dp, n_t, g, own_t, rc,...  16.1 us
    ppermute x6, waiting for transfers between devices, second(): lax.ppermute(outs[r], 'dp', ring(n_dp, r))  14.6 us
    unnamed x100, local copies, waits for them, and re-layouts  12.9 us
    convert_element_type x4, other arithmetic, factors_of(): return [x.astype(jnp.bfloat16) for x in (dgate, dup, dup * up_value)]  11.4 us
    ppermute x6, starting transfers between devices, second(): lax.ppermute(outs[r], 'dp', ring(n_dp, r))  9.3 us
    ppermute x2, waiting for transfers between devices, per_device(): lax.ppermute(x, 'tensor', ring(n_t, 2 * s))  8.21 us
  transfers between devices with their start and end apart: 29, of which 10 were waited for; matrix products, arithmetic and copies ran while one was open for 12% of the time, Pallas kernels for 34%

profile of v1, /device:TPU:0, one launch (start us, length us, event | category | flops | bytes accessed | tf_op | source)
XLA Modules:
  0.0 186.8 jit_solution(2345631154902265482)
XLA Ops:
  1.7 3.1 %collective-permute-start.5 = (bf16[1,64,2048]{2,1,0:T(8,128)(2,1)S(1)}, bf16[1,64,2048]{2,1,0:T(8,128)(2,1)S(1)}, u32[]{:S(2)}, u32[]{:S(2)}) collective-permute-start(bf16[1,64,2048]{2,1,0:T(8,128)(2,1)S(1)} %get-tuple-element.42.refs_0_.refs_4_), channel_id=1, source_target_pairs={{0,1},{1,2},{2,3},{3,0},{4,5},{5,6},{6,7},{7,4},{8,9},{9,10},{10,1... | collective-permute-start | bytes 786440 | tf_op jit(solution)/shard_map/ppermute | solution.py:409
  6.4 7.5 %collective-permute-done.5.refs_1_.refs_5_ = bf16[1,64,2048]{2,1,0:T(8,128)(2,1)S(1)} collective-permute-done((bf16[1,64,2048]{2,1,0:T(8,128)(2,1)S(1)}, bf16[1,64,2048]{2,1,0:T(8,128)(2,1)S(1)}, u32[]{:S(2)}, u32[]{:S(2)}) %collective-permute-start.5) | collective-permute-done | bytes 262176 | tf_op jit(solution)/shard_map/ppermute | solution.py:409
  14.0 5.6 %collective-permute-done.refs_1_ = bf16[1,64,2048]{2,1,0:T(8,128)(2,1)S(1)} collective-permute-done((bf16[1,64,2048]{2,1,0:T(8,128)(2,1)S(1)}, bf16[1,64,2048]{2,1,0:T(8,128)(2,1)S(1)}, u32[]{:S(2)}, u32[]{:S(2)}) %collective-permute-start) | collective-permute-done | bytes 262176 | tf_op jit(solution)/shard_map/ppermute | solution.py:409
  20.3 4.9 %collective-permute-done.6.refs_2_.refs_6_ = bf16[1,64,2048]{2,1,0:T(8,128)(2,1)S(1)} collective-permute-done((bf16[1,64,2048]{2,1,0:T(8,128)(2,1)S(1)}, bf16[1,64,2048]{2,1,0:T(8,128)(2,1)S(1)}, u32[]{:S(2)}, u32[]{:S(2)}) %collective-permute-start.6) | collective-permute-done | bytes 262176 | tf_op jit(solution)/shard_map/ppermute | solution.py:409
  27.9 3.0 %collective-permute-done.1.refs_2_ = bf16[1,64,2048]{2,1,0:T(8,128)(2,1)} collective-permute-done((bf16[1,64,2048]{2,1,0:T(8,128)(2,1)S(1)}, bf16[1,64,2048]{2,1,0:T(8,128)(2,1)}, u32[]{:S(2)}, u32[]{:S(2)}) %collective-permute-start.1) | collective-permute-done | bytes 262176 | tf_op jit(solution)/shard_map/ppermute | solution.py:409
  31.4 4.2 %collective-permute-done.10.refs_3_.refs_7_ = bf16[1,64,2048]{2,1,0:T(8,128)(2,1)S(1)} collective-permute-done((bf16[1,64,2048]{2,1,0:T(8,128)(2,1)S(1)}, bf16[1,64,2048]{2,1,0:T(8,128)(2,1)S(1)}, u32[]{:S(2)}, u32[]{:S(2)}) %collective-permute-start.10) | collective-permute-done | bytes 262176 | tf_op jit(solution)/shard_map/ppermute | solution.py:409
  36.3 2.3 %fusion.30 = (bf16[128,3584]{1,0:T(8,128)(2,1)S(1)}, bf16[128,3584]{1,0:T(8,128)(2,1)S(1)}) fusion(bf16[128,3584]{1,0:T(8,128)(2,1)} %param.15, bf16[128,3584]{1,0:T(8,128)(2,1)} %param.16), kind=kLoop, calls=%fused_computation.47 | loop fusion | flops 5963776 | bytes 3670016 | tf_op jit(solution)/shard_map/convert_element_type | solution.py:426
  40.3 5.5 %collective-permute-done.7.refs_3_ = bf16[1,64,2048]{2,1,0:T(8,128)(2,1)} collective-permute-done((bf16[1,64,2048]{2,1,0:T(8,128)(2,1)}, bf16[1,64,2048]{2,1,0:T(8,128)(2,1)}, u32[]{:S(2)}, u32[]{:S(2)}) %collective-permute-start.7) | collective-permute-done | bytes 262176 | tf_op jit(solution)/shard_map/ppermute | solution.py:409
  50.0 8.3 %hidden_partial.2 = (bf16[2,64,3712]{2,1,0:T(8,128)(2,1)S(1)}, bf16[2,64,3712]{2,1,0:T(8,128)(2,1)S(1)}) custom-call(s32[6]{0:T(128)S(1)} %pad_add_fusion.meta, bf16[1,64,2048]{2,1,0:T(8,128)(2,1)S(1)} %get-tuple-element.37.refs_0_, bf16[1,64,2048]{2,1,0:T(8,128)(2,1)S(1)} %copy-done.28, bf16[1,64,2048]{2,1,0:T(8,128)(2,1)} %collective-permute-done.1.refs_2_, ...), custom_call_target="tpu_custom_call" | custom-call | flops 1 | bytes 1 | tf_op jit(solution)/shard_map/hidden_partial/pallas_call | solution.py:104
  58.4 8.2 %collective-permute-done.4 = bf16[128,3584]{1,0:T(8,128)(2,1)} collective-permute-done((bf16[128,3584]{1,0:T(8,128)(2,1)}, bf16[128,3584]{1,0:T(8,128)(2,1)}, u32[]{:S(2)}, u32[]{:S(2)}) %collective-permute-start.4) | collective-permute-done | bytes 917536 | tf_op jit(solution)/shard_map/ppermute | solution.py:411
  67.8 3.5 %fusion.13 = (bf16[128,3584]{1,0:T(8,128)(2,1)}, bf16[128,3584]{1,0:T(8,128)(2,1)}) fusion(bf16[128,3584]{1,0:T(8,128)(2,1)} %collective-permute-done.3, bf16[128,3584]{1,0:T(8,128)(2,1)} %collective-permute-done.2), kind=kLoop, calls=%fused_computation.31 | loop fusion | flops 5963776 | bytes 3670016 | tf_op jit(solution)/shard_map/convert_element_type | solution.py:426
  73.1 7.8 %hidden_partial.3 = (bf16[2,64,3712]{2,1,0:T(8,128)(2,1)S(1)}, bf16[2,64,3712]{2,1,0:T(8,128)(2,1)S(1)}) custom-call(s32[6]{0:T(128)S(1)} %pad_add_fusion.meta, bf16[1,64,2048]{2,1,0:T(8,128)(2,1)S(1)} %get-tuple-element.42.refs_0_.refs_4_, bf16[1,64,2048]{2,1,0:T(8,128)(2,1)S(1)} %collective-permute-done.5.refs_1_.refs_5_, ...), custom_call_target="tpu_custom_call" | custom-call | flops 1 | bytes 1 | tf_op jit(solution)/shard_map/hidden_partial/pallas_call | solution.py:104
  81.1 2.1 %fusion.27 = (bf16[128,3584]{1,0:T(8,128)(2,1)}, bf16[128,3584]{1,0:T(8,128)(2,1)}) fusion(bf16[128,3584]{1,0:T(8,128)(2,1)S(1)} %collective-permute-done.13, bf16[128,3584]{1,0:T(8,128)(2,1)S(1)} %collective-permute-done.12), kind=kLoop, calls=%fused_computation.45 | loop fusion | flops 5963776 | bytes 3670016 | tf_op jit(solution)/shard_map/convert_element_type | solution.py:426
  84.6 3.5 %fusion.20 = (bf16[128,3584]{1,0:T(8,128)(2,1)}, bf16[128,3584]{1,0:T(8,128)(2,1)}) fusion(bf16[128,3584]{1,0:T(8,128)(2,1)} %collective-permute-done.8, bf16[128,3584]{1,0:T(8,128)(2,1)} %collective-permute-done.4), kind=kLoop, calls=%fused_computation.38 | loop fusion | flops 5963776 | bytes 3670016 | tf_op jit(solution)/shard_map/convert_element_type | solution.py:426
  88.1 4.1 %down_outer.1 = f32[4,16,2048]{2,1,0:T(8,128)} custom-call(s32[6]{0:T(128)S(1)} %pad_add_fusion.meta, bf16[1,64,2048]{2,1,0:T(8,128)(2,1)S(1)} %get-tuple-element.37.refs_0_, bf16[1,64,2048]{2,1,0:T(8,128)(2,1)S(1)} %copy-done.28, bf16[1,64,2048]{2,1,0:T(8,128)(2,1)} %collective-permute-done.1.refs_2_, bf16[1,64,2048]{2,1,0:T(8,128)(2,1)} %collective-permute-done.7.refs_3_, ...), custom_call_target="tpu_custom_call" | custom-call | flops 1 | bytes 1 | tf_op jit(solution)/shard_map/down_outer/pallas_call | solution.py:229
  92.2 3.4 %collective-permute-done.14 = bf16[2,64,3712]{2,1,0:T(8,128)(2,1)S(1)} collective-permute-done((bf16[2,64,3712]{2,1,0:T(8,128)(2,1)S(1)}, bf16[2,64,3712]{2,1,0:T(8,128)(2,1)S(1)}, u32[]{:S(2)}, u32[]{:S(2)}) %collective-permute-start.14) | collective-permute-done | bytes 950304 | tf_op jit(solution)/shard_map/ppermute | solution.py:435
  99.5 16.5 %input_partial.2 = (bf16[64,2176]{1,0:T(8,128)(2,1)S(1)}, bf16[64,2176]{1,0:T(8,128)(2,1)S(1)}, bf16[64,2176]{1,0:T(8,128)(2,1)S(1)}, bf16[64,2176]{1,0:T(8,128)(2,1)S(1)}) custom-call(s32[6]{0:T(128)S(1)} %pad_add_fusion.meta, bf16[128,3584]{1,0:T(8,128)(2,1)S(1)} %get-tuple-element.76.refs_0_, bf16[128,3584]{1,0:T(8,128)(2,1)S(1)} %get-tuple-element.75.refs_1_, ...), custom_call_target="tpu_custom_call" | custom-call | flops 1 | bytes 1 | tf_op jit(solution)/shard_map/input_partial/pallas_call | solution.py:194
  117.5 2.6 %collective-permute-start.19 = (bf16[64,2176]{1,0:T(8,128)(2,1)S(1)}, bf16[64,2176]{1,0:T(8,128)(2,1)S(1)}, u32[]{:S(2)}, u32[]{:S(2)}) collective-permute-start(bf16[64,2176]{1,0:T(8,128)(2,1)S(1)} %get-tuple-element.51), channel_id=1, source_target_pairs={{0,1},{1,2},{2,3},{3,0},{4,5},{5,6},{6,7},{7,4},{8,9},{9,10},{10,1... | collective-permute-start | bytes 835592 | tf_op jit(solution)/shard_map/ppermute | solution.py:445
  124.0 3.1 %gate_up_outer.2.refs_11_ = f32[4,32,3584]{2,1,0:T(8,128)S(1)} custom-call(s32[6]{0:T(128)S(1)} %pad_add_fusion.meta, bf16[128,3584]{1,0:T(8,128)(2,1)S(1)} %get-tuple-element.76.refs_0_, bf16[128,3584]{1,0:T(8,128)(2,1)S(1)} %get-tuple-element.75.refs_1_, bf16[128,3584]{1,0:T(8,128)(2,1)S(1)} %copy-done.2, bf16[128,3584]{1,0:T(8,128)(2,1)S(1)} %copy-done, ...), custom_call_target="tpu_custom_call" | custom-call | flops 1 | bytes 1 | tf_op jit(solution)/shard_map/gate_up_outer/pallas_call | solution.py:266
  139.8 16.5 %input_partial.3 = (bf16[64,2176]{1,0:T(8,128)(2,1)S(1)}, bf16[64,2176]{1,0:T(8,128)(2,1)S(1)}, bf16[64,2176]{1,0:T(8,128)(2,1)S(1)}, bf16[64,2176]{1,0:T(8,128)(2,1)S(1)}) custom-call(s32[6]{0:T(128)S(1)} %copy-done.39, bf16[128,3584]{1,0:T(8,128)(2,1)S(1)} %get-tuple-element.76.refs_0_, bf16[128,3584]{1,0:T(8,128)(2,1)S(1)} %get-tuple-element.75.refs_1_, ...), custom_call_target="tpu_custom_call" | custom-call | flops 1 | bytes 1 | tf_op jit(solution)/shard_map/input_partial/pallas_call | solution.py:194
  160.4 5.0 %gate_up_outer.3 = f32[4,32,3584]{2,1,0:T(8,128)} custom-call(s32[6]{0:T(128)S(1)} %copy-done.40, bf16[128,3584]{1,0:T(8,128)(2,1)S(1)} %get-tuple-element.76.refs_0_, bf16[128,3584]{1,0:T(8,128)(2,1)S(1)} %get-tuple-element.75.refs_1_, bf16[128,3584]{1,0:T(8,128)(2,1)S(1)} %copy-done.3, bf16[128,3584]{1,0:T(8,128)(2,1)S(1)} %copy-done.1, ...), custom_call_target="tpu_custom_call" | custom-call | flops 1 | bytes 1 | tf_op jit(solution)/shard_map/gate_up_outer/pallas_call | solution.py:266
  165.5 2.2 %spread_a_down.1 = f32[4,16,3584]{2,1,0:T(8,128)} custom-call(s32[6]{0:T(128)S(1)} %copy-done.40, bf16[16,3584]{1,0:T(8,128)(2,1)S(1)} %reduce_sum.9.refs_0_, bf16[16,3584]{1,0:T(8,128)(2,1)S(1)} %collective-permute-done.24.refs_1_, bf16[32,3584]{1,0:T(8,128)(2,1)S(1)} %collective-permute-done.25.refs_2_), custom_call_target="tpu_custom_call" | custom-call | flops 1 | bytes 1 | tf_op jit(solution)/shard_map/spread_a_down/pallas_call | solution.py:299
  167.7 14.6 %collective-permute-done.27.refs_6_ = bf16[64,2176]{1,0:T(8,128)(2,1)S(1)} collective-permute-done((bf16[64,2176]{1,0:T(8,128)(2,1)S(1)}, bf16[64,2176]{1,0:T(8,128)(2,1)S(1)}, u32[]{:S(2)}, u32[]{:S(2)}) %collective-permute-start.27) | collective-permute-done | bytes 278560 | tf_op jit(solution)/shard_map/ppermute | solution.py:445
  183.2 3.5 %in_outer.1 = f32[4,32,2048]{2,1,0:T(8,128)} custom-call(s32[6]{0:T(128)S(1)} %copy-done.40, bf16[64,2176]{1,0:T(8,128)(2,1)S(1)} %copy-done.23, bf16[64,2176]{1,0:T(8,128)(2,1)S(1)} %copy-done.25, bf16[64,2176]{1,0:T(8,128)(2,1)S(1)} %collective-permute-done.22.refs_2_, bf16[64,2176]{1,0:T(8,128)(2,1)S(1)} %collective-permute-done.23.refs_3_, ...), custom_call_target="tpu_custom_call" | custom-call | flops 1 | bytes 1 | tf_op jit(solution)/shard_map/in_outer/pallas_call | solution.py:341
  (174 shorter events, 44.4 us)
Async XLA Ops:
  1.7 12.2 %collective-permute-start.5 = (bf16[1,64,2048]{2,1,0:T(8,128)(2,1)S(1)}, bf16[1,64,2048]{2,1,0:T(8,128)(2,1)S(1)}, u32[]{:S(2)}, u32[]{:S(2)}) collective-permute-start(bf16[1,64,2048]{2,1,0:T(8,128)(2,1)S(1)} %get-tuple-element.42.refs_0_.refs_4_), channel_id=1, source_target_pairs={{0,1},{1,2},{2,3},{3,0},{4,5},{5,6},{6,7},{7,4},{8,9},{9,10},{10,1... | collective-permute-start | bytes 786440 | tf_op jit(solution)/shard_map/ppermute | solution.py:409
  4.8 14.8 %collective-permute-start = (bf16[1,64,2048]{2,1,0:T(8,128)(2,1)S(1)}, bf16[1,64,2048]{2,1,0:T(8,128)(2,1)S(1)}, u32[]{:S(2)}, u32[]{:S(2)}) collective-permute-start(bf16[1,64,2048]{2,1,0:T(8,128)(2,1)S(1)} %get-tuple-element.37.refs_0_), channel_id=1, source_target_pairs={{0,1},{1,2},{2,3},{3,0},{4,5},{5,6},{6,7},{7,4},{8,9},{9,10},{10,1... | collective-permute-start | bytes 786440 | tf_op jit(solution)/shard_map/ppermute | solution.py:409
  13.9 11.2 %collective-permute-start.6 = (bf16[1,64,2048]{2,1,0:T(8,128)(2,1)S(1)}, bf16[1,64,2048]{2,1,0:T(8,128)(2,1)S(1)}, u32[]{:S(2)}, u32[]{:S(2)}) collective-permute-start(bf16[1,64,2048]{2,1,0:T(8,128)(2,1)S(1)} %collective-permute-done.5.refs_1_.refs_5_), channel_id=1, source_target_pairs={{0,1},{1,2},{2,3},{3,0},{4,5},{5,6},{6,7},{7,4},{8,9},{9,10},{10,1... | collective-permute-start | bytes 786440 | tf_op jit(solution)/shard_map/ppermute | solution.py:409
  19.6 11.3 %collective-permute-start.1 = (bf16[1,64,2048]{2,1,0:T(8,128)(2,1)S(1)}, bf16[1,64,2048]{2,1,0:T(8,128)(2,1)}, u32[]{:S(2)}, u32[]{:S(2)}) collective-permute-start(bf16[1,64,2048]{2,1,0:T(8,128)(2,1)S(1)} %collective-permute-done.refs_1_), channel_id=1, source_target_pairs={{0,1},{1,2},{2,3},{3,0},{4,5},{5,6},{6,7},{7,4},{8,9},{9,10},{10,1... | collective-permute-start | bytes 786440 | tf_op jit(solution)/shard_map/ppermute | solution.py:409
  25.2 10.4 %collective-permute-start.10 = (bf16[1,64,2048]{2,1,0:T(8,128)(2,1)S(1)}, bf16[1,64,2048]{2,1,0:T(8,128)(2,1)S(1)}, u32[]{:S(2)}, u32[]{:S(2)}) collective-permute-start(bf16[1,64,2048]{2,1,0:T(8,128)(2,1)S(1)} %collective-permute-done.6.refs_2_.refs_6_), channel_id=1, source_target_pairs={{0,1},{1,2},{2,3},{3,0},{4,5},{5,6},{6,7},{7,4},{8,9},{9,10},{10,1... | collective-permute-start | bytes 786440 | tf_op jit(solution)/shard_map/ppermute | solution.py:409
  25.9 32.4 %collective-permute-start.8 = (bf16[128,3584]{1,0:T(8,128)(2,1)}, bf16[128,3584]{1,0:T(8,128)(2,1)}, u32[]{:S(2)}, u32[]{:S(2)}) collective-permute-start(bf16[128,3584]{1,0:T(8,128)(2,1)} %param.15), channel_id=1, source_target_pairs={{0,8},{4,12},{8,0},{12,4},{1,9},{5,13},{9,1},{13,5},{2,10},{6,14},... | collective-permute-start | bytes 2752520 | tf_op jit(solution)/shard_map/ppermute | solution.py:411
  27.6 38.9 %collective-permute-start.4 = (bf16[128,3584]{1,0:T(8,128)(2,1)}, bf16[128,3584]{1,0:T(8,128)(2,1)}, u32[]{:S(2)}, u32[]{:S(2)}) collective-permute-start(bf16[128,3584]{1,0:T(8,128)(2,1)} %param.16), channel_id=1, source_target_pairs={{0,8},{4,12},{8,0},{12,4},{1,9},{5,13},{9,1},{13,5},{2,10},{6,14},... | collective-permute-start | bytes 2752520 | tf_op jit(solution)/shard_map/ppermute | solution.py:411
  30.9 36.2 %collective-permute-start.3 = (bf16[128,3584]{1,0:T(8,128)(2,1)}, bf16[128,3584]{1,0:T(8,128)(2,1)}, u32[]{:S(2)}, u32[]{:S(2)}) collective-permute-start(bf16[128,3584]{1,0:T(8,128)(2,1)} %param.15), channel_id=1, source_target_pairs={{0,4},{4,0},{8,12},{12,8},{1,5},{5,1},{9,13},{13,9},{2,6},{6,2},{1... | collective-permute-start | bytes 2752520 | tf_op jit(solution)/shard_map/ppermute | solution.py:412
  30.9 36.9 %collective-permute-start.2 = (bf16[128,3584]{1,0:T(8,128)(2,1)}, bf16[128,3584]{1,0:T(8,128)(2,1)}, u32[]{:S(2)}, u32[]{:S(2)}) collective-permute-start(bf16[128,3584]{1,0:T(8,128)(2,1)} %param.16), channel_id=1, source_target_pairs={{0,4},{4,0},{8,12},{12,8},{1,5},{5,1},{9,13},{13,9},{2,6},{6,2},{1... | collective-permute-start | bytes 2752520 | tf_op jit(solution)/shard_map/ppermute | solution.py:412
  45.9 20.7 %collective-permute-start.16 = (bf16[128,2048]{1,0:T(8,128)(2,1)}, bf16[128,2048]{1,0:T(8,128)(2,1)}, u32[]{:S(2)}, u32[]{:S(2)}) collective-permute-start(bf16[128,2048]{1,0:T(8,128)(2,1)} %refs_8_), channel_id=1, source_target_pairs={{0,1},{1,2},{2,3},{3,0},{4,5},{5,6},{6,7},{7,4},{8,9},{9,10},{10,1... | collective-permute-start | bytes 1572872 | tf_op jit(solution)/shard_map/ppermute | solution.py:454
  58.3 13.0 %collective-permute-start.9 = (bf16[2,64,3712]{2,1,0:T(8,128)(2,1)S(1)}, bf16[2,64,3712]{2,1,0:T(8,128)(2,1)S(1)}, u32[]{:S(2)}, u32[]{:S(2)}) collective-permute-start(bf16[2,64,3712]{2,1,0:T(8,128)(2,1)S(1)} %get-tuple-element.41), channel_id=1, source_target_pairs={{0,4},{4,0},{8,12},{12,8},{1,5},{5,1},{9,13},{13,9},{2,6},{6,2},{1... | collective-permute-start | bytes 2850824 | tf_op jit(solution)/shard_map/ppermute | solution.py:431
  66.6 14.5 %collective-permute-start.13 = (bf16[128,3584]{1,0:T(8,128)(2,1)}, bf16[128,3584]{1,0:T(8,128)(2,1)S(1)}, u32[]{:S(2)}, u32[]{:S(2)}) collective-permute-start(bf16[128,3584]{1,0:T(8,128)(2,1)} %collective-permute-done.8), channel_id=1, source_target_pairs={{0,4},{4,0},{8,12},{12,8},{1,5},{5,1},{9,13},{13,9},{2,6},{6,2},{1... | collective-permute-start | bytes 2752520 | tf_op jit(solution)/shard_map/ppermute | solution.py:461
  66.6 14.5 %collective-permute-start.12 = (bf16[128,3584]{1,0:T(8,128)(2,1)}, bf16[128,3584]{1,0:T(8,128)(2,1)S(1)}, u32[]{:S(2)}, u32[]{:S(2)}) collective-permute-start(bf16[128,3584]{1,0:T(8,128)(2,1)} %collective-permute-done.4), channel_id=1, source_target_pairs={{0,4},{4,0},{8,12},{12,8},{1,5},{5,1},{9,13},{13,9},{2,6},{6,2},{1... | collective-permute-start | bytes 2752520 | tf_op jit(solution)/shard_map/ppermute | solution.py:461
  67.1 29.0 %collective-permute-start.17 = (bf16[128,2048]{1,0:T(8,128)(2,1)}, bf16[128,2048]{1,0:T(8,128)(2,1)S(1)}, u32[]{:S(2)}, u32[]{:S(2)}) collective-permute-start(bf16[128,2048]{1,0:T(8,128)(2,1)} %collective-permute-done.16.refs_9_), channel_id=1, source_target_pairs={{0,1},{1,2},{2,3},{3,0},{4,5},{5,6},{6,7},{7,4},{8,9},{9,10},{10,1... | collective-permute-start | bytes 1572872 | tf_op jit(solution)/shard_map/ppermute | solution.py:454
  71.5 24.0 %collective-permute-start.14 = (bf16[2,64,3712]{2,1,0:T(8,128)(2,1)S(1)}, bf16[2,64,3712]{2,1,0:T(8,128)(2,1)S(1)}, u32[]{:S(2)}, u32[]{:S(2)}) collective-permute-start(bf16[2,64,3712]{2,1,0:T(8,128)(2,1)S(1)} %add_convert_fusion.3), channel_id=1, source_target_pairs={{0,8},{4,12},{8,0},{12,4},{1,9},{5,13},{9,1},{13,5},{2,10},{6,14},... | collective-permute-start | bytes 2850824 | tf_op jit(solution)/shard_map/ppermute | solution.py:435
  83.8 36.4 %collective-permute-start.20 = (bf16[2,64,3712]{2,1,0:T(8,128)(2,1)S(1)}, bf16[2,64,3712]{2,1,0:T(8,128)(2,1)}, u32[]{:S(2)}, u32[]{:S(2)}) collective-permute-start(bf16[2,64,3712]{2,1,0:T(8,128)(2,1)S(1)} %add_convert_fusion.2), channel_id=1, source_target_pairs={{0,8},{4,12},{8,0},{12,4},{1,9},{5,13},{9,1},{13,5},{2,10},{6,14},... | collective-permute-start | bytes 2850824 | tf_op jit(solution)/shard_map/ppermute | solution.py:435
  96.1 32.3 %collective-permute-start.18 = (bf16[128,2048]{1,0:T(8,128)(2,1)S(1)}, bf16[128,2048]{1,0:T(8,128)(2,1)S(1)}, u32[]{:S(2)}, u32[]{:S(2)}) collective-permute-start(bf16[128,2048]{1,0:T(8,128)(2,1)S(1)} %collective-permute-done.17.refs_10_), channel_id=1, source_target_pairs={{0,1},{1,2},{2,3},{3,0},{4,5},{5,6},{6,7},{7,4},{8,9},{9,10},{10,1... | collective-permute-start | bytes 1572872 | tf_op jit(solution)/shard_map/ppermute | solution.py:454
  117.5 11.7 %collective-permute-start.19 = (bf16[64,2176]{1,0:T(8,128)(2,1)S(1)}, bf16[64,2176]{1,0:T(8,128)(2,1)S(1)}, u32[]{:S(2)}, u32[]{:S(2)}) collective-permute-start(bf16[64,2176]{1,0:T(8,128)(2,1)S(1)} %get-tuple-element.51), channel_id=1, source_target_pairs={{0,1},{1,2},{2,3},{3,0},{4,5},{5,6},{6,7},{7,4},{8,9},{9,10},{10,1... | collective-permute-start | bytes 835592 | tf_op jit(solution)/shard_map/ppermute | solution.py:445
  134.8 23.7 %collective-permute-start.24 = (bf16[16,3584]{1,0:T(8,128)(2,1)S(1)}, bf16[16,3584]{1,0:T(8,128)(2,1)S(1)}, u32[]{:S(2)}, u32[]{:S(2)}) collective-permute-start(bf16[16,3584]{1,0:T(8,128)(2,1)S(1)} %reduce_sum.9.refs_0_), channel_id=1, source_target_pairs={{0,8},{4,12},{8,0},{12,4},{1,9},{5,13},{9,1},{13,5},{2,10},{6,14},... | collective-permute-start | bytes 344072 | tf_op jit(solution)/shard_map/ppermute | solution.py:475
  136.1 24.0 %collective-permute-start.23 = (bf16[64,2176]{1,0:T(8,128)(2,1)}, bf16[64,2176]{1,0:T(8,128)(2,1)S(1)}, u32[]{:S(2)}, u32[]{:S(2)}) collective-permute-start(bf16[64,2176]{1,0:T(8,128)(2,1)} %copy-done.42), channel_id=1, source_target_pairs={{0,3},{1,0},{2,1},{3,2},{4,7},{5,4},{6,5},{7,6},{8,11},{9,8},{10,9... | collective-permute-start | bytes 835592 | tf_op jit(solution)/shard_map/ppermute | solution.py:445
  137.8 22.4 %collective-permute-start.22 = (bf16[64,2176]{1,0:T(8,128)(2,1)}, bf16[64,2176]{1,0:T(8,128)(2,1)S(1)}, u32[]{:S(2)}, u32[]{:S(2)}) collective-permute-start(bf16[64,2176]{1,0:T(8,128)(2,1)} %copy-done.41), channel_id=1, source_target_pairs={{0,2},{1,3},{2,0},{3,1},{4,6},{5,7},{6,4},{7,5},{8,10},{9,11},{10,... | collective-permute-start | bytes 835592 | tf_op jit(solution)/shard_map/ppermute | solution.py:445
  156.4 11.3 %collective-permute-start.28 = (bf16[64,2176]{1,0:T(8,128)(2,1)S(1)}, bf16[64,2176]{1,0:T(8,128)(2,1)S(1)}, u32[]{:S(2)}, u32[]{:S(2)}) collective-permute-start(bf16[64,2176]{1,0:T(8,128)(2,1)S(1)} %get-tuple-element.64), channel_id=1, source_target_pairs={{0,3},{1,0},{2,1},{3,2},{4,7},{5,4},{6,5},{7,6},{8,11},{9,8},{10,9... | collective-permute-start | bytes 835592 | tf_op jit(solution)/shard_map/ppermute | solution.py:445
  157.8 24.4 %collective-permute-start.27 = (bf16[64,2176]{1,0:T(8,128)(2,1)S(1)}, bf16[64,2176]{1,0:T(8,128)(2,1)S(1)}, u32[]{:S(2)}, u32[]{:S(2)}) collective-permute-start(bf16[64,2176]{1,0:T(8,128)(2,1)S(1)} %get-tuple-element.63), channel_id=1, source_target_pairs={{0,2},{1,3},{2,0},{3,1},{4,6},{5,7},{6,4},{7,5},{8,10},{9,11},{10,... | collective-permute-start | bytes 835592 | tf_op jit(solution)/shard_map/ppermute | solution.py:445
  158.5 23.7 %collective-permute-start.26 = (bf16[64,2176]{1,0:T(8,128)(2,1)S(1)}, bf16[64,2176]{1,0:T(8,128)(2,1)S(1)}, u32[]{:S(2)}, u32[]{:S(2)}) collective-permute-start(bf16[64,2176]{1,0:T(8,128)(2,1)S(1)} %get-tuple-element.62), channel_id=1, source_target_pairs={{0,1},{1,2},{2,3},{3,0},{4,5},{5,6},{6,7},{7,4},{8,9},{9,10},{10,1... | collective-permute-start | bytes 835592 | tf_op jit(solution)/shard_map/ppermute | solution.py:445
  (55 other events, 653.0 us)

commit v2 on v1

--- a/solution.py
+++ b/solution.py
@@ -70,12 +70,12 @@
         for j in range(g):
             owner = lax.rem(z + (n_dp - k), n_dp) * g + j
             away = jnp.where(owner % 2 == c, 0, ny)
-            x_scr[away + lax.rem(owner // 2 + ny - y, ny)] = pieces[k][j]
+            x_scr[away + owner // 2] = pieces[k][j]
     proj = fdot(x_scr[...].reshape(n_t * rc, width), bd_ref[...], NT)
     lane = lax.broadcasted_iota(jnp.int32, (rc, TENANTS * R), 1) // R
     zeros = jnp.zeros((rc, LANES - TENANTS * R), jnp.bfloat16)
     for s in range(n_t):
-        owner = lax.rem(y + s % ny, ny) * 2 + (c if s < ny else 1 - c)
+        owner = (s % ny) * 2 + (c if s < ny else 1 - c)
         own = jnp.where(lane == tenant_of(meta, owner, own_t), proj[s * rc : (s + 1) * rc], 0.0)
         p_scr[s * rc : (s + 1) * rc, :] = (ADAPTER_SCALE * own).astype(jnp.bfloat16)
         out = keep_ref if s < ny else send_ref
@@ -149,7 +149,7 @@
         owner = owner_of(p, y, c, ny)
         slot = lax.rem(owner // g + n_dp - z, n_dp) * g + owner % g
         mine = [factor[q * rc : (q + 1) * rc, :] for factor in factors[p]]
-        g_scr[slot], u_scr[slot] = grads_of(sums[p % 2][(ny - p // 2) % ny, :, :hidden_width], mine)
+        g_scr[slot], u_scr[slot] = grads_of(sums[p % 2][owner // 2, :, :hidden_width], mine)
     q_gate = fdot(g_scr[...].reshape(rows, hidden_width), b_ref[...], NT)
     q_up = fdot(u_scr[...].reshape(rows, hidden_width), b_ref[...], NT)
     lane = lax.broadcasted_iota(jnp.int32, (rc, 2 * R * TENANTS), 1)
@@ -244,40 +244,62 @@
     )(meta, *pieces, left)
 
 
-def gate_up_outer_kernel(n_t, meta, *refs):
+def gate_up_outer_kernel(n_t, chunks, meta, *refs):
     ny = n_t // 2
     factors, refs = [refs[2 * p : 2 * p + 2] for p in range(n_t)], refs[2 * n_t :]
-    sums, (left_ref, so_far, out_ref) = refs[:2], refs[2:]
+    sums, (left_ref, out_ref) = [refs[2 * q : 2 * q + 2] for q in range(chunks)], refs[2 * chunks :]
     y, c = meta[1] // 2, meta[1] % 2
     owners = [owner_of(p, y, c, ny) for p in range(n_t)]
-    grads = [grads_of(sums[p % 2][(ny - p // 2) % ny], factors[p]) for p in range(n_t)]
+    grads = []
+    for p in range(n_t):
+        total = jnp.concatenate([both[p % 2][owners[p] // 2] for both in sums], axis=0)
+        grads.append(grads_of(total, factors[p]))
     for layer in range(2):
         right = jnp.concatenate([grad[layer] for grad in grads], axis=0)
         out = ADAPTER_SCALE * fdot(left_of(left_ref, layer, owners), right, NN)
-        at = slice(layer * R, (layer + 1) * R)
-        out_ref[:, at, :] = so_far[:, at, :] + out.reshape(TENANTS, R, out.shape[1])
-
-
-def gate_up_outer(meta, factors, q, sums, left, so_far):
-    n_t = len(factors)
-    rc, width = sums[0].shape[1], factors[0][0].shape[1]
+        out_ref[:, layer * R : (layer + 1) * R, :] = out.reshape(TENANTS, R, out.shape[1])
+
+
+def gate_up_outer(meta, factors, sums, left):
+    n_t, chunks = len(factors), len(sums)
+    rc = sums[0][0].shape[1]
+    own_t, width = factors[0][0].shape
     tile = tile_of(width, 896)
-    block = pl.BlockSpec((TENANTS, 2 * R, tile), lambda f, *_: (0, 0, f))
-    return pl.pallas_call(
-        functools.partial(gate_up_outer_kernel, n_t),
+    return pl.pallas_call(
+        functools.partial(gate_up_outer_kernel, n_t, chunks),
         out_shape=jax.ShapeDtypeStruct((TENANTS, 2 * R, width), jnp.float32),
         grid_spec=pltpu.PrefetchScalarGridSpec(
             num_scalar_prefetch=1,
             grid=(width // tile,),
-            in_specs=[pl.BlockSpec((rc, tile), lambda f, *_: (q, f))] * (2 * n_t)
-            + [pl.BlockSpec((n_t // 2, rc, tile), lambda f, *_: (0, 0, f))] * 2
-            + [whole(left.shape), block],
-            out_specs=block,
+            in_specs=[pl.BlockSpec((own_t, tile), lambda f, *_: (0, f))] * (2 * n_t)
+            + [pl.BlockSpec((n_t // 2, rc, tile), lambda f, *_: (0, 0, f))] * (2 * chunks)
+            + [whole(left.shape)],
+            out_specs=pl.BlockSpec((TENANTS, 2 * R, tile), lambda f, *_: (0, 0, f)),
         ),
+        compiler_params=pltpu.CompilerParams(vmem_limit_bytes=2 * VMEM_LIMIT),
+        cost_estimate=NO_COST,
+        name="gate_up_outer",
+    )(meta, *[x for pair in factors for x in pair], *[x for both in sums for x in both], left)
+
+
+def down_part_kernel(chunks, meta, *refs):
+    sums, (hidden_ref, out_ref) = refs[:chunks], refs[chunks:]
+    width = hidden_ref.shape[1]
+    low = jnp.concatenate([both[meta[1] // 2][:, width:] for both in sums], axis=0)
+    part = fdot(low, hidden_ref[...], TN)
+    out_ref[...] = sum(part[e * R : (e + 1) * R] for e in range(TENANTS)).astype(jnp.bfloat16)
+
+
+def down_part(meta, sums, hidden):
+    return pl.pallas_call(
+        functools.partial(down_part_kernel, len(sums)),
+        out_shape=jax.ShapeDtypeStruct((R, hidden.shape[1]), jnp.bfloat16),
+        in_specs=[SMEM] + [VMEM] * (len(sums) + 1),
+        out_specs=VMEM,
         compiler_params=pltpu.CompilerParams(vmem_limit_bytes=VMEM_LIMIT),
         cost_estimate=NO_COST,
-        name="gate_up_outer",
-    )(meta, *[x for pair in factors for x in pair], *sums, left, so_far)
+        name="down_part",
+    )(meta, *sums, hidden)
 
 
 def spread_kernel(tenant_at, rows, meta, *refs):
@@ -333,21 +355,13 @@
 
 def in_outer(meta, shares, inputs, g):
     n_dp, chunks = len(inputs), len(shares)
-    shares = [share for there in shares for share in there]
-    rows, width = inputs[0].shape
-    rc = shares[0].shape[0]
-    low = n_dp * 2 * R
-    tile = tile_of(width, 1024)
+    width = inputs[0].shape[1]
+    shares = [share[:, width:] for there in shares for share in there]
     return pl.pallas_call(
         functools.partial(in_outer_kernel, n_dp, chunks, g),
         out_shape=jax.ShapeDtypeStruct((TENANTS, 2 * R, width), jnp.float32),
-        grid_spec=pltpu.PrefetchScalarGridSpec(
-            num_scalar_prefetch=1,
-            grid=(width // tile,),
-            in_specs=[pl.BlockSpec((rc, low), lambda f, *_: (0, width // low))] * len(shares)
-            + [pl.BlockSpec((rows, tile), lambda f, *_: (0, f))] * n_dp,
-            out_specs=pl.BlockSpec((TENANTS, 2 * R, tile), lambda f, *_: (0, 0, f)),
-        ),
+        in_specs=[SMEM] + [VMEM] * (len(shares) + n_dp),
+        out_specs=VMEM,
         compiler_params=pltpu.CompilerParams(vmem_limit_bytes=VMEM_LIMIT),
         cost_estimate=NO_COST,
         name="in_outer",
@@ -403,14 +417,23 @@
     pair = [(k, k ^ 1) for k in range(n_t)]
     z_next = ring(n_dp, 1)
 
-    grads = [[out_grad.reshape(g, own_t, width)[:, at : at + rc]] for at, rc in chunks]
-    for _ in range(n_dp - 1):
-        for pieces in grads:
-            pieces.append(lax.ppermute(pieces[-1], "dp", z_next))
     stored = (gate_pre, up_pre)
     far_stored = [[lax.ppermute(x, "tensor", ring(n_t, 2 * s)) for x in stored] for s in range(1, ny)]
-    pair_stored = [lax.ppermute(after(x, grads[0][2]), "tensor", pair) for x in stored]
-
+    grads = [[out_grad.reshape(g, own_t, width)[:, at : at + rc]] for at, rc in chunks]
+    for step in range(n_dp - 1):
+        for q, pieces in enumerate(grads):
+            piece = pieces[-1]
+            if q == 0 and step == n_dp - 2:
+                piece = after(piece, *[there[0] for there in far_stored])
+            pieces.append(lax.ppermute(piece, "dp", z_next))
+
+    def first(q, done):
+        pieces = [after(grads[q][0], *done)] + grads[q][1:]
+        keep, send = hidden_partial(meta, pieces, down_weight, b_down, a_down, n_t, own_t)
+        return keep, lax.ppermute(send, "tensor", pair)
+
+    keep_a, other_a = first(0, (grads[1][1],))
+    adapter_acts, gate_pre, up_pre = after((adapter_acts, gate_pre, up_pre), keep_a)
     onehot = (
         jnp.arange(TENANTS, dtype=jnp.int32)[:, None] == jnp.repeat(block_tenant, BLOCK)[None, :]
     ).astype(jnp.bfloat16)
@@ -425,18 +448,12 @@
         dup = gate_value * sigmoid_value
         return [x.astype(jnp.bfloat16) for x in (dgate, dup, dup * up_value)]
 
-    def first(q, done):
-        pieces = [after(grads[q][0], *done)] + grads[q][1:]
-        keep, send = hidden_partial(meta, pieces, down_weight, b_down, a_down, n_t, own_t)
-        return keep, lax.ppermute(send, "tensor", pair)
-
     def exchange(keep, other):
         mine = add32(keep, other).astype(jnp.bfloat16)
         return mine, [lax.ppermute(mine, "tensor", ring(n_t, 2 * s)) for s in range(1, ny)]
 
     def total(mine, far):
-        turned = [jnp.roll(there, -(s + 1), axis=0) for s, there in enumerate(far)]
-        both = add32(mine, *turned).astype(jnp.bfloat16)
+        both = add32(mine, *far).astype(jnp.bfloat16)
         return [both, lax.ppermute(both, "tensor", pair)]
 
     def second(q, sums, done):
@@ -447,38 +464,32 @@
     def finish(there, rc):
         return add32(*[x[:, :width] for x in there]).astype(jnp.bfloat16).reshape(g, rc, width)
 
-    keep_a, other_a = first(0, (grads[1][n_dp - 2],))
-    mine_a, far_a = exchange(keep_a, other_a)
+    *near, hidden = factors_of(gate_pre, up_pre)
+    beside = [lax.ppermute(x, "tensor", pair) for x in (gate_pre, up_pre)]
+    mine_a, far_a = exchange(after(keep_a, near[0], *[there[1] for there in far_stored]), other_a)
     inputs = [after(layer_input, grads[-1][-1])]
     for _ in range(n_dp - 1):
         inputs.append(lax.ppermute(inputs[-1], "dp", z_next))
-    *near, hidden = factors_of(*stored)
-    factors = [near, factors_of(*pair_stored)[:2]]
-    keep_b, other_b = first(1, (mine_a, near[0], factors[1][0]))
-    mine_b, far_b = exchange(keep_b, other_b)
+    keep_b, other_b = first(1, (mine_a,))
+    factors = [near, factors_of(after(beside[0], keep_b), beside[1])[:2]]
+    mine_b, far_b = exchange(after(keep_b, factors[1][0]), other_b)
     for there in far_stored:
-        there = [after(x, keep_a) for x in there]
+        there = [after(x, keep_b) for x in there]
         beside = [lax.ppermute(x, "tensor", pair) for x in there]
         there[0] = after(there[0], mine_b)
         factors += [factors_of(*there)[:2], factors_of(*beside)[:2]]
-    grad_b_down = down_outer(meta, grads, after(acts[2:], *[pair[0] for pair in factors]))
-    sums_a = total(after(mine_a, grad_b_down), far_a)
+    sums_a = total(after(mine_a, *[pair[0] for pair in factors]), far_a)
     there_a = second(0, sums_a, ())
-    left = [acts[:2, :, :, at : at + rc] for at, rc in chunks]
-    zeros = jnp.zeros((TENANTS, 2 * R, hidden_width), jnp.float32)
-    grad_b_gu = gate_up_outer(meta, factors, 0, sums_a, after(left[0], there_a[0]), zeros)
-    sums_b = total(after(mine_b, grad_b_gu, inputs[-1], there_a[1]), far_b)
-
-    low = jnp.concatenate([sums_a[0][0], sums_b[0][0]], axis=0)
-    low = low[:, hidden_width : hidden_width + TENANTS * R]
-    a_part = fdot(low, hidden, TN).reshape(TENANTS, R, hidden_width).sum(0).astype(jnp.bfloat16)
+    sums_b = total(after(mine_b, there_a[0], inputs[-1]), far_b)
+
+    a_part = down_part(meta, [sums_a[0], sums_b[0]], hidden)
     a_column = [a_part] + [lax.ppermute(a_part, "tensor", ring(n_t, 2 * s)) for s in range(1, ny)]
     there_b = second(1, sums_b, (a_part,))
 
     a_column = [after(a_column[0], there_b[0])] + a_column[1:]
     a_beside = lax.ppermute(jnp.concatenate(a_column, axis=0), "tensor", pair)
-    half_a = finish([after(there_a[0], there_b[0])] + there_a[1:], chunks[0][1])
-    grad_b_gu = gate_up_outer(meta, factors, 1, sums_b, after(left[1], half_a), grad_b_gu)
+    grad_b_down = down_outer(meta, grads, after(acts[2:], there_b[0]))
+    grad_b_gu = gate_up_outer(meta, factors, [sums_a, sums_b], after(acts[:2], grad_b_down))
 
     def column_tenant(p, m):
         owner = lax.rem(m[1] // 2 + ny - p % ny, ny) * 2
@@ -488,6 +499,7 @@
     grad_a_down = spread(meta, a_column + [a_beside], column_tenant, R, "spread_a_down")
     there_b[0] = after(there_b[0], grad_a_down)
     grad_a_gu = in_outer(meta, [there_a, there_b], inputs, g)
+    half_a = finish([after(there_a[0], grad_a_down)] + there_a[1:], chunks[0][1])
     half_b = finish(there_b, chunks[1][1])
     block_input_grad = jnp.concatenate([half_a, half_b], axis=1).reshape(own_rows, width)
     return (

time: 188 us -> 172 us (0.915)
  local copies, waits for them, and re-layouts: 21.1 us -> 14.3 us
  starting transfers between devices: 23.6 us -> 17.8 us
  Pallas kernels: 67.1 us -> 63.7 us
    ppermute x2, waiting for transfers between devices: 8.21 us -> 0.01 us  [per_device(): lax.ppermute(x, 'tensor', ring(n_t, 2 * s))]
    unnamed x100 -> x94, local copies, waits for them, and re-layouts: 12.9 us -> 6.21 us
    ppermute x2, waiting for transfers between devices: 3.4 us -> 7.68 us  [exchange(): lax.ppermute(mine, 'tensor', ring(n_t, 2 * s))]
    ppermute x8, waiting for transfers between devices: 30.7 us -> 34.9 us  [the longest x6 34.9 us: per_device(): pieces.append(lax.ppermute(piece, 'dp', z_next))]
    ppermute x6, waiting for transfers between devices: 14.6 us -> 10.4 us  [second(): lax.ppermute(outs[r], 'dp', ring(n_dp, r))]
    ppermute x3, starting transfers between devices: 2.32 us -> 0.07 us  [per_device(): inputs.append(lax.ppermute(inputs[-1], 'dp', z_next))]
    ppermute x8, starting transfers between devices: 5.32 us -> 3.37 us  [the longest x6 3.22 us: per_device(): pieces.append(lax.ppermute(piece, 'dp', z_next))]
    ppermute x2, waiting for transfers between devices: 0.37 us -> 2.28 us  [first(): return (keep, lax.ppermute(send, 'tensor', pair))]
  transfers between devices with their start and end apart: 29 -> 29, of which waited for: 10 -> 15; matrix products, arithmetic and copies ran while one was open for 12% -> 13% of each run, Pallas kernels for 34% -> 36%
where the time goes in v2:
time: 172 us; the launch traced here: 171 us
  Pallas kernels  63.7 us (37%)
  waiting for transfers between devices  58.1 us (34%)
  starting transfers between devices  17.8 us (10%)
  other arithmetic  15.8 us (9%)
  local copies, waits for them, and re-layouts  14.3 us (8%)
    ppermute x6, waiting for transfers between devices, per_device(): pieces.append(lax.ppermute(piece, 'dp', z_next))  34.9 us
    pallas_call x2, Pallas kernels, input_partial(): pl.pallas_call(functools.partial(input_kernel, (n_dp, n_t, g, own_t, rc,...  33 us
    pallas_call x2, Pallas kernels, hidden_partial(): pl.pallas_call(functools.partial(hidden_kernel, (n_dp, n_t, g, own_t, rc,...  15.1 us
    convert_element_type x4, other arithmetic, factors_of(): return [x.astype(jnp.bfloat16) for x in (dgate, dup, dup * up_value)]  10.8 us
    ppermute x6, waiting for transfers between devices, second(): lax.ppermute(outs[r], 'dp', ring(n_dp, r))  10.4 us
    ppermute x6, starting transfers between devices, second(): lax.ppermute(outs[r], 'dp', ring(n_dp, r))  8.61 us
    ppermute x2, waiting for transfers between devices, exchange(): lax.ppermute(mine, 'tensor', ring(n_t, 2 * s))  7.68 us
    pallas_call x1, Pallas kernels, gate_up_outer(): pl.pallas_call(functools.partial(gate_up_outer_kernel, n_t, chunks), out_...  6.21 us
  transfers between devices with their start and end apart: 29, of which 15 were waited for; matrix products, arithmetic and copies ran while one was open for 13% of the time, Pallas kernels for 36%

profile of v2, /device:TPU:0, one launch (start us, length us, event | category | flops | bytes accessed | tf_op | source)
XLA Modules:
  0.0 171.1 jit_solution(6834691427896853884)
XLA Ops:
  0.6 3.0 %collective-permute-start.3 = (bf16[128,3584]{1,0:T(8,128)(2,1)}, bf16[128,3584]{1,0:T(8,128)(2,1)S(1)}, u32[]{:S(2)}, u32[]{:S(2)}) collective-permute-start(bf16[128,3584]{1,0:T(8,128)(2,1)} %param.15), channel_id=1, source_target_pairs={{0,8},{4,12},{8,0},{12,4},{1,9},{5,13},{9,1},{13,5},{2,10},{6,14},... | collective-permute-start | bytes 2752520 | tf_op jit(solution)/shard_map/ppermute | solution.py:421
  7.9 7.9 %collective-permute-done.refs_1_.refs_5_ = bf16[1,64,2048]{2,1,0:T(8,128)(2,1)S(1)} collective-permute-done((bf16[1,64,2048]{2,1,0:T(8,128)(2,1)S(1)}, bf16[1,64,2048]{2,1,0:T(8,128)(2,1)S(1)}, u32[]{:S(2)}, u32[]{:S(2)}) %collective-permute-start) | collective-permute-done | bytes 262176 | tf_op jit(solution)/shard_map/ppermute | solution.py:428
  15.8 5.6 %collective-permute-done.1.refs_1_ = bf16[1,64,2048]{2,1,0:T(8,128)(2,1)S(1)} collective-permute-done((bf16[1,64,2048]{2,1,0:T(8,128)(2,1)S(1)}, bf16[1,64,2048]{2,1,0:T(8,128)(2,1)S(1)}, u32[]{:S(2)}, u32[]{:S(2)}) %collective-permute-start.1) | collective-permute-done | bytes 262176 | tf_op jit(solution)/shard_map/ppermute | solution.py:428
  21.4 5.6 %collective-permute-done.9.refs_2_.refs_6_ = bf16[1,64,2048]{2,1,0:T(8,128)(2,1)S(1)} collective-permute-done((bf16[1,64,2048]{2,1,0:T(8,128)(2,1)S(1)}, bf16[1,64,2048]{2,1,0:T(8,128)(2,1)S(1)}, u32[]{:S(2)}, u32[]{:S(2)}) %collective-permute-start.9) | collective-permute-done | bytes 262176 | tf_op jit(solution)/shard_map/ppermute | solution.py:428
  27.0 5.6 %collective-permute-done.2.refs_2_ = bf16[1,64,2048]{2,1,0:T(8,128)(2,1)S(1)} collective-permute-done((bf16[1,64,2048]{2,1,0:T(8,128)(2,1)S(1)}, bf16[1,64,2048]{2,1,0:T(8,128)(2,1)S(1)}, u32[]{:S(2)}, u32[]{:S(2)}) %collective-permute-start.2) | collective-permute-done | bytes 262176 | tf_op jit(solution)/shard_map/ppermute | solution.py:428
  33.7 4.6 %collective-permute-done.10.refs_3_.refs_7_ = bf16[1,64,2048]{2,1,0:T(8,128)(2,1)S(1)} collective-permute-done((bf16[1,64,2048]{2,1,0:T(8,128)(2,1)S(1)}, bf16[1,64,2048]{2,1,0:T(8,128)(2,1)S(1)}, u32[]{:S(2)}, u32[]{:S(2)}) %collective-permute-start.10) | collective-permute-done | bytes 262176 | tf_op jit(solution)/shard_map/ppermute | solution.py:428
  38.3 5.6 %collective-permute-done.4.refs_3_ = bf16[1,64,2048]{2,1,0:T(8,128)(2,1)S(1)} collective-permute-done((bf16[1,64,2048]{2,1,0:T(8,128)(2,1)S(1)}, bf16[1,64,2048]{2,1,0:T(8,128)(2,1)S(1)}, u32[]{:S(2)}, u32[]{:S(2)}) %collective-permute-start.4) | collective-permute-done | bytes 262176 | tf_op jit(solution)/shard_map/ppermute | solution.py:428
  46.0 7.5 %hidden_partial.2 = (bf16[2,64,3712]{2,1,0:T(8,128)(2,1)S(1)}, bf16[2,64,3712]{2,1,0:T(8,128)(2,1)S(1)}) custom-call(s32[6]{0:T(128)S(1)} %pad_add_fusion.meta, bf16[1,64,2048]{2,1,0:T(8,128)(2,1)S(1)} %get-tuple-element.39.refs_0_, bf16[1,64,2048]{2,1,0:T(8,128)(2,1)S(1)} %collective-permute-done.1.refs_1_, ...), custom_call_target="tpu_custom_call" | custom-call | flops 1 | bytes 1 | tf_op jit(solution)/shard_map/hidden_partial/pallas_call | solution.py:104
  56.5 2.3 %collective-permute-done.8 = bf16[2,64,3712]{2,1,0:T(8,128)(2,1)S(1)} collective-permute-done((bf16[2,64,3712]{2,1,0:T(8,128)(2,1)S(1)}, bf16[2,64,3712]{2,1,0:T(8,128)(2,1)S(1)}, u32[]{:S(2)}, u32[]{:S(2)}) %collective-permute-start.8) | collective-permute-done | bytes 950304 | tf_op jit(solution)/shard_map/ppermute | solution.py:433
  59.3 7.5 %hidden_partial.3 = (bf16[2,64,3712]{2,1,0:T(8,128)(2,1)S(1)}, bf16[2,64,3712]{2,1,0:T(8,128)(2,1)S(1)}) custom-call(s32[6]{0:T(128)S(1)} %pad_add_fusion.meta, bf16[1,64,2048]{2,1,0:T(8,128)(2,1)S(1)} %get-tuple-element.46.refs_0_.refs_4_, bf16[1,64,2048]{2,1,0:T(8,128)(2,1)S(1)} %collective-permute-done.refs_1_.refs_5_, ...), custom_call_target="tpu_custom_call" | custom-call | flops 1 | bytes 1 | tf_op jit(solution)/shard_map/hidden_partial/pallas_call | solution.py:104
  67.5 3.3 %fusion.13 = (bf16[128,3584]{1,0:T(8,128)(2,1)}, bf16[128,3584]{1,0:T(8,128)(2,1)}) fusion(bf16[128,3584]{1,0:T(8,128)(2,1)S(1)} %collective-permute-done.6, bf16[128,3584]{1,0:T(8,128)(2,1)} %collective-permute-done.5), kind=kLoop, calls=%fused_computation.31 | loop fusion | flops 5963776 | bytes 3670016 | tf_op jit(solution)/shard_map/convert_element_type | solution.py:449
  74.7 3.3 %fusion.20 = (bf16[128,3584]{1,0:T(8,128)(2,1)}, bf16[128,3584]{1,0:T(8,128)(2,1)}) fusion(bf16[128,3584]{1,0:T(8,128)(2,1)S(1)} %collective-permute-done.3, bf16[128,3584]{1,0:T(8,128)(2,1)} %collective-permute-done.7), kind=kLoop, calls=%fused_computation.38 | loop fusion | flops 5963776 | bytes 3670016 | tf_op jit(solution)/shard_map/convert_element_type | solution.py:449
  78.0 4.2 %collective-permute-done.14 = bf16[2,64,3712]{2,1,0:T(8,128)(2,1)S(1)} collective-permute-done((bf16[2,64,3712]{2,1,0:T(8,128)(2,1)S(1)}, bf16[2,64,3712]{2,1,0:T(8,128)(2,1)S(1)}, u32[]{:S(2)}, u32[]{:S(2)}) %collective-permute-start.14) | collective-permute-done | bytes 950304 | tf_op jit(solution)/shard_map/ppermute | solution.py:453
  85.9 16.4 %input_partial.2 = (bf16[64,2176]{1,0:T(8,128)(2,1)S(1)}, bf16[64,2176]{1,0:T(8,128)(2,1)S(1)}, bf16[64,2176]{1,0:T(8,128)(2,1)S(1)}, bf16[64,2176]{1,0:T(8,128)(2,1)S(1)}) custom-call(s32[6]{0:T(128)S(1)} %pad_add_fusion.meta, bf16[128,3584]{1,0:T(8,128)(2,1)S(1)} %get-tuple-element.74.refs_0_, bf16[128,3584]{1,0:T(8,128)(2,1)S(1)} %get-tuple-element.75.refs_1_, ...), custom_call_target="tpu_custom_call" | custom-call | flops 1 | bytes 1 | tf_op jit(solution)/shard_map/input_partial/pallas_call | solution.py:194
  102.4 3.5 %collective-permute-done.19 = bf16[2,64,3712]{2,1,0:T(8,128)(2,1)S(1)} collective-permute-done((bf16[2,64,3712]{2,1,0:T(8,128)(2,1)S(1)}, bf16[2,64,3712]{2,1,0:T(8,128)(2,1)S(1)}, u32[]{:S(2)}, u32[]{:S(2)}) %collective-permute-start.19) | collective-permute-done | bytes 950304 | tf_op jit(solution)/shard_map/ppermute | solution.py:453
  117.8 16.6 %input_partial.3 = (bf16[64,2176]{1,0:T(8,128)(2,1)S(1)}, bf16[64,2176]{1,0:T(8,128)(2,1)S(1)}, bf16[64,2176]{1,0:T(8,128)(2,1)S(1)}, bf16[64,2176]{1,0:T(8,128)(2,1)S(1)}) custom-call(s32[6]{0:T(128)S(1)} %pad_add_fusion.meta, bf16[128,3584]{1,0:T(8,128)(2,1)S(1)} %get-tuple-element.74.refs_0_, bf16[128,3584]{1,0:T(8,128)(2,1)S(1)} %copy-done.11, ...), custom_call_target="tpu_custom_call" | custom-call | flops 1 | bytes 1 | tf_op jit(solution)/shard_map/input_partial/pallas_call | solution.py:194
  136.5 2.4 %collective-permute-done.24 = bf16[64,2176]{1,0:T(8,128)(2,1)} collective-permute-done((bf16[64,2176]{1,0:T(8,128)(2,1)}, bf16[64,2176]{1,0:T(8,128)(2,1)}, u32[]{:S(2)}, u32[]{:S(2)}) %collective-permute-start.24) | collective-permute-done | bytes 278560 | tf_op jit(solution)/shard_map/ppermute | solution.py:462
  140.7 3.1 %collective-permute-start.27 = (bf16[64,2176]{1,0:T(8,128)(2,1)S(1)}, bf16[64,2176]{1,0:T(8,128)(2,1)S(1)}, u32[]{:S(2)}, u32[]{:S(2)}) collective-permute-start(bf16[64,2176]{1,0:T(8,128)(2,1)S(1)} %get-tuple-element.71), channel_id=1, source_target_pairs={{0,2},{1,3},{2,0},{3,1},{4,6},{5,7},{6,4},{7,5},{8,10},{9,11},{10,... | collective-permute-start | bytes 835592 | tf_op jit(solution)/shard_map/ppermute | solution.py:462
  145.9 2.7 %down_outer.1 = f32[4,16,2048]{2,1,0:T(8,128)} custom-call(s32[6]{0:T(128)S(1)} %pad_add_fusion.meta, bf16[1,64,2048]{2,1,0:T(8,128)(2,1)S(1)} %get-tuple-element.39.refs_0_, bf16[1,64,2048]{2,1,0:T(8,128)(2,1)S(1)} %copy-done.22, bf16[1,64,2048]{2,1,0:T(8,128)(2,1)S(1)} %copy-done.26, bf16[1,64,2048]{2,1,0:T(8,128)(2,1)S(1)} %copy-done.31, ...), custom_call_target="tpu_custom_call" | custom-call | flops 1 | bytes 1 | tf_op jit(solution)/shard_map/down_outer/pallas_call | solution.py:229
  148.6 6.2 %gate_up_outer.1 = f32[4,32,3584]{2,1,0:T(8,128)} custom-call(s32[6]{0:T(128)S(1)} %pad_add_fusion.meta, bf16[128,3584]{1,0:T(8,128)(2,1)S(1)} %get-tuple-element.74.refs_0_, bf16[128,3584]{1,0:T(8,128)(2,1)S(1)} %copy-done.11, bf16[128,3584]{1,0:T(8,128)(2,1)S(1)} %copy-done.5, bf16[128,3584]{1,0:T(8,128)(2,1)S(1)} %copy-done.4, ...), custom_call_target="tpu_custom_call" | custom-call | flops 1 | bytes 1 | tf_op jit(solution)/shard_map/gate_up_outer/pallas_call | solution.py:268
  154.9 3.5 %spread_a_down.1 = f32[4,16,3584]{2,1,0:T(8,128)} custom-call(s32[6]{0:T(128)S(1)} %pad_add_fusion.meta, bf16[16,3584]{1,0:T(8,128)(2,1)S(1)} %down_part.1.refs_0_, bf16[16,3584]{1,0:T(8,128)(2,1)} %collective-permute-done.21.refs_1_, bf16[32,3584]{1,0:T(8,128)(2,1)S(1)} %collective-permute-done.22.refs_2_), custom_call_target="tpu_custom_call" | custom-call | flops 1 | bytes 1 | tf_op jit(solution)/shard_map/spread_a_down/pallas_call | solution.py:321
  159.8 3.3 %collective-permute-done.26 = bf16[64,2176]{1,0:T(8,128)(2,1)S(1)} collective-permute-done((bf16[64,2176]{1,0:T(8,128)(2,1)S(1)}, bf16[64,2176]{1,0:T(8,128)(2,1)S(1)}, u32[]{:S(2)}, u32[]{:S(2)}) %collective-permute-start.26) | collective-permute-done | bytes 278560 | tf_op jit(solution)/shard_map/ppermute | solution.py:462
  163.2 4.7 %collective-permute-done.27 = bf16[64,2176]{1,0:T(8,128)(2,1)S(1)} collective-permute-done((bf16[64,2176]{1,0:T(8,128)(2,1)S(1)}, bf16[64,2176]{1,0:T(8,128)(2,1)S(1)}, u32[]{:S(2)}, u32[]{:S(2)}) %collective-permute-start.27) | collective-permute-done | bytes 278560 | tf_op jit(solution)/shard_map/ppermute | solution.py:462
  168.8 2.3 %in_outer.1 = f32[4,32,2048]{2,1,0:T(8,128)} custom-call(s32[6]{0:T(128)S(1)} %pad_add_fusion.meta, bf16[64,128]{1,0:T(8,128)(2,1)S(1)} %slice.72.refs_0_, bf16[64,128]{1,0:T(8,128)(2,1)S(1)} %slice.90.refs_1_, bf16[64,128]{1,0:T(8,128)(2,1)S(1)} %slice.91.refs_2_, bf16[64,128]{1,0:T(8,128)(2,1)S(1)} %slice.92.refs_3_, bf16[64,128]{1,0:T(8,128)(2,1)S(1)} %slice.76.refs_4_, ...), custom_call_target="tpu_custom_call" | custom-call | flops 1 | bytes 1 | tf_op jit(solution)/shard_map/in_outer/pallas_call | solution.py:360
  (169 shorter events, 39.1 us)
Async XLA Ops:
  0.6 32.0 %collective-permute-start.3 = (bf16[128,3584]{1,0:T(8,128)(2,1)}, bf16[128,3584]{1,0:T(8,128)(2,1)S(1)}, u32[]{:S(2)}, u32[]{:S(2)}) collective-permute-start(bf16[128,3584]{1,0:T(8,128)(2,1)} %param.15), channel_id=1, source_target_pairs={{0,8},{4,12},{8,0},{12,4},{1,9},{5,13},{9,1},{13,5},{2,10},{6,14},... | collective-permute-start | bytes 2752520 | tf_op jit(solution)/shard_map/ppermute | solution.py:421
  4.7 11.1 %collective-permute-start = (bf16[1,64,2048]{2,1,0:T(8,128)(2,1)S(1)}, bf16[1,64,2048]{2,1,0:T(8,128)(2,1)S(1)}, u32[]{:S(2)}, u32[]{:S(2)}) collective-permute-start(bf16[1,64,2048]{2,1,0:T(8,128)(2,1)S(1)} %get-tuple-element.46.refs_0_.refs_4_), channel_id=1, source_target_pairs={{0,1},{1,2},{2,3},{3,0},{4,5},{5,6},{6,7},{7,4},{8,9},{9,10},{10,1... | collective-permute-start | bytes 786440 | tf_op jit(solution)/shard_map/ppermute | solution.py:428
  6.4 15.1 %collective-permute-start.1 = (bf16[1,64,2048]{2,1,0:T(8,128)(2,1)S(1)}, bf16[1,64,2048]{2,1,0:T(8,128)(2,1)S(1)}, u32[]{:S(2)}, u32[]{:S(2)}) collective-permute-start(bf16[1,64,2048]{2,1,0:T(8,128)(2,1)S(1)} %get-tuple-element.39.refs_0_), channel_id=1, source_target_pairs={{0,1},{1,2},{2,3},{3,0},{4,5},{5,6},{6,7},{7,4},{8,9},{9,10},{10,1... | collective-permute-start | bytes 786440 | tf_op jit(solution)/shard_map/ppermute | solution.py:428
  15.8 11.2 %collective-permute-start.9 = (bf16[1,64,2048]{2,1,0:T(8,128)(2,1)S(1)}, bf16[1,64,2048]{2,1,0:T(8,128)(2,1)S(1)}, u32[]{:S(2)}, u32[]{:S(2)}) collective-permute-start(bf16[1,64,2048]{2,1,0:T(8,128)(2,1)S(1)} %collective-permute-done.refs_1_.refs_5_), channel_id=1, source_target_pairs={{0,1},{1,2},{2,3},{3,0},{4,5},{5,6},{6,7},{7,4},{8,9},{9,10},{10,1... | collective-permute-start | bytes 786440 | tf_op jit(solution)/shard_map/ppermute | solution.py:428
  21.4 11.2 %collective-permute-start.2 = (bf16[1,64,2048]{2,1,0:T(8,128)(2,1)S(1)}, bf16[1,64,2048]{2,1,0:T(8,128)(2,1)S(1)}, u32[]{:S(2)}, u32[]{:S(2)}) collective-permute-start(bf16[1,64,2048]{2,1,0:T(8,128)(2,1)S(1)} %collective-permute-done.1.refs_1_), channel_id=1, source_target_pairs={{0,1},{1,2},{2,3},{3,0},{4,5},{5,6},{6,7},{7,4},{8,9},{9,10},{10,1... | collective-permute-start | bytes 786440 | tf_op jit(solution)/shard_map/ppermute | solution.py:428
  27.0 11.2 %collective-permute-start.10 = (bf16[1,64,2048]{2,1,0:T(8,128)(2,1)S(1)}, bf16[1,64,2048]{2,1,0:T(8,128)(2,1)S(1)}, u32[]{:S(2)}, u32[]{:S(2)}) collective-permute-start(bf16[1,64,2048]{2,1,0:T(8,128)(2,1)S(1)} %collective-permute-done.9.refs_2_.refs_6_), channel_id=1, source_target_pairs={{0,1},{1,2},{2,3},{3,0},{4,5},{5,6},{6,7},{7,4},{8,9},{9,10},{10,1... | collective-permute-start | bytes 786440 | tf_op jit(solution)/shard_map/ppermute | solution.py:428
  32.7 11.2 %collective-permute-start.4 = (bf16[1,64,2048]{2,1,0:T(8,128)(2,1)S(1)}, bf16[1,64,2048]{2,1,0:T(8,128)(2,1)S(1)}, u32[]{:S(2)}, u32[]{:S(2)}) collective-permute-start(bf16[1,64,2048]{2,1,0:T(8,128)(2,1)S(1)} %collective-permute-done.2.refs_2_), channel_id=1, source_target_pairs={{0,1},{1,2},{2,3},{3,0},{4,5},{5,6},{6,7},{7,4},{8,9},{9,10},{10,1... | collective-permute-start | bytes 786440 | tf_op jit(solution)/shard_map/ppermute | solution.py:428
  32.7 23.7 %collective-permute-start.7 = (bf16[128,3584]{1,0:T(8,128)(2,1)}, bf16[128,3584]{1,0:T(8,128)(2,1)}, u32[]{:S(2)}, u32[]{:S(2)}) collective-permute-start(bf16[128,3584]{1,0:T(8,128)(2,1)} %param.16), channel_id=1, source_target_pairs={{0,8},{4,12},{8,0},{12,4},{1,9},{5,13},{9,1},{13,5},{2,10},{6,14},... | collective-permute-start | bytes 2752520 | tf_op jit(solution)/shard_map/ppermute | solution.py:421
  38.3 18.1 %collective-permute-start.16 = (bf16[128,2048]{1,0:T(8,128)(2,1)}, bf16[128,2048]{1,0:T(8,128)(2,1)S(1)}, u32[]{:S(2)}, u32[]{:S(2)}) collective-permute-start(bf16[128,2048]{1,0:T(8,128)(2,1)} %refs_8_), channel_id=1, source_target_pairs={{0,1},{1,2},{2,3},{3,0},{4,5},{5,6},{6,7},{7,4},{8,9},{9,10},{10,1... | collective-permute-start | bytes 1572872 | tf_op jit(solution)/shard_map/ppermute | solution.py:472
  53.6 13.3 %collective-permute-start.6 = (bf16[128,3584]{1,0:T(8,128)(2,1)S(1)}, bf16[128,3584]{1,0:T(8,128)(2,1)S(1)}, u32[]{:S(2)}, u32[]{:S(2)}) collective-permute-start(bf16[128,3584]{1,0:T(8,128)(2,1)S(1)} %copy-done.44), channel_id=1, source_target_pairs={{0,4},{4,0},{8,12},{12,8},{1,5},{5,1},{9,13},{13,9},{2,6},{6,2},{1... | collective-permute-start | bytes 2752520 | tf_op jit(solution)/shard_map/ppermute | solution.py:468
  54.1 13.3 %collective-permute-start.5 = (bf16[128,3584]{1,0:T(8,128)(2,1)}, bf16[128,3584]{1,0:T(8,128)(2,1)}, u32[]{:S(2)}, u32[]{:S(2)}) collective-permute-start(bf16[128,3584]{1,0:T(8,128)(2,1)} %param.16), channel_id=1, source_target_pairs={{0,4},{4,0},{8,12},{12,8},{1,5},{5,1},{9,13},{13,9},{2,6},{6,2},{1... | collective-permute-start | bytes 2752520 | tf_op jit(solution)/shard_map/ppermute | solution.py:468
  56.4 26.4 %collective-permute-start.17 = (bf16[128,2048]{1,0:T(8,128)(2,1)S(1)}, bf16[128,2048]{1,0:T(8,128)(2,1)S(1)}, u32[]{:S(2)}, u32[]{:S(2)}) collective-permute-start(bf16[128,2048]{1,0:T(8,128)(2,1)S(1)} %collective-permute-done.16.refs_9_), channel_id=1, source_target_pairs={{0,1},{1,2},{2,3},{3,0},{4,5},{5,6},{6,7},{7,4},{8,9},{9,10},{10,1... | collective-permute-start | bytes 1572872 | tf_op jit(solution)/shard_map/ppermute | solution.py:472
  59.0 23.2 %collective-permute-start.14 = (bf16[2,64,3712]{2,1,0:T(8,128)(2,1)S(1)}, bf16[2,64,3712]{2,1,0:T(8,128)(2,1)S(1)}, u32[]{:S(2)}, u32[]{:S(2)}) collective-permute-start(bf16[2,64,3712]{2,1,0:T(8,128)(2,1)S(1)} %add_convert_fusion.3), channel_id=1, source_target_pairs={{0,8},{4,12},{8,0},{12,4},{1,9},{5,13},{9,1},{13,5},{2,10},{6,14},... | collective-permute-start | bytes 2850824 | tf_op jit(solution)/shard_map/ppermute | solution.py:453
  82.5 23.5 %collective-permute-start.19 = (bf16[2,64,3712]{2,1,0:T(8,128)(2,1)S(1)}, bf16[2,64,3712]{2,1,0:T(8,128)(2,1)S(1)}, u32[]{:S(2)}, u32[]{:S(2)}) collective-permute-start(bf16[2,64,3712]{2,1,0:T(8,128)(2,1)S(1)} %add_convert_fusion.2), channel_id=1, source_target_pairs={{0,8},{4,12},{8,0},{12,4},{1,9},{5,13},{9,1},{13,5},{2,10},{6,14},... | collective-permute-start | bytes 2850824 | tf_op jit(solution)/shard_map/ppermute | solution.py:453
  82.8 19.6 %collective-permute-start.18 = (bf16[128,2048]{1,0:T(8,128)(2,1)S(1)}, bf16[128,2048]{1,0:T(8,128)(2,1)S(1)}, u32[]{:S(2)}, u32[]{:S(2)}) collective-permute-start(bf16[128,2048]{1,0:T(8,128)(2,1)S(1)} %collective-permute-done.17.refs_10_), channel_id=1, source_target_pairs={{0,1},{1,2},{2,3},{3,0},{4,5},{5,6},{6,7},{7,4},{8,9},{9,10},{10,1... | collective-permute-start | bytes 1572872 | tf_op jit(solution)/shard_map/ppermute | solution.py:472
  106.2 9.3 %collective-permute-start.20 = (bf16[2,64,3712]{2,1,0:T(8,128)(2,1)S(1)}, bf16[2,64,3712]{2,1,0:T(8,128)(2,1)}, u32[]{:S(2)}, u32[]{:S(2)}) collective-permute-start(bf16[2,64,3712]{2,1,0:T(8,128)(2,1)S(1)} %add_convert_fusion.refs_1_.refs_8_.refs_10_), channel_id=1, source_target_pairs={{0,4},{4,0},{8,12},{12,8},{1,5},{5,1},{9,13},{13,9},{2,6},{6,2},{1... | collective-permute-start | bytes 2850824 | tf_op jit(solution)/shard_map/ppermute | solution.py:457
  107.4 27.0 %collective-permute-start.21 = (bf16[16,3584]{1,0:T(8,128)(2,1)S(1)}, bf16[16,3584]{1,0:T(8,128)(2,1)}, u32[]{:S(2)}, u32[]{:S(2)}) collective-permute-start(bf16[16,3584]{1,0:T(8,128)(2,1)S(1)} %down_part.1.refs_0_), channel_id=1, source_target_pairs={{0,8},{4,12},{8,0},{12,4},{1,9},{5,13},{9,1},{13,5},{2,10},{6,14},... | collective-permute-start | bytes 344072 | tf_op jit(solution)/shard_map/ppermute | solution.py:486
  112.4 27.1 %collective-permute-start.25 = (bf16[64,2176]{1,0:T(8,128)(2,1)}, bf16[64,2176]{1,0:T(8,128)(2,1)}, u32[]{:S(2)}, u32[]{:S(2)}) collective-permute-start(bf16[64,2176]{1,0:T(8,128)(2,1)} %copy-done.41), channel_id=1, source_target_pairs={{0,3},{1,0},{2,1},{3,2},{4,7},{5,4},{6,5},{7,6},{8,11},{9,8},{10,9... | collective-permute-start | bytes 835592 | tf_op jit(solution)/shard_map/ppermute | solution.py:462
  114.5 24.4 %collective-permute-start.24 = (bf16[64,2176]{1,0:T(8,128)(2,1)}, bf16[64,2176]{1,0:T(8,128)(2,1)}, u32[]{:S(2)}, u32[]{:S(2)}) collective-permute-start(bf16[64,2176]{1,0:T(8,128)(2,1)} %copy-done.42), channel_id=1, source_target_pairs={{0,2},{1,3},{2,0},{3,1},{4,6},{5,7},{6,4},{7,5},{8,10},{9,11},{10,... | collective-permute-start | bytes 835592 | tf_op jit(solution)/shard_map/ppermute | solution.py:462
  114.5 21.1 %collective-permute-start.23 = (bf16[64,2176]{1,0:T(8,128)(2,1)}, bf16[64,2176]{1,0:T(8,128)(2,1)}, u32[]{:S(2)}, u32[]{:S(2)}) collective-permute-start(bf16[64,2176]{1,0:T(8,128)(2,1)} %copy-done.43), channel_id=1, source_target_pairs={{0,1},{1,2},{2,3},{3,0},{4,5},{5,6},{6,7},{7,4},{8,9},{9,10},{10,1... | collective-permute-start | bytes 835592 | tf_op jit(solution)/shard_map/ppermute | solution.py:462
  135.4 19.4 %collective-permute-start.22 = (bf16[32,3584]{1,0:T(8,128)(2,1)S(1)}, bf16[32,3584]{1,0:T(8,128)(2,1)S(1)}, u32[]{:S(2)}, u32[]{:S(2)}) collective-permute-start(bf16[32,3584]{1,0:T(8,128)(2,1)S(1)} %pad_maximum_fusion), channel_id=1, source_target_pairs={{0,4},{4,0},{8,12},{12,8},{1,5},{5,1},{9,13},{13,9},{2,6},{6,2},{1... | collective-permute-start | bytes 688136 | tf_op jit(solution)/shard_map/ppermute | solution.py:490
  140.3 27.5 %collective-permute-start.28 = (bf16[64,2176]{1,0:T(8,128)(2,1)S(1)}, bf16[64,2176]{1,0:T(8,128)(2,1)S(1)}, u32[]{:S(2)}, u32[]{:S(2)}) collective-permute-start(bf16[64,2176]{1,0:T(8,128)(2,1)S(1)} %get-tuple-element.72), channel_id=1, source_target_pairs={{0,3},{1,0},{2,1},{3,2},{4,7},{5,4},{6,5},{7,6},{8,11},{9,8},{10,9... | collective-permute-start | bytes 835592 | tf_op jit(solution)/shard_map/ppermute | solution.py:462
  140.7 27.1 %collective-permute-start.27 = (bf16[64,2176]{1,0:T(8,128)(2,1)S(1)}, bf16[64,2176]{1,0:T(8,128)(2,1)S(1)}, u32[]{:S(2)}, u32[]{:S(2)}) collective-permute-start(bf16[64,2176]{1,0:T(8,128)(2,1)S(1)} %get-tuple-element.71), channel_id=1, source_target_pairs={{0,2},{1,3},{2,0},{3,1},{4,6},{5,7},{6,4},{7,5},{8,10},{9,11},{10,... | collective-permute-start | bytes 835592 | tf_op jit(solution)/shard_map/ppermute | solution.py:462
  143.8 19.3 %collective-permute-start.26 = (bf16[64,2176]{1,0:T(8,128)(2,1)S(1)}, bf16[64,2176]{1,0:T(8,128)(2,1)S(1)}, u32[]{:S(2)}, u32[]{:S(2)}) collective-permute-start(bf16[64,2176]{1,0:T(8,128)(2,1)S(1)} %get-tuple-element.70), channel_id=1, source_target_pairs={{0,1},{1,2},{2,3},{3,0},{4,5},{5,6},{6,7},{7,4},{8,9},{9,10},{10,1... | collective-permute-start | bytes 835592 | tf_op jit(solution)/shard_map/ppermute | solution.py:462
  (52 other events, 710.5 us)

commit v3 on v2

--- a/solution.py
+++ b/solution.py
@@ -209,6 +209,29 @@
     )(meta, *[x for pair in factors for x in pair], *sums, gate_weight, up_weight, b_gu, a_gu)
 
 
+def acts_kernel(meta, acts_ref, out_ref):
+    layers, n_t, _, own_t = out_ref.shape
+    for owner in range(n_t):
+        tenant = tenant_of(meta, owner, own_t)
+        for layer in range(layers):
+            mine = acts_ref[layer * R : (layer + 1) * R, owner * own_t : (owner + 1) * own_t]
+            for e in range(TENANTS):
+                chosen = jnp.where(tenant == e, mine.astype(jnp.float32), 0.0)
+                out_ref[layer, owner, e * R : (e + 1) * R, :] = chosen.astype(jnp.bfloat16)
+
+
+def masked_acts(meta, acts, n_t):
+    return pl.pallas_call(
+        acts_kernel,
+        out_shape=jax.ShapeDtypeStruct((3, n_t, TENANTS * R, acts.shape[1] // n_t), jnp.bfloat16),
+        in_specs=[SMEM, VMEM],
+        out_specs=VMEM,
+        compiler_params=pltpu.CompilerParams(vmem_limit_bytes=VMEM_LIMIT),
+        cost_estimate=NO_COST,
+        name="masked_acts",
+    )(meta, acts)
+
+
 def left_of(left_ref, layer, owners):
     return jnp.concatenate([left_ref[layer, owner] for owner in owners], axis=1)
 
@@ -217,7 +240,7 @@
     pieces, (left_ref, out_ref) = refs[: n_dp * chunks], refs[n_dp * chunks :]
     owners = [lax.rem(meta[0] + (n_dp - k), n_dp) * g + j for k in range(n_dp) for j in range(g)]
     right = [pieces[q * n_dp + k][j] for k in range(n_dp) for j in range(g) for q in range(chunks)]
-    out = ADAPTER_SCALE * fdot(left_of(left_ref, 0, owners), jnp.concatenate(right, axis=0), NN)
+    out = ADAPTER_SCALE * fdot(left_of(left_ref, 2, owners), jnp.concatenate(right, axis=0), NN)
     out_ref[...] = out.reshape(out_ref.shape)
 
 
@@ -334,38 +357,39 @@
 
 
 def in_outer_kernel(n_dp, chunks, g, meta, *refs):
-    shares, inputs, out_ref = refs[: n_dp * chunks], refs[n_dp * chunks : -1], refs[-1]
+    shares, inputs_ref, out_ref = refs[: n_dp * chunks], refs[-2], refs[-1]
     out_ref[...] = jnp.zeros_like(out_ref)
-    own_t = inputs[0].shape[0] // g
+    _, rows, width = inputs_ref.shape
+    own_t = rows // g
     rc = own_t // chunks
     for k in range(n_dp):
-        tenant = meta[2 + lax.rem(meta[0] + n_dp - k, n_dp)]
-        total = 0.0
+        block = lax.rem(meta[0] + n_dp - k, n_dp)
+        queries = []
         for q in range(chunks):
             query = 0.0
             for s in range(n_dp):
-                at = (s + n_dp - k) % n_dp * 2 * R
+                at = width + (s + n_dp - k) % n_dp * 2 * R
                 query = query + shares[q * n_dp + s][:, at : at + 2 * R].astype(jnp.float32)
-            query = query.astype(jnp.bfloat16)
-            for j in range(g):
-                rows = inputs[k][j * own_t + q * rc : j * own_t + (q + 1) * rc, :]
-                total = total + fdot(query[j * rc : (j + 1) * rc], rows, TN)
+            queries.append(query.astype(jnp.bfloat16))
+        low = [queries[q][j * rc : (j + 1) * rc] for j in range(g) for q in range(chunks)]
+        total = fdot(jnp.concatenate(low, axis=0), inputs_ref[block], TN)
+        tenant = meta[2 + block]
         out_ref[tenant] = out_ref[tenant] + ADAPTER_SCALE * total
 
 
 def in_outer(meta, shares, inputs, g):
-    n_dp, chunks = len(inputs), len(shares)
-    width = inputs[0].shape[1]
-    shares = [share[:, width:] for there in shares for share in there]
+    n_dp, _, width = inputs.shape
+    chunks = len(shares)
+    shares = [share for there in shares for share in there]
     return pl.pallas_call(
         functools.partial(in_outer_kernel, n_dp, chunks, g),
         out_shape=jax.ShapeDtypeStruct((TENANTS, 2 * R, width), jnp.float32),
-        in_specs=[SMEM] + [VMEM] * (len(shares) + n_dp),
+        in_specs=[SMEM] + [VMEM] * (len(shares) + 1),
         out_specs=VMEM,
         compiler_params=pltpu.CompilerParams(vmem_limit_bytes=VMEM_LIMIT),
         cost_estimate=NO_COST,
         name="in_outer",
-    )(meta, *shares, *inputs)
+    )(meta, *shares, inputs)
 
 
 def ring(n, by):
@@ -417,32 +441,24 @@
     pair = [(k, k ^ 1) for k in range(n_t)]
     z_next = ring(n_dp, 1)
 
-    stored = (gate_pre, up_pre)
+    stored = [gate_pre, up_pre]
     far_stored = [[lax.ppermute(x, "tensor", ring(n_t, 2 * s)) for x in stored] for s in range(1, ny)]
     grads = [[out_grad.reshape(g, own_t, width)[:, at : at + rc]] for at, rc in chunks]
-    for step in range(n_dp - 1):
-        for q, pieces in enumerate(grads):
-            piece = pieces[-1]
-            if q == 0 and step == n_dp - 2:
-                piece = after(piece, *[there[0] for there in far_stored])
-            pieces.append(lax.ppermute(piece, "dp", z_next))
+    for _ in range(n_dp - 1):
+        grads[0].append(lax.ppermute(grads[0][-1], "dp", z_next))
+    stored[0] = after(stored[0], grads[0][1])
+    beside_stored = [lax.ppermute(x, "tensor", pair) for x in stored]
+    grads[1][0] = after(grads[1][0], grads[0][2])
+    for _ in range(n_dp - 2):
+        grads[1].append(lax.ppermute(grads[1][-1], "dp", z_next))
 
     def first(q, done):
         pieces = [after(grads[q][0], *done)] + grads[q][1:]
         keep, send = hidden_partial(meta, pieces, down_weight, b_down, a_down, n_t, own_t)
-        return keep, lax.ppermute(send, "tensor", pair)
-
-    keep_a, other_a = first(0, (grads[1][1],))
-    adapter_acts, gate_pre, up_pre = after((adapter_acts, gate_pre, up_pre), keep_a)
-    onehot = (
-        jnp.arange(TENANTS, dtype=jnp.int32)[:, None] == jnp.repeat(block_tenant, BLOCK)[None, :]
-    ).astype(jnp.bfloat16)
-    acts = adapter_acts.T.reshape(3, 1, R, tokens) * onehot[None, :, None, :]
-    acts = acts.reshape(3, TENANTS * R, n_t, own_t).transpose(0, 2, 1, 3)
-
-    def factors_of(gate_pre, up_pre):
-        gate_value = gate_pre.astype(jnp.float32)
-        up_value = up_pre.astype(jnp.float32)
+        return keep, send
+
+    def factors_of(stored):
+        gate_value, up_value = [x.astype(jnp.float32) for x in stored]
         sigmoid_value = jax.nn.sigmoid(gate_value)
         dgate = up_value * sigmoid_value * (1.0 + gate_value * (1.0 - sigmoid_value))
         dup = gate_value * sigmoid_value
@@ -464,42 +480,42 @@
     def finish(there, rc):
         return add32(*[x[:, :width] for x in there]).astype(jnp.bfloat16).reshape(g, rc, width)
 
-    *near, hidden = factors_of(gate_pre, up_pre)
-    beside = [lax.ppermute(x, "tensor", pair) for x in (gate_pre, up_pre)]
-    mine_a, far_a = exchange(after(keep_a, near[0], *[there[1] for there in far_stored]), other_a)
-    inputs = [after(layer_input, grads[-1][-1])]
-    for _ in range(n_dp - 1):
-        inputs.append(lax.ppermute(inputs[-1], "dp", z_next))
-    keep_b, other_b = first(1, (mine_a,))
-    factors = [near, factors_of(after(beside[0], keep_b), beside[1])[:2]]
-    mine_b, far_b = exchange(after(keep_b, factors[1][0]), other_b)
+    *near, hidden = factors_of(stored)
+    factors = [near, factors_of(beside_stored)[:2]]
+    keep_a, send_a = first(0, (grads[1][1], near[0], factors[1][0]))
+    other_a = lax.ppermute(after(send_a, *[x for there in far_stored for x in there]), "tensor", pair)
+    mine_a, far_a = exchange(keep_a, other_a)
+    grads[1].append(lax.ppermute(after(grads[1][-1], mine_a), "dp", z_next))
+    inputs = lax.all_gather(after(layer_input, grads[0][-1]), "dp")
+    keep_b, send_b = first(1, (mine_a,))
+    other_b = lax.ppermute(send_b, "tensor", pair)
+    mine_b, far_b = exchange(keep_b, other_b)
     for there in far_stored:
-        there = [after(x, keep_b) for x in there]
-        beside = [lax.ppermute(x, "tensor", pair) for x in there]
-        there[0] = after(there[0], mine_b)
-        factors += [factors_of(*there)[:2], factors_of(*beside)[:2]]
-    sums_a = total(after(mine_a, *[pair[0] for pair in factors]), far_a)
+        beside = [lax.ppermute(x, "tensor", pair) for x in (after(there[0], mine_a), there[1])]
+        for both in (there, beside):
+            factors.append(factors_of([after(both[0], keep_b), both[1]])[:2])
+    sums_a = total(after(mine_a, mine_b, *[pair[0] for pair in factors]), far_a)
     there_a = second(0, sums_a, ())
-    sums_b = total(after(mine_b, there_a[0], inputs[-1]), far_b)
-
+    sums_b = total(after(mine_b, there_a[0]), far_b)
     a_part = down_part(meta, [sums_a[0], sums_b[0]], hidden)
-    a_column = [a_part] + [lax.ppermute(a_part, "tensor", ring(n_t, 2 * s)) for s in range(1, ny)]
-    there_b = second(1, sums_b, (a_part,))
-
-    a_column = [after(a_column[0], there_b[0])] + a_column[1:]
-    a_beside = lax.ppermute(jnp.concatenate(a_column, axis=0), "tensor", pair)
-    grad_b_down = down_outer(meta, grads, after(acts[2:], there_b[0]))
-    grad_b_gu = gate_up_outer(meta, factors, [sums_a, sums_b], after(acts[:2], grad_b_down))
+    a_parts = [a_part] + [lax.ppermute(a_part, "tensor", ring(n_t, 2 * s)) for s in range(1, ny)]
+    there_b = second(1, sums_b, (a_part, inputs))
+
+    half_a = finish([after(x, there_b[0]) for x in there_a], chunks[0][1])
+    acts = masked_acts(meta, after(adapter_acts.T, half_a), n_t)
+    grad_b_down = down_outer(meta, grads, acts)
+    a_parts = [after(x, half_a) for x in a_parts]
+    a_parts += [lax.ppermute(x, "tensor", pair) for x in a_parts]
+    grad_b_gu = gate_up_outer(meta, factors, [sums_a, sums_b], after(acts, grad_b_down))
 
     def column_tenant(p, m):
         owner = lax.rem(m[1] // 2 + ny - p % ny, ny) * 2
         return tenant_of(m, owner + (m[1] % 2 if p < ny else 1 - m[1] % 2), own_t)
 
-    a_column[0] = after(a_column[0], grad_b_gu)
-    grad_a_down = spread(meta, a_column + [a_beside], column_tenant, R, "spread_a_down")
+    a_parts[0] = after(a_parts[0], grad_b_gu)
+    grad_a_down = spread(meta, a_parts, column_tenant, R, "spread_a_down")
     there_b[0] = after(there_b[0], grad_a_down)
     grad_a_gu = in_outer(meta, [there_a, there_b], inputs, g)
-    half_a = finish([after(there_a[0], grad_a_down)] + there_a[1:], chunks[0][1])
     half_b = finish(there_b, chunks[1][1])
     block_input_grad = jnp.concatenate([half_a, half_b], axis=1).reshape(own_rows, width)
     return (

time: 172 us -> 178 us (1.035)
  between operations: 1.29 us -> 14.5 us
  local copies, waits for them, and re-layouts: 14.3 us -> 6.26 us
  waiting for transfers between devices: 58.1 us -> 51.1 us
  Pallas kernels: 63.7 us -> 68.2 us
  starting transfers between devices: 17.8 us -> 20.2 us
    ppermute x2, waiting for transfers between devices: 7.68 us -> 2.47 us  [exchange(): lax.ppermute(mine, 'tensor', ring(n_t, 2 * s))]
    mul x5 -> x0, local copies, waits for them, and re-layouts: 4.67 us -> none  [per_device(): acts = adapter_acts.T.reshape(3, 1, R, tokens) * onehot[None, :, None, :]]
    ppermute x6, waiting for transfers between devices: 10.4 us -> 6.68 us  [second(): lax.ppermute(outs[r], 'dp', ring(n_dp, r))]
    ppermute x2, starting transfers between devices: 0.67 us -> 3.08 us  [exchange(): lax.ppermute(mine, 'tensor', ring(n_t, 2 * s))]
    slice x10 -> x0, local copies, waits for them, and re-layouts: 2.34 us -> none  [the longest x8 2.32 us: in_outer(): shares = [share[:, width:] for there in shares for share in there]]
    ppermute x16 -> x14, waiting for transfers between devices: 38.7 us -> 40.4 us  [the longest x3 17 us: per_device(): grads[0].append(lax.ppermute(grads[0][-1], 'dp', z_next))]
    ppermute x16 -> x14, starting transfers between devices: 4.65 us -> 5.71 us  [the longest x3 3.14 us: per_device(): grads[0].append(lax.ppermute(grads[0][-1], 'dp', z_next))]
    unnamed x94 -> x68, local copies, waits for them, and re-layouts: 6.21 us -> 5.19 us
  transfers between devices with their start and end apart: 29 -> 28, of which waited for: 15 -> 11; matrix products, arithmetic and copies ran while one was open for 13% -> 9% of each run, Pallas kernels for 36% -> 37%
where the time goes in v3:
time: 178 us
  Pallas kernels  68.2 us (38%)
  waiting for transfers between devices  51.1 us (29%)
  starting transfers between devices  20.2 us (11%)
  other arithmetic  17.4 us (10%)
  between operations  14.5 us (8%)
  local copies, waits for them, and re-layouts  6.26 us (4%)
    pallas_call x2, Pallas kernels, input_partial(): pl.pallas_call(functools.partial(input_kernel, (n_dp, n_t, g, own_t, rc,...  34.1 us
    ppermute x3, waiting for transfers between devices, per_device(): grads[0].append(lax.ppermute(grads[0][-1], 'dp', z_next))  17 us
    pallas_call x2, Pallas kernels, hidden_partial(): pl.pallas_call(functools.partial(hidden_kernel, (n_dp, n_t, g, own_t, rc,...  15.6 us
    ppermute x2, waiting for transfers between devices, per_device(): grads[1].append(lax.ppermute(grads[1][-1], 'dp', z_next))  14.4 us
    convert_element_type x4, other arithmetic, factors_of(): return [x.astype(jnp.bfloat16) for x in (dgate, dup, dup * up_value)]  12.6 us
    ppermute x1, waiting for transfers between devices, per_device(): grads[1].append(lax.ppermute(after(grads[1][-1], mine_a), 'dp', z_next))  8.13 us
    ppermute x6, starting transfers between devices, second(): lax.ppermute(outs[r], 'dp', ring(n_dp, r))  7.05 us
    ppermute x6, waiting for transfers between devices, second(): lax.ppermute(outs[r], 'dp', ring(n_dp, r))  6.68 us
  transfers between devices with their start and end apart: 28, of which 11 were waited for; matrix products, arithmetic and copies ran while one was open for 9% of the time, Pallas kernels for 37%

profile of v3, /device:TPU:0, one launch (start us, length us, event | category | flops | bytes accessed | tf_op | source)
XLA Modules:
  0.0 177.6 jit_solution(9304594016292875586)
XLA Ops:
  8.3 3.1 %collective-permute-start = (bf16[1,64,2048]{2,1,0:T(8,128)(2,1)S(1)}, bf16[1,64,2048]{2,1,0:T(8,128)(2,1)S(1)}, u32[]{:S(2)}, u32[]{:S(2)}) collective-permute-start(bf16[1,64,2048]{2,1,0:T(8,128)(2,1)S(1)} %get-tuple-element.42.refs_0_), channel_id=1, source_target_pairs={{0,1},{1,2},{2,3},{3,0},{4,5},{5,6},{6,7},{7,4},{8,9},{9,10},{10,1... | collective-permute-start | bytes 786440 | tf_op jit(solution)/shard_map/ppermute | solution.py:448
  14.1 5.6 %collective-permute-done.refs_1_ = bf16[1,64,2048]{2,1,0:T(8,128)(2,1)S(1)} collective-permute-done((bf16[1,64,2048]{2,1,0:T(8,128)(2,1)S(1)}, bf16[1,64,2048]{2,1,0:T(8,128)(2,1)S(1)}, u32[]{:S(2)}, u32[]{:S(2)}) %collective-permute-start) | collective-permute-done | bytes 262176 | tf_op jit(solution)/shard_map/ppermute | solution.py:448
  19.7 3.4 %fusion.2 = (bf16[128,3584]{1,0:T(8,128)(2,1)}, bf16[128,3584]{1,0:T(8,128)(2,1)S(1)}, bf16[128,3584]{1,0:T(8,128)(2,1)S(1)}) fusion(bf16[128,3584]{1,0:T(8,128)(2,1)} %param.16, bf16[128,3584]{1,0:T(8,128)(2,1)} %param.15), kind=kLoop, calls=%fused_computation.20 | loop fusion | flops 6881280 | bytes 4587520 | tf_op jit(solution)/shard_map/convert_element_type | solution.py:465
  23.1 7.1 %collective-permute-done.5.refs_2_ = bf16[1,64,2048]{2,1,0:T(8,128)(2,1)S(1)} collective-permute-done((bf16[1,64,2048]{2,1,0:T(8,128)(2,1)S(1)}, bf16[1,64,2048]{2,1,0:T(8,128)(2,1)S(1)}, u32[]{:S(2)}, u32[]{:S(2)}) %collective-permute-start.5) | collective-permute-done | bytes 262176 | tf_op jit(solution)/shard_map/ppermute | solution.py:448
  30.4 3.5 %fusion.13 = (bf16[128,3584]{1,0:T(8,128)(2,1)}, bf16[128,3584]{1,0:T(8,128)(2,1)}) fusion(bf16[128,3584]{1,0:T(8,128)(2,1)S(1)} %collective-permute-done.2, bf16[128,3584]{1,0:T(8,128)(2,1)} %collective-permute-done.1), kind=kLoop, calls=%fused_computation.31 | loop fusion | flops 5963776 | bytes 3670016 | tf_op jit(solution)/shard_map/convert_element_type | solution.py:465
  33.9 7.4 %collective-permute-done.6.refs_1_.refs_5_ = bf16[1,64,2048]{2,1,0:T(8,128)(2,1)S(1)} collective-permute-done((bf16[1,64,2048]{2,1,0:T(8,128)(2,1)S(1)}, bf16[1,64,2048]{2,1,0:T(8,128)(2,1)S(1)}, u32[]{:S(2)}, u32[]{:S(2)}) %collective-permute-start.6) | collective-permute-done | bytes 262176 | tf_op jit(solution)/shard_map/ppermute | solution.py:453
  41.3 4.3 %collective-permute-done.7.refs_3_ = bf16[1,64,2048]{2,1,0:T(8,128)(2,1)S(1)} collective-permute-done((bf16[1,64,2048]{2,1,0:T(8,128)(2,1)S(1)}, bf16[1,64,2048]{2,1,0:T(8,128)(2,1)S(1)}, u32[]{:S(2)}, u32[]{:S(2)}) %collective-permute-start.7) | collective-permute-done | bytes 262176 | tf_op jit(solution)/shard_map/ppermute | solution.py:448
  45.7 7.5 %hidden_partial.2 = (bf16[2,64,3712]{2,1,0:T(8,128)(2,1)S(1)}, bf16[2,64,3712]{2,1,0:T(8,128)(2,1)S(1)}) custom-call(s32[6]{0:T(128)S(1)} %pad_add_fusion.meta, bf16[1,64,2048]{2,1,0:T(8,128)(2,1)S(1)} %get-tuple-element.42.refs_0_, bf16[1,64,2048]{2,1,0:T(8,128)(2,1)S(1)} %copy-done.23, bf16[1,64,2048]{2,1,0:T(8,128)(2,1)S(1)} %collective-permute-done.5.refs_2_, ...), custom_call_target="tpu_custom_call" | custom-call | flops 1 | bytes 1 | tf_op jit(solution)/shard_map/hidden_partial/pallas_call | solution.py:104
  54.1 1.6 collective-permute-start.9
  57.8 7.0 %collective-permute-done.9.refs_2_.refs_6_ = bf16[1,64,2048]{2,1,0:T(8,128)(2,1)} collective-permute-done((bf16[1,64,2048]{2,1,0:T(8,128)(2,1)S(1)}, bf16[1,64,2048]{2,1,0:T(8,128)(2,1)}, u32[]{:S(2)}, u32[]{:S(2)}) %collective-permute-start.9) | collective-permute-done | bytes 262176 | tf_op jit(solution)/shard_map/ppermute | solution.py:453
  66.6 8.1 %collective-permute-done.10.refs_3_.refs_7_ = bf16[1,64,2048]{2,1,0:T(8,128)(2,1)} collective-permute-done((bf16[1,64,2048]{2,1,0:T(8,128)(2,1)}, bf16[1,64,2048]{2,1,0:T(8,128)(2,1)}, u32[]{:S(2)}, u32[]{:S(2)}) %collective-permute-start.10) | collective-permute-done | bytes 262176 | tf_op jit(solution)/shard_map/ppermute | solution.py:488
  75.7 8.0 %hidden_partial.3 = (bf16[2,64,3712]{2,1,0:T(8,128)(2,1)S(1)}, bf16[2,64,3712]{2,1,0:T(8,128)(2,1)S(1)}) custom-call(s32[6]{0:T(128)S(1)} %pad_add_fusion.meta, bf16[1,64,2048]{2,1,0:T(8,128)(2,1)S(1)} %get-tuple-element.46.refs_0_.refs_4_, bf16[1,64,2048]{2,1,0:T(8,128)(2,1)S(1)} %copy-done.28, bf16[1,64,2048]{2,1,0:T(8,128)(2,1)} %collective-permute-done.9.refs_2_.refs_6_, ...), custom_call_target="tpu_custom_call" | custom-call | flops 1 | bytes 1 | tf_op jit(solution)/shard_map/hidden_partial/pallas_call | solution.py:104
  83.8 3.6 %fusion.20 = (bf16[128,3584]{1,0:T(8,128)(2,1)}, bf16[128,3584]{1,0:T(8,128)(2,1)}) fusion(bf16[128,3584]{1,0:T(8,128)(2,1)} %collective-permute-done.4, bf16[128,3584]{1,0:T(8,128)(2,1)} %collective-permute-done.3), kind=kLoop, calls=%fused_computation.38 | loop fusion | flops 5963776 | bytes 3670016 | tf_op jit(solution)/shard_map/convert_element_type | solution.py:465
  87.4 2.1 %fusion.27 = (bf16[128,3584]{1,0:T(8,128)(2,1)}, bf16[128,3584]{1,0:T(8,128)(2,1)}) fusion(bf16[128,3584]{1,0:T(8,128)(2,1)S(1)} %collective-permute-done.12, bf16[128,3584]{1,0:T(8,128)(2,1)S(1)} %collective-permute-done.11), kind=kLoop, calls=%fused_computation.45 | loop fusion | flops 5963776 | bytes 3670016 | tf_op jit(solution)/shard_map/convert_element_type | solution.py:465
  94.6 17.4 %input_partial.2 = (bf16[64,2176]{1,0:T(8,128)(2,1)S(1)}, bf16[64,2176]{1,0:T(8,128)(2,1)}, bf16[64,2176]{1,0:T(8,128)(2,1)}, bf16[64,2176]{1,0:T(8,128)(2,1)}) custom-call(s32[6]{0:T(128)S(1)} %pad_add_fusion.meta, bf16[128,3584]{1,0:T(8,128)(2,1)S(1)} %get-tuple-element.76.refs_0_, bf16[128,3584]{1,0:T(8,128)(2,1)S(1)} %get-tuple-element.77.refs_1_, ...), custom_call_target="tpu_custom_call" | custom-call | flops 1 | bytes 1 | tf_op jit(solution)/shard_map/input_partial/pallas_call | solution.py:194
  112.1 2.5 %collective-permute-done.16 = bf16[2,64,3712]{2,1,0:T(8,128)(2,1)S(1)} collective-permute-done((bf16[2,64,3712]{2,1,0:T(8,128)(2,1)S(1)}, bf16[2,64,3712]{2,1,0:T(8,128)(2,1)S(1)}, u32[]{:S(2)}, u32[]{:S(2)}) %collective-permute-start.16) | collective-permute-done | bytes 950304 | tf_op jit(solution)/shard_map/ppermute | solution.py:469
  114.9 1.6 collective-permute-start.20
  122.1 16.7 %input_partial.3 = (bf16[64,2176]{1,0:T(8,128)(2,1)S(1)}, bf16[64,2176]{1,0:T(8,128)(2,1)S(1)}, bf16[64,2176]{1,0:T(8,128)(2,1)S(1)}, bf16[64,2176]{1,0:T(8,128)(2,1)S(1)}) custom-call(s32[6]{0:T(128)S(1)} %pad_add_fusion.meta, bf16[128,3584]{1,0:T(8,128)(2,1)S(1)} %get-tuple-element.76.refs_0_, bf16[128,3584]{1,0:T(8,128)(2,1)S(1)} %copy-done.11, ...), custom_call_target="tpu_custom_call" | custom-call | flops 1 | bytes 1 | tf_op jit(solution)/shard_map/input_partial/pallas_call | solution.py:194
  138.8 3.2 %collective-permute-start.26 = (bf16[64,2176]{1,0:T(8,128)(2,1)S(1)}, bf16[64,2176]{1,0:T(8,128)(2,1)S(1)}, u32[]{:S(2)}, u32[]{:S(2)}) collective-permute-start(bf16[64,2176]{1,0:T(8,128)(2,1)S(1)} %get-tuple-element.74), channel_id=1, source_target_pairs={{0,3},{1,0},{2,1},{3,2},{4,7},{5,4},{6,5},{7,6},{8,11},{9,8},{10,9... | collective-permute-start | bytes 835592 | tf_op jit(solution)/shard_map/ppermute | solution.py:478
  146.1 4.1 %down_outer.1 = f32[4,16,2048]{2,1,0:T(8,128)} custom-call(s32[6]{0:T(128)S(1)} %pad_add_fusion.meta, bf16[1,64,2048]{2,1,0:T(8,128)(2,1)S(1)} %get-tuple-element.42.refs_0_, bf16[1,64,2048]{2,1,0:T(8,128)(2,1)S(1)} %copy-done.24, bf16[1,64,2048]{2,1,0:T(8,128)(2,1)S(1)} %copy-done.26, bf16[1,64,2048]{2,1,0:T(8,128)(2,1)S(1)} %copy-done.31, ...), custom_call_target="tpu_custom_call" | custom-call | flops 1 | bytes 1 | tf_op jit(solution)/shard_map/down_outer/pallas_call | solution.py:252
  150.3 6.3 %gate_up_outer.1 = f32[4,32,3584]{2,1,0:T(8,128)} custom-call(s32[6]{0:T(128)S(1)} %pad_add_fusion.meta, bf16[128,3584]{1,0:T(8,128)(2,1)S(1)} %get-tuple-element.76.refs_0_, bf16[128,3584]{1,0:T(8,128)(2,1)S(1)} %copy-done.11, bf16[128,3584]{1,0:T(8,128)(2,1)S(1)} %copy-done.5, bf16[128,3584]{1,0:T(8,128)(2,1)S(1)} %copy-done.4, ...), custom_call_target="tpu_custom_call" | custom-call | flops 1 | bytes 1 | tf_op jit(solution)/shard_map/gate_up_outer/pallas_call | solution.py:291
  156.6 3.6 %spread_a_down.1 = f32[4,16,3584]{2,1,0:T(8,128)} custom-call(s32[6]{0:T(128)S(1)} %pad_add_fusion.meta, bf16[16,3584]{1,0:T(8,128)(2,1)S(1)} %down_part.1.refs_0_, bf16[16,3584]{1,0:T(8,128)(2,1)} %collective-permute-done.21.refs_1_, bf16[16,3584]{1,0:T(8,128)(2,1)S(1)} %collective-permute-done.22.refs_2_, bf16[16,3584]{1,0:T(8,128)(2,1)S(1)} %collective-permute-done.23.refs_3_), custom_call_target="tpu_custom_call" | custom-call | flops 1 | bytes 1 | tf_op jit(solution)/shard_map/spread_a_down/pallas_call | solution.py:344
  160.2 6.7 %collective-permute-done.25.refs_6_ = bf16[64,2176]{1,0:T(8,128)(2,1)S(1)} collective-permute-done((bf16[64,2176]{1,0:T(8,128)(2,1)S(1)}, bf16[64,2176]{1,0:T(8,128)(2,1)S(1)}, u32[]{:S(2)}, u32[]{:S(2)}) %collective-permute-start.25) | collective-permute-done | bytes 278560 | tf_op jit(solution)/shard_map/ppermute | solution.py:478
  167.9 2.8 %in_outer.1 = f32[4,32,2048]{2,1,0:T(8,128)} custom-call(s32[6]{0:T(128)S(1)} %pad_add_fusion.meta, bf16[64,2176]{1,0:T(8,128)(2,1)S(1)} %copy-done.20, bf16[64,2176]{1,0:T(8,128)(2,1)} %collective-permute-done.18.refs_1_, bf16[64,2176]{1,0:T(8,128)(2,1)} %collective-permute-done.19.refs_2_, bf16[64,2176]{1,0:T(8,128)(2,1)} %collective-permute-done.20.refs_3_, ...), custom_call_target="tpu_custom_call" | custom-call | flops 1 | bytes 1 | tf_op jit(solution)/shard_map/in_outer/pallas_call | solution.py:384
  (124 shorter events, 25.8 us)
Async XLA Ops:
  7.2 112.6 %all-gather.3.cloned.1.call-start = ((), (), s32[]{:S(2)}) async-start(), calls=%async_computation | async-start | bytes 2621440 | tf_op jit(solution)/shard_map/all_gather | solution.py:489
  8.3 11.4 %collective-permute-start = (bf16[1,64,2048]{2,1,0:T(8,128)(2,1)S(1)}, bf16[1,64,2048]{2,1,0:T(8,128)(2,1)S(1)}, u32[]{:S(2)}, u32[]{:S(2)}) collective-permute-start(bf16[1,64,2048]{2,1,0:T(8,128)(2,1)S(1)} %get-tuple-element.42.refs_0_), channel_id=1, source_target_pairs={{0,1},{1,2},{2,3},{3,0},{4,5},{5,6},{6,7},{7,4},{8,9},{9,10},{10,1... | collective-permute-start | bytes 786440 | tf_op jit(solution)/shard_map/ppermute | solution.py:448
  11.4 18.9 %collective-permute-start.1 = (bf16[128,3584]{1,0:T(8,128)(2,1)}, bf16[128,3584]{1,0:T(8,128)(2,1)}, u32[]{:S(2)}, u32[]{:S(2)}) collective-permute-start(bf16[128,3584]{1,0:T(8,128)(2,1)} %param.16), channel_id=1, source_target_pairs={{0,4},{4,0},{8,12},{12,8},{1,5},{5,1},{9,13},{13,9},{2,6},{6,2},{1... | collective-permute-start | bytes 2752520 | tf_op jit(solution)/shard_map/ppermute | solution.py:450
  11.4 42.7 %collective-permute-start.3 = (bf16[128,3584]{1,0:T(8,128)(2,1)}, bf16[128,3584]{1,0:T(8,128)(2,1)}, u32[]{:S(2)}, u32[]{:S(2)}) collective-permute-start(bf16[128,3584]{1,0:T(8,128)(2,1)} %param.16), channel_id=1, source_target_pairs={{0,8},{4,12},{8,0},{12,4},{1,9},{5,13},{9,1},{13,5},{2,10},{6,14},... | collective-permute-start | bytes 2752520 | tf_op jit(solution)/shard_map/ppermute | solution.py:445
  12.9 41.2 %collective-permute-start.4 = (bf16[128,3584]{1,0:T(8,128)(2,1)}, bf16[128,3584]{1,0:T(8,128)(2,1)}, u32[]{:S(2)}, u32[]{:S(2)}) collective-permute-start(bf16[128,3584]{1,0:T(8,128)(2,1)} %param.15), channel_id=1, source_target_pairs={{0,8},{4,12},{8,0},{12,4},{1,9},{5,13},{9,1},{13,5},{2,10},{6,14},... | collective-permute-start | bytes 2752520 | tf_op jit(solution)/shard_map/ppermute | solution.py:445
  19.7 10.7 %collective-permute-start.2 = (bf16[128,3584]{1,0:T(8,128)(2,1)}, bf16[128,3584]{1,0:T(8,128)(2,1)S(1)}, u32[]{:S(2)}, u32[]{:S(2)}) collective-permute-start(bf16[128,3584]{1,0:T(8,128)(2,1)} %param.15), channel_id=1, source_target_pairs={{0,4},{4,0},{8,12},{12,8},{1,5},{5,1},{9,13},{13,9},{2,6},{6,2},{1... | collective-permute-start | bytes 2752520 | tf_op jit(solution)/shard_map/ppermute | solution.py:450
  19.7 10.5 %collective-permute-start.5 = (bf16[1,64,2048]{2,1,0:T(8,128)(2,1)S(1)}, bf16[1,64,2048]{2,1,0:T(8,128)(2,1)S(1)}, u32[]{:S(2)}, u32[]{:S(2)}) collective-permute-start(bf16[1,64,2048]{2,1,0:T(8,128)(2,1)S(1)} %collective-permute-done.refs_1_), channel_id=1, source_target_pairs={{0,1},{1,2},{2,3},{3,0},{4,5},{5,6},{6,7},{7,4},{8,9},{9,10},{10,1... | collective-permute-start | bytes 786440 | tf_op jit(solution)/shard_map/ppermute | solution.py:448
  30.2 11.1 %collective-permute-start.6 = (bf16[1,64,2048]{2,1,0:T(8,128)(2,1)S(1)}, bf16[1,64,2048]{2,1,0:T(8,128)(2,1)S(1)}, u32[]{:S(2)}, u32[]{:S(2)}) collective-permute-start(bf16[1,64,2048]{2,1,0:T(8,128)(2,1)S(1)} %get-tuple-element.46.refs_0_.refs_4_), channel_id=1, source_target_pairs={{0,1},{1,2},{2,3},{3,0},{4,5},{5,6},{6,7},{7,4},{8,9},{9,10},{10,1... | collective-permute-start | bytes 786440 | tf_op jit(solution)/shard_map/ppermute | solution.py:453
  30.3 15.3 %collective-permute-start.7 = (bf16[1,64,2048]{2,1,0:T(8,128)(2,1)S(1)}, bf16[1,64,2048]{2,1,0:T(8,128)(2,1)S(1)}, u32[]{:S(2)}, u32[]{:S(2)}) collective-permute-start(bf16[1,64,2048]{2,1,0:T(8,128)(2,1)S(1)} %collective-permute-done.5.refs_2_), channel_id=1, source_target_pairs={{0,1},{1,2},{2,3},{3,0},{4,5},{5,6},{6,7},{7,4},{8,9},{9,10},{10,1... | collective-permute-start | bytes 786440 | tf_op jit(solution)/shard_map/ppermute | solution.py:448
  54.1 10.6 %collective-permute-start.9 = (bf16[1,64,2048]{2,1,0:T(8,128)(2,1)S(1)}, bf16[1,64,2048]{2,1,0:T(8,128)(2,1)}, u32[]{:S(2)}, u32[]{:S(2)}) collective-permute-start(bf16[1,64,2048]{2,1,0:T(8,128)(2,1)S(1)} %collective-permute-done.6.refs_1_.refs_5_), channel_id=1, source_target_pairs={{0,1},{1,2},{2,3},{3,0},{4,5},{5,6},{6,7},{7,4},{8,9},{9,10},{10,1... | collective-permute-start | bytes 786440 | tf_op jit(solution)/shard_map/ppermute | solution.py:453
  64.7 10.0 %collective-permute-start.10 = (bf16[1,64,2048]{2,1,0:T(8,128)(2,1)}, bf16[1,64,2048]{2,1,0:T(8,128)(2,1)}, u32[]{:S(2)}, u32[]{:S(2)}) collective-permute-start(bf16[1,64,2048]{2,1,0:T(8,128)(2,1)} %collective-permute-done.9.refs_2_.refs_6_), channel_id=1, source_target_pairs={{0,1},{1,2},{2,3},{3,0},{4,5},{5,6},{6,7},{7,4},{8,9},{9,10},{10,1... | collective-permute-start | bytes 786440 | tf_op jit(solution)/shard_map/ppermute | solution.py:488
  64.8 22.7 %collective-permute-start.11 = (bf16[128,3584]{1,0:T(8,128)(2,1)}, bf16[128,3584]{1,0:T(8,128)(2,1)S(1)}, u32[]{:S(2)}, u32[]{:S(2)}) collective-permute-start(bf16[128,3584]{1,0:T(8,128)(2,1)} %collective-permute-done.3), channel_id=1, source_target_pairs={{0,4},{4,0},{8,12},{12,8},{1,5},{5,1},{9,13},{13,9},{2,6},{6,2},{1... | collective-permute-start | bytes 2752520 | tf_op jit(solution)/shard_map/ppermute | solution.py:494
  64.8 24.9 %collective-permute-start.14 = (bf16[2,64,3712]{2,1,0:T(8,128)(2,1)}, bf16[2,64,3712]{2,1,0:T(8,128)(2,1)S(1)}, u32[]{:S(2)}, u32[]{:S(2)}) collective-permute-start(bf16[2,64,3712]{2,1,0:T(8,128)(2,1)} %add_convert_fusion.3), channel_id=1, source_target_pairs={{0,8},{4,12},{8,0},{12,4},{1,9},{5,13},{9,1},{13,5},{2,10},{6,14},... | collective-permute-start | bytes 2850824 | tf_op jit(solution)/shard_map/ppermute | solution.py:469
  66.4 21.0 %collective-permute-start.12 = (bf16[128,3584]{1,0:T(8,128)(2,1)}, bf16[128,3584]{1,0:T(8,128)(2,1)S(1)}, u32[]{:S(2)}, u32[]{:S(2)}) collective-permute-start(bf16[128,3584]{1,0:T(8,128)(2,1)} %collective-permute-done.4), channel_id=1, source_target_pairs={{0,4},{4,0},{8,12},{12,8},{1,5},{5,1},{9,13},{13,9},{2,6},{6,2},{1... | collective-permute-start | bytes 2752520 | tf_op jit(solution)/shard_map/ppermute | solution.py:494
  91.5 23.0 %collective-permute-start.16 = (bf16[2,64,3712]{2,1,0:T(8,128)(2,1)S(1)}, bf16[2,64,3712]{2,1,0:T(8,128)(2,1)S(1)}, u32[]{:S(2)}, u32[]{:S(2)}) collective-permute-start(bf16[2,64,3712]{2,1,0:T(8,128)(2,1)S(1)} %add_convert_fusion.2), channel_id=1, source_target_pairs={{0,8},{4,12},{8,0},{12,4},{1,9},{5,13},{9,1},{13,5},{2,10},{6,14},... | collective-permute-start | bytes 2850824 | tf_op jit(solution)/shard_map/ppermute | solution.py:469
  114.9 27.1 %collective-permute-start.20 = (bf16[64,2176]{1,0:T(8,128)(2,1)}, bf16[64,2176]{1,0:T(8,128)(2,1)}, u32[]{:S(2)}, u32[]{:S(2)}) collective-permute-start(bf16[64,2176]{1,0:T(8,128)(2,1)} %get-tuple-element.64), channel_id=1, source_target_pairs={{0,3},{1,0},{2,1},{3,2},{4,7},{5,4},{6,5},{7,6},{8,11},{9,8},{10,9... | collective-permute-start | bytes 835592 | tf_op jit(solution)/shard_map/ppermute | solution.py:478
  116.5 26.6 %collective-permute-start.19 = (bf16[64,2176]{1,0:T(8,128)(2,1)}, bf16[64,2176]{1,0:T(8,128)(2,1)}, u32[]{:S(2)}, u32[]{:S(2)}) collective-permute-start(bf16[64,2176]{1,0:T(8,128)(2,1)} %get-tuple-element.62), channel_id=1, source_target_pairs={{0,2},{1,3},{2,0},{3,1},{4,6},{5,7},{6,4},{7,5},{8,10},{9,11},{10,... | collective-permute-start | bytes 835592 | tf_op jit(solution)/shard_map/ppermute | solution.py:478
  116.5 27.1 %collective-permute-start.18 = (bf16[64,2176]{1,0:T(8,128)(2,1)}, bf16[64,2176]{1,0:T(8,128)(2,1)}, u32[]{:S(2)}, u32[]{:S(2)}) collective-permute-start(bf16[64,2176]{1,0:T(8,128)(2,1)} %get-tuple-element.60), channel_id=1, source_target_pairs={{0,1},{1,2},{2,3},{3,0},{4,5},{5,6},{6,7},{7,4},{8,9},{9,10},{10,1... | collective-permute-start | bytes 835592 | tf_op jit(solution)/shard_map/ppermute | solution.py:478
  118.2 26.7 %collective-permute-start.21 = (bf16[16,3584]{1,0:T(8,128)(2,1)S(1)}, bf16[16,3584]{1,0:T(8,128)(2,1)}, u32[]{:S(2)}, u32[]{:S(2)}) collective-permute-start(bf16[16,3584]{1,0:T(8,128)(2,1)S(1)} %down_part.1.refs_0_), channel_id=1, source_target_pairs={{0,8},{4,12},{8,0},{12,4},{1,9},{5,13},{9,1},{13,5},{2,10},{6,14},... | collective-permute-start | bytes 344072 | tf_op jit(solution)/shard_map/ppermute | solution.py:501
  138.8 21.4 %collective-permute-start.26 = (bf16[64,2176]{1,0:T(8,128)(2,1)S(1)}, bf16[64,2176]{1,0:T(8,128)(2,1)S(1)}, u32[]{:S(2)}, u32[]{:S(2)}) collective-permute-start(bf16[64,2176]{1,0:T(8,128)(2,1)S(1)} %get-tuple-element.74), channel_id=1, source_target_pairs={{0,3},{1,0},{2,1},{3,2},{4,7},{5,4},{6,5},{7,6},{8,11},{9,8},{10,9... | collective-permute-start | bytes 835592 | tf_op jit(solution)/shard_map/ppermute | solution.py:478
  142.0 24.9 %collective-permute-start.25 = (bf16[64,2176]{1,0:T(8,128)(2,1)S(1)}, bf16[64,2176]{1,0:T(8,128)(2,1)S(1)}, u32[]{:S(2)}, u32[]{:S(2)}) collective-permute-start(bf16[64,2176]{1,0:T(8,128)(2,1)S(1)} %get-tuple-element.73), channel_id=1, source_target_pairs={{0,2},{1,3},{2,0},{3,1},{4,6},{5,7},{6,4},{7,5},{8,10},{9,11},{10,... | collective-permute-start | bytes 835592 | tf_op jit(solution)/shard_map/ppermute | solution.py:478
  143.1 23.8 %collective-permute-start.24 = (bf16[64,2176]{1,0:T(8,128)(2,1)S(1)}, bf16[64,2176]{1,0:T(8,128)(2,1)S(1)}, u32[]{:S(2)}, u32[]{:S(2)}) collective-permute-start(bf16[64,2176]{1,0:T(8,128)(2,1)S(1)} %get-tuple-element.72), channel_id=1, source_target_pairs={{0,1},{1,2},{2,3},{3,0},{4,5},{5,6},{6,7},{7,4},{8,9},{9,10},{10,1... | collective-permute-start | bytes 835592 | tf_op jit(solution)/shard_map/ppermute | solution.py:478
  144.9 11.7 %collective-permute-start.22 = (bf16[16,3584]{1,0:T(8,128)(2,1)S(1)}, bf16[16,3584]{1,0:T(8,128)(2,1)S(1)}, u32[]{:S(2)}, u32[]{:S(2)}) collective-permute-start(bf16[16,3584]{1,0:T(8,128)(2,1)S(1)} %down_part.1.refs_0_), channel_id=1, source_target_pairs={{0,4},{4,0},{8,12},{12,8},{1,5},{5,1},{9,13},{13,9},{2,6},{6,2},{1... | collective-permute-start | bytes 344072 | tf_op jit(solution)/shard_map/ppermute | solution.py:508
  145.0 11.6 %collective-permute-start.23 = (bf16[16,3584]{1,0:T(8,128)(2,1)}, bf16[16,3584]{1,0:T(8,128)(2,1)S(1)}, u32[]{:S(2)}, u32[]{:S(2)}) collective-permute-start(bf16[16,3584]{1,0:T(8,128)(2,1)} %collective-permute-done.21.refs_1_), channel_id=1, source_target_pairs={{0,4},{4,0},{8,12},{12,8},{1,5},{5,1},{9,13},{13,9},{2,6},{6,2},{1... | collective-permute-start | bytes 344072 | tf_op jit(solution)/shard_map/ppermute | solution.py:508
  (38 other events, 494.9 us)
Sparse Core Ops, SparseCore 0:
  64.9 47.3 all-gather.2

commit v4 on v3

--- a/solution.py
+++ b/solution.py
@@ -53,7 +53,7 @@
     n_dp, n_t, g, own_t, rc, tile = sizes
     ny = n_t // 2
     pieces, (w_ref, bd_ref, ad_ref, keep_ref, send_ref), refs = refs[:n_dp], refs[n_dp : n_dp + 5], refs[n_dp + 5 :]
-    x_scr, p_scr, w_scr, w_sem = refs
+    x_scr, xt_scr, p_scr, w_scr, w_sem = refs
     z, t = meta[0], meta[1]
     y, c = t // 2, t % 2
     hidden_width, width = w_ref.shape
@@ -71,6 +71,7 @@
             owner = lax.rem(z + (n_dp - k), n_dp) * g + j
             away = jnp.where(owner % 2 == c, 0, ny)
             x_scr[away + owner // 2] = pieces[k][j]
+    xt_scr[...] = x_scr[...].reshape(n_t * rc, width).T
     proj = fdot(x_scr[...].reshape(n_t * rc, width), bd_ref[...], NT)
     lane = lax.broadcasted_iota(jnp.int32, (rc, TENANTS * R), 1) // R
     zeros = jnp.zeros((rc, LANES - TENANTS * R), jnp.bfloat16)
@@ -84,7 +85,7 @@
     def body(step, carry):
         at = pl.ds(pl.multiple_of(step * tile, LANES), tile)
         fetch(step).wait()
-        acc = fdot(x_scr[...].reshape(n_t * rc, width), w_scr[step], NT)
+        acc = fdot(w_scr[step], xt_scr[...], NN).T
         acc = (acc + fdot(p_scr[...], ad_ref[:, at], NN)).astype(jnp.bfloat16).reshape(n_t, rc, tile)
         keep_ref[:, :, at] = acc[:ny]
         send_ref[:, :, at] = acc[ny:]
@@ -108,6 +109,7 @@
         out_specs=[VMEM] * 2,
         scratch_shapes=[
             pltpu.VMEM((n_t, rc, width), jnp.bfloat16),
+            pltpu.VMEM((width, n_t * rc), jnp.bfloat16),
             pltpu.VMEM((n_t * rc, low), jnp.bfloat16),
             pltpu.VMEM((hidden_width // tile, tile, width), jnp.bfloat16),
             pltpu.SemaphoreType.DMA((hidden_width // tile,)),
@@ -357,9 +359,9 @@
 
 
 def in_outer_kernel(n_dp, chunks, g, meta, *refs):
-    shares, inputs_ref, out_ref = refs[: n_dp * chunks], refs[-2], refs[-1]
+    shares, inputs, out_ref = refs[: n_dp * chunks], refs[n_dp * chunks : -1], refs[-1]
     out_ref[...] = jnp.zeros_like(out_ref)
-    _, rows, width = inputs_ref.shape
+    rows, width = inputs[0].shape
     own_t = rows // g
     rc = own_t // chunks
     for k in range(n_dp):
@@ -372,24 +374,24 @@
                 query = query + shares[q * n_dp + s][:, at : at + 2 * R].astype(jnp.float32)
             queries.append(query.astype(jnp.bfloat16))
         low = [queries[q][j * rc : (j + 1) * rc] for j in range(g) for q in range(chunks)]
-        total = fdot(jnp.concatenate(low, axis=0), inputs_ref[block], TN)
+        total = fdot(jnp.concatenate(low, axis=0), inputs[k][...], TN)
         tenant = meta[2 + block]
         out_ref[tenant] = out_ref[tenant] + ADAPTER_SCALE * total
 
 
 def in_outer(meta, shares, inputs, g):
-    n_dp, _, width = inputs.shape
+    n_dp, width = len(inputs), inputs[0].shape[1]
     chunks = len(shares)
     shares = [share for there in shares for share in there]
     return pl.pallas_call(
         functools.partial(in_outer_kernel, n_dp, chunks, g),
         out_shape=jax.ShapeDtypeStruct((TENANTS, 2 * R, width), jnp.float32),
-        in_specs=[SMEM] + [VMEM] * (len(shares) + 1),
+        in_specs=[SMEM] + [VMEM] * (len(shares) + n_dp),
         out_specs=VMEM,
         compiler_params=pltpu.CompilerParams(vmem_limit_bytes=VMEM_LIMIT),
         cost_estimate=NO_COST,
         name="in_outer",
-    )(meta, *shares, inputs)
+    )(meta, *shares, *inputs)
 
 
 def ring(n, by):
@@ -446,8 +448,6 @@
     grads = [[out_grad.reshape(g, own_t, width)[:, at : at + rc]] for at, rc in chunks]
     for _ in range(n_dp - 1):
         grads[0].append(lax.ppermute(grads[0][-1], "dp", z_next))
-    stored[0] = after(stored[0], grads[0][1])
-    beside_stored = [lax.ppermute(x, "tensor", pair) for x in stored]
     grads[1][0] = after(grads[1][0], grads[0][2])
     for _ in range(n_dp - 2):
         grads[1].append(lax.ppermute(grads[1][-1], "dp", z_next))
@@ -480,31 +480,37 @@
     def finish(there, rc):
         return add32(*[x[:, :width] for x in there]).astype(jnp.bfloat16).reshape(g, rc, width)
 
+    keep_a, send_a = first(0, (grads[1][1],))
+    stored[0] = after(stored[0], keep_a)
+    beside_stored = [lax.ppermute(x, "tensor", pair) for x in stored]
     *near, hidden = factors_of(stored)
-    factors = [near, factors_of(beside_stored)[:2]]
-    keep_a, send_a = first(0, (grads[1][1], near[0], factors[1][0]))
     other_a = lax.ppermute(after(send_a, *[x for there in far_stored for x in there]), "tensor", pair)
-    mine_a, far_a = exchange(keep_a, other_a)
+    mine_a, far_a = exchange(after(keep_a, near[0]), other_a)
     grads[1].append(lax.ppermute(after(grads[1][-1], mine_a), "dp", z_next))
-    inputs = lax.all_gather(after(layer_input, grads[0][-1]), "dp")
     keep_b, send_b = first(1, (mine_a,))
     other_b = lax.ppermute(send_b, "tensor", pair)
     mine_b, far_b = exchange(keep_b, other_b)
+    beside_stored[0] = after(beside_stored[0], keep_b)
+    factors = [near, factors_of(beside_stored)[:2]]
     for there in far_stored:
         beside = [lax.ppermute(x, "tensor", pair) for x in (after(there[0], mine_a), there[1])]
         for both in (there, beside):
             factors.append(factors_of([after(both[0], keep_b), both[1]])[:2])
-    sums_a = total(after(mine_a, mine_b, *[pair[0] for pair in factors]), far_a)
+    inputs = [layer_input, lax.ppermute(after(layer_input, grads[1][-1]), "dp", z_next)]
+    inputs.append(lax.ppermute(after(inputs[-1], mine_b), "dp", z_next))
+    sums_a = total(after(mine_a, mine_b, inputs[1], *[pair[0] for pair in factors]), far_a)
     there_a = second(0, sums_a, ())
-    sums_b = total(after(mine_b, there_a[0]), far_b)
-    a_part = down_part(meta, [sums_a[0], sums_b[0]], hidden)
-    a_parts = [a_part] + [lax.ppermute(a_part, "tensor", ring(n_t, 2 * s)) for s in range(1, ny)]
-    there_b = second(1, sums_b, (a_part, inputs))
-
-    half_a = finish([after(x, there_b[0]) for x in there_a], chunks[0][1])
+    for step in range(n_dp - 3):
+        inputs.append(lax.ppermute(after(inputs[-1], there_a[0]), "dp", z_next))
+    sums_b = total(after(mine_b, there_a[0], inputs[2]), far_b)
+    there_b = second(1, sums_b, ())
+
+    half_a = finish([after(x, there_b[0], inputs[-1]) for x in there_a], chunks[0][1])
     acts = masked_acts(meta, after(adapter_acts.T, half_a), n_t)
     grad_b_down = down_outer(meta, grads, acts)
-    a_parts = [after(x, half_a) for x in a_parts]
+    a_part = down_part(meta, [sums_a[0], after(sums_b[0], half_a)], hidden)
+    a_parts = [a_part] + [lax.ppermute(a_part, "tensor", ring(n_t, 2 * s)) for s in range(1, ny)]
+    a_parts = [after(x, grad_b_down) for x in a_parts]
     a_parts += [lax.ppermute(x, "tensor", pair) for x in a_parts]
     grad_b_gu = gate_up_outer(meta, factors, [sums_a, sums_b], after(acts, grad_b_down))
 

time: 178 us -> 183 us (1.028); the launches traced: 178 us -> 180 us
  waiting for transfers between devices: 51.1 us -> 73.8 us
  between operations: 14.5 us -> 1 us
  Pallas kernels: 68.2 us -> 63.7 us
  other arithmetic: 17.4 us -> 15.5 us
    ppermute x6, waiting for transfers between devices: 6.68 us -> 16.4 us  [second(): lax.ppermute(outs[r], 'dp', ring(n_dp, r))]
    ppermute x0 -> x3, waiting for transfers between devices: none -> 5.02 us  [the longest x1 5.02 us: per_device(): lax.ppermute(after(layer_input, grads[1][-1]), 'dp', z_next)]
    ppermute x2, waiting for transfers between devices: 14.4 us -> 19.1 us  [per_device(): grads[1].append(lax.ppermute(grads[1][-1], 'dp', z_next))]
    ppermute x3, waiting for transfers between devices: 17 us -> 19.2 us  [per_device(): grads[0].append(lax.ppermute(grads[0][-1], 'dp', z_next))]
    unnamed x68 -> x48, local copies, waits for them, and re-layouts: 5.19 us -> 6.33 us
  transfers between devices with their start and end apart: 28 -> 30, of which waited for: 11 -> 14; matrix products, arithmetic and copies ran while one was open for 9% -> 8% of each run, Pallas kernels for 37% -> 34%
where the time goes in v4:
time: 183 us; the launch traced here: 180 us
  waiting for transfers between devices  73.8 us (40%)
  Pallas kernels  63.7 us (35%)
  starting transfers between devices  18.7 us (10%)
  other arithmetic  15.5 us (8%)
  local copies, waits for them, and re-layouts  7.39 us (4%)
    pallas_call x2, Pallas kernels, input_partial(): pl.pallas_call(functools.partial(input_kernel, (n_dp, n_t, g, own_t, rc,...  33 us
    ppermute x3, waiting for transfers between devices, per_device(): grads[0].append(lax.ppermute(grads[0][-1], 'dp', z_next))  19.2 us
    ppermute x2, waiting for transfers between devices, per_device(): grads[1].append(lax.ppermute(grads[1][-1], 'dp', z_next))  19.1 us
    pallas_call x2, Pallas kernels, hidden_partial(): pl.pallas_call(functools.partial(hidden_kernel, (n_dp, n_t, g, own_t, rc,...  16.5 us
    ppermute x6, waiting for transfers between devices, second(): lax.ppermute(outs[r], 'dp', ring(n_dp, r))  16.4 us
    convert_element_type x4, other arithmetic, factors_of(): return [x.astype(jnp.bfloat16) for x in (dgate, dup, dup * up_value)]  12.8 us
    ppermute x6, starting transfers between devices, second(): lax.ppermute(outs[r], 'dp', ring(n_dp, r))  8.2 us
    ppermute x1, waiting for transfers between devices, per_device(): grads[1].append(lax.ppermute(after(grads[1][-1], mine_a), 'dp', z_next))  7.89 us
  transfers between devices with their start and end apart: 30, of which 14 were waited for; matrix products, arithmetic and copies ran while one was open for 8% of the time, Pallas kernels for 34%

profile of v4, /device:TPU:0, one launch (start us, length us, event | category | flops | bytes accessed | tf_op | source)
XLA Modules:
  0.0 180.0 jit_solution(13352427392951464654)
XLA Ops:
  0.6 3.0 %collective-permute-start.6 = (bf16[128,3584]{1,0:T(8,128)(2,1)}, bf16[128,3584]{1,0:T(8,128)(2,1)S(1)}, u32[]{:S(2)}, u32[]{:S(2)}) collective-permute-start(bf16[128,3584]{1,0:T(8,128)(2,1)} %param.15), channel_id=1, source_target_pairs={{0,8},{4,12},{8,0},{12,4},{1,9},{5,13},{9,1},{13,5},{2,10},{6,14},... | collective-permute-start | bytes 2752520 | tf_op jit(solution)/shard_map/ppermute | solution.py:447
  6.9 7.8 %collective-permute-done.refs_1_ = bf16[1,64,2048]{2,1,0:T(8,128)(2,1)S(1)} collective-permute-done((bf16[1,64,2048]{2,1,0:T(8,128)(2,1)S(1)}, bf16[1,64,2048]{2,1,0:T(8,128)(2,1)S(1)}, u32[]{:S(2)}, u32[]{:S(2)}) %collective-permute-start) | collective-permute-done | bytes 262176 | tf_op jit(solution)/shard_map/ppermute | solution.py:450
  14.6 8.7 %collective-permute-done.1.refs_2_ = bf16[1,64,2048]{2,1,0:T(8,128)(2,1)S(1)} collective-permute-done((bf16[1,64,2048]{2,1,0:T(8,128)(2,1)S(1)}, bf16[1,64,2048]{2,1,0:T(8,128)(2,1)S(1)}, u32[]{:S(2)}, u32[]{:S(2)}) %collective-permute-start.1) | collective-permute-done | bytes 262176 | tf_op jit(solution)/shard_map/ppermute | solution.py:450
  24.0 9.8 %collective-permute-done.2.refs_1_.refs_5_ = bf16[1,64,2048]{2,1,0:T(8,128)(2,1)S(1)} collective-permute-done((bf16[1,64,2048]{2,1,0:T(8,128)(2,1)S(1)}, bf16[1,64,2048]{2,1,0:T(8,128)(2,1)S(1)}, u32[]{:S(2)}, u32[]{:S(2)}) %collective-permute-start.2) | collective-permute-done | bytes 262176 | tf_op jit(solution)/shard_map/ppermute | solution.py:453
  33.8 2.8 %collective-permute-done.3.refs_3_ = bf16[1,64,2048]{2,1,0:T(8,128)(2,1)S(1)} collective-permute-done((bf16[1,64,2048]{2,1,0:T(8,128)(2,1)S(1)}, bf16[1,64,2048]{2,1,0:T(8,128)(2,1)S(1)}, u32[]{:S(2)}, u32[]{:S(2)}) %collective-permute-start.3) | collective-permute-done | bytes 262176 | tf_op jit(solution)/shard_map/ppermute | solution.py:450
  38.6 8.2 %hidden_partial.2 = (bf16[2,64,3712]{2,1,0:T(8,128)(2,1)S(1)}, bf16[2,64,3712]{2,1,0:T(8,128)(2,1)S(1)}) custom-call(s32[6]{0:T(128)S(1)} %pad_add_fusion.meta, bf16[1,64,2048]{2,1,0:T(8,128)(2,1)S(1)} %get-tuple-element.45.refs_0_, bf16[1,64,2048]{2,1,0:T(8,128)(2,1)S(1)} %collective-permute-done.refs_1_, ...), custom_call_target="tpu_custom_call" | custom-call | flops 1 | bytes 1 | tf_op jit(solution)/shard_map/hidden_partial/pallas_call | solution.py:105
  47.5 2.4 %fusion.2 = (bf16[128,3584]{1,0:T(8,128)(2,1)S(1)}, bf16[128,3584]{1,0:T(8,128)(2,1)S(1)}, bf16[128,3584]{1,0:T(8,128)(2,1)S(1)}) fusion(bf16[128,3584]{1,0:T(8,128)(2,1)} %param.16, bf16[128,3584]{1,0:T(8,128)(2,1)} %param.15), kind=kLoop, calls=%fused_computation.20 | loop fusion | flops 6881280 | bytes 4587520 | tf_op jit(solution)/shard_map/convert_element_type | solution.py:465
  51.0 9.3 %collective-permute-done.9.refs_2_.refs_6_ = bf16[1,64,2048]{2,1,0:T(8,128)(2,1)S(1)} collective-permute-done((bf16[1,64,2048]{2,1,0:T(8,128)(2,1)S(1)}, bf16[1,64,2048]{2,1,0:T(8,128)(2,1)S(1)}, u32[]{:S(2)}, u32[]{:S(2)}) %collective-permute-start.9) | collective-permute-done | bytes 262176 | tf_op jit(solution)/shard_map/ppermute | solution.py:453
  61.9 7.9 %collective-permute-done.10.refs_3_.refs_7_ = bf16[1,64,2048]{2,1,0:T(8,128)(2,1)S(1)} collective-permute-done((bf16[1,64,2048]{2,1,0:T(8,128)(2,1)S(1)}, bf16[1,64,2048]{2,1,0:T(8,128)(2,1)S(1)}, u32[]{:S(2)}, u32[]{:S(2)}) %collective-permute-start.10) | collective-permute-done | bytes 262176 | tf_op jit(solution)/shard_map/ppermute | solution.py:489
  69.8 8.2 %hidden_partial.3 = (bf16[2,64,3712]{2,1,0:T(8,128)(2,1)S(1)}, bf16[2,64,3712]{2,1,0:T(8,128)(2,1)S(1)}) custom-call(s32[6]{0:T(128)S(1)} %pad_add_fusion.meta, bf16[1,64,2048]{2,1,0:T(8,128)(2,1)S(1)} %get-tuple-element.51.refs_0_.refs_4_, bf16[1,64,2048]{2,1,0:T(8,128)(2,1)S(1)} %collective-permute-done.2.refs_1_.refs_5_, ...), custom_call_target="tpu_custom_call" | custom-call | flops 1 | bytes 1 | tf_op jit(solution)/shard_map/hidden_partial/pallas_call | solution.py:105
  78.1 3.5 %fusion.20 = (bf16[128,3584]{1,0:T(8,128)(2,1)}, bf16[128,3584]{1,0:T(8,128)(2,1)}) fusion(bf16[128,3584]{1,0:T(8,128)(2,1)S(1)} %copy-done.22, bf16[128,3584]{1,0:T(8,128)(2,1)} %collective-permute-done.7), kind=kLoop, calls=%fused_computation.38 | loop fusion | flops 5963776 | bytes 3670016 | tf_op jit(solution)/shard_map/convert_element_type | solution.py:465
  82.2 3.5 %fusion.13 = (bf16[128,3584]{1,0:T(8,128)(2,1)}, bf16[128,3584]{1,0:T(8,128)(2,1)}) fusion(bf16[128,3584]{1,0:T(8,128)(2,1)} %copy-done.23, bf16[128,3584]{1,0:T(8,128)(2,1)} %collective-permute-done.4), kind=kLoop, calls=%fused_computation.31 | loop fusion | flops 5963776 | bytes 3670016 | tf_op jit(solution)/shard_map/convert_element_type | solution.py:465
  85.7 3.3 %fusion.27 = (bf16[128,3584]{1,0:T(8,128)(2,1)}, bf16[128,3584]{1,0:T(8,128)(2,1)}) fusion(bf16[128,3584]{1,0:T(8,128)(2,1)} %collective-permute-done.12, bf16[128,3584]{1,0:T(8,128)(2,1)S(1)} %collective-permute-done.11), kind=kLoop, calls=%fused_computation.45 | loop fusion | flops 5963776 | bytes 3670016 | tf_op jit(solution)/shard_map/convert_element_type | solution.py:465
  89.2 5.0 %collective-permute-done.14.refs_9_ = bf16[128,2048]{1,0:T(8,128)(2,1)S(1)} collective-permute-done((bf16[128,2048]{1,0:T(8,128)(2,1)S(1)}, bf16[128,2048]{1,0:T(8,128)(2,1)S(1)}, u32[]{:S(2)}, u32[]{:S(2)}) %collective-permute-start.14) | collective-permute-done | bytes 524320 | tf_op jit(solution)/shard_map/ppermute | solution.py:499
  98.0 16.4 %input_partial.2 = (bf16[64,2176]{1,0:T(8,128)(2,1)S(1)}, bf16[64,2176]{1,0:T(8,128)(2,1)S(1)}, bf16[64,2176]{1,0:T(8,128)(2,1)S(1)}, bf16[64,2176]{1,0:T(8,128)(2,1)S(1)}) custom-call(s32[6]{0:T(128)S(1)} %pad_add_fusion.meta, bf16[128,3584]{1,0:T(8,128)(2,1)S(1)} %get-tuple-element.84.refs_0_, bf16[128,3584]{1,0:T(8,128)(2,1)S(1)} %get-tuple-element.85.refs_1_, ...), custom_call_target="tpu_custom_call" | custom-call | flops 1 | bytes 1 | tf_op jit(solution)/shard_map/input_partial/pallas_call | solution.py:196
  114.4 3.6 %collective-permute-done.18 = bf16[2,64,3712]{2,1,0:T(8,128)(2,1)S(1)} collective-permute-done((bf16[2,64,3712]{2,1,0:T(8,128)(2,1)S(1)}, bf16[2,64,3712]{2,1,0:T(8,128)(2,1)S(1)}, u32[]{:S(2)}, u32[]{:S(2)}) %collective-permute-start.18) | collective-permute-done | bytes 950304 | tf_op jit(solution)/shard_map/ppermute | solution.py:469
  118.4 3.8 %collective-permute-start.23 = (bf16[64,2176]{1,0:T(8,128)(2,1)S(1)}, bf16[64,2176]{1,0:T(8,128)(2,1)S(1)}, u32[]{:S(2)}, u32[]{:S(2)}) collective-permute-start(bf16[64,2176]{1,0:T(8,128)(2,1)S(1)} %get-tuple-element.71), channel_id=1, source_target_pairs={{0,3},{1,0},{2,1},{3,2},{4,7},{5,4},{6,5},{7,6},{8,11},{9,8},{10,9... | collective-permute-start | bytes 835592 | tf_op jit(solution)/shard_map/ppermute | solution.py:478
  123.7 16.6 %input_partial.3 = (bf16[64,2176]{1,0:T(8,128)(2,1)S(1)}, bf16[64,2176]{1,0:T(8,128)(2,1)S(1)}, bf16[64,2176]{1,0:T(8,128)(2,1)S(1)}, bf16[64,2176]{1,0:T(8,128)(2,1)S(1)}) custom-call(s32[6]{0:T(128)S(1)} %pad_add_fusion.meta, bf16[128,3584]{1,0:T(8,128)(2,1)S(1)} %get-tuple-element.84.refs_0_, bf16[128,3584]{1,0:T(8,128)(2,1)S(1)} %get-tuple-element.85.refs_1_, ...), custom_call_target="tpu_custom_call" | custom-call | flops 1 | bytes 1 | tf_op jit(solution)/shard_map/input_partial/pallas_call | solution.py:196
  142.4 12.2 %collective-permute-done.22.refs_2_ = bf16[64,2176]{1,0:T(8,128)(2,1)S(1)} collective-permute-done((bf16[64,2176]{1,0:T(8,128)(2,1)S(1)}, bf16[64,2176]{1,0:T(8,128)(2,1)S(1)}, u32[]{:S(2)}, u32[]{:S(2)}) %collective-permute-start.22) | collective-permute-done | bytes 278560 | tf_op jit(solution)/shard_map/ppermute | solution.py:478
  154.8 3.7 %collective-permute-start.29 = (bf16[64,2176]{1,0:T(8,128)(2,1)S(1)}, bf16[64,2176]{1,0:T(8,128)(2,1)S(1)}, u32[]{:S(2)}, u32[]{:S(2)}) collective-permute-start(bf16[64,2176]{1,0:T(8,128)(2,1)S(1)} %get-tuple-element.82), channel_id=1, source_target_pairs={{0,3},{1,0},{2,1},{3,2},{4,7},{5,4},{6,5},{7,6},{8,11},{9,8},{10,9... | collective-permute-start | bytes 835592 | tf_op jit(solution)/shard_map/ppermute | solution.py:478
  162.6 2.7 %down_outer.1 = f32[4,16,2048]{2,1,0:T(8,128)} custom-call(s32[6]{0:T(128)S(1)} %pad_add_fusion.meta, bf16[1,64,2048]{2,1,0:T(8,128)(2,1)S(1)} %get-tuple-element.45.refs_0_, bf16[1,64,2048]{2,1,0:T(8,128)(2,1)S(1)} %collective-permute-done.refs_1_, bf16[1,64,2048]{2,1,0:T(8,128)(2,1)S(1)} %collective-permute-done.1.refs_2_, ...), custom_call_target="tpu_custom_call" | custom-call | flops 1 | bytes 1 | tf_op jit(solution)/shard_map/down_outer/pallas_call | solution.py:254
  167.0 5.6 %gate_up_outer.1 = f32[4,32,3584]{2,1,0:T(8,128)} custom-call(s32[6]{0:T(128)S(1)} %pad_add_fusion.meta, bf16[128,3584]{1,0:T(8,128)(2,1)S(1)} %get-tuple-element.84.refs_0_, bf16[128,3584]{1,0:T(8,128)(2,1)S(1)} %get-tuple-element.85.refs_1_, bf16[128,3584]{1,0:T(8,128)(2,1)S(1)} %copy-done.8, bf16[128,3584]{1,0:T(8,128)(2,1)S(1)} %copy-done.7, ...), custom_call_target="tpu_custom_call" | custom-call | flops 1 | bytes 1 | tf_op jit(solution)/shard_map/gate_up_outer/pallas_call | solution.py:293
  172.6 2.2 %spread_a_down.1 = f32[4,16,3584]{2,1,0:T(8,128)} custom-call(s32[6]{0:T(128)S(1)} %pad_add_fusion.meta, bf16[16,3584]{1,0:T(8,128)(2,1)S(1)} %down_part.1.refs_0_, bf16[16,3584]{1,0:T(8,128)(2,1)S(1)} %collective-permute-done.24.refs_1_, bf16[16,3584]{1,0:T(8,128)(2,1)S(1)} %collective-permute-done.25.refs_2_, ...), custom_call_target="tpu_custom_call" | custom-call | flops 1 | bytes 1 | tf_op jit(solution)/shard_map/spread_a_down/pallas_call | solution.py:346
  177.8 2.3 %in_outer.1 = f32[4,32,2048]{2,1,0:T(8,128)} custom-call(s32[6]{0:T(128)S(1)} %pad_add_fusion.meta, bf16[64,2176]{1,0:T(8,128)(2,1)S(1)} %get-tuple-element.66.refs_0_, bf16[64,2176]{1,0:T(8,128)(2,1)S(1)} %collective-permute-done.21.refs_1_, bf16[64,2176]{1,0:T(8,128)(2,1)S(1)} %collective-permute-done.22.refs_2_, ...), custom_call_target="tpu_custom_call" | custom-call | flops 1 | bytes 1 | tf_op jit(solution)/shard_map/in_outer/pallas_call | solution.py:386
  (107 shorter events, 26.6 us)
Async XLA Ops:
  0.6 46.3 %collective-permute-start.6 = (bf16[128,3584]{1,0:T(8,128)(2,1)}, bf16[128,3584]{1,0:T(8,128)(2,1)S(1)}, u32[]{:S(2)}, u32[]{:S(2)}) collective-permute-start(bf16[128,3584]{1,0:T(8,128)(2,1)} %param.15), channel_id=1, source_target_pairs={{0,8},{4,12},{8,0},{12,4},{1,9},{5,13},{9,1},{13,5},{2,10},{6,14},... | collective-permute-start | bytes 2752520 | tf_op jit(solution)/shard_map/ppermute | solution.py:447
  3.7 43.3 %collective-permute-start.7 = (bf16[128,3584]{1,0:T(8,128)(2,1)}, bf16[128,3584]{1,0:T(8,128)(2,1)}, u32[]{:S(2)}, u32[]{:S(2)}) collective-permute-start(bf16[128,3584]{1,0:T(8,128)(2,1)} %param.16), channel_id=1, source_target_pairs={{0,8},{4,12},{8,0},{12,4},{1,9},{5,13},{9,1},{13,5},{2,10},{6,14},... | collective-permute-start | bytes 2752520 | tf_op jit(solution)/shard_map/ppermute | solution.py:447
  4.8 9.8 %collective-permute-start = (bf16[1,64,2048]{2,1,0:T(8,128)(2,1)S(1)}, bf16[1,64,2048]{2,1,0:T(8,128)(2,1)S(1)}, u32[]{:S(2)}, u32[]{:S(2)}) collective-permute-start(bf16[1,64,2048]{2,1,0:T(8,128)(2,1)S(1)} %get-tuple-element.45.refs_0_), channel_id=1, source_target_pairs={{0,1},{1,2},{2,3},{3,0},{4,5},{5,6},{6,7},{7,4},{8,9},{9,10},{10,1... | collective-permute-start | bytes 786440 | tf_op jit(solution)/shard_map/ppermute | solution.py:450
  14.6 8.7 %collective-permute-start.1 = (bf16[1,64,2048]{2,1,0:T(8,128)(2,1)S(1)}, bf16[1,64,2048]{2,1,0:T(8,128)(2,1)S(1)}, u32[]{:S(2)}, u32[]{:S(2)}) collective-permute-start(bf16[1,64,2048]{2,1,0:T(8,128)(2,1)S(1)} %collective-permute-done.refs_1_), channel_id=1, source_target_pairs={{0,1},{1,2},{2,3},{3,0},{4,5},{5,6},{6,7},{7,4},{8,9},{9,10},{10,1... | collective-permute-start | bytes 786440 | tf_op jit(solution)/shard_map/ppermute | solution.py:450
  23.3 10.5 %collective-permute-start.2 = (bf16[1,64,2048]{2,1,0:T(8,128)(2,1)S(1)}, bf16[1,64,2048]{2,1,0:T(8,128)(2,1)S(1)}, u32[]{:S(2)}, u32[]{:S(2)}) collective-permute-start(bf16[1,64,2048]{2,1,0:T(8,128)(2,1)S(1)} %get-tuple-element.51.refs_0_.refs_4_), channel_id=1, source_target_pairs={{0,1},{1,2},{2,3},{3,0},{4,5},{5,6},{6,7},{7,4},{8,9},{9,10},{10,1... | collective-permute-start | bytes 786440 | tf_op jit(solution)/shard_map/ppermute | solution.py:453
  23.3 13.3 %collective-permute-start.3 = (bf16[1,64,2048]{2,1,0:T(8,128)(2,1)S(1)}, bf16[1,64,2048]{2,1,0:T(8,128)(2,1)S(1)}, u32[]{:S(2)}, u32[]{:S(2)}) collective-permute-start(bf16[1,64,2048]{2,1,0:T(8,128)(2,1)S(1)} %collective-permute-done.1.refs_2_), channel_id=1, source_target_pairs={{0,1},{1,2},{2,3},{3,0},{4,5},{5,6},{6,7},{7,4},{8,9},{9,10},{10,1... | collective-permute-start | bytes 786440 | tf_op jit(solution)/shard_map/ppermute | solution.py:450
  46.8 31.2 %collective-permute-start.5 = (bf16[128,3584]{1,0:T(8,128)(2,1)}, bf16[128,3584]{1,0:T(8,128)(2,1)S(1)}, u32[]{:S(2)}, u32[]{:S(2)}) collective-permute-start(bf16[128,3584]{1,0:T(8,128)(2,1)} %param.15), channel_id=1, source_target_pairs={{0,4},{4,0},{8,12},{12,8},{1,5},{5,1},{9,13},{13,9},{2,6},{6,2},{1... | collective-permute-start | bytes 2752520 | tf_op jit(solution)/shard_map/ppermute | solution.py:485
  50.0 10.3 %collective-permute-start.9 = (bf16[1,64,2048]{2,1,0:T(8,128)(2,1)S(1)}, bf16[1,64,2048]{2,1,0:T(8,128)(2,1)S(1)}, u32[]{:S(2)}, u32[]{:S(2)}) collective-permute-start(bf16[1,64,2048]{2,1,0:T(8,128)(2,1)S(1)} %collective-permute-done.2.refs_1_.refs_5_), channel_id=1, source_target_pairs={{0,1},{1,2},{2,3},{3,0},{4,5},{5,6},{6,7},{7,4},{8,9},{9,10},{10,1... | collective-permute-start | bytes 786440 | tf_op jit(solution)/shard_map/ppermute | solution.py:453
  60.3 9.5 %collective-permute-start.10 = (bf16[1,64,2048]{2,1,0:T(8,128)(2,1)S(1)}, bf16[1,64,2048]{2,1,0:T(8,128)(2,1)S(1)}, u32[]{:S(2)}, u32[]{:S(2)}) collective-permute-start(bf16[1,64,2048]{2,1,0:T(8,128)(2,1)S(1)} %collective-permute-done.9.refs_2_.refs_6_), channel_id=1, source_target_pairs={{0,1},{1,2},{2,3},{3,0},{4,5},{5,6},{6,7},{7,4},{8,9},{9,10},{10,1... | collective-permute-start | bytes 786440 | tf_op jit(solution)/shard_map/ppermute | solution.py:489
  60.3 21.4 %collective-permute-start.4 = (bf16[128,3584]{1,0:T(8,128)(2,1)}, bf16[128,3584]{1,0:T(8,128)(2,1)}, u32[]{:S(2)}, u32[]{:S(2)}) collective-permute-start(bf16[128,3584]{1,0:T(8,128)(2,1)} %param.16), channel_id=1, source_target_pairs={{0,4},{4,0},{8,12},{12,8},{1,5},{5,1},{9,13},{13,9},{2,6},{6,2},{1... | collective-permute-start | bytes 2752520 | tf_op jit(solution)/shard_map/ppermute | solution.py:485
  60.3 25.4 %collective-permute-start.11 = (bf16[128,3584]{1,0:T(8,128)(2,1)}, bf16[128,3584]{1,0:T(8,128)(2,1)S(1)}, u32[]{:S(2)}, u32[]{:S(2)}) collective-permute-start(bf16[128,3584]{1,0:T(8,128)(2,1)} %collective-permute-done.7), channel_id=1, source_target_pairs={{0,4},{4,0},{8,12},{12,8},{1,5},{5,1},{9,13},{13,9},{2,6},{6,2},{1... | collective-permute-start | bytes 2752520 | tf_op jit(solution)/shard_map/ppermute | solution.py:496
  60.8 33.4 %collective-permute-start.15 = (bf16[2,64,3712]{2,1,0:T(8,128)(2,1)S(1)}, bf16[2,64,3712]{2,1,0:T(8,128)(2,1)S(1)}, u32[]{:S(2)}, u32[]{:S(2)}) collective-permute-start(bf16[2,64,3712]{2,1,0:T(8,128)(2,1)S(1)} %add_convert_fusion.3), channel_id=1, source_target_pairs={{0,8},{4,12},{8,0},{12,4},{1,9},{5,13},{9,1},{13,5},{2,10},{6,14},... | collective-permute-start | bytes 2850824 | tf_op jit(solution)/shard_map/ppermute | solution.py:469
  69.8 15.9 %collective-permute-start.12 = (bf16[128,3584]{1,0:T(8,128)(2,1)S(1)}, bf16[128,3584]{1,0:T(8,128)(2,1)}, u32[]{:S(2)}, u32[]{:S(2)}) collective-permute-start(bf16[128,3584]{1,0:T(8,128)(2,1)S(1)} %copy-done.22), channel_id=1, source_target_pairs={{0,4},{4,0},{8,12},{12,8},{1,5},{5,1},{9,13},{13,9},{2,6},{6,2},{1... | collective-permute-start | bytes 2752520 | tf_op jit(solution)/shard_map/ppermute | solution.py:496
  78.0 16.2 %collective-permute-start.14 = (bf16[128,2048]{1,0:T(8,128)(2,1)S(1)}, bf16[128,2048]{1,0:T(8,128)(2,1)S(1)}, u32[]{:S(2)}, u32[]{:S(2)}) collective-permute-start(bf16[128,2048]{1,0:T(8,128)(2,1)S(1)} %copy-done.19), channel_id=1, source_target_pairs={{0,1},{1,2},{2,3},{3,0},{4,5},{5,6},{6,7},{7,4},{8,9},{9,10},{10,1... | collective-permute-start | bytes 1572872 | tf_op jit(solution)/shard_map/ppermute | solution.py:499
  94.5 23.5 %collective-permute-start.18 = (bf16[2,64,3712]{2,1,0:T(8,128)(2,1)S(1)}, bf16[2,64,3712]{2,1,0:T(8,128)(2,1)S(1)}, u32[]{:S(2)}, u32[]{:S(2)}) collective-permute-start(bf16[2,64,3712]{2,1,0:T(8,128)(2,1)S(1)} %add_convert_fusion.2), channel_id=1, source_target_pairs={{0,8},{4,12},{8,0},{12,4},{1,9},{5,13},{9,1},{13,5},{2,10},{6,14},... | collective-permute-start | bytes 2850824 | tf_op jit(solution)/shard_map/ppermute | solution.py:469
  95.7 18.8 %collective-permute-start.17 = (bf16[128,2048]{1,0:T(8,128)(2,1)S(1)}, bf16[128,2048]{1,0:T(8,128)(2,1)S(1)}, u32[]{:S(2)}, u32[]{:S(2)}) collective-permute-start(bf16[128,2048]{1,0:T(8,128)(2,1)S(1)} %collective-permute-done.14.refs_9_), channel_id=1, source_target_pairs={{0,1},{1,2},{2,3},{3,0},{4,5},{5,6},{6,7},{7,4},{8,9},{9,10},{10,1... | collective-permute-start | bytes 1572872 | tf_op jit(solution)/shard_map/ppermute | solution.py:500
  118.3 24.1 %collective-permute-start.20 = (bf16[128,2048]{1,0:T(8,128)(2,1)S(1)}, bf16[128,2048]{1,0:T(8,128)(2,1)S(1)}, u32[]{:S(2)}, u32[]{:S(2)}) collective-permute-start(bf16[128,2048]{1,0:T(8,128)(2,1)S(1)} %collective-permute-done.17.refs_10_), channel_id=1, source_target_pairs={{0,1},{1,2},{2,3},{3,0},{4,5},{5,6},{6,7},{7,4},{8,9},{9,10},{10,1... | collective-permute-start | bytes 1572872 | tf_op jit(solution)/shard_map/ppermute | solution.py:504
  118.4 24.0 %collective-permute-start.23 = (bf16[64,2176]{1,0:T(8,128)(2,1)S(1)}, bf16[64,2176]{1,0:T(8,128)(2,1)S(1)}, u32[]{:S(2)}, u32[]{:S(2)}) collective-permute-start(bf16[64,2176]{1,0:T(8,128)(2,1)S(1)} %get-tuple-element.71), channel_id=1, source_target_pairs={{0,3},{1,0},{2,1},{3,2},{4,7},{5,4},{6,5},{7,6},{8,11},{9,8},{10,9... | collective-permute-start | bytes 835592 | tf_op jit(solution)/shard_map/ppermute | solution.py:478
  122.2 32.5 %collective-permute-start.22 = (bf16[64,2176]{1,0:T(8,128)(2,1)S(1)}, bf16[64,2176]{1,0:T(8,128)(2,1)S(1)}, u32[]{:S(2)}, u32[]{:S(2)}) collective-permute-start(bf16[64,2176]{1,0:T(8,128)(2,1)S(1)} %get-tuple-element.69), channel_id=1, source_target_pairs={{0,2},{1,3},{2,0},{3,1},{4,6},{5,7},{6,4},{7,5},{8,10},{9,11},{10,... | collective-permute-start | bytes 835592 | tf_op jit(solution)/shard_map/ppermute | solution.py:478
  122.2 32.5 %collective-permute-start.21 = (bf16[64,2176]{1,0:T(8,128)(2,1)S(1)}, bf16[64,2176]{1,0:T(8,128)(2,1)S(1)}, u32[]{:S(2)}, u32[]{:S(2)}) collective-permute-start(bf16[64,2176]{1,0:T(8,128)(2,1)S(1)} %get-tuple-element.67), channel_id=1, source_target_pairs={{0,1},{1,2},{2,3},{3,0},{4,5},{5,6},{6,7},{7,4},{8,9},{9,10},{10,1... | collective-permute-start | bytes 835592 | tf_op jit(solution)/shard_map/ppermute | solution.py:478
  154.7 20.2 %collective-permute-start.27 = (bf16[64,2176]{1,0:T(8,128)(2,1)S(1)}, bf16[64,2176]{1,0:T(8,128)(2,1)S(1)}, u32[]{:S(2)}, u32[]{:S(2)}) collective-permute-start(bf16[64,2176]{1,0:T(8,128)(2,1)S(1)} %get-tuple-element.80), channel_id=1, source_target_pairs={{0,1},{1,2},{2,3},{3,0},{4,5},{5,6},{6,7},{7,4},{8,9},{9,10},{10,1... | collective-permute-start | bytes 835592 | tf_op jit(solution)/shard_map/ppermute | solution.py:478
  154.7 22.1 %collective-permute-start.28 = (bf16[64,2176]{1,0:T(8,128)(2,1)S(1)}, bf16[64,2176]{1,0:T(8,128)(2,1)S(1)}, u32[]{:S(2)}, u32[]{:S(2)}) collective-permute-start(bf16[64,2176]{1,0:T(8,128)(2,1)S(1)} %get-tuple-element.81), channel_id=1, source_target_pairs={{0,2},{1,3},{2,0},{3,1},{4,6},{5,7},{6,4},{7,5},{8,10},{9,11},{10,... | collective-permute-start | bytes 835592 | tf_op jit(solution)/shard_map/ppermute | solution.py:478
  154.8 22.0 %collective-permute-start.29 = (bf16[64,2176]{1,0:T(8,128)(2,1)S(1)}, bf16[64,2176]{1,0:T(8,128)(2,1)S(1)}, u32[]{:S(2)}, u32[]{:S(2)}) collective-permute-start(bf16[64,2176]{1,0:T(8,128)(2,1)S(1)} %get-tuple-element.82), channel_id=1, source_target_pairs={{0,3},{1,0},{2,1},{3,2},{4,7},{5,4},{6,5},{7,6},{8,11},{9,8},{10,9... | collective-permute-start | bytes 835592 | tf_op jit(solution)/shard_map/ppermute | solution.py:478
  165.3 7.3 %collective-permute-start.25 = (bf16[16,3584]{1,0:T(8,128)(2,1)S(1)}, bf16[16,3584]{1,0:T(8,128)(2,1)S(1)}, u32[]{:S(2)}, u32[]{:S(2)}) collective-permute-start(bf16[16,3584]{1,0:T(8,128)(2,1)S(1)} %down_part.1.refs_0_), channel_id=1, source_target_pairs={{0,4},{4,0},{8,12},{12,8},{1,5},{5,1},{9,13},{13,9},{2,6},{6,2},{1... | collective-permute-start | bytes 344072 | tf_op jit(solution)/shard_map/ppermute | solution.py:514
  (30 other events, 268.0 us)

commit v5 on v4

--- a/solution.py
+++ b/solution.py
@@ -53,7 +53,7 @@
     n_dp, n_t, g, own_t, rc, tile = sizes
     ny = n_t // 2
     pieces, (w_ref, bd_ref, ad_ref, keep_ref, send_ref), refs = refs[:n_dp], refs[n_dp : n_dp + 5], refs[n_dp + 5 :]
-    x_scr, xt_scr, p_scr, w_scr, w_sem = refs
+    x_scr, p_scr, w_scr, w_sem = refs
     z, t = meta[0], meta[1]
     y, c = t // 2, t % 2
     hidden_width, width = w_ref.shape
@@ -71,7 +71,6 @@
             owner = lax.rem(z + (n_dp - k), n_dp) * g + j
             away = jnp.where(owner % 2 == c, 0, ny)
             x_scr[away + owner // 2] = pieces[k][j]
-    xt_scr[...] = x_scr[...].reshape(n_t * rc, width).T
     proj = fdot(x_scr[...].reshape(n_t * rc, width), bd_ref[...], NT)
     lane = lax.broadcasted_iota(jnp.int32, (rc, TENANTS * R), 1) // R
     zeros = jnp.zeros((rc, LANES - TENANTS * R), jnp.bfloat16)
@@ -85,7 +84,7 @@
     def body(step, carry):
         at = pl.ds(pl.multiple_of(step * tile, LANES), tile)
         fetch(step).wait()
-        acc = fdot(w_scr[step], xt_scr[...], NN).T
+        acc = fdot(x_scr[...].reshape(n_t * rc, width), w_scr[step], NT)
         acc = (acc + fdot(p_scr[...], ad_ref[:, at], NN)).astype(jnp.bfloat16).reshape(n_t, rc, tile)
         keep_ref[:, :, at] = acc[:ny]
         send_ref[:, :, at] = acc[ny:]
@@ -109,7 +108,6 @@
         out_specs=[VMEM] * 2,
         scratch_shapes=[
             pltpu.VMEM((n_t, rc, width), jnp.bfloat16),
-            pltpu.VMEM((width, n_t * rc), jnp.bfloat16),
             pltpu.VMEM((n_t * rc, low), jnp.bfloat16),
             pltpu.VMEM((hidden_width // tile, tile, width), jnp.bfloat16),
             pltpu.SemaphoreType.DMA((hidden_width // tile,)),
@@ -449,7 +447,7 @@
     for _ in range(n_dp - 1):
         grads[0].append(lax.ppermute(grads[0][-1], "dp", z_next))
     grads[1][0] = after(grads[1][0], grads[0][2])
-    for _ in range(n_dp - 2):
+    for _ in range(n_dp - 1):
         grads[1].append(lax.ppermute(grads[1][-1], "dp", z_next))
 
     def first(q, done):
@@ -480,32 +478,34 @@
     def finish(there, rc):
         return add32(*[x[:, :width] for x in there]).astype(jnp.bfloat16).reshape(g, rc, width)
 
-    keep_a, send_a = first(0, (grads[1][1],))
+    keep_a, send_a = first(0, (grads[1][n_dp - 2],))
     stored[0] = after(stored[0], keep_a)
-    beside_stored = [lax.ppermute(x, "tensor", pair) for x in stored]
     *near, hidden = factors_of(stored)
     other_a = lax.ppermute(after(send_a, *[x for there in far_stored for x in there]), "tensor", pair)
     mine_a, far_a = exchange(after(keep_a, near[0]), other_a)
-    grads[1].append(lax.ppermute(after(grads[1][-1], mine_a), "dp", z_next))
+    beside_stored = [lax.ppermute(after(x, mine_a), "tensor", pair) for x in stored]
     keep_b, send_b = first(1, (mine_a,))
     other_b = lax.ppermute(send_b, "tensor", pair)
     mine_b, far_b = exchange(keep_b, other_b)
     beside_stored[0] = after(beside_stored[0], keep_b)
     factors = [near, factors_of(beside_stored)[:2]]
     for there in far_stored:
-        beside = [lax.ppermute(x, "tensor", pair) for x in (after(there[0], mine_a), there[1])]
+        beside = [lax.ppermute(x, "tensor", pair) for x in [after(x, *beside_stored) for x in there]]
         for both in (there, beside):
             factors.append(factors_of([after(both[0], keep_b), both[1]])[:2])
-    inputs = [layer_input, lax.ppermute(after(layer_input, grads[1][-1]), "dp", z_next)]
-    inputs.append(lax.ppermute(after(inputs[-1], mine_b), "dp", z_next))
-    sums_a = total(after(mine_a, mine_b, inputs[1], *[pair[0] for pair in factors]), far_a)
+    inputs = [after(layer_input, grads[1][-1], mine_a)] + [None] * (n_dp - 1)
+    inputs[1] = lax.ppermute(inputs[0], "dp", z_next)
+    inputs[-1] = lax.ppermute(inputs[0], "dp", ring(n_dp, -1))
+    for k in range(2, n_dp // 2 + 1):
+        inputs[k] = lax.ppermute(inputs[k - 1], "dp", z_next)
+    for k in range(2, (n_dp + 1) // 2):
+        inputs[-k] = lax.ppermute(inputs[1 - k], "dp", ring(n_dp, -1))
+    sums_a = total(after(mine_a, mine_b, inputs[1], inputs[-1], *[pair[0] for pair in factors]), far_a)
     there_a = second(0, sums_a, ())
-    for step in range(n_dp - 3):
-        inputs.append(lax.ppermute(after(inputs[-1], there_a[0]), "dp", z_next))
-    sums_b = total(after(mine_b, there_a[0], inputs[2]), far_b)
+    sums_b = total(after(mine_b, there_a[0], inputs[n_dp // 2]), far_b)
     there_b = second(1, sums_b, ())
 
-    half_a = finish([after(x, there_b[0], inputs[-1]) for x in there_a], chunks[0][1])
+    half_a = finish([after(x, there_b[0]) for x in there_a], chunks[0][1])
     acts = masked_acts(meta, after(adapter_acts.T, half_a), n_t)
     grad_b_down = down_outer(meta, grads, acts)
     a_part = down_part(meta, [sums_a[0], after(sums_b[0], half_a)], hidden)

time: 183 us -> 172 us (0.940)
  the two profiles are of different devices: /device:TPU:0 before, /device:TPU:9 now
where the time goes in v5:
time: 172 us; the launch traced here: 171 us
  Pallas kernels  62.4 us (36%)
  waiting for transfers between devices  56.9 us (33%)
  starting transfers between devices  29 us (17%)
  other arithmetic  14.7 us (9%)
  local copies, waits for them, and re-layouts  7.39 us (4%)
    pallas_call x2, Pallas kernels, input_partial(): pl.pallas_call(functools.partial(input_kernel, (n_dp, n_t, g, own_t, rc,...  33 us
    ppermute x3, waiting for transfers between devices, per_device(): grads[1].append(lax.ppermute(grads[1][-1], 'dp', z_next))  22.1 us
    ppermute x3, waiting for transfers between devices, per_device(): grads[0].append(lax.ppermute(grads[0][-1], 'dp', z_next))  16 us
    pallas_call x2, Pallas kernels, hidden_partial(): pl.pallas_call(functools.partial(hidden_kernel, (n_dp, n_t, g, own_t, rc,...  15.1 us
    ppermute x6, waiting for transfers between devices, second(): lax.ppermute(outs[r], 'dp', ring(n_dp, r))  11.9 us
    convert_element_type x4, other arithmetic, factors_of(): return [x.astype(jnp.bfloat16) for x in (dgate, dup, dup * up_value)]  10.8 us
    ppermute x6, starting transfers between devices, second(): lax.ppermute(outs[r], 'dp', ring(n_dp, r))  7.25 us
    unnamed x48, local copies, waits for them, and re-layouts  6.32 us
  transfers between devices with their start and end apart: 30, of which 13 were waited for; matrix products, arithmetic and copies ran while one was open for 7% of the time, Pallas kernels for 35%

profile of v5, /device:TPU:9, one launch (start us, length us, event | category | flops | bytes accessed | tf_op | source)
XLA Modules:
  0.0 171.3 jit_solution(15910902093928131908)
XLA Ops:
  4.5 4.4 %collective-permute-done.refs_1_ = bf16[1,64,2048]{2,1,0:T(8,128)(2,1)S(1)} collective-permute-done((bf16[1,64,2048]{2,1,0:T(8,128)(2,1)S(1)}, bf16[1,64,2048]{2,1,0:T(8,128)(2,1)S(1)}, u32[]{:S(2)}, u32[]{:S(2)}) %collective-permute-start) | collective-permute-done | bytes 262176 | tf_op jit(solution)/shard_map/ppermute | solution.py:448
  10.2 6.5 %collective-permute-done.1.refs_2_ = bf16[1,64,2048]{2,1,0:T(8,128)(2,1)S(1)} collective-permute-done((bf16[1,64,2048]{2,1,0:T(8,128)(2,1)S(1)}, bf16[1,64,2048]{2,1,0:T(8,128)(2,1)S(1)}, u32[]{:S(2)}, u32[]{:S(2)}) %collective-permute-start.1) | collective-permute-done | bytes 262176 | tf_op jit(solution)/shard_map/ppermute | solution.py:448
  16.7 7.4 %collective-permute-done.2.refs_1_.refs_5_ = bf16[1,64,2048]{2,1,0:T(8,128)(2,1)S(1)} collective-permute-done((bf16[1,64,2048]{2,1,0:T(8,128)(2,1)S(1)}, bf16[1,64,2048]{2,1,0:T(8,128)(2,1)S(1)}, u32[]{:S(2)}, u32[]{:S(2)}) %collective-permute-start.2) | collective-permute-done | bytes 262176 | tf_op jit(solution)/shard_map/ppermute | solution.py:451
  26.1 5.2 %collective-permute-done.3.refs_2_.refs_6_ = bf16[1,64,2048]{2,1,0:T(8,128)(2,1)S(1)} collective-permute-done((bf16[1,64,2048]{2,1,0:T(8,128)(2,1)S(1)}, bf16[1,64,2048]{2,1,0:T(8,128)(2,1)S(1)}, u32[]{:S(2)}, u32[]{:S(2)}) %collective-permute-start.3) | collective-permute-done | bytes 262176 | tf_op jit(solution)/shard_map/ppermute | solution.py:451
  31.3 5.1 %collective-permute-done.4.refs_3_ = bf16[1,64,2048]{2,1,0:T(8,128)(2,1)S(1)} collective-permute-done((bf16[1,64,2048]{2,1,0:T(8,128)(2,1)S(1)}, bf16[1,64,2048]{2,1,0:T(8,128)(2,1)S(1)}, u32[]{:S(2)}, u32[]{:S(2)}) %collective-permute-start.4) | collective-permute-done | bytes 262176 | tf_op jit(solution)/shard_map/ppermute | solution.py:448
  38.3 7.6 %hidden_partial.2 = (bf16[2,64,3712]{2,1,0:T(8,128)(2,1)S(1)}, bf16[2,64,3712]{2,1,0:T(8,128)(2,1)S(1)}) custom-call(s32[6]{0:T(128)S(1)} %pad_add_fusion.meta, bf16[1,64,2048]{2,1,0:T(8,128)(2,1)S(1)} %get-tuple-element.45.refs_0_, bf16[1,64,2048]{2,1,0:T(8,128)(2,1)S(1)} %collective-permute-done.refs_1_, ...), custom_call_target="tpu_custom_call" | custom-call | flops 1 | bytes 1 | tf_op jit(solution)/shard_map/hidden_partial/pallas_call | solution.py:104
  45.9 3.7 %collective-permute-start.7 = (bf16[2,64,3712]{2,1,0:T(8,128)(2,1)S(1)}, bf16[2,64,3712]{2,1,0:T(8,128)(2,1)S(1)}, u32[]{:S(2)}, u32[]{:S(2)}) collective-permute-start(bf16[2,64,3712]{2,1,0:T(8,128)(2,1)S(1)} %get-tuple-element.50), channel_id=1, source_target_pairs={{0,4},{4,0},{8,12},{12,8},{1,5},{5,1},{9,13},{13,9},{2,6},{6,2},{1... | collective-permute-start | bytes 2850824 | tf_op jit(solution)/shard_map/ppermute | solution.py:484
  49.6 2.2 %fusion.2 = (bf16[128,3584]{1,0:T(8,128)(2,1)S(1)}, bf16[128,3584]{1,0:T(8,128)(2,1)S(1)}, bf16[128,3584]{1,0:T(8,128)(2,1)S(1)}) fusion(bf16[128,3584]{1,0:T(8,128)(2,1)} %param.16, bf16[128,3584]{1,0:T(8,128)(2,1)S(1)} %copy-done.23), kind=kLoop, calls=%fused_computation.20 | loop fusion | flops 6881280 | bytes 4587520 | tf_op jit(solution)/shard_map/convert_element_type | solution.py:463
  52.1 9.5 %collective-permute-done.10.refs_3_.refs_7_ = bf16[1,64,2048]{2,1,0:T(8,128)(2,1)S(1)} collective-permute-done((bf16[1,64,2048]{2,1,0:T(8,128)(2,1)S(1)}, bf16[1,64,2048]{2,1,0:T(8,128)(2,1)S(1)}, u32[]{:S(2)}, u32[]{:S(2)}) %collective-permute-start.10) | collective-permute-done | bytes 262176 | tf_op jit(solution)/shard_map/ppermute | solution.py:451
  61.6 2.9 %collective-permute-start.15 = (bf16[128,2048]{1,0:T(8,128)(2,1)S(1)}, bf16[128,2048]{1,0:T(8,128)(2,1)S(1)}, u32[]{:S(2)}, u32[]{:S(2)}) collective-permute-start(bf16[128,2048]{1,0:T(8,128)(2,1)S(1)} %copy-done.19), channel_id=1, source_target_pairs={{0,3},{1,0},{2,1},{3,2},{4,7},{5,4},{6,5},{7,6},{8,11},{9,8},{10,9... | collective-permute-start | bytes 1572872 | tf_op jit(solution)/shard_map/ppermute | solution.py:498
  66.6 7.6 %hidden_partial.3 = (bf16[2,64,3712]{2,1,0:T(8,128)(2,1)S(1)}, bf16[2,64,3712]{2,1,0:T(8,128)(2,1)S(1)}) custom-call(s32[6]{0:T(128)S(1)} %pad_add_fusion.meta, bf16[1,64,2048]{2,1,0:T(8,128)(2,1)S(1)} %get-tuple-element.53.refs_0_.refs_4_, bf16[1,64,2048]{2,1,0:T(8,128)(2,1)S(1)} %collective-permute-done.2.refs_1_.refs_5_, ...), custom_call_target="tpu_custom_call" | custom-call | flops 1 | bytes 1 | tf_op jit(solution)/shard_map/hidden_partial/pallas_call | solution.py:104
  74.2 3.3 %fusion.20 = (bf16[128,3584]{1,0:T(8,128)(2,1)}, bf16[128,3584]{1,0:T(8,128)(2,1)}) fusion(bf16[128,3584]{1,0:T(8,128)(2,1)S(1)} %copy-done.22, bf16[128,3584]{1,0:T(8,128)(2,1)} %collective-permute-done.6), kind=kLoop, calls=%fused_computation.38 | loop fusion | flops 5963776 | bytes 3670016 | tf_op jit(solution)/shard_map/convert_element_type | solution.py:463
  78.0 3.3 %fusion.13 = (bf16[128,3584]{1,0:T(8,128)(2,1)}, bf16[128,3584]{1,0:T(8,128)(2,1)}) fusion(bf16[128,3584]{1,0:T(8,128)(2,1)} %collective-permute-done.9, bf16[128,3584]{1,0:T(8,128)(2,1)S(1)} %collective-permute-done.8), kind=kLoop, calls=%fused_computation.31 | loop fusion | flops 5963776 | bytes 3670016 | tf_op jit(solution)/shard_map/convert_element_type | solution.py:463
  83.9 2.1 %fusion.27 = (bf16[128,3584]{1,0:T(8,128)(2,1)}, bf16[128,3584]{1,0:T(8,128)(2,1)}) fusion(bf16[128,3584]{1,0:T(8,128)(2,1)S(1)} %collective-permute-done.12, bf16[128,3584]{1,0:T(8,128)(2,1)S(1)} %collective-permute-done.11), kind=kLoop, calls=%fused_computation.45 | loop fusion | flops 5963776 | bytes 3670016 | tf_op jit(solution)/shard_map/convert_element_type | solution.py:463
  93.3 16.4 %input_partial.2 = (bf16[64,2176]{1,0:T(8,128)(2,1)S(1)}, bf16[64,2176]{1,0:T(8,128)(2,1)S(1)}, bf16[64,2176]{1,0:T(8,128)(2,1)S(1)}, bf16[64,2176]{1,0:T(8,128)(2,1)S(1)}) custom-call(s32[6]{0:T(128)S(1)} %pad_add_fusion.meta, bf16[128,3584]{1,0:T(8,128)(2,1)S(1)} %get-tuple-element.84.refs_0_, bf16[128,3584]{1,0:T(8,128)(2,1)S(1)} %get-tuple-element.85.refs_1_, ...), custom_call_target="tpu_custom_call" | custom-call | flops 1 | bytes 1 | tf_op jit(solution)/shard_map/input_partial/pallas_call | solution.py:194
  109.8 3.1 %collective-permute-done.19 = bf16[2,64,3712]{2,1,0:T(8,128)(2,1)S(1)} collective-permute-done((bf16[2,64,3712]{2,1,0:T(8,128)(2,1)S(1)}, bf16[2,64,3712]{2,1,0:T(8,128)(2,1)S(1)}, u32[]{:S(2)}, u32[]{:S(2)}) %collective-permute-start.19) | collective-permute-done | bytes 950304 | tf_op jit(solution)/shard_map/ppermute | solution.py:467
  118.8 16.6 %input_partial.3 = (bf16[64,2176]{1,0:T(8,128)(2,1)S(1)}, bf16[64,2176]{1,0:T(8,128)(2,1)S(1)}, bf16[64,2176]{1,0:T(8,128)(2,1)S(1)}, bf16[64,2176]{1,0:T(8,128)(2,1)S(1)}) custom-call(s32[6]{0:T(128)S(1)} %pad_add_fusion.meta, bf16[128,3584]{1,0:T(8,128)(2,1)S(1)} %get-tuple-element.84.refs_0_, bf16[128,3584]{1,0:T(8,128)(2,1)S(1)} %get-tuple-element.85.refs_1_, ...), custom_call_target="tpu_custom_call" | custom-call | flops 1 | bytes 1 | tf_op jit(solution)/shard_map/input_partial/pallas_call | solution.py:194
  135.4 5.2 %collective-permute-done.21.refs_1_ = bf16[64,2176]{1,0:T(8,128)(2,1)S(1)} collective-permute-done((bf16[64,2176]{1,0:T(8,128)(2,1)S(1)}, bf16[64,2176]{1,0:T(8,128)(2,1)S(1)}, u32[]{:S(2)}, u32[]{:S(2)}) %collective-permute-start.21) | collective-permute-done | bytes 278560 | tf_op jit(solution)/shard_map/ppermute | solution.py:476
  140.6 2.2 %collective-permute-start.27 = (bf16[64,2176]{1,0:T(8,128)(2,1)S(1)}, bf16[64,2176]{1,0:T(8,128)(2,1)S(1)}, u32[]{:S(2)}, u32[]{:S(2)}) collective-permute-start(bf16[64,2176]{1,0:T(8,128)(2,1)S(1)} %get-tuple-element.80), channel_id=1, source_target_pairs={{0,1},{1,2},{2,3},{3,0},{4,5},{5,6},{6,7},{7,4},{8,9},{9,10},{10,1... | collective-permute-start | bytes 835592 | tf_op jit(solution)/shard_map/ppermute | solution.py:476
  147.3 2.7 %down_outer.1 = f32[4,16,2048]{2,1,0:T(8,128)} custom-call(s32[6]{0:T(128)S(1)} %pad_add_fusion.meta, bf16[1,64,2048]{2,1,0:T(8,128)(2,1)S(1)} %get-tuple-element.45.refs_0_, bf16[1,64,2048]{2,1,0:T(8,128)(2,1)S(1)} %collective-permute-done.refs_1_, bf16[1,64,2048]{2,1,0:T(8,128)(2,1)S(1)} %collective-permute-done.1.refs_2_, ...), custom_call_target="tpu_custom_call" | custom-call | flops 1 | bytes 1 | tf_op jit(solution)/shard_map/down_outer/pallas_call | solution.py:252
  153.6 5.6 %gate_up_outer.1 = f32[4,32,3584]{2,1,0:T(8,128)} custom-call(s32[6]{0:T(128)S(1)} %pad_add_fusion.meta, bf16[128,3584]{1,0:T(8,128)(2,1)S(1)} %get-tuple-element.84.refs_0_, bf16[128,3584]{1,0:T(8,128)(2,1)S(1)} %get-tuple-element.85.refs_1_, bf16[128,3584]{1,0:T(8,128)(2,1)S(1)} %copy-done.8, bf16[128,3584]{1,0:T(8,128)(2,1)S(1)} %copy-done.7, ...), custom_call_target="tpu_custom_call" | custom-call | flops 1 | bytes 1 | tf_op jit(solution)/shard_map/gate_up_outer/pallas_call | solution.py:291
  159.2 2.2 %spread_a_down.1 = f32[4,16,3584]{2,1,0:T(8,128)} custom-call(s32[6]{0:T(128)S(1)} %pad_add_fusion.meta, bf16[16,3584]{1,0:T(8,128)(2,1)S(1)} %down_part.1.refs_0_, bf16[16,3584]{1,0:T(8,128)(2,1)S(1)} %collective-permute-done.24.refs_1_, bf16[16,3584]{1,0:T(8,128)(2,1)S(1)} %collective-permute-done.25.refs_2_, ...), custom_call_target="tpu_custom_call" | custom-call | flops 1 | bytes 1 | tf_op jit(solution)/shard_map/spread_a_down/pallas_call | solution.py:344
  161.4 4.7 %collective-permute-done.28.refs_6_ = bf16[64,2176]{1,0:T(8,128)(2,1)S(1)} collective-permute-done((bf16[64,2176]{1,0:T(8,128)(2,1)S(1)}, bf16[64,2176]{1,0:T(8,128)(2,1)S(1)}, u32[]{:S(2)}, u32[]{:S(2)}) %collective-permute-start.28) | collective-permute-done | bytes 278560 | tf_op jit(solution)/shard_map/ppermute | solution.py:476
  169.1 2.3 %in_outer.1 = f32[4,32,2048]{2,1,0:T(8,128)} custom-call(s32[6]{0:T(128)S(1)} %pad_add_fusion.meta, bf16[64,2176]{1,0:T(8,128)(2,1)S(1)} %get-tuple-element.66.refs_0_, bf16[64,2176]{1,0:T(8,128)(2,1)S(1)} %collective-permute-done.21.refs_1_, bf16[64,2176]{1,0:T(8,128)(2,1)S(1)} %collective-permute-done.22.refs_2_, ...), custom_call_target="tpu_custom_call" | custom-call | flops 1 | bytes 1 | tf_op jit(solution)/shard_map/in_outer/pallas_call | solution.py:384
  (107 shorter events, 38.9 us)
Async XLA Ops:
  1.7 7.2 %collective-permute-start = (bf16[1,64,2048]{2,1,0:T(8,128)(2,1)S(1)}, bf16[1,64,2048]{2,1,0:T(8,128)(2,1)S(1)}, u32[]{:S(2)}, u32[]{:S(2)}) collective-permute-start(bf16[1,64,2048]{2,1,0:T(8,128)(2,1)S(1)} %get-tuple-element.45.refs_0_), channel_id=1, source_target_pairs={{0,1},{1,2},{2,3},{3,0},{4,5},{5,6},{6,7},{7,4},{8,9},{9,10},{10,1... | collective-permute-start | bytes 786440 | tf_op jit(solution)/shard_map/ppermute | solution.py:448
  3.0 42.9 %collective-permute-start.5 = (bf16[128,3584]{1,0:T(8,128)(2,1)}, bf16[128,3584]{1,0:T(8,128)(2,1)S(1)}, u32[]{:S(2)}, u32[]{:S(2)}) collective-permute-start(bf16[128,3584]{1,0:T(8,128)(2,1)} %param.15), channel_id=1, source_target_pairs={{0,8},{4,12},{8,0},{12,4},{1,9},{5,13},{9,1},{13,5},{2,10},{6,14},... | collective-permute-start | bytes 2752520 | tf_op jit(solution)/shard_map/ppermute | solution.py:445
  4.3 41.6 %collective-permute-start.6 = (bf16[128,3584]{1,0:T(8,128)(2,1)}, bf16[128,3584]{1,0:T(8,128)(2,1)}, u32[]{:S(2)}, u32[]{:S(2)}) collective-permute-start(bf16[128,3584]{1,0:T(8,128)(2,1)} %param.16), channel_id=1, source_target_pairs={{0,8},{4,12},{8,0},{12,4},{1,9},{5,13},{9,1},{13,5},{2,10},{6,14},... | collective-permute-start | bytes 2752520 | tf_op jit(solution)/shard_map/ppermute | solution.py:445
  8.9 7.7 %collective-permute-start.1 = (bf16[1,64,2048]{2,1,0:T(8,128)(2,1)S(1)}, bf16[1,64,2048]{2,1,0:T(8,128)(2,1)S(1)}, u32[]{:S(2)}, u32[]{:S(2)}) collective-permute-start(bf16[1,64,2048]{2,1,0:T(8,128)(2,1)S(1)} %collective-permute-done.refs_1_), channel_id=1, source_target_pairs={{0,1},{1,2},{2,3},{3,0},{4,5},{5,6},{6,7},{7,4},{8,9},{9,10},{10,1... | collective-permute-start | bytes 786440 | tf_op jit(solution)/shard_map/ppermute | solution.py:448
  16.7 7.4 %collective-permute-start.2 = (bf16[1,64,2048]{2,1,0:T(8,128)(2,1)S(1)}, bf16[1,64,2048]{2,1,0:T(8,128)(2,1)S(1)}, u32[]{:S(2)}, u32[]{:S(2)}) collective-permute-start(bf16[1,64,2048]{2,1,0:T(8,128)(2,1)S(1)} %get-tuple-element.53.refs_0_.refs_4_), channel_id=1, source_target_pairs={{0,1},{1,2},{2,3},{3,0},{4,5},{5,6},{6,7},{7,4},{8,9},{9,10},{10,1... | collective-permute-start | bytes 786440 | tf_op jit(solution)/shard_map/ppermute | solution.py:451
  24.1 7.1 %collective-permute-start.3 = (bf16[1,64,2048]{2,1,0:T(8,128)(2,1)S(1)}, bf16[1,64,2048]{2,1,0:T(8,128)(2,1)S(1)}, u32[]{:S(2)}, u32[]{:S(2)}) collective-permute-start(bf16[1,64,2048]{2,1,0:T(8,128)(2,1)S(1)} %collective-permute-done.2.refs_1_.refs_5_), channel_id=1, source_target_pairs={{0,1},{1,2},{2,3},{3,0},{4,5},{5,6},{6,7},{7,4},{8,9},{9,10},{10,1... | collective-permute-start | bytes 786440 | tf_op jit(solution)/shard_map/ppermute | solution.py:451
  24.1 12.2 %collective-permute-start.4 = (bf16[1,64,2048]{2,1,0:T(8,128)(2,1)S(1)}, bf16[1,64,2048]{2,1,0:T(8,128)(2,1)S(1)}, u32[]{:S(2)}, u32[]{:S(2)}) collective-permute-start(bf16[1,64,2048]{2,1,0:T(8,128)(2,1)S(1)} %collective-permute-done.1.refs_2_), channel_id=1, source_target_pairs={{0,1},{1,2},{2,3},{3,0},{4,5},{5,6},{6,7},{7,4},{8,9},{9,10},{10,1... | collective-permute-start | bytes 786440 | tf_op jit(solution)/shard_map/ppermute | solution.py:448
  45.9 5.9 %collective-permute-start.7 = (bf16[2,64,3712]{2,1,0:T(8,128)(2,1)S(1)}, bf16[2,64,3712]{2,1,0:T(8,128)(2,1)S(1)}, u32[]{:S(2)}, u32[]{:S(2)}) collective-permute-start(bf16[2,64,3712]{2,1,0:T(8,128)(2,1)S(1)} %get-tuple-element.50), channel_id=1, source_target_pairs={{0,4},{4,0},{8,12},{12,8},{1,5},{5,1},{9,13},{13,9},{2,6},{6,2},{1... | collective-permute-start | bytes 2850824 | tf_op jit(solution)/shard_map/ppermute | solution.py:484
  51.8 9.8 %collective-permute-start.10 = (bf16[1,64,2048]{2,1,0:T(8,128)(2,1)S(1)}, bf16[1,64,2048]{2,1,0:T(8,128)(2,1)S(1)}, u32[]{:S(2)}, u32[]{:S(2)}) collective-permute-start(bf16[1,64,2048]{2,1,0:T(8,128)(2,1)S(1)} %collective-permute-done.3.refs_2_.refs_6_), channel_id=1, source_target_pairs={{0,1},{1,2},{2,3},{3,0},{4,5},{5,6},{6,7},{7,4},{8,9},{9,10},{10,1... | collective-permute-start | bytes 786440 | tf_op jit(solution)/shard_map/ppermute | solution.py:451
  61.6 24.3 %collective-permute-start.15 = (bf16[128,2048]{1,0:T(8,128)(2,1)S(1)}, bf16[128,2048]{1,0:T(8,128)(2,1)S(1)}, u32[]{:S(2)}, u32[]{:S(2)}) collective-permute-start(bf16[128,2048]{1,0:T(8,128)(2,1)S(1)} %copy-done.19), channel_id=1, source_target_pairs={{0,3},{1,0},{2,1},{3,2},{4,7},{5,4},{6,5},{7,6},{8,11},{9,8},{10,9... | collective-permute-start | bytes 1572872 | tf_op jit(solution)/shard_map/ppermute | solution.py:498
  64.6 22.6 %collective-permute-start.14 = (bf16[128,2048]{1,0:T(8,128)(2,1)S(1)}, bf16[128,2048]{1,0:T(8,128)(2,1)S(1)}, u32[]{:S(2)}, u32[]{:S(2)}) collective-permute-start(bf16[128,2048]{1,0:T(8,128)(2,1)S(1)} %copy-done.19), channel_id=1, source_target_pairs={{0,1},{1,2},{2,3},{3,0},{4,5},{5,6},{6,7},{7,4},{8,9},{9,10},{10,1... | collective-permute-start | bytes 1572872 | tf_op jit(solution)/shard_map/ppermute | solution.py:497
  64.6 22.6 %collective-permute-start.16 = (bf16[2,64,3712]{2,1,0:T(8,128)(2,1)S(1)}, bf16[2,64,3712]{2,1,0:T(8,128)(2,1)}, u32[]{:S(2)}, u32[]{:S(2)}) collective-permute-start(bf16[2,64,3712]{2,1,0:T(8,128)(2,1)S(1)} %add_convert_fusion.3), channel_id=1, source_target_pairs={{0,8},{4,12},{8,0},{12,4},{1,9},{5,13},{9,1},{13,5},{2,10},{6,14},... | collective-permute-start | bytes 2850824 | tf_op jit(solution)/shard_map/ppermute | solution.py:467
  64.9 13.1 %collective-permute-start.8 = (bf16[128,3584]{1,0:T(8,128)(2,1)}, bf16[128,3584]{1,0:T(8,128)(2,1)S(1)}, u32[]{:S(2)}, u32[]{:S(2)}) collective-permute-start(bf16[128,3584]{1,0:T(8,128)(2,1)} %param.16), channel_id=1, source_target_pairs={{0,4},{4,0},{8,12},{12,8},{1,5},{5,1},{9,13},{13,9},{2,6},{6,2},{1... | collective-permute-start | bytes 2752520 | tf_op jit(solution)/shard_map/ppermute | solution.py:486
  66.6 10.9 %collective-permute-start.9 = (bf16[128,3584]{1,0:T(8,128)(2,1)S(1)}, bf16[128,3584]{1,0:T(8,128)(2,1)}, u32[]{:S(2)}, u32[]{:S(2)}) collective-permute-start(bf16[128,3584]{1,0:T(8,128)(2,1)S(1)} %copy-done.23), channel_id=1, source_target_pairs={{0,4},{4,0},{8,12},{12,8},{1,5},{5,1},{9,13},{13,9},{2,6},{6,2},{1... | collective-permute-start | bytes 2752520 | tf_op jit(solution)/shard_map/ppermute | solution.py:486
  90.2 22.6 %collective-permute-start.19 = (bf16[2,64,3712]{2,1,0:T(8,128)(2,1)S(1)}, bf16[2,64,3712]{2,1,0:T(8,128)(2,1)S(1)}, u32[]{:S(2)}, u32[]{:S(2)}) collective-permute-start(bf16[2,64,3712]{2,1,0:T(8,128)(2,1)S(1)} %add_convert_fusion.2), channel_id=1, source_target_pairs={{0,8},{4,12},{8,0},{12,4},{1,9},{5,13},{9,1},{13,5},{2,10},{6,14},... | collective-permute-start | bytes 2850824 | tf_op jit(solution)/shard_map/ppermute | solution.py:467
  90.5 19.2 %collective-permute-start.18 = (bf16[128,2048]{1,0:T(8,128)(2,1)S(1)}, bf16[128,2048]{1,0:T(8,128)(2,1)S(1)}, u32[]{:S(2)}, u32[]{:S(2)}) collective-permute-start(bf16[128,2048]{1,0:T(8,128)(2,1)S(1)} %collective-permute-done.14.refs_9_), channel_id=1, source_target_pairs={{0,1},{1,2},{2,3},{3,0},{4,5},{5,6},{6,7},{7,4},{8,9},{9,10},{10,1... | collective-permute-start | bytes 1572872 | tf_op jit(solution)/shard_map/ppermute | solution.py:500
  114.0 21.4 %collective-permute-start.23 = (bf16[64,2176]{1,0:T(8,128)(2,1)S(1)}, bf16[64,2176]{1,0:T(8,128)(2,1)S(1)}, u32[]{:S(2)}, u32[]{:S(2)}) collective-permute-start(bf16[64,2176]{1,0:T(8,128)(2,1)S(1)} %get-tuple-element.71), channel_id=1, source_target_pairs={{0,3},{1,0},{2,1},{3,2},{4,7},{5,4},{6,5},{7,6},{8,11},{9,8},{10,9... | collective-permute-start | bytes 835592 | tf_op jit(solution)/shard_map/ppermute | solution.py:476
  115.4 20.0 %collective-permute-start.22 = (bf16[64,2176]{1,0:T(8,128)(2,1)S(1)}, bf16[64,2176]{1,0:T(8,128)(2,1)S(1)}, u32[]{:S(2)}, u32[]{:S(2)}) collective-permute-start(bf16[64,2176]{1,0:T(8,128)(2,1)S(1)} %get-tuple-element.69), channel_id=1, source_target_pairs={{0,2},{1,3},{2,0},{3,1},{4,6},{5,7},{6,4},{7,5},{8,10},{9,11},{10,... | collective-permute-start | bytes 835592 | tf_op jit(solution)/shard_map/ppermute | solution.py:476
  116.3 24.3 %collective-permute-start.21 = (bf16[64,2176]{1,0:T(8,128)(2,1)S(1)}, bf16[64,2176]{1,0:T(8,128)(2,1)S(1)}, u32[]{:S(2)}, u32[]{:S(2)}) collective-permute-start(bf16[64,2176]{1,0:T(8,128)(2,1)S(1)} %get-tuple-element.67), channel_id=1, source_target_pairs={{0,1},{1,2},{2,3},{3,0},{4,5},{5,6},{6,7},{7,4},{8,9},{9,10},{10,1... | collective-permute-start | bytes 835592 | tf_op jit(solution)/shard_map/ppermute | solution.py:476
  140.6 20.8 %collective-permute-start.27 = (bf16[64,2176]{1,0:T(8,128)(2,1)S(1)}, bf16[64,2176]{1,0:T(8,128)(2,1)S(1)}, u32[]{:S(2)}, u32[]{:S(2)}) collective-permute-start(bf16[64,2176]{1,0:T(8,128)(2,1)S(1)} %get-tuple-element.80), channel_id=1, source_target_pairs={{0,1},{1,2},{2,3},{3,0},{4,5},{5,6},{6,7},{7,4},{8,9},{9,10},{10,1... | collective-permute-start | bytes 835592 | tf_op jit(solution)/shard_map/ppermute | solution.py:476
  142.8 23.4 %collective-permute-start.28 = (bf16[64,2176]{1,0:T(8,128)(2,1)S(1)}, bf16[64,2176]{1,0:T(8,128)(2,1)S(1)}, u32[]{:S(2)}, u32[]{:S(2)}) collective-permute-start(bf16[64,2176]{1,0:T(8,128)(2,1)S(1)} %get-tuple-element.81), channel_id=1, source_target_pairs={{0,2},{1,3},{2,0},{3,1},{4,6},{5,7},{6,4},{7,5},{8,10},{9,11},{10,... | collective-permute-start | bytes 835592 | tf_op jit(solution)/shard_map/ppermute | solution.py:476
  143.4 24.7 %collective-permute-start.29 = (bf16[64,2176]{1,0:T(8,128)(2,1)S(1)}, bf16[64,2176]{1,0:T(8,128)(2,1)S(1)}, u32[]{:S(2)}, u32[]{:S(2)}) collective-permute-start(bf16[64,2176]{1,0:T(8,128)(2,1)S(1)} %get-tuple-element.82), channel_id=1, source_target_pairs={{0,3},{1,0},{2,1},{3,2},{4,7},{5,4},{6,5},{7,6},{8,11},{9,8},{10,9... | collective-permute-start | bytes 835592 | tf_op jit(solution)/shard_map/ppermute | solution.py:476
  150.0 9.2 %collective-permute-start.25 = (bf16[16,3584]{1,0:T(8,128)(2,1)S(1)}, bf16[16,3584]{1,0:T(8,128)(2,1)S(1)}, u32[]{:S(2)}, u32[]{:S(2)}) collective-permute-start(bf16[16,3584]{1,0:T(8,128)(2,1)S(1)} %down_part.1.refs_0_), channel_id=1, source_target_pairs={{0,4},{4,0},{8,12},{12,8},{1,5},{5,1},{9,13},{13,9},{2,6},{6,2},{1... | collective-permute-start | bytes 344072 | tf_op jit(solution)/shard_map/ppermute | solution.py:514
  151.4 7.8 %collective-permute-start.26 = (bf16[16,3584]{1,0:T(8,128)(2,1)S(1)}, bf16[16,3584]{1,0:T(8,128)(2,1)S(1)}, u32[]{:S(2)}, u32[]{:S(2)}) collective-permute-start(bf16[16,3584]{1,0:T(8,128)(2,1)S(1)} %collective-permute-done.24.refs_1_), channel_id=1, source_target_pairs={{0,4},{4,0},{8,12},{12,8},{1,5},{5,1},{9,13},{13,9},{2,6},{6,2},{1... | collective-permute-start | bytes 344072 | tf_op jit(solution)/shard_map/ppermute | solution.py:514
  (30 other events, 230.5 us)

commit v6 on v5

--- a/solution.py
+++ b/solution.py
@@ -478,21 +478,21 @@
     def finish(there, rc):
         return add32(*[x[:, :width] for x in there]).astype(jnp.bfloat16).reshape(g, rc, width)
 
-    keep_a, send_a = first(0, (grads[1][n_dp - 2],))
+    keep_a, send_a = first(0, (grads[1][1],))
     stored[0] = after(stored[0], keep_a)
     *near, hidden = factors_of(stored)
-    other_a = lax.ppermute(after(send_a, *[x for there in far_stored for x in there]), "tensor", pair)
-    mine_a, far_a = exchange(after(keep_a, near[0]), other_a)
+    other_a = lax.ppermute(after(send_a, grads[1][n_dp - 2], *[x for there in far_stored for x in there]), "tensor", pair)
+    mine_a, far_a = exchange(after(keep_a, near[0], grads[1][-1]), other_a)
     beside_stored = [lax.ppermute(after(x, mine_a), "tensor", pair) for x in stored]
     keep_b, send_b = first(1, (mine_a,))
     other_b = lax.ppermute(send_b, "tensor", pair)
-    mine_b, far_b = exchange(keep_b, other_b)
     beside_stored[0] = after(beside_stored[0], keep_b)
     factors = [near, factors_of(beside_stored)[:2]]
     for there in far_stored:
         beside = [lax.ppermute(x, "tensor", pair) for x in [after(x, *beside_stored) for x in there]]
         for both in (there, beside):
             factors.append(factors_of([after(both[0], keep_b), both[1]])[:2])
+    mine_b, far_b = exchange(after(keep_b, *far_a, *[pair[0] for pair in factors]), other_b)
     inputs = [after(layer_input, grads[1][-1], mine_a)] + [None] * (n_dp - 1)
     inputs[1] = lax.ppermute(inputs[0], "dp", z_next)
     inputs[-1] = lax.ppermute(inputs[0], "dp", ring(n_dp, -1))
@@ -500,9 +500,9 @@
         inputs[k] = lax.ppermute(inputs[k - 1], "dp", z_next)
     for k in range(2, (n_dp + 1) // 2):
         inputs[-k] = lax.ppermute(inputs[1 - k], "dp", ring(n_dp, -1))
-    sums_a = total(after(mine_a, mine_b, inputs[1], inputs[-1], *[pair[0] for pair in factors]), far_a)
-    there_a = second(0, sums_a, ())
-    sums_b = total(after(mine_b, there_a[0], inputs[n_dp // 2]), far_b)
+    sums_a = total(after(mine_a, mine_b), far_a)
+    there_a = second(0, sums_a, (inputs[1],))
+    sums_b = total(after(mine_b, there_a[0], inputs[n_dp // 2], inputs[-1]), far_b)
     there_b = second(1, sums_b, ())
 
     half_a = finish([after(x, there_b[0]) for x in there_a], chunks[0][1])

time: 172 us -> 166 us (0.965)
  the two profiles are of different devices: /device:TPU:9 before, /device:TPU:0 now
where the time goes in v6:
time: 166 us; the launch traced here: 163 us
  Pallas kernels  62.4 us (38%)
  waiting for transfers between devices  57.4 us (35%)
  starting transfers between devices  19.6 us (12%)
  other arithmetic  15.1 us (9%)
  local copies, waits for them, and re-layouts  7.39 us (4%)
    pallas_call x2, Pallas kernels, input_partial(): pl.pallas_call(functools.partial(input_kernel, (n_dp, n_t, g, own_t, rc,...  33 us
    ppermute x3, waiting for transfers between devices, per_device(): grads[0].append(lax.ppermute(grads[0][-1], 'dp', z_next))  20.5 us
    ppermute x3, waiting for transfers between devices, per_device(): grads[1].append(lax.ppermute(grads[1][-1], 'dp', z_next))  18.9 us
    pallas_call x2, Pallas kernels, hidden_partial(): pl.pallas_call(functools.partial(hidden_kernel, (n_dp, n_t, g, own_t, rc,...  15.1 us
    convert_element_type x4, other arithmetic, factors_of(): return [x.astype(jnp.bfloat16) for x in (dgate, dup, dup * up_value)]  11.2 us
    ppermute x6, starting transfers between devices, second(): lax.ppermute(outs[r], 'dp', ring(n_dp, r))  7.64 us
    ppermute x6, waiting for transfers between devices, second(): lax.ppermute(outs[r], 'dp', ring(n_dp, r))  7.4 us
    unnamed x46, local copies, waits for them, and re-layouts  6.33 us
  transfers between devices with their start and end apart: 30, of which 11 were waited for; matrix products, arithmetic and copies ran while one was open for 8% of the time, Pallas kernels for 37%

profile of v6, /device:TPU:0, one launch (start us, length us, event | category | flops | bytes accessed | tf_op | source)
XLA Modules:
  0.0 162.9 jit_solution(5014935988351316896)
XLA Ops:
  1.7 3.1 %collective-permute-start = (bf16[1,64,2048]{2,1,0:T(8,128)(2,1)S(1)}, bf16[1,64,2048]{2,1,0:T(8,128)(2,1)S(1)}, u32[]{:S(2)}, u32[]{:S(2)}) collective-permute-start(bf16[1,64,2048]{2,1,0:T(8,128)(2,1)S(1)} %get-tuple-element.47.refs_0_), channel_id=1, source_target_pairs={{0,1},{1,2},{2,3},{3,0},{4,5},{5,6},{6,7},{7,4},{8,9},{9,10},{10,1... | collective-permute-start | bytes 786440 | tf_op jit(solution)/shard_map/ppermute | solution.py:448
  6.8 6.3 %collective-permute-done.refs_1_ = bf16[1,64,2048]{2,1,0:T(8,128)(2,1)S(1)} collective-permute-done((bf16[1,64,2048]{2,1,0:T(8,128)(2,1)S(1)}, bf16[1,64,2048]{2,1,0:T(8,128)(2,1)S(1)}, u32[]{:S(2)}, u32[]{:S(2)}) %collective-permute-start) | collective-permute-done | bytes 262176 | tf_op jit(solution)/shard_map/ppermute | solution.py:448
  13.1 9.3 %collective-permute-done.1.refs_2_ = bf16[1,64,2048]{2,1,0:T(8,128)(2,1)S(1)} collective-permute-done((bf16[1,64,2048]{2,1,0:T(8,128)(2,1)S(1)}, bf16[1,64,2048]{2,1,0:T(8,128)(2,1)S(1)}, u32[]{:S(2)}, u32[]{:S(2)}) %collective-permute-start.1) | collective-permute-done | bytes 262176 | tf_op jit(solution)/shard_map/ppermute | solution.py:448
  22.4 11.0 %collective-permute-done.2.refs_1_.refs_5_ = bf16[1,64,2048]{2,1,0:T(8,128)(2,1)S(1)} collective-permute-done((bf16[1,64,2048]{2,1,0:T(8,128)(2,1)S(1)}, bf16[1,64,2048]{2,1,0:T(8,128)(2,1)S(1)}, u32[]{:S(2)}, u32[]{:S(2)}) %collective-permute-start.2) | collective-permute-done | bytes 262176 | tf_op jit(solution)/shard_map/ppermute | solution.py:451
  34.2 4.9 %collective-permute-done.3.refs_3_ = bf16[1,64,2048]{2,1,0:T(8,128)(2,1)S(1)} collective-permute-done((bf16[1,64,2048]{2,1,0:T(8,128)(2,1)S(1)}, bf16[1,64,2048]{2,1,0:T(8,128)(2,1)S(1)}, u32[]{:S(2)}, u32[]{:S(2)}) %collective-permute-start.3) | collective-permute-done | bytes 262176 | tf_op jit(solution)/shard_map/ppermute | solution.py:448
  41.0 7.6 %hidden_partial.2 = (bf16[2,64,3712]{2,1,0:T(8,128)(2,1)S(1)}, bf16[2,64,3712]{2,1,0:T(8,128)(2,1)S(1)}) custom-call(s32[6]{0:T(128)S(1)} %pad_add_fusion.meta, bf16[1,64,2048]{2,1,0:T(8,128)(2,1)S(1)} %get-tuple-element.47.refs_0_, bf16[1,64,2048]{2,1,0:T(8,128)(2,1)S(1)} %collective-permute-done.refs_1_, ...), custom_call_target="tpu_custom_call" | custom-call | flops 1 | bytes 1 | tf_op jit(solution)/shard_map/hidden_partial/pallas_call | solution.py:104
  48.8 2.6 %fusion.2 = (bf16[128,3584]{1,0:T(8,128)(2,1)S(1)}, bf16[128,3584]{1,0:T(8,128)(2,1)S(1)}, bf16[128,3584]{1,0:T(8,128)(2,1)S(1)}) fusion(bf16[128,3584]{1,0:T(8,128)(2,1)} %param.16, bf16[128,3584]{1,0:T(8,128)(2,1)} %param.15), kind=kLoop, calls=%fused_computation.20 | loop fusion | flops 6881280 | bytes 4587520 | tf_op jit(solution)/shard_map/convert_element_type | solution.py:463
  51.4 7.8 %collective-permute-done.5.refs_3_.refs_7_ = bf16[1,64,2048]{2,1,0:T(8,128)(2,1)S(1)} collective-permute-done((bf16[1,64,2048]{2,1,0:T(8,128)(2,1)S(1)}, bf16[1,64,2048]{2,1,0:T(8,128)(2,1)S(1)}, u32[]{:S(2)}, u32[]{:S(2)}) %collective-permute-start.5) | collective-permute-done | bytes 262176 | tf_op jit(solution)/shard_map/ppermute | solution.py:451
  61.2 7.6 %hidden_partial.3 = (bf16[2,64,3712]{2,1,0:T(8,128)(2,1)S(1)}, bf16[2,64,3712]{2,1,0:T(8,128)(2,1)S(1)}) custom-call(s32[6]{0:T(128)S(1)} %pad_add_fusion.meta, bf16[1,64,2048]{2,1,0:T(8,128)(2,1)S(1)} %get-tuple-element.55.refs_0_.refs_4_, bf16[1,64,2048]{2,1,0:T(8,128)(2,1)S(1)} %collective-permute-done.2.refs_1_.refs_5_, ...), custom_call_target="tpu_custom_call" | custom-call | flops 1 | bytes 1 | tf_op jit(solution)/shard_map/hidden_partial/pallas_call | solution.py:104
  68.9 3.3 %fusion.20 = (bf16[128,3584]{1,0:T(8,128)(2,1)}, bf16[128,3584]{1,0:T(8,128)(2,1)}) fusion(bf16[128,3584]{1,0:T(8,128)(2,1)S(1)} %copy-done.22, bf16[128,3584]{1,0:T(8,128)(2,1)} %collective-permute-done.7), kind=kLoop, calls=%fused_computation.38 | loop fusion | flops 5963776 | bytes 3670016 | tf_op jit(solution)/shard_map/convert_element_type | solution.py:463
  72.7 3.3 %fusion.13 = (bf16[128,3584]{1,0:T(8,128)(2,1)}, bf16[128,3584]{1,0:T(8,128)(2,1)}) fusion(bf16[128,3584]{1,0:T(8,128)(2,1)} %collective-permute-done.10, bf16[128,3584]{1,0:T(8,128)(2,1)S(1)} %collective-permute-done.9), kind=kLoop, calls=%fused_computation.31 | loop fusion | flops 5963776 | bytes 3670016 | tf_op jit(solution)/shard_map/convert_element_type | solution.py:463
  76.0 2.1 %fusion.27 = (bf16[128,3584]{1,0:T(8,128)(2,1)}, bf16[128,3584]{1,0:T(8,128)(2,1)}) fusion(bf16[128,3584]{1,0:T(8,128)(2,1)S(1)} %collective-permute-done.12, bf16[128,3584]{1,0:T(8,128)(2,1)S(1)} %collective-permute-done.11), kind=kLoop, calls=%fused_computation.45 | loop fusion | flops 5963776 | bytes 3670016 | tf_op jit(solution)/shard_map/convert_element_type | solution.py:463
  78.1 4.1 %collective-permute-done.13 = bf16[2,64,3712]{2,1,0:T(8,128)(2,1)} collective-permute-done((bf16[2,64,3712]{2,1,0:T(8,128)(2,1)S(1)}, bf16[2,64,3712]{2,1,0:T(8,128)(2,1)}, u32[]{:S(2)}, u32[]{:S(2)}) %collective-permute-start.13) | collective-permute-done | bytes 950304 | tf_op jit(solution)/shard_map/ppermute | solution.py:467
  85.3 2.0 %collective-permute-start.17 = (bf16[128,2048]{1,0:T(8,128)(2,1)S(1)}, bf16[128,2048]{1,0:T(8,128)(2,1)S(1)}, u32[]{:S(2)}, u32[]{:S(2)}) collective-permute-start(bf16[128,2048]{1,0:T(8,128)(2,1)S(1)} %collective-permute-done.15.refs_9_), channel_id=1, source_target_pairs={{0,1},{1,2},{2,3},{3,0},{4,5},{5,6},{6,7},{7,4},{8,9},{9,10},{10,1... | collective-permute-start | bytes 1572872 | tf_op jit(solution)/shard_map/ppermute | solution.py:500
  88.3 16.4 %input_partial.2 = (bf16[64,2176]{1,0:T(8,128)(2,1)S(1)}, bf16[64,2176]{1,0:T(8,128)(2,1)S(1)}, bf16[64,2176]{1,0:T(8,128)(2,1)S(1)}, bf16[64,2176]{1,0:T(8,128)(2,1)S(1)}) custom-call(s32[6]{0:T(128)S(1)} %pad_add_fusion.meta, bf16[128,3584]{1,0:T(8,128)(2,1)S(1)} %get-tuple-element.88.refs_0_, bf16[128,3584]{1,0:T(8,128)(2,1)S(1)} %get-tuple-element.89.refs_1_, ...), custom_call_target="tpu_custom_call" | custom-call | flops 1 | bytes 1 | tf_op jit(solution)/shard_map/input_partial/pallas_call | solution.py:194
  104.7 5.8 %collective-permute-done.18.refs_11_ = bf16[128,2048]{1,0:T(8,128)(2,1)S(1)} collective-permute-done((bf16[128,2048]{1,0:T(8,128)(2,1)S(1)}, bf16[128,2048]{1,0:T(8,128)(2,1)S(1)}, u32[]{:S(2)}, u32[]{:S(2)}) %collective-permute-start.18) | collective-permute-done | bytes 524320 | tf_op jit(solution)/shard_map/ppermute | solution.py:498
  111.1 1.5 collective-permute-start.22
  115.0 16.6 %input_partial.3 = (bf16[64,2176]{1,0:T(8,128)(2,1)S(1)}, bf16[64,2176]{1,0:T(8,128)(2,1)S(1)}, bf16[64,2176]{1,0:T(8,128)(2,1)S(1)}, bf16[64,2176]{1,0:T(8,128)(2,1)S(1)}) custom-call(s32[6]{0:T(128)S(1)} %pad_add_fusion.meta, bf16[128,3584]{1,0:T(8,128)(2,1)S(1)} %get-tuple-element.88.refs_0_, bf16[128,3584]{1,0:T(8,128)(2,1)S(1)} %get-tuple-element.89.refs_1_, ...), custom_call_target="tpu_custom_call" | custom-call | flops 1 | bytes 1 | tf_op jit(solution)/shard_map/input_partial/pallas_call | solution.py:194
  131.6 5.9 %collective-permute-done.22.refs_2_ = bf16[64,2176]{1,0:T(8,128)(2,1)S(1)} collective-permute-done((bf16[64,2176]{1,0:T(8,128)(2,1)S(1)}, bf16[64,2176]{1,0:T(8,128)(2,1)S(1)}, u32[]{:S(2)}, u32[]{:S(2)}) %collective-permute-start.22) | collective-permute-done | bytes 278560 | tf_op jit(solution)/shard_map/ppermute | solution.py:476
  139.0 2.9 %collective-permute-start.29 = (bf16[64,2176]{1,0:T(8,128)(2,1)S(1)}, bf16[64,2176]{1,0:T(8,128)(2,1)S(1)}, u32[]{:S(2)}, u32[]{:S(2)}) collective-permute-start(bf16[64,2176]{1,0:T(8,128)(2,1)S(1)} %get-tuple-element.86), channel_id=1, source_target_pairs={{0,3},{1,0},{2,1},{3,2},{4,7},{5,4},{6,5},{7,6},{8,11},{9,8},{10,9... | collective-permute-start | bytes 835592 | tf_op jit(solution)/shard_map/ppermute | solution.py:476
  145.9 2.7 %down_outer.1 = f32[4,16,2048]{2,1,0:T(8,128)} custom-call(s32[6]{0:T(128)S(1)} %pad_add_fusion.meta, bf16[1,64,2048]{2,1,0:T(8,128)(2,1)S(1)} %get-tuple-element.47.refs_0_, bf16[1,64,2048]{2,1,0:T(8,128)(2,1)S(1)} %collective-permute-done.refs_1_, bf16[1,64,2048]{2,1,0:T(8,128)(2,1)S(1)} %collective-permute-done.1.refs_2_, ...), custom_call_target="tpu_custom_call" | custom-call | flops 1 | bytes 1 | tf_op jit(solution)/shard_map/down_outer/pallas_call | solution.py:252
  150.5 5.6 %gate_up_outer.1 = f32[4,32,3584]{2,1,0:T(8,128)} custom-call(s32[6]{0:T(128)S(1)} %pad_add_fusion.meta, bf16[128,3584]{1,0:T(8,128)(2,1)S(1)} %get-tuple-element.88.refs_0_, bf16[128,3584]{1,0:T(8,128)(2,1)S(1)} %get-tuple-element.89.refs_1_, bf16[128,3584]{1,0:T(8,128)(2,1)S(1)} %copy-done.8, bf16[128,3584]{1,0:T(8,128)(2,1)S(1)} %copy-done.7, ...), custom_call_target="tpu_custom_call" | custom-call | flops 1 | bytes 1 | tf_op jit(solution)/shard_map/gate_up_outer/pallas_call | solution.py:291
  156.1 2.2 %spread_a_down.1 = f32[4,16,3584]{2,1,0:T(8,128)} custom-call(s32[6]{0:T(128)S(1)} %pad_add_fusion.meta, bf16[16,3584]{1,0:T(8,128)(2,1)S(1)} %down_part.1.refs_0_, bf16[16,3584]{1,0:T(8,128)(2,1)S(1)} %collective-permute-done.24.refs_1_, bf16[16,3584]{1,0:T(8,128)(2,1)S(1)} %collective-permute-done.25.refs_2_, ...), custom_call_target="tpu_custom_call" | custom-call | flops 1 | bytes 1 | tf_op jit(solution)/shard_map/spread_a_down/pallas_call | solution.py:344
  160.7 2.3 %in_outer.1 = f32[4,32,2048]{2,1,0:T(8,128)} custom-call(s32[6]{0:T(128)S(1)} %pad_add_fusion.meta, bf16[64,2176]{1,0:T(8,128)(2,1)S(1)} %get-tuple-element.70.refs_0_, bf16[64,2176]{1,0:T(8,128)(2,1)S(1)} %collective-permute-done.21.refs_1_, bf16[64,2176]{1,0:T(8,128)(2,1)S(1)} %collective-permute-done.22.refs_2_, ...), custom_call_target="tpu_custom_call" | custom-call | flops 1 | bytes 1 | tf_op jit(solution)/shard_map/in_outer/pallas_call | solution.py:384
  (105 shorter events, 25.2 us)
Async XLA Ops:
  1.7 11.4 %collective-permute-start = (bf16[1,64,2048]{2,1,0:T(8,128)(2,1)S(1)}, bf16[1,64,2048]{2,1,0:T(8,128)(2,1)S(1)}, u32[]{:S(2)}, u32[]{:S(2)}) collective-permute-start(bf16[1,64,2048]{2,1,0:T(8,128)(2,1)S(1)} %get-tuple-element.47.refs_0_), channel_id=1, source_target_pairs={{0,1},{1,2},{2,3},{3,0},{4,5},{5,6},{6,7},{7,4},{8,9},{9,10},{10,1... | collective-permute-start | bytes 786440 | tf_op jit(solution)/shard_map/ppermute | solution.py:448
  4.8 43.8 %collective-permute-start.6 = (bf16[128,3584]{1,0:T(8,128)(2,1)}, bf16[128,3584]{1,0:T(8,128)(2,1)S(1)}, u32[]{:S(2)}, u32[]{:S(2)}) collective-permute-start(bf16[128,3584]{1,0:T(8,128)(2,1)} %param.15), channel_id=1, source_target_pairs={{0,8},{4,12},{8,0},{12,4},{1,9},{5,13},{9,1},{13,5},{2,10},{6,14},... | collective-permute-start | bytes 2752520 | tf_op jit(solution)/shard_map/ppermute | solution.py:445
  6.3 42.3 %collective-permute-start.7 = (bf16[128,3584]{1,0:T(8,128)(2,1)}, bf16[128,3584]{1,0:T(8,128)(2,1)}, u32[]{:S(2)}, u32[]{:S(2)}) collective-permute-start(bf16[128,3584]{1,0:T(8,128)(2,1)} %param.16), channel_id=1, source_target_pairs={{0,8},{4,12},{8,0},{12,4},{1,9},{5,13},{9,1},{13,5},{2,10},{6,14},... | collective-permute-start | bytes 2752520 | tf_op jit(solution)/shard_map/ppermute | solution.py:445
  13.1 9.3 %collective-permute-start.1 = (bf16[1,64,2048]{2,1,0:T(8,128)(2,1)S(1)}, bf16[1,64,2048]{2,1,0:T(8,128)(2,1)S(1)}, u32[]{:S(2)}, u32[]{:S(2)}) collective-permute-start(bf16[1,64,2048]{2,1,0:T(8,128)(2,1)S(1)} %collective-permute-done.refs_1_), channel_id=1, source_target_pairs={{0,1},{1,2},{2,3},{3,0},{4,5},{5,6},{6,7},{7,4},{8,9},{9,10},{10,1... | collective-permute-start | bytes 786440 | tf_op jit(solution)/shard_map/ppermute | solution.py:448
  22.4 11.0 %collective-permute-start.2 = (bf16[1,64,2048]{2,1,0:T(8,128)(2,1)S(1)}, bf16[1,64,2048]{2,1,0:T(8,128)(2,1)S(1)}, u32[]{:S(2)}, u32[]{:S(2)}) collective-permute-start(bf16[1,64,2048]{2,1,0:T(8,128)(2,1)S(1)} %get-tuple-element.55.refs_0_.refs_4_), channel_id=1, source_target_pairs={{0,1},{1,2},{2,3},{3,0},{4,5},{5,6},{6,7},{7,4},{8,9},{9,10},{10,1... | collective-permute-start | bytes 786440 | tf_op jit(solution)/shard_map/ppermute | solution.py:451
  22.4 16.7 %collective-permute-start.3 = (bf16[1,64,2048]{2,1,0:T(8,128)(2,1)S(1)}, bf16[1,64,2048]{2,1,0:T(8,128)(2,1)S(1)}, u32[]{:S(2)}, u32[]{:S(2)}) collective-permute-start(bf16[1,64,2048]{2,1,0:T(8,128)(2,1)S(1)} %collective-permute-done.1.refs_2_), channel_id=1, source_target_pairs={{0,1},{1,2},{2,3},{3,0},{4,5},{5,6},{6,7},{7,4},{8,9},{9,10},{10,1... | collective-permute-start | bytes 786440 | tf_op jit(solution)/shard_map/ppermute | solution.py:448
  33.4 15.2 %collective-permute-start.4 = (bf16[1,64,2048]{2,1,0:T(8,128)(2,1)S(1)}, bf16[1,64,2048]{2,1,0:T(8,128)(2,1)S(1)}, u32[]{:S(2)}, u32[]{:S(2)}) collective-permute-start(bf16[1,64,2048]{2,1,0:T(8,128)(2,1)S(1)} %collective-permute-done.2.refs_1_.refs_5_), channel_id=1, source_target_pairs={{0,1},{1,2},{2,3},{3,0},{4,5},{5,6},{6,7},{7,4},{8,9},{9,10},{10,1... | collective-permute-start | bytes 786440 | tf_op jit(solution)/shard_map/ppermute | solution.py:451
  48.6 10.6 %collective-permute-start.8 = (bf16[2,64,3712]{2,1,0:T(8,128)(2,1)S(1)}, bf16[2,64,3712]{2,1,0:T(8,128)(2,1)S(1)}, u32[]{:S(2)}, u32[]{:S(2)}) collective-permute-start(bf16[2,64,3712]{2,1,0:T(8,128)(2,1)S(1)} %get-tuple-element.52), channel_id=1, source_target_pairs={{0,4},{4,0},{8,12},{12,8},{1,5},{5,1},{9,13},{13,9},{2,6},{6,2},{1... | collective-permute-start | bytes 2850824 | tf_op jit(solution)/shard_map/ppermute | solution.py:484
  48.7 10.5 %collective-permute-start.5 = (bf16[1,64,2048]{2,1,0:T(8,128)(2,1)S(1)}, bf16[1,64,2048]{2,1,0:T(8,128)(2,1)S(1)}, u32[]{:S(2)}, u32[]{:S(2)}) collective-permute-start(bf16[1,64,2048]{2,1,0:T(8,128)(2,1)S(1)} %collective-permute-done.4.refs_2_.refs_6_), channel_id=1, source_target_pairs={{0,1},{1,2},{2,3},{3,0},{4,5},{5,6},{6,7},{7,4},{8,9},{9,10},{10,1... | collective-permute-start | bytes 786440 | tf_op jit(solution)/shard_map/ppermute | solution.py:451
  59.5 22.8 %collective-permute-start.13 = (bf16[2,64,3712]{2,1,0:T(8,128)(2,1)S(1)}, bf16[2,64,3712]{2,1,0:T(8,128)(2,1)}, u32[]{:S(2)}, u32[]{:S(2)}) collective-permute-start(bf16[2,64,3712]{2,1,0:T(8,128)(2,1)S(1)} %add_convert_fusion.3), channel_id=1, source_target_pairs={{0,8},{4,12},{8,0},{12,4},{1,9},{5,13},{9,1},{13,5},{2,10},{6,14},... | collective-permute-start | bytes 2850824 | tf_op jit(solution)/shard_map/ppermute | solution.py:467
  60.7 24.6 %collective-permute-start.15 = (bf16[128,2048]{1,0:T(8,128)(2,1)S(1)}, bf16[128,2048]{1,0:T(8,128)(2,1)S(1)}, u32[]{:S(2)}, u32[]{:S(2)}) collective-permute-start(bf16[128,2048]{1,0:T(8,128)(2,1)S(1)} %copy-done.19), channel_id=1, source_target_pairs={{0,1},{1,2},{2,3},{3,0},{4,5},{5,6},{6,7},{7,4},{8,9},{9,10},{10,1... | collective-permute-start | bytes 1572872 | tf_op jit(solution)/shard_map/ppermute | solution.py:497
  60.7 11.5 %collective-permute-start.9 = (bf16[128,3584]{1,0:T(8,128)(2,1)}, bf16[128,3584]{1,0:T(8,128)(2,1)S(1)}, u32[]{:S(2)}, u32[]{:S(2)}) collective-permute-start(bf16[128,3584]{1,0:T(8,128)(2,1)} %param.16), channel_id=1, source_target_pairs={{0,4},{4,0},{8,12},{12,8},{1,5},{5,1},{9,13},{13,9},{2,6},{6,2},{1... | collective-permute-start | bytes 2752520 | tf_op jit(solution)/shard_map/ppermute | solution.py:486
  60.7 11.5 %collective-permute-start.10 = (bf16[128,3584]{1,0:T(8,128)(2,1)}, bf16[128,3584]{1,0:T(8,128)(2,1)}, u32[]{:S(2)}, u32[]{:S(2)}) collective-permute-start(bf16[128,3584]{1,0:T(8,128)(2,1)} %param.15), channel_id=1, source_target_pairs={{0,4},{4,0},{8,12},{12,8},{1,5},{5,1},{9,13},{13,9},{2,6},{6,2},{1... | collective-permute-start | bytes 2752520 | tf_op jit(solution)/shard_map/ppermute | solution.py:486
  68.8 13.5 %collective-permute-start.14 = (bf16[2,64,3712]{2,1,0:T(8,128)(2,1)S(1)}, bf16[2,64,3712]{2,1,0:T(8,128)(2,1)S(1)}, u32[]{:S(2)}, u32[]{:S(2)}) collective-permute-start(bf16[2,64,3712]{2,1,0:T(8,128)(2,1)S(1)} %get-tuple-element.63), channel_id=1, source_target_pairs={{0,4},{4,0},{8,12},{12,8},{1,5},{5,1},{9,13},{13,9},{2,6},{6,2},{1... | collective-permute-start | bytes 2850824 | tf_op jit(solution)/shard_map/ppermute | solution.py:488
  84.0 26.5 %collective-permute-start.19 = (bf16[2,64,3712]{2,1,0:T(8,128)(2,1)S(1)}, bf16[2,64,3712]{2,1,0:T(8,128)(2,1)S(1)}, u32[]{:S(2)}, u32[]{:S(2)}) collective-permute-start(bf16[2,64,3712]{2,1,0:T(8,128)(2,1)S(1)} %add_convert_fusion.2), channel_id=1, source_target_pairs={{0,8},{4,12},{8,0},{12,4},{1,9},{5,13},{9,1},{13,5},{2,10},{6,14},... | collective-permute-start | bytes 2850824 | tf_op jit(solution)/shard_map/ppermute | solution.py:467
  85.3 25.2 %collective-permute-start.18 = (bf16[128,2048]{1,0:T(8,128)(2,1)S(1)}, bf16[128,2048]{1,0:T(8,128)(2,1)S(1)}, u32[]{:S(2)}, u32[]{:S(2)}) collective-permute-start(bf16[128,2048]{1,0:T(8,128)(2,1)S(1)} %copy-done.19), channel_id=1, source_target_pairs={{0,3},{1,0},{2,1},{3,2},{4,7},{5,4},{6,5},{7,6},{8,11},{9,8},{10,9... | collective-permute-start | bytes 1572872 | tf_op jit(solution)/shard_map/ppermute | solution.py:498
  85.3 25.2 %collective-permute-start.17 = (bf16[128,2048]{1,0:T(8,128)(2,1)S(1)}, bf16[128,2048]{1,0:T(8,128)(2,1)S(1)}, u32[]{:S(2)}, u32[]{:S(2)}) collective-permute-start(bf16[128,2048]{1,0:T(8,128)(2,1)S(1)} %collective-permute-done.15.refs_9_), channel_id=1, source_target_pairs={{0,1},{1,2},{2,3},{3,0},{4,5},{5,6},{6,7},{7,4},{8,9},{9,10},{10,1... | collective-permute-start | bytes 1572872 | tf_op jit(solution)/shard_map/ppermute | solution.py:500
  110.8 20.8 %collective-permute-start.23 = (bf16[64,2176]{1,0:T(8,128)(2,1)S(1)}, bf16[64,2176]{1,0:T(8,128)(2,1)S(1)}, u32[]{:S(2)}, u32[]{:S(2)}) collective-permute-start(bf16[64,2176]{1,0:T(8,128)(2,1)S(1)} %get-tuple-element.75), channel_id=1, source_target_pairs={{0,3},{1,0},{2,1},{3,2},{4,7},{5,4},{6,5},{7,6},{8,11},{9,8},{10,9... | collective-permute-start | bytes 835592 | tf_op jit(solution)/shard_map/ppermute | solution.py:476
  111.1 26.4 %collective-permute-start.22 = (bf16[64,2176]{1,0:T(8,128)(2,1)S(1)}, bf16[64,2176]{1,0:T(8,128)(2,1)S(1)}, u32[]{:S(2)}, u32[]{:S(2)}) collective-permute-start(bf16[64,2176]{1,0:T(8,128)(2,1)S(1)} %get-tuple-element.73), channel_id=1, source_target_pairs={{0,2},{1,3},{2,0},{3,1},{4,6},{5,7},{6,4},{7,5},{8,10},{9,11},{10,... | collective-permute-start | bytes 835592 | tf_op jit(solution)/shard_map/ppermute | solution.py:476
  112.7 24.9 %collective-permute-start.21 = (bf16[64,2176]{1,0:T(8,128)(2,1)S(1)}, bf16[64,2176]{1,0:T(8,128)(2,1)S(1)}, u32[]{:S(2)}, u32[]{:S(2)}) collective-permute-start(bf16[64,2176]{1,0:T(8,128)(2,1)S(1)} %get-tuple-element.71), channel_id=1, source_target_pairs={{0,1},{1,2},{2,3},{3,0},{4,5},{5,6},{6,7},{7,4},{8,9},{9,10},{10,1... | collective-permute-start | bytes 835592 | tf_op jit(solution)/shard_map/ppermute | solution.py:476
  137.6 20.7 %collective-permute-start.27 = (bf16[64,2176]{1,0:T(8,128)(2,1)S(1)}, bf16[64,2176]{1,0:T(8,128)(2,1)S(1)}, u32[]{:S(2)}, u32[]{:S(2)}) collective-permute-start(bf16[64,2176]{1,0:T(8,128)(2,1)S(1)} %get-tuple-element.84), channel_id=1, source_target_pairs={{0,1},{1,2},{2,3},{3,0},{4,5},{5,6},{6,7},{7,4},{8,9},{9,10},{10,1... | collective-permute-start | bytes 835592 | tf_op jit(solution)/shard_map/ppermute | solution.py:476
  137.6 22.1 %collective-permute-start.28 = (bf16[64,2176]{1,0:T(8,128)(2,1)S(1)}, bf16[64,2176]{1,0:T(8,128)(2,1)S(1)}, u32[]{:S(2)}, u32[]{:S(2)}) collective-permute-start(bf16[64,2176]{1,0:T(8,128)(2,1)S(1)} %get-tuple-element.85), channel_id=1, source_target_pairs={{0,2},{1,3},{2,0},{3,1},{4,6},{5,7},{6,4},{7,5},{8,10},{9,11},{10,... | collective-permute-start | bytes 835592 | tf_op jit(solution)/shard_map/ppermute | solution.py:476
  139.0 20.7 %collective-permute-start.29 = (bf16[64,2176]{1,0:T(8,128)(2,1)S(1)}, bf16[64,2176]{1,0:T(8,128)(2,1)S(1)}, u32[]{:S(2)}, u32[]{:S(2)}) collective-permute-start(bf16[64,2176]{1,0:T(8,128)(2,1)S(1)} %get-tuple-element.86), channel_id=1, source_target_pairs={{0,3},{1,0},{2,1},{3,2},{4,7},{5,4},{6,5},{7,6},{8,11},{9,8},{10,9... | collective-permute-start | bytes 835592 | tf_op jit(solution)/shard_map/ppermute | solution.py:476
  148.5 7.5 %collective-permute-start.25 = (bf16[16,3584]{1,0:T(8,128)(2,1)S(1)}, bf16[16,3584]{1,0:T(8,128)(2,1)S(1)}, u32[]{:S(2)}, u32[]{:S(2)}) collective-permute-start(bf16[16,3584]{1,0:T(8,128)(2,1)S(1)} %down_part.1.refs_0_), channel_id=1, source_target_pairs={{0,4},{4,0},{8,12},{12,8},{1,5},{5,1},{9,13},{13,9},{2,6},{6,2},{1... | collective-permute-start | bytes 344072 | tf_op jit(solution)/shard_map/ppermute | solution.py:514
  (29 other events, 193.6 us)

commit v7 on v6

--- a/solution.py
+++ b/solution.py
@@ -49,11 +49,12 @@
     return lax.rem(y + ny - p // 2, ny) * 2 + (c if p % 2 == 0 else 1 - c)
 
 
-def hidden_kernel(sizes, meta, *refs):
-    n_dp, n_t, g, own_t, rc, tile = sizes
+def hidden_kernel(sizes, chunks, meta, *refs):
+    n_dp, n_t, g, own_t, tile = sizes
     ny = n_t // 2
-    pieces, (w_ref, bd_ref, ad_ref, keep_ref, send_ref), refs = refs[:n_dp], refs[n_dp : n_dp + 5], refs[n_dp + 5 :]
-    x_scr, p_scr, w_scr, w_sem = refs
+    pieces, (w_ref, bd_ref, ad_ref), refs = refs[:n_dp], refs[n_dp : n_dp + 3], refs[n_dp + 3 :]
+    outs, (x_scr, p_scr, w_scr, w_sem) = refs[: 2 * len(chunks)], refs[2 * len(chunks) :]
+    keeps, sends = outs[: len(chunks)], outs[len(chunks) :]
     z, t = meta[0], meta[1]
     y, c = t // 2, t % 2
     hidden_width, width = w_ref.shape
@@ -71,44 +72,46 @@
             owner = lax.rem(z + (n_dp - k), n_dp) * g + j
             away = jnp.where(owner % 2 == c, 0, ny)
             x_scr[away + owner // 2] = pieces[k][j]
-    proj = fdot(x_scr[...].reshape(n_t * rc, width), bd_ref[...], NT)
-    lane = lax.broadcasted_iota(jnp.int32, (rc, TENANTS * R), 1) // R
-    zeros = jnp.zeros((rc, LANES - TENANTS * R), jnp.bfloat16)
+    proj = fdot(x_scr[...].reshape(n_t * own_t, width), bd_ref[...], NT)
+    lane = lax.broadcasted_iota(jnp.int32, (own_t, TENANTS * R), 1) // R
+    zeros = jnp.zeros((own_t, LANES - TENANTS * R), jnp.bfloat16)
     for s in range(n_t):
         owner = (s % ny) * 2 + (c if s < ny else 1 - c)
-        own = jnp.where(lane == tenant_of(meta, owner, own_t), proj[s * rc : (s + 1) * rc], 0.0)
-        p_scr[s * rc : (s + 1) * rc, :] = (ADAPTER_SCALE * own).astype(jnp.bfloat16)
-        out = keep_ref if s < ny else send_ref
-        out[s % ny, :, hidden_width:] = jnp.concatenate([own.astype(jnp.bfloat16), zeros], axis=1)
+        own = jnp.where(lane == tenant_of(meta, owner, own_t), proj[s * own_t : (s + 1) * own_t], 0.0)
+        p_scr[s * own_t : (s + 1) * own_t, :] = (ADAPTER_SCALE * own).astype(jnp.bfloat16)
+        padded = jnp.concatenate([own.astype(jnp.bfloat16), zeros], axis=1)
+        for (first, rc), out in zip(chunks, keeps if s < ny else sends):
+            out[s % ny, :, hidden_width:] = padded[first : first + rc]
 
     def body(step, carry):
         at = pl.ds(pl.multiple_of(step * tile, LANES), tile)
         fetch(step).wait()
-        acc = fdot(x_scr[...].reshape(n_t * rc, width), w_scr[step], NT)
-        acc = (acc + fdot(p_scr[...], ad_ref[:, at], NN)).astype(jnp.bfloat16).reshape(n_t, rc, tile)
-        keep_ref[:, :, at] = acc[:ny]
-        send_ref[:, :, at] = acc[ny:]
+        acc = fdot(x_scr[...].reshape(n_t * own_t, width), w_scr[step], NT)
+        acc = (acc + fdot(p_scr[...], ad_ref[:, at], NN)).astype(jnp.bfloat16).reshape(n_t, own_t, tile)
+        for (first, rc), keep, send in zip(chunks, keeps, sends):
+            keep[:, :, at] = acc[:ny, first : first + rc]
+            send[:, :, at] = acc[ny:, first : first + rc]
         return carry
 
     lax.fori_loop(0, steps, body, 0)
 
 
-def hidden_partial(meta, pieces, down_weight, b_down, a_down, n_t, own_t):
+def hidden_partial(meta, pieces, down_weight, b_down, a_down, n_t, chunks):
     n_dp = len(pieces)
-    g, rc, width = pieces[0].shape
+    g, own_t, width = pieces[0].shape
     ny = n_t // 2
     hidden_width = down_weight.shape[0]
     tile = tile_of(hidden_width, 512)
     low = TENANTS * R
-    out = jax.ShapeDtypeStruct((ny, rc, hidden_width + LANES), jnp.bfloat16)
-    return pl.pallas_call(
-        functools.partial(hidden_kernel, (n_dp, n_t, g, own_t, rc, tile)),
-        out_shape=(out, out),
+    outs = [jax.ShapeDtypeStruct((ny, rc, hidden_width + LANES), jnp.bfloat16) for _, rc in chunks]
+    result = pl.pallas_call(
+        functools.partial(hidden_kernel, (n_dp, n_t, g, own_t, tile), chunks),
+        out_shape=outs * 2,
         in_specs=[SMEM] + [VMEM] * n_dp + [ANY] + [VMEM] * 2,
-        out_specs=[VMEM] * 2,
+        out_specs=[VMEM] * (2 * len(chunks)),
         scratch_shapes=[
-            pltpu.VMEM((n_t, rc, width), jnp.bfloat16),
-            pltpu.VMEM((n_t * rc, low), jnp.bfloat16),
+            pltpu.VMEM((n_t, own_t, width), jnp.bfloat16),
+            pltpu.VMEM((n_t * own_t, low), jnp.bfloat16),
             pltpu.VMEM((hidden_width // tile, tile, width), jnp.bfloat16),
             pltpu.SemaphoreType.DMA((hidden_width // tile,)),
         ],
@@ -116,6 +119,7 @@
         cost_estimate=NO_COST,
         name="hidden_partial",
     )(meta, *pieces, down_weight, b_down, a_down)
+    return list(result[: len(chunks)]), list(result[len(chunks) :])
 
 
 def grads_of(total, factors):
@@ -236,27 +240,26 @@
     return jnp.concatenate([left_ref[layer, owner] for owner in owners], axis=1)
 
 
-def down_outer_kernel(n_dp, g, chunks, meta, *refs):
-    pieces, (left_ref, out_ref) = refs[: n_dp * chunks], refs[n_dp * chunks :]
+def down_outer_kernel(n_dp, g, meta, *refs):
+    pieces, (left_ref, out_ref) = refs[:n_dp], refs[n_dp:]
     owners = [lax.rem(meta[0] + (n_dp - k), n_dp) * g + j for k in range(n_dp) for j in range(g)]
-    right = [pieces[q * n_dp + k][j] for k in range(n_dp) for j in range(g) for q in range(chunks)]
+    right = [pieces[k][j] for k in range(n_dp) for j in range(g)]
     out = ADAPTER_SCALE * fdot(left_of(left_ref, 2, owners), jnp.concatenate(right, axis=0), NN)
     out_ref[...] = out.reshape(out_ref.shape)
 
 
 def down_outer(meta, grads, left):
-    n_dp, chunks = len(grads[0]), len(grads)
-    pieces = [piece for pieces in grads for piece in pieces]
-    g, _, width = pieces[0].shape
+    n_dp = len(grads)
+    g, _, width = grads[0].shape
     tile = tile_of(width, 512)
     return pl.pallas_call(
-        functools.partial(down_outer_kernel, n_dp, g, chunks),
+        functools.partial(down_outer_kernel, n_dp, g),
         out_shape=jax.ShapeDtypeStruct((TENANTS, R, width), jnp.float32),
         grid_spec=pltpu.PrefetchScalarGridSpec(
             num_scalar_prefetch=1,
             grid=(width // tile,),
             in_specs=[
-                pl.BlockSpec(piece.shape[:2] + (tile,), lambda f, *_: (0, 0, f)) for piece in pieces
+                pl.BlockSpec(piece.shape[:2] + (tile,), lambda f, *_: (0, 0, f)) for piece in grads
             ]
             + [whole(left.shape)],
             out_specs=pl.BlockSpec((TENANTS, R, tile), lambda f, *_: (0, 0, f)),
@@ -264,7 +267,7 @@
         compiler_params=pltpu.CompilerParams(vmem_limit_bytes=VMEM_LIMIT),
         cost_estimate=NO_COST,
         name="down_outer",
-    )(meta, *pieces, left)
+    )(meta, *grads, left)
 
 
 def gate_up_outer_kernel(n_t, chunks, meta, *refs):
@@ -442,18 +445,13 @@
     z_next = ring(n_dp, 1)
 
     stored = [gate_pre, up_pre]
-    far_stored = [[lax.ppermute(x, "tensor", ring(n_t, 2 * s)) for x in stored] for s in range(1, ny)]
-    grads = [[out_grad.reshape(g, own_t, width)[:, at : at + rc]] for at, rc in chunks]
-    for _ in range(n_dp - 1):
-        grads[0].append(lax.ppermute(grads[0][-1], "dp", z_next))
-    grads[1][0] = after(grads[1][0], grads[0][2])
-    for _ in range(n_dp - 1):
-        grads[1].append(lax.ppermute(grads[1][-1], "dp", z_next))
-
-    def first(q, done):
-        pieces = [after(grads[q][0], *done)] + grads[q][1:]
-        keep, send = hidden_partial(meta, pieces, down_weight, b_down, a_down, n_t, own_t)
-        return keep, send
+    far_gates = [lax.ppermute(gate_pre, "tensor", ring(n_t, 2 * s)) for s in range(1, ny)]
+    late_up = after(up_pre, *far_gates)
+    far_stored = [[x, lax.ppermute(late_up, "tensor", ring(n_t, 2 * s + 2))] for s, x in enumerate(far_gates)]
+    grads = [out_grad.reshape(g, own_t, width)]
+    for step in range(n_dp - 1):
+        piece = grads[-1] if step < n_dp - 2 else after(grads[-1], *far_gates)
+        grads.append(lax.ppermute(piece, "dp", z_next))
 
     def factors_of(stored):
         gate_value, up_value = [x.astype(jnp.float32) for x in stored]
@@ -478,31 +476,27 @@
     def finish(there, rc):
         return add32(*[x[:, :width] for x in there]).astype(jnp.bfloat16).reshape(g, rc, width)
 
-    keep_a, send_a = first(0, (grads[1][1],))
-    stored[0] = after(stored[0], keep_a)
-    *near, hidden = factors_of(stored)
-    other_a = lax.ppermute(after(send_a, grads[1][n_dp - 2], *[x for there in far_stored for x in there]), "tensor", pair)
-    mine_a, far_a = exchange(after(keep_a, near[0], grads[1][-1]), other_a)
+    (keep_a, keep_b), sends = hidden_partial(meta, grads, down_weight, b_down, a_down, n_t, chunks)
+    inputs = [after(layer_input, grads[-1])]
+    inputs.append(lax.ppermute(inputs[0], "dp", z_next))
+    *near, hidden = factors_of([after(stored[0], keep_a), stored[1]])
+    sends[0] = after(sends[0], *[x for there in far_stored for x in there])
+    other_a, other_b = [lax.ppermute(send, "tensor", pair) for send in sends]
+    mine_a, far_a = exchange(after(keep_a, near[0]), other_a)
     beside_stored = [lax.ppermute(after(x, mine_a), "tensor", pair) for x in stored]
-    keep_b, send_b = first(1, (mine_a,))
-    other_b = lax.ppermute(send_b, "tensor", pair)
-    beside_stored[0] = after(beside_stored[0], keep_b)
     factors = [near, factors_of(beside_stored)[:2]]
+    inputs.append(lax.ppermute(after(inputs[1], factors[1][0]), "dp", z_next))
     for there in far_stored:
-        beside = [lax.ppermute(x, "tensor", pair) for x in [after(x, *beside_stored) for x in there]]
+        beside = [lax.ppermute(after(x, *beside_stored), "tensor", pair) for x in there]
         for both in (there, beside):
-            factors.append(factors_of([after(both[0], keep_b), both[1]])[:2])
+            factors.append(factors_of([after(both[0], mine_a, inputs[1]), both[1]])[:2])
     mine_b, far_b = exchange(after(keep_b, *far_a, *[pair[0] for pair in factors]), other_b)
-    inputs = [after(layer_input, grads[1][-1], mine_a)] + [None] * (n_dp - 1)
-    inputs[1] = lax.ppermute(inputs[0], "dp", z_next)
-    inputs[-1] = lax.ppermute(inputs[0], "dp", ring(n_dp, -1))
-    for k in range(2, n_dp // 2 + 1):
-        inputs[k] = lax.ppermute(inputs[k - 1], "dp", z_next)
-    for k in range(2, (n_dp + 1) // 2):
-        inputs[-k] = lax.ppermute(inputs[1 - k], "dp", ring(n_dp, -1))
+    inputs[2] = after(inputs[2], mine_b)
     sums_a = total(after(mine_a, mine_b), far_a)
-    there_a = second(0, sums_a, (inputs[1],))
-    sums_b = total(after(mine_b, there_a[0], inputs[n_dp // 2], inputs[-1]), far_b)
+    for _ in range(n_dp - 3):
+        inputs.append(lax.ppermute(after(inputs[-1], sums_a[0]), "dp", z_next))
+    there_a = second(0, sums_a, (inputs[2],))
+    sums_b = total(after(mine_b, there_a[0], inputs[-1]), far_b)
     there_b = second(1, sums_b, ())
 
     half_a = finish([after(x, there_b[0]) for x in there_a], chunks[0][1])

time: 166 us -> 180 us (1.084)
  the two profiles are of different devices: /device:TPU:0 before, /device:TPU:19 now
where the time goes in v7:
time: 180 us; the launch traced here: 179 us
  waiting for transfers between devices  62.8 us (35%)
  Pallas kernels  60.5 us (34%)
  starting transfers between devices  36.5 us (20%)
  other arithmetic  11.2 us (6%)
  local copies, waits for them, and re-layouts  7.35 us (4%)
    pallas_call x2, Pallas kernels, input_partial(): pl.pallas_call(functools.partial(input_kernel, (n_dp, n_t, g, own_t, rc,...  33 us
    ppermute x3, waiting for transfers between devices, per_device(): grads.append(lax.ppermute(piece, 'dp', z_next))  22.9 us
    ppermute x6, waiting for transfers between devices, second(): lax.ppermute(outs[r], 'dp', ring(n_dp, r))  14.8 us
    pallas_call x1, Pallas kernels, hidden_partial(): pl.pallas_call(functools.partial(hidden_kernel, (n_dp, n_t, g, own_t, til...  13.3 us
    ppermute x1, waiting for transfers between devices, per_device(): inputs.append(lax.ppermute(inputs[0], 'dp', z_next))  10.8 us
    ppermute x6, starting transfers between devices, second(): lax.ppermute(outs[r], 'dp', ring(n_dp, r))  9.4 us
    convert_element_type x4, other arithmetic, factors_of(): return [x.astype(jnp.bfloat16) for x in (dgate, dup, dup * up_value)]  8.53 us
    ppermute x1, waiting for transfers between devices, per_device(): inputs.append(lax.ppermute(after(inputs[1], factors[1][0]), 'dp', z_next))  8.13 us
  transfers between devices with their start and end apart: 27, of which 7 were waited for; matrix products, arithmetic and copies ran while one was open for 6% of the time, Pallas kernels for 32%

profile of v7, /device:TPU:19, one launch (start us, length us, event | category | flops | bytes accessed | tf_op | source)
XLA Modules:
  0.0 179.4 jit_solution(16025170798344335211)
XLA Ops:
  3.2 11.4 %collective-permute-done.refs_1_ = bf16[1,128,2048]{2,1,0:T(8,128)(2,1)S(1)} collective-permute-done((bf16[1,128,2048]{2,1,0:T(8,128)(2,1)}, bf16[1,128,2048]{2,1,0:T(8,128)(2,1)S(1)}, u32[]{:S(2)}, u32[]{:S(2)}) %collective-permute-start) | collective-permute-done | bytes 524320 | tf_op jit(solution)/shard_map/ppermute | solution.py:454
  15.9 6.2 %collective-permute-done.2 = bf16[128,3584]{1,0:T(8,128)(2,1)S(1)} collective-permute-done((bf16[128,3584]{1,0:T(8,128)(2,1)}, bf16[128,3584]{1,0:T(8,128)(2,1)S(1)}, u32[]{:S(2)}, u32[]{:S(2)}) %collective-permute-start.2) | collective-permute-done | bytes 917536 | tf_op jit(solution)/shard_map/ppermute | solution.py:448
  23.4 2.8 %collective-permute-done.1.refs_2_ = bf16[1,128,2048]{2,1,0:T(8,128)(2,1)S(1)} collective-permute-done((bf16[1,128,2048]{2,1,0:T(8,128)(2,1)S(1)}, bf16[1,128,2048]{2,1,0:T(8,128)(2,1)S(1)}, u32[]{:S(2)}, u32[]{:S(2)}) %collective-permute-start.1) | collective-permute-done | bytes 524320 | tf_op jit(solution)/shard_map/ppermute | solution.py:454
  28.2 8.7 %collective-permute-done.3.refs_3_ = bf16[1,128,2048]{2,1,0:T(8,128)(2,1)S(1)} collective-permute-done((bf16[1,128,2048]{2,1,0:T(8,128)(2,1)S(1)}, bf16[1,128,2048]{2,1,0:T(8,128)(2,1)S(1)}, u32[]{:S(2)}, u32[]{:S(2)}) %collective-permute-start.3) | collective-permute-done | bytes 524320 | tf_op jit(solution)/shard_map/ppermute | solution.py:454
  39.9 13.3 %hidden_partial.1 = (bf16[2,64,3712]{2,1,0:T(8,128)(2,1)S(1)}, bf16[2,64,3712]{2,1,0:T(8,128)(2,1)}, bf16[2,64,3712]{2,1,0:T(8,128)(2,1)}, bf16[2,64,3712]{2,1,0:T(8,128)(2,1)}) custom-call(s32[6]{0:T(128)S(1)} %pad_add_fusion.meta, bf16[1,128,2048]{2,1,0:T(8,128)(2,1)S(1)} %bitcast.23, bf16[1,128,2048]{2,1,0:T(8,128)(2,1)S(1)} %collective-permute-done.refs_1_, ...), custom_call_target="tpu_custom_call" | custom-call | flops 1 | bytes 1 | tf_op jit(solution)/shard_map/hidden_partial/pallas_call | solution.py:107
  53.3 3.7 %collective-permute-start.5 = (bf16[2,64,3712]{2,1,0:T(8,128)(2,1)}, bf16[2,64,3712]{2,1,0:T(8,128)(2,1)S(1)}, u32[]{:S(2)}, u32[]{:S(2)}) collective-permute-start(bf16[2,64,3712]{2,1,0:T(8,128)(2,1)} %get-tuple-element.53), channel_id=1, source_target_pairs={{0,4},{4,0},{8,12},{12,8},{1,5},{5,1},{9,13},{13,9},{2,6},{6,2},{1... | collective-permute-start | bytes 2850824 | tf_op jit(solution)/shard_map/ppermute | solution.py:484
  58.0 2.9 %collective-permute-start.8 = (bf16[128,2048]{1,0:T(8,128)(2,1)S(1)}, bf16[128,2048]{1,0:T(8,128)(2,1)S(1)}, u32[]{:S(2)}, u32[]{:S(2)}) collective-permute-start(bf16[128,2048]{1,0:T(8,128)(2,1)S(1)} %copy-done.18), channel_id=1, source_target_pairs={{0,1},{1,2},{2,3},{3,0},{4,5},{5,6},{6,7},{7,4},{8,9},{9,10},{10,1... | collective-permute-start | bytes 1572872 | tf_op jit(solution)/shard_map/ppermute | solution.py:481
  62.3 10.8 %collective-permute-done.8.refs_9_ = bf16[128,2048]{1,0:T(8,128)(2,1)S(1)} collective-permute-done((bf16[128,2048]{1,0:T(8,128)(2,1)S(1)}, bf16[128,2048]{1,0:T(8,128)(2,1)S(1)}, u32[]{:S(2)}, u32[]{:S(2)}) %collective-permute-start.8) | collective-permute-done | bytes 524320 | tf_op jit(solution)/shard_map/ppermute | solution.py:481
  73.0 3.2 %fusion.20 = (bf16[128,3584]{1,0:T(8,128)(2,1)}, bf16[128,3584]{1,0:T(8,128)(2,1)}) fusion(bf16[128,3584]{1,0:T(8,128)(2,1)S(1)} %collective-permute-done.2, bf16[128,3584]{1,0:T(8,128)(2,1)} %collective-permute-done.4), kind=kLoop, calls=%fused_computation.38 | loop fusion | flops 5963776 | bytes 3670016 | tf_op jit(solution)/shard_map/convert_element_type | solution.py:461
  77.0 2.1 %fusion.13 = (bf16[128,3584]{1,0:T(8,128)(2,1)}, bf16[128,3584]{1,0:T(8,128)(2,1)}) fusion(bf16[128,3584]{1,0:T(8,128)(2,1)S(1)} %collective-permute-done.7, bf16[128,3584]{1,0:T(8,128)(2,1)S(1)} %collective-permute-done.6), kind=kLoop, calls=%fused_computation.31 | loop fusion | flops 5963776 | bytes 3670016 | tf_op jit(solution)/shard_map/convert_element_type | solution.py:461
  79.1 3.4 %collective-permute-start.13 = (bf16[128,2048]{1,0:T(8,128)(2,1)S(1)}, bf16[128,2048]{1,0:T(8,128)(2,1)S(1)}, u32[]{:S(2)}, u32[]{:S(2)}) collective-permute-start(bf16[128,2048]{1,0:T(8,128)(2,1)S(1)} %collective-permute-done.8.refs_9_), channel_id=1, source_target_pairs={{0,1},{1,2},{2,3},{3,0},{4,5},{5,6},{6,7},{7,4},{8,9},{9,10},{10,1... | collective-permute-start | bytes 1572872 | tf_op jit(solution)/shard_map/ppermute | solution.py:488
  82.5 2.1 %fusion.27 = (bf16[128,3584]{1,0:T(8,128)(2,1)}, bf16[128,3584]{1,0:T(8,128)(2,1)}) fusion(bf16[128,3584]{1,0:T(8,128)(2,1)S(1)} %collective-permute-done.10, bf16[128,3584]{1,0:T(8,128)(2,1)S(1)} %collective-permute-done.9), kind=kLoop, calls=%fused_computation.45 | loop fusion | flops 5963776 | bytes 3670016 | tf_op jit(solution)/shard_map/convert_element_type | solution.py:461
  86.1 8.1 %collective-permute-done.13.refs_10_ = bf16[128,2048]{1,0:T(8,128)(2,1)S(1)} collective-permute-done((bf16[128,2048]{1,0:T(8,128)(2,1)S(1)}, bf16[128,2048]{1,0:T(8,128)(2,1)S(1)}, u32[]{:S(2)}, u32[]{:S(2)}) %collective-permute-start.13) | collective-permute-done | bytes 524320 | tf_op jit(solution)/shard_map/ppermute | solution.py:488
  94.2 3.1 %collective-permute-start.15 = (bf16[128,2048]{1,0:T(8,128)(2,1)S(1)}, bf16[128,2048]{1,0:T(8,128)(2,1)S(1)}, u32[]{:S(2)}, u32[]{:S(2)}) collective-permute-start(bf16[128,2048]{1,0:T(8,128)(2,1)S(1)} %collective-permute-done.13.refs_10_), channel_id=1, source_target_pairs={{0,1},{1,2},{2,3},{3,0},{4,5},{5,6},{6,7},{7,4},{8,9},{9,10},{10,1... | collective-permute-start | bytes 1572872 | tf_op jit(solution)/shard_map/ppermute | solution.py:497
  98.3 16.4 %input_partial.2 = (bf16[64,2176]{1,0:T(8,128)(2,1)S(1)}, bf16[64,2176]{1,0:T(8,128)(2,1)S(1)}, bf16[64,2176]{1,0:T(8,128)(2,1)S(1)}, bf16[64,2176]{1,0:T(8,128)(2,1)S(1)}) custom-call(s32[6]{0:T(128)S(1)} %pad_add_fusion.meta, bf16[128,3584]{1,0:T(8,128)(2,1)S(1)} %get-tuple-element.90.refs_0_, bf16[128,3584]{1,0:T(8,128)(2,1)S(1)} %get-tuple-element.91.refs_1_, ...), custom_call_target="tpu_custom_call" | custom-call | flops 1 | bytes 1 | tf_op jit(solution)/shard_map/input_partial/pallas_call | solution.py:198
  116.6 6.1 %collective-permute-start.19 = (bf16[64,2176]{1,0:T(8,128)(2,1)S(1)}, bf16[64,2176]{1,0:T(8,128)(2,1)S(1)}, u32[]{:S(2)}, u32[]{:S(2)}) collective-permute-start(bf16[64,2176]{1,0:T(8,128)(2,1)S(1)} %get-tuple-element.75), channel_id=1, source_target_pairs={{0,2},{1,3},{2,0},{3,1},{4,6},{5,7},{6,4},{7,5},{8,10},{9,11},{10,... | collective-permute-start | bytes 835592 | tf_op jit(solution)/shard_map/ppermute | solution.py:474
  123.7 16.6 %input_partial.3 = (bf16[64,2176]{1,0:T(8,128)(2,1)S(1)}, bf16[64,2176]{1,0:T(8,128)(2,1)S(1)}, bf16[64,2176]{1,0:T(8,128)(2,1)S(1)}, bf16[64,2176]{1,0:T(8,128)(2,1)S(1)}) custom-call(s32[6]{0:T(128)S(1)} %pad_add_fusion.meta, bf16[128,3584]{1,0:T(8,128)(2,1)S(1)} %get-tuple-element.90.refs_0_, bf16[128,3584]{1,0:T(8,128)(2,1)S(1)} %get-tuple-element.91.refs_1_, ...), custom_call_target="tpu_custom_call" | custom-call | flops 1 | bytes 1 | tf_op jit(solution)/shard_map/input_partial/pallas_call | solution.py:198
  141.8 1.8 %collective-permute-start.25 = (bf16[64,2176]{1,0:T(8,128)(2,1)S(1)}, bf16[64,2176]{1,0:T(8,128)(2,1)S(1)}, u32[]{:S(2)}, u32[]{:S(2)}) collective-permute-start(bf16[64,2176]{1,0:T(8,128)(2,1)S(1)} %get-tuple-element.87), channel_id=1, source_target_pairs={{0,2},{1,3},{2,0},{3,1},{4,6},{5,7},{6,4},{7,5},{8,10},{9,11},{10,... | collective-permute-start | bytes 835592 | tf_op jit(solution)/shard_map/ppermute | solution.py:474
  143.6 14.8 %collective-permute-done.18.refs_1_ = bf16[64,2176]{1,0:T(8,128)(2,1)S(1)} collective-permute-done((bf16[64,2176]{1,0:T(8,128)(2,1)S(1)}, bf16[64,2176]{1,0:T(8,128)(2,1)S(1)}, u32[]{:S(2)}, u32[]{:S(2)}) %collective-permute-start.18) | collective-permute-done | bytes 278560 | tf_op jit(solution)/shard_map/ppermute | solution.py:474
  161.6 2.6 %down_outer.1 = f32[4,16,2048]{2,1,0:T(8,128)} custom-call(s32[6]{0:T(128)S(1)} %pad_add_fusion.meta, bf16[1,128,2048]{2,1,0:T(8,128)(2,1)S(1)} %bitcast.24, bf16[1,128,2048]{2,1,0:T(8,128)(2,1)S(1)} %collective-permute-done.refs_1_, bf16[1,128,2048]{2,1,0:T(8,128)(2,1)S(1)} %collective-permute-done.1.refs_2_, ...), custom_call_target="tpu_custom_call" | custom-call | flops 1 | bytes 1 | tf_op jit(solution)/shard_map/down_outer/pallas_call | solution.py:255
  164.3 1.8 %collective-permute-start.22 = (bf16[16,3584]{1,0:T(8,128)(2,1)S(1)}, bf16[16,3584]{1,0:T(8,128)(2,1)S(1)}, u32[]{:S(2)}, u32[]{:S(2)}) collective-permute-start(bf16[16,3584]{1,0:T(8,128)(2,1)S(1)} %down_part.1.refs_0_), channel_id=1, source_target_pairs={{0,4},{4,0},{8,12},{12,8},{1,5},{5,1},{9,13},{13,9},{2,6},{6,2},{1... | collective-permute-start | bytes 344072 | tf_op jit(solution)/shard_map/ppermute | solution.py:508
  168.4 5.6 %gate_up_outer.1 = f32[4,32,3584]{2,1,0:T(8,128)} custom-call(s32[6]{0:T(128)S(1)} %pad_add_fusion.meta, bf16[128,3584]{1,0:T(8,128)(2,1)S(1)} %get-tuple-element.90.refs_0_, bf16[128,3584]{1,0:T(8,128)(2,1)S(1)} %get-tuple-element.91.refs_1_, bf16[128,3584]{1,0:T(8,128)(2,1)S(1)} %copy-done.8, bf16[128,3584]{1,0:T(8,128)(2,1)S(1)} %copy-done.7, ...), custom_call_target="tpu_custom_call" | custom-call | flops 1 | bytes 1 | tf_op jit(solution)/shard_map/gate_up_outer/pallas_call | solution.py:294
  173.9 2.2 %spread_a_down.1 = f32[4,16,3584]{2,1,0:T(8,128)} custom-call(s32[6]{0:T(128)S(1)} %pad_add_fusion.meta, bf16[16,3584]{1,0:T(8,128)(2,1)S(1)} %down_part.1.refs_0_, bf16[16,3584]{1,0:T(8,128)(2,1)S(1)} %collective-permute-done.21.refs_1_, bf16[16,3584]{1,0:T(8,128)(2,1)S(1)} %collective-permute-done.22.refs_2_, ...), custom_call_target="tpu_custom_call" | custom-call | flops 1 | bytes 1 | tf_op jit(solution)/shard_map/spread_a_down/pallas_call | solution.py:347
  177.1 2.3 %in_outer.1 = f32[4,32,2048]{2,1,0:T(8,128)} custom-call(s32[6]{0:T(128)S(1)} %pad_add_fusion.meta, bf16[64,2176]{1,0:T(8,128)(2,1)S(1)} %get-tuple-element.72.refs_0_, bf16[64,2176]{1,0:T(8,128)(2,1)S(1)} %collective-permute-done.18.refs_1_, bf16[64,2176]{1,0:T(8,128)(2,1)S(1)} %collective-permute-done.19.refs_2_, ...), custom_call_target="tpu_custom_call" | custom-call | flops 1 | bytes 1 | tf_op jit(solution)/shard_map/in_outer/pallas_call | solution.py:387
  (105 shorter events, 26.5 us)
Async XLA Ops:
  0.6 21.5 %collective-permute-start.2 = (bf16[128,3584]{1,0:T(8,128)(2,1)}, bf16[128,3584]{1,0:T(8,128)(2,1)S(1)}, u32[]{:S(2)}, u32[]{:S(2)}) collective-permute-start(bf16[128,3584]{1,0:T(8,128)(2,1)} %param.15), channel_id=1, source_target_pairs={{0,8},{4,12},{8,0},{12,4},{1,9},{5,13},{9,1},{13,5},{2,10},{6,14},... | collective-permute-start | bytes 2752520 | tf_op jit(solution)/shard_map/ppermute | solution.py:448
  1.9 12.7 %collective-permute-start = (bf16[1,128,2048]{2,1,0:T(8,128)(2,1)}, bf16[1,128,2048]{2,1,0:T(8,128)(2,1)S(1)}, u32[]{:S(2)}, u32[]{:S(2)}) collective-permute-start(bf16[1,128,2048]{2,1,0:T(8,128)(2,1)} %bitcast.22), channel_id=1, source_target_pairs={{0,1},{1,2},{2,3},{3,0},{4,5},{5,6},{6,7},{7,4},{8,9},{9,10},{10,1... | collective-permute-start | bytes 1572872 | tf_op jit(solution)/shard_map/ppermute | solution.py:454
  14.6 11.6 %collective-permute-start.1 = (bf16[1,128,2048]{2,1,0:T(8,128)(2,1)S(1)}, bf16[1,128,2048]{2,1,0:T(8,128)(2,1)S(1)}, u32[]{:S(2)}, u32[]{:S(2)}) collective-permute-start(bf16[1,128,2048]{2,1,0:T(8,128)(2,1)S(1)} %collective-permute-done.refs_1_), channel_id=1, source_target_pairs={{0,1},{1,2},{2,3},{3,0},{4,5},{5,6},{6,7},{7,4},{8,9},{9,10},{10,1... | collective-permute-start | bytes 1572872 | tf_op jit(solution)/shard_map/ppermute | solution.py:454
  22.1 31.1 %collective-permute-start.4 = (bf16[128,3584]{1,0:T(8,128)(2,1)}, bf16[128,3584]{1,0:T(8,128)(2,1)}, u32[]{:S(2)}, u32[]{:S(2)}) collective-permute-start(bf16[128,3584]{1,0:T(8,128)(2,1)} %param.16), channel_id=1, source_target_pairs={{0,8},{4,12},{8,0},{12,4},{1,9},{5,13},{9,1},{13,5},{2,10},{6,14},... | collective-permute-start | bytes 2752520 | tf_op jit(solution)/shard_map/ppermute | solution.py:450
  26.2 10.7 %collective-permute-start.3 = (bf16[1,128,2048]{2,1,0:T(8,128)(2,1)S(1)}, bf16[1,128,2048]{2,1,0:T(8,128)(2,1)S(1)}, u32[]{:S(2)}, u32[]{:S(2)}) collective-permute-start(bf16[1,128,2048]{2,1,0:T(8,128)(2,1)S(1)} %collective-permute-done.1.refs_2_), channel_id=1, source_target_pairs={{0,1},{1,2},{2,3},{3,0},{4,5},{5,6},{6,7},{7,4},{8,9},{9,10},{10,1... | collective-permute-start | bytes 1572872 | tf_op jit(solution)/shard_map/ppermute | solution.py:454
  53.3 8.0 %collective-permute-start.5 = (bf16[2,64,3712]{2,1,0:T(8,128)(2,1)}, bf16[2,64,3712]{2,1,0:T(8,128)(2,1)S(1)}, u32[]{:S(2)}, u32[]{:S(2)}) collective-permute-start(bf16[2,64,3712]{2,1,0:T(8,128)(2,1)} %get-tuple-element.53), channel_id=1, source_target_pairs={{0,4},{4,0},{8,12},{12,8},{1,5},{5,1},{9,13},{13,9},{2,6},{6,2},{1... | collective-permute-start | bytes 2850824 | tf_op jit(solution)/shard_map/ppermute | solution.py:484
  58.0 15.0 %collective-permute-start.8 = (bf16[128,2048]{1,0:T(8,128)(2,1)S(1)}, bf16[128,2048]{1,0:T(8,128)(2,1)S(1)}, u32[]{:S(2)}, u32[]{:S(2)}) collective-permute-start(bf16[128,2048]{1,0:T(8,128)(2,1)S(1)} %copy-done.18), channel_id=1, source_target_pairs={{0,1},{1,2},{2,3},{3,0},{4,5},{5,6},{6,7},{7,4},{8,9},{9,10},{10,1... | collective-permute-start | bytes 1572872 | tf_op jit(solution)/shard_map/ppermute | solution.py:481
  60.9 23.7 %collective-permute-start.12 = (bf16[2,64,3712]{2,1,0:T(8,128)(2,1)S(1)}, bf16[2,64,3712]{2,1,0:T(8,128)(2,1)S(1)}, u32[]{:S(2)}, u32[]{:S(2)}) collective-permute-start(bf16[2,64,3712]{2,1,0:T(8,128)(2,1)S(1)} %copy-done.26), channel_id=1, source_target_pairs={{0,4},{4,0},{8,12},{12,8},{1,5},{5,1},{9,13},{13,9},{2,6},{6,2},{1... | collective-permute-start | bytes 2850824 | tf_op jit(solution)/shard_map/ppermute | solution.py:484
  61.4 23.2 %collective-permute-start.11 = (bf16[2,64,3712]{2,1,0:T(8,128)(2,1)S(1)}, bf16[2,64,3712]{2,1,0:T(8,128)(2,1)S(1)}, u32[]{:S(2)}, u32[]{:S(2)}) collective-permute-start(bf16[2,64,3712]{2,1,0:T(8,128)(2,1)S(1)} %add_convert_fusion.3), channel_id=1, source_target_pairs={{0,8},{4,12},{8,0},{12,4},{1,9},{5,13},{9,1},{13,5},{2,10},{6,14},... | collective-permute-start | bytes 2850824 | tf_op jit(solution)/shard_map/ppermute | solution.py:465
  61.7 14.5 %collective-permute-start.7 = (bf16[128,3584]{1,0:T(8,128)(2,1)S(1)}, bf16[128,3584]{1,0:T(8,128)(2,1)S(1)}, u32[]{:S(2)}, u32[]{:S(2)}) collective-permute-start(bf16[128,3584]{1,0:T(8,128)(2,1)S(1)} %copy-done.23), channel_id=1, source_target_pairs={{0,4},{4,0},{8,12},{12,8},{1,5},{5,1},{9,13},{13,9},{2,6},{6,2},{1... | collective-permute-start | bytes 2752520 | tf_op jit(solution)/shard_map/ppermute | solution.py:486
  62.2 14.0 %collective-permute-start.6 = (bf16[128,3584]{1,0:T(8,128)(2,1)S(1)}, bf16[128,3584]{1,0:T(8,128)(2,1)S(1)}, u32[]{:S(2)}, u32[]{:S(2)}) collective-permute-start(bf16[128,3584]{1,0:T(8,128)(2,1)S(1)} %copy-done.25), channel_id=1, source_target_pairs={{0,4},{4,0},{8,12},{12,8},{1,5},{5,1},{9,13},{13,9},{2,6},{6,2},{1... | collective-permute-start | bytes 2752520 | tf_op jit(solution)/shard_map/ppermute | solution.py:486
  79.1 15.2 %collective-permute-start.13 = (bf16[128,2048]{1,0:T(8,128)(2,1)S(1)}, bf16[128,2048]{1,0:T(8,128)(2,1)S(1)}, u32[]{:S(2)}, u32[]{:S(2)}) collective-permute-start(bf16[128,2048]{1,0:T(8,128)(2,1)S(1)} %collective-permute-done.8.refs_9_), channel_id=1, source_target_pairs={{0,1},{1,2},{2,3},{3,0},{4,5},{5,6},{6,7},{7,4},{8,9},{9,10},{10,1... | collective-permute-start | bytes 1572872 | tf_op jit(solution)/shard_map/ppermute | solution.py:488
  85.1 12.3 %collective-permute-start.14 = (bf16[2,64,3712]{2,1,0:T(8,128)(2,1)S(1)}, bf16[2,64,3712]{2,1,0:T(8,128)(2,1)S(1)}, u32[]{:S(2)}, u32[]{:S(2)}) collective-permute-start(bf16[2,64,3712]{2,1,0:T(8,128)(2,1)S(1)} %add_convert_fusion.1.refs_8_.refs_0_), channel_id=1, source_target_pairs={{0,4},{4,0},{8,12},{12,8},{1,5},{5,1},{9,13},{13,9},{2,6},{6,2},{1... | collective-permute-start | bytes 2850824 | tf_op jit(solution)/shard_map/ppermute | solution.py:469
  85.9 28.9 %collective-permute-start.16 = (bf16[2,64,3712]{2,1,0:T(8,128)(2,1)S(1)}, bf16[2,64,3712]{2,1,0:T(8,128)(2,1)S(1)}, u32[]{:S(2)}, u32[]{:S(2)}) collective-permute-start(bf16[2,64,3712]{2,1,0:T(8,128)(2,1)S(1)} %add_convert_fusion.2), channel_id=1, source_target_pairs={{0,8},{4,12},{8,0},{12,4},{1,9},{5,13},{9,1},{13,5},{2,10},{6,14},... | collective-permute-start | bytes 2850824 | tf_op jit(solution)/shard_map/ppermute | solution.py:465
  94.2 20.5 %collective-permute-start.15 = (bf16[128,2048]{1,0:T(8,128)(2,1)S(1)}, bf16[128,2048]{1,0:T(8,128)(2,1)S(1)}, u32[]{:S(2)}, u32[]{:S(2)}) collective-permute-start(bf16[128,2048]{1,0:T(8,128)(2,1)S(1)} %collective-permute-done.13.refs_10_), channel_id=1, source_target_pairs={{0,1},{1,2},{2,3},{3,0},{4,5},{5,6},{6,7},{7,4},{8,9},{9,10},{10,1... | collective-permute-start | bytes 1572872 | tf_op jit(solution)/shard_map/ppermute | solution.py:497
  115.0 7.7 %collective-permute-start.17 = (bf16[2,64,3712]{2,1,0:T(8,128)(2,1)S(1)}, bf16[2,64,3712]{2,1,0:T(8,128)(2,1)S(1)}, u32[]{:S(2)}, u32[]{:S(2)}) collective-permute-start(bf16[2,64,3712]{2,1,0:T(8,128)(2,1)S(1)} %add_convert_fusion.refs_8_.refs_1_.refs_10_), channel_id=1, source_target_pairs={{0,4},{4,0},{8,12},{12,8},{1,5},{5,1},{9,13},{13,9},{2,6},{6,2},{1... | collective-permute-start | bytes 2850824 | tf_op jit(solution)/shard_map/ppermute | solution.py:469
  116.6 26.9 %collective-permute-start.20 = (bf16[64,2176]{1,0:T(8,128)(2,1)S(1)}, bf16[64,2176]{1,0:T(8,128)(2,1)S(1)}, u32[]{:S(2)}, u32[]{:S(2)}) collective-permute-start(bf16[64,2176]{1,0:T(8,128)(2,1)S(1)} %get-tuple-element.77), channel_id=1, source_target_pairs={{0,3},{1,0},{2,1},{3,2},{4,7},{5,4},{6,5},{7,6},{8,11},{9,8},{10,9... | collective-permute-start | bytes 835592 | tf_op jit(solution)/shard_map/ppermute | solution.py:474
  116.6 26.9 %collective-permute-start.19 = (bf16[64,2176]{1,0:T(8,128)(2,1)S(1)}, bf16[64,2176]{1,0:T(8,128)(2,1)S(1)}, u32[]{:S(2)}, u32[]{:S(2)}) collective-permute-start(bf16[64,2176]{1,0:T(8,128)(2,1)S(1)} %get-tuple-element.75), channel_id=1, source_target_pairs={{0,2},{1,3},{2,0},{3,1},{4,6},{5,7},{6,4},{7,5},{8,10},{9,11},{10,... | collective-permute-start | bytes 835592 | tf_op jit(solution)/shard_map/ppermute | solution.py:474
  122.7 35.6 %collective-permute-start.18 = (bf16[64,2176]{1,0:T(8,128)(2,1)S(1)}, bf16[64,2176]{1,0:T(8,128)(2,1)S(1)}, u32[]{:S(2)}, u32[]{:S(2)}) collective-permute-start(bf16[64,2176]{1,0:T(8,128)(2,1)S(1)} %get-tuple-element.73), channel_id=1, source_target_pairs={{0,1},{1,2},{2,3},{3,0},{4,5},{5,6},{6,7},{7,4},{8,9},{9,10},{10,1... | collective-permute-start | bytes 835592 | tf_op jit(solution)/shard_map/ppermute | solution.py:474
  140.2 35.9 %collective-permute-start.26 = (bf16[64,2176]{1,0:T(8,128)(2,1)S(1)}, bf16[64,2176]{1,0:T(8,128)(2,1)S(1)}, u32[]{:S(2)}, u32[]{:S(2)}) collective-permute-start(bf16[64,2176]{1,0:T(8,128)(2,1)S(1)} %get-tuple-element.88), channel_id=1, source_target_pairs={{0,3},{1,0},{2,1},{3,2},{4,7},{5,4},{6,5},{7,6},{8,11},{9,8},{10,9... | collective-permute-start | bytes 835592 | tf_op jit(solution)/shard_map/ppermute | solution.py:474
  141.8 34.4 %collective-permute-start.25 = (bf16[64,2176]{1,0:T(8,128)(2,1)S(1)}, bf16[64,2176]{1,0:T(8,128)(2,1)S(1)}, u32[]{:S(2)}, u32[]{:S(2)}) collective-permute-start(bf16[64,2176]{1,0:T(8,128)(2,1)S(1)} %get-tuple-element.87), channel_id=1, source_target_pairs={{0,2},{1,3},{2,0},{3,1},{4,6},{5,7},{6,4},{7,5},{8,10},{9,11},{10,... | collective-permute-start | bytes 835592 | tf_op jit(solution)/shard_map/ppermute | solution.py:474
  143.6 32.6 %collective-permute-start.24 = (bf16[64,2176]{1,0:T(8,128)(2,1)S(1)}, bf16[64,2176]{1,0:T(8,128)(2,1)S(1)}, u32[]{:S(2)}, u32[]{:S(2)}) collective-permute-start(bf16[64,2176]{1,0:T(8,128)(2,1)S(1)} %get-tuple-element.86), channel_id=1, source_target_pairs={{0,1},{1,2},{2,3},{3,0},{4,5},{5,6},{6,7},{7,4},{8,9},{9,10},{10,1... | collective-permute-start | bytes 835592 | tf_op jit(solution)/shard_map/ppermute | solution.py:474
  164.3 9.7 %collective-permute-start.22 = (bf16[16,3584]{1,0:T(8,128)(2,1)S(1)}, bf16[16,3584]{1,0:T(8,128)(2,1)S(1)}, u32[]{:S(2)}, u32[]{:S(2)}) collective-permute-start(bf16[16,3584]{1,0:T(8,128)(2,1)S(1)} %down_part.1.refs_0_), channel_id=1, source_target_pairs={{0,4},{4,0},{8,12},{12,8},{1,5},{5,1},{9,13},{13,9},{2,6},{6,2},{1... | collective-permute-start | bytes 344072 | tf_op jit(solution)/shard_map/ppermute | solution.py:508
  166.1 7.9 %collective-permute-start.23 = (bf16[16,3584]{1,0:T(8,128)(2,1)S(1)}, bf16[16,3584]{1,0:T(8,128)(2,1)S(1)}, u32[]{:S(2)}, u32[]{:S(2)}) collective-permute-start(bf16[16,3584]{1,0:T(8,128)(2,1)S(1)} %collective-permute-done.21.refs_1_), channel_id=1, source_target_pairs={{0,4},{4,0},{8,12},{12,8},{1,5},{5,1},{9,13},{13,9},{2,6},{6,2},{1... | collective-permute-start | bytes 344072 | tf_op jit(solution)/shard_map/ppermute | solution.py:508
  (30 other events, 316.4 us)

commit v8 on v6

--- a/solution.py
+++ b/solution.py
@@ -482,7 +482,7 @@
     stored[0] = after(stored[0], keep_a)
     *near, hidden = factors_of(stored)
     other_a = lax.ppermute(after(send_a, grads[1][n_dp - 2], *[x for there in far_stored for x in there]), "tensor", pair)
-    mine_a, far_a = exchange(after(keep_a, near[0], grads[1][-1]), other_a)
+    mine_a, far_a = exchange(after(keep_a, near[0]), other_a)
     beside_stored = [lax.ppermute(after(x, mine_a), "tensor", pair) for x in stored]
     keep_b, send_b = first(1, (mine_a,))
     other_b = lax.ppermute(send_b, "tensor", pair)

time: 166 us -> 166 us (level)
    ppermute x1, waiting for transfers between devices: 5.79 us -> 0.01 us  [per_device(): inputs[-1] = lax.ppermute(inputs[0], 'dp', ring(n_dp, -1))]
    ppermute x1, waiting for transfers between devices: 0.01 us -> 5.75 us  [per_device(): inputs[k] = lax.ppermute(inputs[k - 1], 'dp', z_next)]
    ppermute x2, waiting for transfers between devices: 4.12 us -> 0.01 us  [exchange(): lax.ppermute(mine, 'tensor', ring(n_t, 2 * s))]
    ppermute x1, starting transfers between devices: 0.01 us -> 3.81 us  [per_device(): inputs[-1] = lax.ppermute(inputs[0], 'dp', ring(n_dp, -1))]
    ppermute x1, starting transfers between devices: 2.02 us -> 0.01 us  [per_device(): inputs[k] = lax.ppermute(inputs[k - 1], 'dp', z_next)]
    ppermute x6, waiting for transfers between devices: 7.4 us -> 9.37 us  [second(): lax.ppermute(outs[r], 'dp', ring(n_dp, r))]
  transfers between devices with their start and end apart: 30 -> 30, of which waited for: 11 -> 10; matrix products, arithmetic and copies ran while one was open for 8% -> 9% of each run, Pallas kernels for 37% -> 37%
where the time goes in v8:
time: 166 us; the launch traced here: 163 us
  Pallas kernels  62.4 us (38%)
  waiting for transfers between devices  56.2 us (34%)
  starting transfers between devices  21.2 us (13%)
  other arithmetic  15.2 us (9%)
  local copies, waits for them, and re-layouts  7.37 us (4%)
    pallas_call x2, Pallas kernels, input_partial(): pl.pallas_call(functools.partial(input_kernel, (n_dp, n_t, g, own_t, rc,...  33 us
    ppermute x3, waiting for transfers between devices, per_device(): grads[0].append(lax.ppermute(grads[0][-1], 'dp', z_next))  20.5 us
    ppermute x3, waiting for transfers between devices, per_device(): grads[1].append(lax.ppermute(grads[1][-1], 'dp', z_next))  19.8 us
    pallas_call x2, Pallas kernels, hidden_partial(): pl.pallas_call(functools.partial(hidden_kernel, (n_dp, n_t, g, own_t, rc,...  15.1 us
    convert_element_type x4, other arithmetic, factors_of(): return [x.astype(jnp.bfloat16) for x in (dgate, dup, dup * up_value)]  11.3 us
    ppermute x6, waiting for transfers between devices, second(): lax.ppermute(outs[r], 'dp', ring(n_dp, r))  9.37 us
    ppermute x6, starting transfers between devices, second(): lax.ppermute(outs[r], 'dp', ring(n_dp, r))  7.13 us
    unnamed x46, local copies, waits for them, and re-layouts  6.3 us
  transfers between devices with their start and end apart: 30, of which 10 were waited for; matrix products, arithmetic and copies ran while one was open for 9% of the time, Pallas kernels for 37%

profile of v8, /device:TPU:0, one launch (start us, length us, event | category | flops | bytes accessed | tf_op | source)
XLA Modules:
  0.0 163.4 jit_solution(15450855743736957569)
XLA Ops:
  1.7 3.1 %collective-permute-start = (bf16[1,64,2048]{2,1,0:T(8,128)(2,1)S(1)}, bf16[1,64,2048]{2,1,0:T(8,128)(2,1)S(1)}, u32[]{:S(2)}, u32[]{:S(2)}) collective-permute-start(bf16[1,64,2048]{2,1,0:T(8,128)(2,1)S(1)} %get-tuple-element.47.refs_0_), channel_id=1, source_target_pairs={{0,1},{1,2},{2,3},{3,0},{4,5},{5,6},{6,7},{7,4},{8,9},{9,10},{10,1... | collective-permute-start | bytes 786440 | tf_op jit(solution)/shard_map/ppermute | solution.py:448
  6.8 6.3 %collective-permute-done.refs_1_ = bf16[1,64,2048]{2,1,0:T(8,128)(2,1)S(1)} collective-permute-done((bf16[1,64,2048]{2,1,0:T(8,128)(2,1)S(1)}, bf16[1,64,2048]{2,1,0:T(8,128)(2,1)S(1)}, u32[]{:S(2)}, u32[]{:S(2)}) %collective-permute-start) | collective-permute-done | bytes 262176 | tf_op jit(solution)/shard_map/ppermute | solution.py:448
  13.1 9.3 %collective-permute-done.1.refs_2_ = bf16[1,64,2048]{2,1,0:T(8,128)(2,1)S(1)} collective-permute-done((bf16[1,64,2048]{2,1,0:T(8,128)(2,1)S(1)}, bf16[1,64,2048]{2,1,0:T(8,128)(2,1)S(1)}, u32[]{:S(2)}, u32[]{:S(2)}) %collective-permute-start.1) | collective-permute-done | bytes 262176 | tf_op jit(solution)/shard_map/ppermute | solution.py:448
  22.4 11.0 %collective-permute-done.2.refs_1_.refs_5_ = bf16[1,64,2048]{2,1,0:T(8,128)(2,1)S(1)} collective-permute-done((bf16[1,64,2048]{2,1,0:T(8,128)(2,1)S(1)}, bf16[1,64,2048]{2,1,0:T(8,128)(2,1)S(1)}, u32[]{:S(2)}, u32[]{:S(2)}) %collective-permute-start.2) | collective-permute-done | bytes 262176 | tf_op jit(solution)/shard_map/ppermute | solution.py:451
  34.2 4.9 %collective-permute-done.3.refs_3_ = bf16[1,64,2048]{2,1,0:T(8,128)(2,1)S(1)} collective-permute-done((bf16[1,64,2048]{2,1,0:T(8,128)(2,1)S(1)}, bf16[1,64,2048]{2,1,0:T(8,128)(2,1)S(1)}, u32[]{:S(2)}, u32[]{:S(2)}) %collective-permute-start.3) | collective-permute-done | bytes 262176 | tf_op jit(solution)/shard_map/ppermute | solution.py:448
  41.0 7.6 %hidden_partial.2 = (bf16[2,64,3712]{2,1,0:T(8,128)(2,1)S(1)}, bf16[2,64,3712]{2,1,0:T(8,128)(2,1)S(1)}) custom-call(s32[6]{0:T(128)S(1)} %pad_add_fusion.meta, bf16[1,64,2048]{2,1,0:T(8,128)(2,1)S(1)} %get-tuple-element.47.refs_0_, bf16[1,64,2048]{2,1,0:T(8,128)(2,1)S(1)} %collective-permute-done.refs_1_, ...), custom_call_target="tpu_custom_call" | custom-call | flops 1 | bytes 1 | tf_op jit(solution)/shard_map/hidden_partial/pallas_call | solution.py:104
  48.7 2.7 %fusion.2 = (bf16[128,3584]{1,0:T(8,128)(2,1)S(1)}, bf16[128,3584]{1,0:T(8,128)(2,1)S(1)}, bf16[128,3584]{1,0:T(8,128)(2,1)S(1)}) fusion(bf16[128,3584]{1,0:T(8,128)(2,1)} %param.16, bf16[128,3584]{1,0:T(8,128)(2,1)} %param.15), kind=kLoop, calls=%fused_computation.20 | loop fusion | flops 6881280 | bytes 4587520 | tf_op jit(solution)/shard_map/convert_element_type | solution.py:463
  52.9 8.8 %collective-permute-done.10.refs_3_.refs_7_ = bf16[1,64,2048]{2,1,0:T(8,128)(2,1)S(1)} collective-permute-done((bf16[1,64,2048]{2,1,0:T(8,128)(2,1)S(1)}, bf16[1,64,2048]{2,1,0:T(8,128)(2,1)S(1)}, u32[]{:S(2)}, u32[]{:S(2)}) %collective-permute-start.10) | collective-permute-done | bytes 262176 | tf_op jit(solution)/shard_map/ppermute | solution.py:451
  62.2 7.6 %hidden_partial.3 = (bf16[2,64,3712]{2,1,0:T(8,128)(2,1)S(1)}, bf16[2,64,3712]{2,1,0:T(8,128)(2,1)S(1)}) custom-call(s32[6]{0:T(128)S(1)} %pad_add_fusion.meta, bf16[1,64,2048]{2,1,0:T(8,128)(2,1)S(1)} %get-tuple-element.55.refs_0_.refs_4_, bf16[1,64,2048]{2,1,0:T(8,128)(2,1)S(1)} %collective-permute-done.2.refs_1_.refs_5_, ...), custom_call_target="tpu_custom_call" | custom-call | flops 1 | bytes 1 | tf_op jit(solution)/shard_map/hidden_partial/pallas_call | solution.py:104
  69.9 3.3 %fusion.20 = (bf16[128,3584]{1,0:T(8,128)(2,1)}, bf16[128,3584]{1,0:T(8,128)(2,1)}) fusion(bf16[128,3584]{1,0:T(8,128)(2,1)S(1)} %copy-done.22, bf16[128,3584]{1,0:T(8,128)(2,1)} %collective-permute-done.6), kind=kLoop, calls=%fused_computation.38 | loop fusion | flops 5963776 | bytes 3670016 | tf_op jit(solution)/shard_map/convert_element_type | solution.py:463
  73.7 3.3 %fusion.13 = (bf16[128,3584]{1,0:T(8,128)(2,1)}, bf16[128,3584]{1,0:T(8,128)(2,1)}) fusion(bf16[128,3584]{1,0:T(8,128)(2,1)} %collective-permute-done.9, bf16[128,3584]{1,0:T(8,128)(2,1)S(1)} %collective-permute-done.8), kind=kLoop, calls=%fused_computation.31 | loop fusion | flops 5963776 | bytes 3670016 | tf_op jit(solution)/shard_map/convert_element_type | solution.py:463
  77.1 2.1 %fusion.27 = (bf16[128,3584]{1,0:T(8,128)(2,1)}, bf16[128,3584]{1,0:T(8,128)(2,1)}) fusion(bf16[128,3584]{1,0:T(8,128)(2,1)S(1)} %collective-permute-done.12, bf16[128,3584]{1,0:T(8,128)(2,1)S(1)} %collective-permute-done.11), kind=kLoop, calls=%fused_computation.45 | loop fusion | flops 5963776 | bytes 3670016 | tf_op jit(solution)/shard_map/convert_element_type | solution.py:463
  82.5 3.8 %collective-permute-start.18 = (bf16[128,2048]{1,0:T(8,128)(2,1)S(1)}, bf16[128,2048]{1,0:T(8,128)(2,1)S(1)}, u32[]{:S(2)}, u32[]{:S(2)}) collective-permute-start(bf16[128,2048]{1,0:T(8,128)(2,1)S(1)} %copy-done.19), channel_id=1, source_target_pairs={{0,3},{1,0},{2,1},{3,2},{4,7},{5,4},{6,5},{7,6},{8,11},{9,8},{10,9... | collective-permute-start | bytes 1572872 | tf_op jit(solution)/shard_map/ppermute | solution.py:498
  87.3 16.4 %input_partial.2 = (bf16[64,2176]{1,0:T(8,128)(2,1)S(1)}, bf16[64,2176]{1,0:T(8,128)(2,1)S(1)}, bf16[64,2176]{1,0:T(8,128)(2,1)S(1)}, bf16[64,2176]{1,0:T(8,128)(2,1)S(1)}) custom-call(s32[6]{0:T(128)S(1)} %pad_add_fusion.meta, bf16[128,3584]{1,0:T(8,128)(2,1)S(1)} %get-tuple-element.88.refs_0_, bf16[128,3584]{1,0:T(8,128)(2,1)S(1)} %get-tuple-element.89.refs_1_, ...), custom_call_target="tpu_custom_call" | custom-call | flops 1 | bytes 1 | tf_op jit(solution)/shard_map/input_partial/pallas_call | solution.py:194
  103.7 5.7 %collective-permute-done.17.refs_10_ = bf16[128,2048]{1,0:T(8,128)(2,1)S(1)} collective-permute-done((bf16[128,2048]{1,0:T(8,128)(2,1)S(1)}, bf16[128,2048]{1,0:T(8,128)(2,1)S(1)}, u32[]{:S(2)}, u32[]{:S(2)}) %collective-permute-start.17) | collective-permute-done | bytes 524320 | tf_op jit(solution)/shard_map/ppermute | solution.py:500
  109.8 1.8 %collective-permute-start.23 = (bf16[64,2176]{1,0:T(8,128)(2,1)S(1)}, bf16[64,2176]{1,0:T(8,128)(2,1)S(1)}, u32[]{:S(2)}, u32[]{:S(2)}) collective-permute-start(bf16[64,2176]{1,0:T(8,128)(2,1)S(1)} %get-tuple-element.75), channel_id=1, source_target_pairs={{0,3},{1,0},{2,1},{3,2},{4,7},{5,4},{6,5},{7,6},{8,11},{9,8},{10,9... | collective-permute-start | bytes 835592 | tf_op jit(solution)/shard_map/ppermute | solution.py:476
  114.1 16.6 %input_partial.3 = (bf16[64,2176]{1,0:T(8,128)(2,1)S(1)}, bf16[64,2176]{1,0:T(8,128)(2,1)S(1)}, bf16[64,2176]{1,0:T(8,128)(2,1)S(1)}, bf16[64,2176]{1,0:T(8,128)(2,1)S(1)}) custom-call(s32[6]{0:T(128)S(1)} %pad_add_fusion.meta, bf16[128,3584]{1,0:T(8,128)(2,1)S(1)} %get-tuple-element.88.refs_0_, bf16[128,3584]{1,0:T(8,128)(2,1)S(1)} %get-tuple-element.89.refs_1_, ...), custom_call_target="tpu_custom_call" | custom-call | flops 1 | bytes 1 | tf_op jit(solution)/shard_map/input_partial/pallas_call | solution.py:194
  130.6 7.4 %collective-permute-done.22.refs_2_ = bf16[64,2176]{1,0:T(8,128)(2,1)S(1)} collective-permute-done((bf16[64,2176]{1,0:T(8,128)(2,1)S(1)}, bf16[64,2176]{1,0:T(8,128)(2,1)S(1)}, u32[]{:S(2)}, u32[]{:S(2)}) %collective-permute-start.22) | collective-permute-done | bytes 278560 | tf_op jit(solution)/shard_map/ppermute | solution.py:476
  138.6 3.3 %collective-permute-start.29 = (bf16[64,2176]{1,0:T(8,128)(2,1)S(1)}, bf16[64,2176]{1,0:T(8,128)(2,1)S(1)}, u32[]{:S(2)}, u32[]{:S(2)}) collective-permute-start(bf16[64,2176]{1,0:T(8,128)(2,1)S(1)} %get-tuple-element.86), channel_id=1, source_target_pairs={{0,3},{1,0},{2,1},{3,2},{4,7},{5,4},{6,5},{7,6},{8,11},{9,8},{10,9... | collective-permute-start | bytes 835592 | tf_op jit(solution)/shard_map/ppermute | solution.py:476
  145.7 2.7 %down_outer.1 = f32[4,16,2048]{2,1,0:T(8,128)} custom-call(s32[6]{0:T(128)S(1)} %pad_add_fusion.meta, bf16[1,64,2048]{2,1,0:T(8,128)(2,1)S(1)} %get-tuple-element.47.refs_0_, bf16[1,64,2048]{2,1,0:T(8,128)(2,1)S(1)} %collective-permute-done.refs_1_, bf16[1,64,2048]{2,1,0:T(8,128)(2,1)S(1)} %collective-permute-done.1.refs_2_, ...), custom_call_target="tpu_custom_call" | custom-call | flops 1 | bytes 1 | tf_op jit(solution)/shard_map/down_outer/pallas_call | solution.py:252
  150.4 5.6 %gate_up_outer.1 = f32[4,32,3584]{2,1,0:T(8,128)} custom-call(s32[6]{0:T(128)S(1)} %pad_add_fusion.meta, bf16[128,3584]{1,0:T(8,128)(2,1)S(1)} %get-tuple-element.88.refs_0_, bf16[128,3584]{1,0:T(8,128)(2,1)S(1)} %get-tuple-element.89.refs_1_, bf16[128,3584]{1,0:T(8,128)(2,1)S(1)} %copy-done.8, bf16[128,3584]{1,0:T(8,128)(2,1)S(1)} %copy-done.7, ...), custom_call_target="tpu_custom_call" | custom-call | flops 1 | bytes 1 | tf_op jit(solution)/shard_map/gate_up_outer/pallas_call | solution.py:291
  155.9 2.2 %spread_a_down.1 = f32[4,16,3584]{2,1,0:T(8,128)} custom-call(s32[6]{0:T(128)S(1)} %pad_add_fusion.meta, bf16[16,3584]{1,0:T(8,128)(2,1)S(1)} %down_part.1.refs_0_, bf16[16,3584]{1,0:T(8,128)(2,1)S(1)} %collective-permute-done.24.refs_1_, bf16[16,3584]{1,0:T(8,128)(2,1)S(1)} %collective-permute-done.25.refs_2_, ...), custom_call_target="tpu_custom_call" | custom-call | flops 1 | bytes 1 | tf_op jit(solution)/shard_map/spread_a_down/pallas_call | solution.py:344
  158.1 2.0 %collective-permute-done.28.refs_6_ = bf16[64,2176]{1,0:T(8,128)(2,1)S(1)} collective-permute-done((bf16[64,2176]{1,0:T(8,128)(2,1)S(1)}, bf16[64,2176]{1,0:T(8,128)(2,1)S(1)}, u32[]{:S(2)}, u32[]{:S(2)}) %collective-permute-start.28) | collective-permute-done | bytes 278560 | tf_op jit(solution)/shard_map/ppermute | solution.py:476
  161.1 2.3 %in_outer.1 = f32[4,32,2048]{2,1,0:T(8,128)} custom-call(s32[6]{0:T(128)S(1)} %pad_add_fusion.meta, bf16[64,2176]{1,0:T(8,128)(2,1)S(1)} %get-tuple-element.70.refs_0_, bf16[64,2176]{1,0:T(8,128)(2,1)S(1)} %collective-permute-done.21.refs_1_, bf16[64,2176]{1,0:T(8,128)(2,1)S(1)} %collective-permute-done.22.refs_2_, ...), custom_call_target="tpu_custom_call" | custom-call | flops 1 | bytes 1 | tf_op jit(solution)/shard_map/in_outer/pallas_call | solution.py:384
  (105 shorter events, 22.9 us)
Async XLA Ops:
  1.7 11.4 %collective-permute-start = (bf16[1,64,2048]{2,1,0:T(8,128)(2,1)S(1)}, bf16[1,64,2048]{2,1,0:T(8,128)(2,1)S(1)}, u32[]{:S(2)}, u32[]{:S(2)}) collective-permute-start(bf16[1,64,2048]{2,1,0:T(8,128)(2,1)S(1)} %get-tuple-element.47.refs_0_), channel_id=1, source_target_pairs={{0,1},{1,2},{2,3},{3,0},{4,5},{5,6},{6,7},{7,4},{8,9},{9,10},{10,1... | collective-permute-start | bytes 786440 | tf_op jit(solution)/shard_map/ppermute | solution.py:448
  4.8 43.8 %collective-permute-start.5 = (bf16[128,3584]{1,0:T(8,128)(2,1)}, bf16[128,3584]{1,0:T(8,128)(2,1)S(1)}, u32[]{:S(2)}, u32[]{:S(2)}) collective-permute-start(bf16[128,3584]{1,0:T(8,128)(2,1)} %param.15), channel_id=1, source_target_pairs={{0,8},{4,12},{8,0},{12,4},{1,9},{5,13},{9,1},{13,5},{2,10},{6,14},... | collective-permute-start | bytes 2752520 | tf_op jit(solution)/shard_map/ppermute | solution.py:445
  6.3 42.3 %collective-permute-start.6 = (bf16[128,3584]{1,0:T(8,128)(2,1)}, bf16[128,3584]{1,0:T(8,128)(2,1)}, u32[]{:S(2)}, u32[]{:S(2)}) collective-permute-start(bf16[128,3584]{1,0:T(8,128)(2,1)} %param.16), channel_id=1, source_target_pairs={{0,8},{4,12},{8,0},{12,4},{1,9},{5,13},{9,1},{13,5},{2,10},{6,14},... | collective-permute-start | bytes 2752520 | tf_op jit(solution)/shard_map/ppermute | solution.py:445
  13.1 9.3 %collective-permute-start.1 = (bf16[1,64,2048]{2,1,0:T(8,128)(2,1)S(1)}, bf16[1,64,2048]{2,1,0:T(8,128)(2,1)S(1)}, u32[]{:S(2)}, u32[]{:S(2)}) collective-permute-start(bf16[1,64,2048]{2,1,0:T(8,128)(2,1)S(1)} %collective-permute-done.refs_1_), channel_id=1, source_target_pairs={{0,1},{1,2},{2,3},{3,0},{4,5},{5,6},{6,7},{7,4},{8,9},{9,10},{10,1... | collective-permute-start | bytes 786440 | tf_op jit(solution)/shard_map/ppermute | solution.py:448
  22.4 11.0 %collective-permute-start.2 = (bf16[1,64,2048]{2,1,0:T(8,128)(2,1)S(1)}, bf16[1,64,2048]{2,1,0:T(8,128)(2,1)S(1)}, u32[]{:S(2)}, u32[]{:S(2)}) collective-permute-start(bf16[1,64,2048]{2,1,0:T(8,128)(2,1)S(1)} %get-tuple-element.55.refs_0_.refs_4_), channel_id=1, source_target_pairs={{0,1},{1,2},{2,3},{3,0},{4,5},{5,6},{6,7},{7,4},{8,9},{9,10},{10,1... | collective-permute-start | bytes 786440 | tf_op jit(solution)/shard_map/ppermute | solution.py:451
  22.4 16.7 %collective-permute-start.3 = (bf16[1,64,2048]{2,1,0:T(8,128)(2,1)S(1)}, bf16[1,64,2048]{2,1,0:T(8,128)(2,1)S(1)}, u32[]{:S(2)}, u32[]{:S(2)}) collective-permute-start(bf16[1,64,2048]{2,1,0:T(8,128)(2,1)S(1)} %collective-permute-done.1.refs_2_), channel_id=1, source_target_pairs={{0,1},{1,2},{2,3},{3,0},{4,5},{5,6},{6,7},{7,4},{8,9},{9,10},{10,1... | collective-permute-start | bytes 786440 | tf_op jit(solution)/shard_map/ppermute | solution.py:448
  33.4 15.2 %collective-permute-start.4 = (bf16[1,64,2048]{2,1,0:T(8,128)(2,1)S(1)}, bf16[1,64,2048]{2,1,0:T(8,128)(2,1)S(1)}, u32[]{:S(2)}, u32[]{:S(2)}) collective-permute-start(bf16[1,64,2048]{2,1,0:T(8,128)(2,1)S(1)} %collective-permute-done.2.refs_1_.refs_5_), channel_id=1, source_target_pairs={{0,1},{1,2},{2,3},{3,0},{4,5},{5,6},{6,7},{7,4},{8,9},{9,10},{10,1... | collective-permute-start | bytes 786440 | tf_op jit(solution)/shard_map/ppermute | solution.py:451
  51.4 10.3 %collective-permute-start.10 = (bf16[1,64,2048]{2,1,0:T(8,128)(2,1)S(1)}, bf16[1,64,2048]{2,1,0:T(8,128)(2,1)S(1)}, u32[]{:S(2)}, u32[]{:S(2)}) collective-permute-start(bf16[1,64,2048]{2,1,0:T(8,128)(2,1)S(1)} %collective-permute-done.4.refs_2_.refs_6_), channel_id=1, source_target_pairs={{0,1},{1,2},{2,3},{3,0},{4,5},{5,6},{6,7},{7,4},{8,9},{9,10},{10,1... | collective-permute-start | bytes 786440 | tf_op jit(solution)/shard_map/ppermute | solution.py:451
  51.7 27.4 %collective-permute-start.13 = (bf16[2,64,3712]{2,1,0:T(8,128)(2,1)S(1)}, bf16[2,64,3712]{2,1,0:T(8,128)(2,1)}, u32[]{:S(2)}, u32[]{:S(2)}) collective-permute-start(bf16[2,64,3712]{2,1,0:T(8,128)(2,1)S(1)} %add_convert_fusion.3), channel_id=1, source_target_pairs={{0,8},{4,12},{8,0},{12,4},{1,9},{5,13},{9,1},{13,5},{2,10},{6,14},... | collective-permute-start | bytes 2850824 | tf_op jit(solution)/shard_map/ppermute | solution.py:467
  61.7 24.6 %collective-permute-start.15 = (bf16[128,2048]{1,0:T(8,128)(2,1)S(1)}, bf16[128,2048]{1,0:T(8,128)(2,1)S(1)}, u32[]{:S(2)}, u32[]{:S(2)}) collective-permute-start(bf16[128,2048]{1,0:T(8,128)(2,1)S(1)} %copy-done.19), channel_id=1, source_target_pairs={{0,1},{1,2},{2,3},{3,0},{4,5},{5,6},{6,7},{7,4},{8,9},{9,10},{10,1... | collective-permute-start | bytes 1572872 | tf_op jit(solution)/shard_map/ppermute | solution.py:497
  61.7 11.5 %collective-permute-start.8 = (bf16[128,3584]{1,0:T(8,128)(2,1)}, bf16[128,3584]{1,0:T(8,128)(2,1)S(1)}, u32[]{:S(2)}, u32[]{:S(2)}) collective-permute-start(bf16[128,3584]{1,0:T(8,128)(2,1)} %param.16), channel_id=1, source_target_pairs={{0,4},{4,0},{8,12},{12,8},{1,5},{5,1},{9,13},{13,9},{2,6},{6,2},{1... | collective-permute-start | bytes 2752520 | tf_op jit(solution)/shard_map/ppermute | solution.py:486
  61.7 11.5 %collective-permute-start.9 = (bf16[128,3584]{1,0:T(8,128)(2,1)}, bf16[128,3584]{1,0:T(8,128)(2,1)}, u32[]{:S(2)}, u32[]{:S(2)}) collective-permute-start(bf16[128,3584]{1,0:T(8,128)(2,1)} %param.15), channel_id=1, source_target_pairs={{0,4},{4,0},{8,12},{12,8},{1,5},{5,1},{9,13},{13,9},{2,6},{6,2},{1... | collective-permute-start | bytes 2752520 | tf_op jit(solution)/shard_map/ppermute | solution.py:486
  69.8 9.4 %collective-permute-start.14 = (bf16[2,64,3712]{2,1,0:T(8,128)(2,1)S(1)}, bf16[2,64,3712]{2,1,0:T(8,128)(2,1)S(1)}, u32[]{:S(2)}, u32[]{:S(2)}) collective-permute-start(bf16[2,64,3712]{2,1,0:T(8,128)(2,1)S(1)} %get-tuple-element.63), channel_id=1, source_target_pairs={{0,4},{4,0},{8,12},{12,8},{1,5},{5,1},{9,13},{13,9},{2,6},{6,2},{1... | collective-permute-start | bytes 2850824 | tf_op jit(solution)/shard_map/ppermute | solution.py:488
  81.3 28.2 %collective-permute-start.19 = (bf16[2,64,3712]{2,1,0:T(8,128)(2,1)S(1)}, bf16[2,64,3712]{2,1,0:T(8,128)(2,1)S(1)}, u32[]{:S(2)}, u32[]{:S(2)}) collective-permute-start(bf16[2,64,3712]{2,1,0:T(8,128)(2,1)S(1)} %add_convert_fusion.2), channel_id=1, source_target_pairs={{0,8},{4,12},{8,0},{12,4},{1,9},{5,13},{9,1},{13,5},{2,10},{6,14},... | collective-permute-start | bytes 2850824 | tf_op jit(solution)/shard_map/ppermute | solution.py:467
  82.5 21.2 %collective-permute-start.18 = (bf16[128,2048]{1,0:T(8,128)(2,1)S(1)}, bf16[128,2048]{1,0:T(8,128)(2,1)S(1)}, u32[]{:S(2)}, u32[]{:S(2)}) collective-permute-start(bf16[128,2048]{1,0:T(8,128)(2,1)S(1)} %copy-done.19), channel_id=1, source_target_pairs={{0,3},{1,0},{2,1},{3,2},{4,7},{5,4},{6,5},{7,6},{8,11},{9,8},{10,9... | collective-permute-start | bytes 1572872 | tf_op jit(solution)/shard_map/ppermute | solution.py:498
  86.3 23.2 %collective-permute-start.17 = (bf16[128,2048]{1,0:T(8,128)(2,1)S(1)}, bf16[128,2048]{1,0:T(8,128)(2,1)S(1)}, u32[]{:S(2)}, u32[]{:S(2)}) collective-permute-start(bf16[128,2048]{1,0:T(8,128)(2,1)S(1)} %collective-permute-done.15.refs_9_), channel_id=1, source_target_pairs={{0,1},{1,2},{2,3},{3,0},{4,5},{5,6},{6,7},{7,4},{8,9},{9,10},{10,1... | collective-permute-start | bytes 1572872 | tf_op jit(solution)/shard_map/ppermute | solution.py:500
  109.8 20.8 %collective-permute-start.23 = (bf16[64,2176]{1,0:T(8,128)(2,1)S(1)}, bf16[64,2176]{1,0:T(8,128)(2,1)S(1)}, u32[]{:S(2)}, u32[]{:S(2)}) collective-permute-start(bf16[64,2176]{1,0:T(8,128)(2,1)S(1)} %get-tuple-element.75), channel_id=1, source_target_pairs={{0,3},{1,0},{2,1},{3,2},{4,7},{5,4},{6,5},{7,6},{8,11},{9,8},{10,9... | collective-permute-start | bytes 835592 | tf_op jit(solution)/shard_map/ppermute | solution.py:476
  111.6 26.4 %collective-permute-start.22 = (bf16[64,2176]{1,0:T(8,128)(2,1)S(1)}, bf16[64,2176]{1,0:T(8,128)(2,1)S(1)}, u32[]{:S(2)}, u32[]{:S(2)}) collective-permute-start(bf16[64,2176]{1,0:T(8,128)(2,1)S(1)} %get-tuple-element.73), channel_id=1, source_target_pairs={{0,2},{1,3},{2,0},{3,1},{4,6},{5,7},{6,4},{7,5},{8,10},{9,11},{10,... | collective-permute-start | bytes 835592 | tf_op jit(solution)/shard_map/ppermute | solution.py:476
  113.1 24.9 %collective-permute-start.21 = (bf16[64,2176]{1,0:T(8,128)(2,1)S(1)}, bf16[64,2176]{1,0:T(8,128)(2,1)S(1)}, u32[]{:S(2)}, u32[]{:S(2)}) collective-permute-start(bf16[64,2176]{1,0:T(8,128)(2,1)S(1)} %get-tuple-element.71), channel_id=1, source_target_pairs={{0,1},{1,2},{2,3},{3,0},{4,5},{5,6},{6,7},{7,4},{8,9},{9,10},{10,1... | collective-permute-start | bytes 835592 | tf_op jit(solution)/shard_map/ppermute | solution.py:476
  138.0 20.1 %collective-permute-start.27 = (bf16[64,2176]{1,0:T(8,128)(2,1)S(1)}, bf16[64,2176]{1,0:T(8,128)(2,1)S(1)}, u32[]{:S(2)}, u32[]{:S(2)}) collective-permute-start(bf16[64,2176]{1,0:T(8,128)(2,1)S(1)} %get-tuple-element.84), channel_id=1, source_target_pairs={{0,1},{1,2},{2,3},{3,0},{4,5},{5,6},{6,7},{7,4},{8,9},{9,10},{10,1... | collective-permute-start | bytes 835592 | tf_op jit(solution)/shard_map/ppermute | solution.py:476
  138.0 22.1 %collective-permute-start.28 = (bf16[64,2176]{1,0:T(8,128)(2,1)S(1)}, bf16[64,2176]{1,0:T(8,128)(2,1)S(1)}, u32[]{:S(2)}, u32[]{:S(2)}) collective-permute-start(bf16[64,2176]{1,0:T(8,128)(2,1)S(1)} %get-tuple-element.85), channel_id=1, source_target_pairs={{0,2},{1,3},{2,0},{3,1},{4,6},{5,7},{6,4},{7,5},{8,10},{9,11},{10,... | collective-permute-start | bytes 835592 | tf_op jit(solution)/shard_map/ppermute | solution.py:476
  138.6 21.6 %collective-permute-start.29 = (bf16[64,2176]{1,0:T(8,128)(2,1)S(1)}, bf16[64,2176]{1,0:T(8,128)(2,1)S(1)}, u32[]{:S(2)}, u32[]{:S(2)}) collective-permute-start(bf16[64,2176]{1,0:T(8,128)(2,1)S(1)} %get-tuple-element.86), channel_id=1, source_target_pairs={{0,3},{1,0},{2,1},{3,2},{4,7},{5,4},{6,5},{7,6},{8,11},{9,8},{10,9... | collective-permute-start | bytes 835592 | tf_op jit(solution)/shard_map/ppermute | solution.py:476
  148.4 7.5 %collective-permute-start.25 = (bf16[16,3584]{1,0:T(8,128)(2,1)S(1)}, bf16[16,3584]{1,0:T(8,128)(2,1)S(1)}, u32[]{:S(2)}, u32[]{:S(2)}) collective-permute-start(bf16[16,3584]{1,0:T(8,128)(2,1)S(1)} %down_part.1.refs_0_), channel_id=1, source_target_pairs={{0,4},{4,0},{8,12},{12,8},{1,5},{5,1},{9,13},{13,9},{2,6},{6,2},{1... | collective-permute-start | bytes 344072 | tf_op jit(solution)/shard_map/ppermute | solution.py:514
  149.1 6.8 %collective-permute-start.26 = (bf16[16,3584]{1,0:T(8,128)(2,1)S(1)}, bf16[16,3584]{1,0:T(8,128)(2,1)S(1)}, u32[]{:S(2)}, u32[]{:S(2)}) collective-permute-start(bf16[16,3584]{1,0:T(8,128)(2,1)S(1)} %collective-permute-done.24.refs_1_), channel_id=1, source_target_pairs={{0,4},{4,0},{8,12},{12,8},{1,5},{5,1},{9,13},{13,9},{2,6},{6,2},{1... | collective-permute-start | bytes 344072 | tf_op jit(solution)/shard_map/ppermute | solution.py:514
  (29 other events, 209.7 us)

commit v9 on v8

--- a/solution.py
+++ b/solution.py
@@ -495,13 +495,13 @@
     mine_b, far_b = exchange(after(keep_b, *far_a, *[pair[0] for pair in factors]), other_b)
     inputs = [after(layer_input, grads[1][-1], mine_a)] + [None] * (n_dp - 1)
     inputs[1] = lax.ppermute(inputs[0], "dp", z_next)
-    inputs[-1] = lax.ppermute(inputs[0], "dp", ring(n_dp, -1))
+    inputs[-1] = lax.ppermute(after(inputs[0], keep_b), "dp", ring(n_dp, -1))
     for k in range(2, n_dp // 2 + 1):
         inputs[k] = lax.ppermute(inputs[k - 1], "dp", z_next)
     for k in range(2, (n_dp + 1) // 2):
         inputs[-k] = lax.ppermute(inputs[1 - k], "dp", ring(n_dp, -1))
-    sums_a = total(after(mine_a, mine_b), far_a)
-    there_a = second(0, sums_a, (inputs[1],))
+    sums_a = total(after(mine_a, mine_b, inputs[1], inputs[-1]), far_a)
+    there_a = second(0, sums_a, ())
     sums_b = total(after(mine_b, there_a[0], inputs[n_dp // 2], inputs[-1]), far_b)
     there_b = second(1, sums_b, ())
 

time: 166 us -> 169 us (1.018)
  waiting for transfers between devices: 56.2 us -> 58.7 us
    ppermute x1, waiting for transfers between devices: 5.75 us -> 0.01 us  [per_device(): inputs[k] = lax.ppermute(inputs[k - 1], 'dp', z_next)]
    ppermute x1, waiting for transfers between devices: 0.01 us -> 4.41 us  [per_device(): inputs[-1] = lax.ppermute(after(inputs[0], keep_b), 'dp', ring(n_dp, -1))]
    ppermute x2, waiting for transfers between devices: 0.01 us -> 3.55 us  [exchange(): lax.ppermute(mine, 'tensor', ring(n_t, 2 * s))]
    ppermute x6, waiting for transfers between devices: 9.37 us -> 7.62 us  [second(): lax.ppermute(outs[r], 'dp', ring(n_dp, r))]
  transfers between devices with their start and end apart: 30 -> 30, of which waited for: 10 -> 13; matrix products, arithmetic and copies ran while one was open for 9% -> 7% of each run, Pallas kernels for 37% -> 36%
where the time goes in v9:
time: 169 us; the launch traced here: 166 us
  Pallas kernels  62.4 us (37%)
  waiting for transfers between devices  58.7 us (35%)
  starting transfers between devices  22.1 us (13%)
  other arithmetic  14 us (8%)
  local copies, waits for them, and re-layouts  7.39 us (4%)
    pallas_call x2, Pallas kernels, input_partial(): pl.pallas_call(functools.partial(input_kernel, (n_dp, n_t, g, own_t, rc,...  33 us
    ppermute x3, waiting for transfers between devices, per_device(): grads[0].append(lax.ppermute(grads[0][-1], 'dp', z_next))  20.5 us
    ppermute x3, waiting for transfers between devices, per_device(): grads[1].append(lax.ppermute(grads[1][-1], 'dp', z_next))  19.8 us
    pallas_call x2, Pallas kernels, hidden_partial(): pl.pallas_call(functools.partial(hidden_kernel, (n_dp, n_t, g, own_t, rc,...  15.1 us
    convert_element_type x4, other arithmetic, factors_of(): return [x.astype(jnp.bfloat16) for x in (dgate, dup, dup * up_value)]  10.1 us
    ppermute x6, waiting for transfers between devices, second(): lax.ppermute(outs[r], 'dp', ring(n_dp, r))  7.62 us
    ppermute x6, starting transfers between devices, second(): lax.ppermute(outs[r], 'dp', ring(n_dp, r))  7.42 us
    unnamed x46, local copies, waits for them, and re-layouts  6.32 us
  transfers between devices with their start and end apart: 30, of which 13 were waited for; matrix products, arithmetic and copies ran while one was open for 7% of the time, Pallas kernels for 36%

profile of v9, /device:TPU:0, one launch (start us, length us, event | category | flops | bytes accessed | tf_op | source)
XLA Modules:
  0.0 165.6 jit_solution(13514539671932096399)
XLA Ops:
  1.7 3.1 %collective-permute-start = (bf16[1,64,2048]{2,1,0:T(8,128)(2,1)S(1)}, bf16[1,64,2048]{2,1,0:T(8,128)(2,1)S(1)}, u32[]{:S(2)}, u32[]{:S(2)}) collective-permute-start(bf16[1,64,2048]{2,1,0:T(8,128)(2,1)S(1)} %get-tuple-element.47.refs_0_), channel_id=1, source_target_pairs={{0,1},{1,2},{2,3},{3,0},{4,5},{5,6},{6,7},{7,4},{8,9},{9,10},{10,1... | collective-permute-start | bytes 786440 | tf_op jit(solution)/shard_map/ppermute | solution.py:448
  6.8 6.3 %collective-permute-done.refs_1_ = bf16[1,64,2048]{2,1,0:T(8,128)(2,1)S(1)} collective-permute-done((bf16[1,64,2048]{2,1,0:T(8,128)(2,1)S(1)}, bf16[1,64,2048]{2,1,0:T(8,128)(2,1)S(1)}, u32[]{:S(2)}, u32[]{:S(2)}) %collective-permute-start) | collective-permute-done | bytes 262176 | tf_op jit(solution)/shard_map/ppermute | solution.py:448
  13.1 9.3 %collective-permute-done.1.refs_2_ = bf16[1,64,2048]{2,1,0:T(8,128)(2,1)S(1)} collective-permute-done((bf16[1,64,2048]{2,1,0:T(8,128)(2,1)S(1)}, bf16[1,64,2048]{2,1,0:T(8,128)(2,1)S(1)}, u32[]{:S(2)}, u32[]{:S(2)}) %collective-permute-start.1) | collective-permute-done | bytes 262176 | tf_op jit(solution)/shard_map/ppermute | solution.py:448
  22.4 11.0 %collective-permute-done.2.refs_1_.refs_5_ = bf16[1,64,2048]{2,1,0:T(8,128)(2,1)S(1)} collective-permute-done((bf16[1,64,2048]{2,1,0:T(8,128)(2,1)S(1)}, bf16[1,64,2048]{2,1,0:T(8,128)(2,1)S(1)}, u32[]{:S(2)}, u32[]{:S(2)}) %collective-permute-start.2) | collective-permute-done | bytes 262176 | tf_op jit(solution)/shard_map/ppermute | solution.py:451
  34.2 4.9 %collective-permute-done.3.refs_3_ = bf16[1,64,2048]{2,1,0:T(8,128)(2,1)S(1)} collective-permute-done((bf16[1,64,2048]{2,1,0:T(8,128)(2,1)S(1)}, bf16[1,64,2048]{2,1,0:T(8,128)(2,1)S(1)}, u32[]{:S(2)}, u32[]{:S(2)}) %collective-permute-start.3) | collective-permute-done | bytes 262176 | tf_op jit(solution)/shard_map/ppermute | solution.py:448
  41.0 7.6 %hidden_partial.2 = (bf16[2,64,3712]{2,1,0:T(8,128)(2,1)S(1)}, bf16[2,64,3712]{2,1,0:T(8,128)(2,1)S(1)}) custom-call(s32[6]{0:T(128)S(1)} %pad_add_fusion.meta, bf16[1,64,2048]{2,1,0:T(8,128)(2,1)S(1)} %get-tuple-element.47.refs_0_, bf16[1,64,2048]{2,1,0:T(8,128)(2,1)S(1)} %collective-permute-done.refs_1_, ...), custom_call_target="tpu_custom_call" | custom-call | flops 1 | bytes 1 | tf_op jit(solution)/shard_map/hidden_partial/pallas_call | solution.py:104
  48.7 2.7 %fusion.2 = (bf16[128,3584]{1,0:T(8,128)(2,1)S(1)}, bf16[128,3584]{1,0:T(8,128)(2,1)S(1)}, bf16[128,3584]{1,0:T(8,128)(2,1)S(1)}) fusion(bf16[128,3584]{1,0:T(8,128)(2,1)} %param.16, bf16[128,3584]{1,0:T(8,128)(2,1)} %param.15), kind=kLoop, calls=%fused_computation.20 | loop fusion | flops 6881280 | bytes 4587520 | tf_op jit(solution)/shard_map/convert_element_type | solution.py:463
  53.0 8.8 %collective-permute-done.10.refs_3_.refs_7_ = bf16[1,64,2048]{2,1,0:T(8,128)(2,1)S(1)} collective-permute-done((bf16[1,64,2048]{2,1,0:T(8,128)(2,1)S(1)}, bf16[1,64,2048]{2,1,0:T(8,128)(2,1)S(1)}, u32[]{:S(2)}, u32[]{:S(2)}) %collective-permute-start.10) | collective-permute-done | bytes 262176 | tf_op jit(solution)/shard_map/ppermute | solution.py:451
  62.2 7.6 %hidden_partial.3 = (bf16[2,64,3712]{2,1,0:T(8,128)(2,1)S(1)}, bf16[2,64,3712]{2,1,0:T(8,128)(2,1)S(1)}) custom-call(s32[6]{0:T(128)S(1)} %pad_add_fusion.meta, bf16[1,64,2048]{2,1,0:T(8,128)(2,1)S(1)} %get-tuple-element.55.refs_0_.refs_4_, bf16[1,64,2048]{2,1,0:T(8,128)(2,1)S(1)} %collective-permute-done.2.refs_1_.refs_5_, ...), custom_call_target="tpu_custom_call" | custom-call | flops 1 | bytes 1 | tf_op jit(solution)/shard_map/hidden_partial/pallas_call | solution.py:104
  69.8 3.9 %collective-permute-start.16 = (bf16[128,2048]{1,0:T(8,128)(2,1)S(1)}, bf16[128,2048]{1,0:T(8,128)(2,1)S(1)}, u32[]{:S(2)}, u32[]{:S(2)}) collective-permute-start(bf16[128,2048]{1,0:T(8,128)(2,1)S(1)} %copy-done.19), channel_id=1, source_target_pairs={{0,3},{1,0},{2,1},{3,2},{4,7},{5,4},{6,5},{7,6},{8,11},{9,8},{10,9... | collective-permute-start | bytes 1572872 | tf_op jit(solution)/shard_map/ppermute | solution.py:498
  73.7 3.3 %fusion.20 = (bf16[128,3584]{1,0:T(8,128)(2,1)}, bf16[128,3584]{1,0:T(8,128)(2,1)}) fusion(bf16[128,3584]{1,0:T(8,128)(2,1)} %collective-permute-done.5, bf16[128,3584]{1,0:T(8,128)(2,1)S(1)} %copy-done.22), kind=kLoop, calls=%fused_computation.38 | loop fusion | flops 5963776 | bytes 3670016 | tf_op jit(solution)/shard_map/convert_element_type | solution.py:463
  77.5 2.1 %fusion.13 = (bf16[128,3584]{1,0:T(8,128)(2,1)}, bf16[128,3584]{1,0:T(8,128)(2,1)}) fusion(bf16[128,3584]{1,0:T(8,128)(2,1)S(1)} %collective-permute-done.9, bf16[128,3584]{1,0:T(8,128)(2,1)S(1)} %collective-permute-done.8), kind=kLoop, calls=%fused_computation.31 | loop fusion | flops 5963776 | bytes 3670016 | tf_op jit(solution)/shard_map/convert_element_type | solution.py:463
  81.1 2.1 %fusion.27 = (bf16[128,3584]{1,0:T(8,128)(2,1)}, bf16[128,3584]{1,0:T(8,128)(2,1)}) fusion(bf16[128,3584]{1,0:T(8,128)(2,1)S(1)} %collective-permute-done.12, bf16[128,3584]{1,0:T(8,128)(2,1)S(1)} %collective-permute-done.11), kind=kLoop, calls=%fused_computation.45 | loop fusion | flops 5963776 | bytes 3670016 | tf_op jit(solution)/shard_map/convert_element_type | solution.py:463
  83.7 4.4 %collective-permute-done.16.refs_11_ = bf16[128,2048]{1,0:T(8,128)(2,1)S(1)} collective-permute-done((bf16[128,2048]{1,0:T(8,128)(2,1)S(1)}, bf16[128,2048]{1,0:T(8,128)(2,1)S(1)}, u32[]{:S(2)}, u32[]{:S(2)}) %collective-permute-start.16) | collective-permute-done | bytes 524320 | tf_op jit(solution)/shard_map/ppermute | solution.py:498
  93.1 16.4 %input_partial.2 = (bf16[64,2176]{1,0:T(8,128)(2,1)S(1)}, bf16[64,2176]{1,0:T(8,128)(2,1)S(1)}, bf16[64,2176]{1,0:T(8,128)(2,1)S(1)}, bf16[64,2176]{1,0:T(8,128)(2,1)S(1)}) custom-call(s32[6]{0:T(128)S(1)} %pad_add_fusion.meta, bf16[128,3584]{1,0:T(8,128)(2,1)S(1)} %get-tuple-element.88.refs_0_, bf16[128,3584]{1,0:T(8,128)(2,1)S(1)} %get-tuple-element.89.refs_1_, ...), custom_call_target="tpu_custom_call" | custom-call | flops 1 | bytes 1 | tf_op jit(solution)/shard_map/input_partial/pallas_call | solution.py:194
  109.5 3.5 %collective-permute-done.19 = bf16[2,64,3712]{2,1,0:T(8,128)(2,1)S(1)} collective-permute-done((bf16[2,64,3712]{2,1,0:T(8,128)(2,1)S(1)}, bf16[2,64,3712]{2,1,0:T(8,128)(2,1)S(1)}, u32[]{:S(2)}, u32[]{:S(2)}) %collective-permute-start.19) | collective-permute-done | bytes 950304 | tf_op jit(solution)/shard_map/ppermute | solution.py:467
  117.0 16.6 %input_partial.3 = (bf16[64,2176]{1,0:T(8,128)(2,1)S(1)}, bf16[64,2176]{1,0:T(8,128)(2,1)S(1)}, bf16[64,2176]{1,0:T(8,128)(2,1)S(1)}, bf16[64,2176]{1,0:T(8,128)(2,1)S(1)}) custom-call(s32[6]{0:T(128)S(1)} %pad_add_fusion.meta, bf16[128,3584]{1,0:T(8,128)(2,1)S(1)} %get-tuple-element.88.refs_0_, bf16[128,3584]{1,0:T(8,128)(2,1)S(1)} %get-tuple-element.89.refs_1_, ...), custom_call_target="tpu_custom_call" | custom-call | flops 1 | bytes 1 | tf_op jit(solution)/shard_map/input_partial/pallas_call | solution.py:194
  133.6 6.7 %collective-permute-done.22.refs_2_ = bf16[64,2176]{1,0:T(8,128)(2,1)S(1)} collective-permute-done((bf16[64,2176]{1,0:T(8,128)(2,1)S(1)}, bf16[64,2176]{1,0:T(8,128)(2,1)S(1)}, u32[]{:S(2)}, u32[]{:S(2)}) %collective-permute-start.22) | collective-permute-done | bytes 278560 | tf_op jit(solution)/shard_map/ppermute | solution.py:476
  140.3 1.9 %collective-permute-start.28 = (bf16[64,2176]{1,0:T(8,128)(2,1)S(1)}, bf16[64,2176]{1,0:T(8,128)(2,1)S(1)}, u32[]{:S(2)}, u32[]{:S(2)}) collective-permute-start(bf16[64,2176]{1,0:T(8,128)(2,1)S(1)} %get-tuple-element.85), channel_id=1, source_target_pairs={{0,2},{1,3},{2,0},{3,1},{4,6},{5,7},{6,4},{7,5},{8,10},{9,11},{10,... | collective-permute-start | bytes 835592 | tf_op jit(solution)/shard_map/ppermute | solution.py:476
  142.2 2.9 %collective-permute-start.29 = (bf16[64,2176]{1,0:T(8,128)(2,1)S(1)}, bf16[64,2176]{1,0:T(8,128)(2,1)S(1)}, u32[]{:S(2)}, u32[]{:S(2)}) collective-permute-start(bf16[64,2176]{1,0:T(8,128)(2,1)S(1)} %get-tuple-element.86), channel_id=1, source_target_pairs={{0,3},{1,0},{2,1},{3,2},{4,7},{5,4},{6,5},{7,6},{8,11},{9,8},{10,9... | collective-permute-start | bytes 835592 | tf_op jit(solution)/shard_map/ppermute | solution.py:476
  149.3 2.7 %down_outer.1 = f32[4,16,2048]{2,1,0:T(8,128)} custom-call(s32[6]{0:T(128)S(1)} %pad_add_fusion.meta, bf16[1,64,2048]{2,1,0:T(8,128)(2,1)S(1)} %get-tuple-element.47.refs_0_, bf16[1,64,2048]{2,1,0:T(8,128)(2,1)S(1)} %collective-permute-done.refs_1_, bf16[1,64,2048]{2,1,0:T(8,128)(2,1)S(1)} %collective-permute-done.1.refs_2_, ...), custom_call_target="tpu_custom_call" | custom-call | flops 1 | bytes 1 | tf_op jit(solution)/shard_map/down_outer/pallas_call | solution.py:252
  153.7 5.6 %gate_up_outer.1 = f32[4,32,3584]{2,1,0:T(8,128)} custom-call(s32[6]{0:T(128)S(1)} %pad_add_fusion.meta, bf16[128,3584]{1,0:T(8,128)(2,1)S(1)} %get-tuple-element.88.refs_0_, bf16[128,3584]{1,0:T(8,128)(2,1)S(1)} %get-tuple-element.89.refs_1_, bf16[128,3584]{1,0:T(8,128)(2,1)S(1)} %copy-done.8, bf16[128,3584]{1,0:T(8,128)(2,1)S(1)} %copy-done.7, ...), custom_call_target="tpu_custom_call" | custom-call | flops 1 | bytes 1 | tf_op jit(solution)/shard_map/gate_up_outer/pallas_call | solution.py:291
  159.3 2.2 %spread_a_down.1 = f32[4,16,3584]{2,1,0:T(8,128)} custom-call(s32[6]{0:T(128)S(1)} %pad_add_fusion.meta, bf16[16,3584]{1,0:T(8,128)(2,1)S(1)} %down_part.1.refs_0_, bf16[16,3584]{1,0:T(8,128)(2,1)S(1)} %collective-permute-done.24.refs_1_, bf16[16,3584]{1,0:T(8,128)(2,1)S(1)} %collective-permute-done.25.refs_2_, ...), custom_call_target="tpu_custom_call" | custom-call | flops 1 | bytes 1 | tf_op jit(solution)/shard_map/spread_a_down/pallas_call | solution.py:344
  163.4 2.2 %in_outer.1 = f32[4,32,2048]{2,1,0:T(8,128)} custom-call(s32[6]{0:T(128)S(1)} %pad_add_fusion.meta, bf16[64,2176]{1,0:T(8,128)(2,1)S(1)} %get-tuple-element.70.refs_0_, bf16[64,2176]{1,0:T(8,128)(2,1)S(1)} %collective-permute-done.21.refs_1_, bf16[64,2176]{1,0:T(8,128)(2,1)S(1)} %collective-permute-done.22.refs_2_, ...), custom_call_target="tpu_custom_call" | custom-call | flops 1 | bytes 1 | tf_op jit(solution)/shard_map/in_outer/pallas_call | solution.py:384
  (105 shorter events, 27.1 us)
Async XLA Ops:
  1.7 11.4 %collective-permute-start = (bf16[1,64,2048]{2,1,0:T(8,128)(2,1)S(1)}, bf16[1,64,2048]{2,1,0:T(8,128)(2,1)S(1)}, u32[]{:S(2)}, u32[]{:S(2)}) collective-permute-start(bf16[1,64,2048]{2,1,0:T(8,128)(2,1)S(1)} %get-tuple-element.47.refs_0_), channel_id=1, source_target_pairs={{0,1},{1,2},{2,3},{3,0},{4,5},{5,6},{6,7},{7,4},{8,9},{9,10},{10,1... | collective-permute-start | bytes 786440 | tf_op jit(solution)/shard_map/ppermute | solution.py:448
  4.8 43.8 %collective-permute-start.5 = (bf16[128,3584]{1,0:T(8,128)(2,1)}, bf16[128,3584]{1,0:T(8,128)(2,1)}, u32[]{:S(2)}, u32[]{:S(2)}) collective-permute-start(bf16[128,3584]{1,0:T(8,128)(2,1)} %param.15), channel_id=1, source_target_pairs={{0,8},{4,12},{8,0},{12,4},{1,9},{5,13},{9,1},{13,5},{2,10},{6,14},... | collective-permute-start | bytes 2752520 | tf_op jit(solution)/shard_map/ppermute | solution.py:445
  6.3 42.3 %collective-permute-start.6 = (bf16[128,3584]{1,0:T(8,128)(2,1)}, bf16[128,3584]{1,0:T(8,128)(2,1)S(1)}, u32[]{:S(2)}, u32[]{:S(2)}) collective-permute-start(bf16[128,3584]{1,0:T(8,128)(2,1)} %param.16), channel_id=1, source_target_pairs={{0,8},{4,12},{8,0},{12,4},{1,9},{5,13},{9,1},{13,5},{2,10},{6,14},... | collective-permute-start | bytes 2752520 | tf_op jit(solution)/shard_map/ppermute | solution.py:445
  13.1 9.3 %collective-permute-start.1 = (bf16[1,64,2048]{2,1,0:T(8,128)(2,1)S(1)}, bf16[1,64,2048]{2,1,0:T(8,128)(2,1)S(1)}, u32[]{:S(2)}, u32[]{:S(2)}) collective-permute-start(bf16[1,64,2048]{2,1,0:T(8,128)(2,1)S(1)} %collective-permute-done.refs_1_), channel_id=1, source_target_pairs={{0,1},{1,2},{2,3},{3,0},{4,5},{5,6},{6,7},{7,4},{8,9},{9,10},{10,1... | collective-permute-start | bytes 786440 | tf_op jit(solution)/shard_map/ppermute | solution.py:448
  22.4 11.0 %collective-permute-start.2 = (bf16[1,64,2048]{2,1,0:T(8,128)(2,1)S(1)}, bf16[1,64,2048]{2,1,0:T(8,128)(2,1)S(1)}, u32[]{:S(2)}, u32[]{:S(2)}) collective-permute-start(bf16[1,64,2048]{2,1,0:T(8,128)(2,1)S(1)} %get-tuple-element.55.refs_0_.refs_4_), channel_id=1, source_target_pairs={{0,1},{1,2},{2,3},{3,0},{4,5},{5,6},{6,7},{7,4},{8,9},{9,10},{10,1... | collective-permute-start | bytes 786440 | tf_op jit(solution)/shard_map/ppermute | solution.py:451
  22.4 16.7 %collective-permute-start.3 = (bf16[1,64,2048]{2,1,0:T(8,128)(2,1)S(1)}, bf16[1,64,2048]{2,1,0:T(8,128)(2,1)S(1)}, u32[]{:S(2)}, u32[]{:S(2)}) collective-permute-start(bf16[1,64,2048]{2,1,0:T(8,128)(2,1)S(1)} %collective-permute-done.1.refs_2_), channel_id=1, source_target_pairs={{0,1},{1,2},{2,3},{3,0},{4,5},{5,6},{6,7},{7,4},{8,9},{9,10},{10,1... | collective-permute-start | bytes 786440 | tf_op jit(solution)/shard_map/ppermute | solution.py:448
  33.4 15.2 %collective-permute-start.4 = (bf16[1,64,2048]{2,1,0:T(8,128)(2,1)S(1)}, bf16[1,64,2048]{2,1,0:T(8,128)(2,1)S(1)}, u32[]{:S(2)}, u32[]{:S(2)}) collective-permute-start(bf16[1,64,2048]{2,1,0:T(8,128)(2,1)S(1)} %collective-permute-done.2.refs_1_.refs_5_), channel_id=1, source_target_pairs={{0,1},{1,2},{2,3},{3,0},{4,5},{5,6},{6,7},{7,4},{8,9},{9,10},{10,1... | collective-permute-start | bytes 786440 | tf_op jit(solution)/shard_map/ppermute | solution.py:451
  51.4 10.3 %collective-permute-start.10 = (bf16[1,64,2048]{2,1,0:T(8,128)(2,1)S(1)}, bf16[1,64,2048]{2,1,0:T(8,128)(2,1)S(1)}, u32[]{:S(2)}, u32[]{:S(2)}) collective-permute-start(bf16[1,64,2048]{2,1,0:T(8,128)(2,1)S(1)} %collective-permute-done.4.refs_2_.refs_6_), channel_id=1, source_target_pairs={{0,1},{1,2},{2,3},{3,0},{4,5},{5,6},{6,7},{7,4},{8,9},{9,10},{10,1... | collective-permute-start | bytes 786440 | tf_op jit(solution)/shard_map/ppermute | solution.py:451
  51.7 31.4 %collective-permute-start.13 = (bf16[2,64,3712]{2,1,0:T(8,128)(2,1)S(1)}, bf16[2,64,3712]{2,1,0:T(8,128)(2,1)}, u32[]{:S(2)}, u32[]{:S(2)}) collective-permute-start(bf16[2,64,3712]{2,1,0:T(8,128)(2,1)S(1)} %add_convert_fusion.3), channel_id=1, source_target_pairs={{0,8},{4,12},{8,0},{12,4},{1,9},{5,13},{9,1},{13,5},{2,10},{6,14},... | collective-permute-start | bytes 2850824 | tf_op jit(solution)/shard_map/ppermute | solution.py:467
  61.7 22.0 %collective-permute-start.15 = (bf16[128,2048]{1,0:T(8,128)(2,1)S(1)}, bf16[128,2048]{1,0:T(8,128)(2,1)S(1)}, u32[]{:S(2)}, u32[]{:S(2)}) collective-permute-start(bf16[128,2048]{1,0:T(8,128)(2,1)S(1)} %copy-done.19), channel_id=1, source_target_pairs={{0,1},{1,2},{2,3},{3,0},{4,5},{5,6},{6,7},{7,4},{8,9},{9,10},{10,1... | collective-permute-start | bytes 1572872 | tf_op jit(solution)/shard_map/ppermute | solution.py:497
  61.7 15.2 %collective-permute-start.8 = (bf16[128,3584]{1,0:T(8,128)(2,1)}, bf16[128,3584]{1,0:T(8,128)(2,1)S(1)}, u32[]{:S(2)}, u32[]{:S(2)}) collective-permute-start(bf16[128,3584]{1,0:T(8,128)(2,1)} %param.16), channel_id=1, source_target_pairs={{0,4},{4,0},{8,12},{12,8},{1,5},{5,1},{9,13},{13,9},{2,6},{6,2},{1... | collective-permute-start | bytes 2752520 | tf_op jit(solution)/shard_map/ppermute | solution.py:486
  61.7 15.2 %collective-permute-start.9 = (bf16[128,3584]{1,0:T(8,128)(2,1)}, bf16[128,3584]{1,0:T(8,128)(2,1)S(1)}, u32[]{:S(2)}, u32[]{:S(2)}) collective-permute-start(bf16[128,3584]{1,0:T(8,128)(2,1)} %param.15), channel_id=1, source_target_pairs={{0,4},{4,0},{8,12},{12,8},{1,5},{5,1},{9,13},{13,9},{2,6},{6,2},{1... | collective-permute-start | bytes 2752520 | tf_op jit(solution)/shard_map/ppermute | solution.py:486
  69.8 18.3 %collective-permute-start.16 = (bf16[128,2048]{1,0:T(8,128)(2,1)S(1)}, bf16[128,2048]{1,0:T(8,128)(2,1)S(1)}, u32[]{:S(2)}, u32[]{:S(2)}) collective-permute-start(bf16[128,2048]{1,0:T(8,128)(2,1)S(1)} %copy-done.19), channel_id=1, source_target_pairs={{0,3},{1,0},{2,1},{3,2},{4,7},{5,4},{6,5},{7,6},{8,11},{9,8},{10,9... | collective-permute-start | bytes 1572872 | tf_op jit(solution)/shard_map/ppermute | solution.py:498
  89.6 23.5 %collective-permute-start.19 = (bf16[2,64,3712]{2,1,0:T(8,128)(2,1)S(1)}, bf16[2,64,3712]{2,1,0:T(8,128)(2,1)S(1)}, u32[]{:S(2)}, u32[]{:S(2)}) collective-permute-start(bf16[2,64,3712]{2,1,0:T(8,128)(2,1)S(1)} %add_convert_fusion.2), channel_id=1, source_target_pairs={{0,8},{4,12},{8,0},{12,4},{1,9},{5,13},{9,1},{13,5},{2,10},{6,14},... | collective-permute-start | bytes 2850824 | tf_op jit(solution)/shard_map/ppermute | solution.py:467
  90.9 18.7 %collective-permute-start.18 = (bf16[128,2048]{1,0:T(8,128)(2,1)S(1)}, bf16[128,2048]{1,0:T(8,128)(2,1)S(1)}, u32[]{:S(2)}, u32[]{:S(2)}) collective-permute-start(bf16[128,2048]{1,0:T(8,128)(2,1)S(1)} %collective-permute-done.15.refs_9_), channel_id=1, source_target_pairs={{0,1},{1,2},{2,3},{3,0},{4,5},{5,6},{6,7},{7,4},{8,9},{9,10},{10,1... | collective-permute-start | bytes 1572872 | tf_op jit(solution)/shard_map/ppermute | solution.py:500
  113.4 20.1 %collective-permute-start.23 = (bf16[64,2176]{1,0:T(8,128)(2,1)S(1)}, bf16[64,2176]{1,0:T(8,128)(2,1)S(1)}, u32[]{:S(2)}, u32[]{:S(2)}) collective-permute-start(bf16[64,2176]{1,0:T(8,128)(2,1)S(1)} %get-tuple-element.75), channel_id=1, source_target_pairs={{0,3},{1,0},{2,1},{3,2},{4,7},{5,4},{6,5},{7,6},{8,11},{9,8},{10,9... | collective-permute-start | bytes 835592 | tf_op jit(solution)/shard_map/ppermute | solution.py:476
  114.6 25.6 %collective-permute-start.22 = (bf16[64,2176]{1,0:T(8,128)(2,1)S(1)}, bf16[64,2176]{1,0:T(8,128)(2,1)S(1)}, u32[]{:S(2)}, u32[]{:S(2)}) collective-permute-start(bf16[64,2176]{1,0:T(8,128)(2,1)S(1)} %get-tuple-element.73), channel_id=1, source_target_pairs={{0,2},{1,3},{2,0},{3,1},{4,6},{5,7},{6,4},{7,5},{8,10},{9,11},{10,... | collective-permute-start | bytes 835592 | tf_op jit(solution)/shard_map/ppermute | solution.py:476
  115.4 24.9 %collective-permute-start.21 = (bf16[64,2176]{1,0:T(8,128)(2,1)S(1)}, bf16[64,2176]{1,0:T(8,128)(2,1)S(1)}, u32[]{:S(2)}, u32[]{:S(2)}) collective-permute-start(bf16[64,2176]{1,0:T(8,128)(2,1)S(1)} %get-tuple-element.71), channel_id=1, source_target_pairs={{0,1},{1,2},{2,3},{3,0},{4,5},{5,6},{6,7},{7,4},{8,9},{9,10},{10,1... | collective-permute-start | bytes 835592 | tf_op jit(solution)/shard_map/ppermute | solution.py:476
  140.3 21.2 %collective-permute-start.27 = (bf16[64,2176]{1,0:T(8,128)(2,1)S(1)}, bf16[64,2176]{1,0:T(8,128)(2,1)S(1)}, u32[]{:S(2)}, u32[]{:S(2)}) collective-permute-start(bf16[64,2176]{1,0:T(8,128)(2,1)S(1)} %get-tuple-element.84), channel_id=1, source_target_pairs={{0,1},{1,2},{2,3},{3,0},{4,5},{5,6},{6,7},{7,4},{8,9},{9,10},{10,1... | collective-permute-start | bytes 835592 | tf_op jit(solution)/shard_map/ppermute | solution.py:476
  140.3 22.1 %collective-permute-start.28 = (bf16[64,2176]{1,0:T(8,128)(2,1)S(1)}, bf16[64,2176]{1,0:T(8,128)(2,1)S(1)}, u32[]{:S(2)}, u32[]{:S(2)}) collective-permute-start(bf16[64,2176]{1,0:T(8,128)(2,1)S(1)} %get-tuple-element.85), channel_id=1, source_target_pairs={{0,2},{1,3},{2,0},{3,1},{4,6},{5,7},{6,4},{7,5},{8,10},{9,11},{10,... | collective-permute-start | bytes 835592 | tf_op jit(solution)/shard_map/ppermute | solution.py:476
  142.2 20.3 %collective-permute-start.29 = (bf16[64,2176]{1,0:T(8,128)(2,1)S(1)}, bf16[64,2176]{1,0:T(8,128)(2,1)S(1)}, u32[]{:S(2)}, u32[]{:S(2)}) collective-permute-start(bf16[64,2176]{1,0:T(8,128)(2,1)S(1)} %get-tuple-element.86), channel_id=1, source_target_pairs={{0,3},{1,0},{2,1},{3,2},{4,7},{5,4},{6,5},{7,6},{8,11},{9,8},{10,9... | collective-permute-start | bytes 835592 | tf_op jit(solution)/shard_map/ppermute | solution.py:476
  147.5 4.9 %collective-permute-start.24 = (bf16[16,3584]{1,0:T(8,128)(2,1)S(1)}, bf16[16,3584]{1,0:T(8,128)(2,1)S(1)}, u32[]{:S(2)}, u32[]{:S(2)}) collective-permute-start(bf16[16,3584]{1,0:T(8,128)(2,1)S(1)} %down_part.1.refs_0_), channel_id=1, source_target_pairs={{0,8},{4,12},{8,0},{12,4},{1,9},{5,13},{9,1},{13,5},{2,10},{6,14},... | collective-permute-start | bytes 344072 | tf_op jit(solution)/shard_map/ppermute | solution.py:512
  152.0 7.3 %collective-permute-start.25 = (bf16[16,3584]{1,0:T(8,128)(2,1)S(1)}, bf16[16,3584]{1,0:T(8,128)(2,1)S(1)}, u32[]{:S(2)}, u32[]{:S(2)}) collective-permute-start(bf16[16,3584]{1,0:T(8,128)(2,1)S(1)} %down_part.1.refs_0_), channel_id=1, source_target_pairs={{0,4},{4,0},{8,12},{12,8},{1,5},{5,1},{9,13},{13,9},{2,6},{6,2},{1... | collective-permute-start | bytes 344072 | tf_op jit(solution)/shard_map/ppermute | solution.py:514
  152.3 7.0 %collective-permute-start.26 = (bf16[16,3584]{1,0:T(8,128)(2,1)S(1)}, bf16[16,3584]{1,0:T(8,128)(2,1)S(1)}, u32[]{:S(2)}, u32[]{:S(2)}) collective-permute-start(bf16[16,3584]{1,0:T(8,128)(2,1)S(1)} %collective-permute-done.24.refs_1_), channel_id=1, source_target_pairs={{0,4},{4,0},{8,12},{12,8},{1,5},{5,1},{9,13},{13,9},{2,6},{6,2},{1... | collective-permute-start | bytes 344072 | tf_op jit(solution)/shard_map/ppermute | solution.py:514
  (29 other events, 208.5 us)
